TPU v7x, 512 devices: a whole 4x4x16 slice. The times are simulated.
512 devices in a mesh: lon: 128 (over x_lo, y, z), lat: 4 (over x_hi, core).
Axes of the slice: x: 4 (x_hi: 2, x_lo: 2; x = x_hi * 2 + x_lo), y: 4, z: 16, core: 2. Of those that a mesh axis runs over, the one named last changes fastest.
Arguments:
- y_block: bfloat16 [2, 24, 1536, 768], P(None, 'lat', 'lon'), may hold values from -6 to 6
- merge_gain: float32 [3072], replicated, may hold values from 0.25 to 1.75
- merge_weight: bfloat16 [3072, 1536], P('lon'), may hold values from -0.109375 to 0.109375
- d_merged: bfloat16 [2, 12, 768, 1536], P(None, 'lat', 'lon'), may hold values from -6 to 6
- q_proj: bfloat16 [2, 24, 1536, 768], P(None, 'lat', 'lon'), may hold values from -8 to 8
- k_proj: bfloat16 [2, 24, 1536, 768], P(None, 'lat', 'lon'), may hold values from -8 to 8
- v_proj: bfloat16 [2, 24, 1536, 768], P(None, 'lat', 'lon'), may hold values from -6 to 6
- bias_table: float32 [4, 24, 3312], P('lat'), may hold values from -5 to 5
Outputs:
- q_grad: bfloat16 [2, 24, 1536, 768], P(None, 'lat', 'lon')
- k_grad: bfloat16 [2, 24, 1536, 768], P(None, 'lat', 'lon')
- v_grad: bfloat16 [2, 24, 1536, 768], P(None, 'lat', 'lon')
- table_grad: float32 [4, 24, 3312], P('lat')
All inputs are finite; a program needn't handle non-finite values.
Results may differ from a plain program's by a relative error of at most 0.011.
Values may be sent and summed in bfloat16 or wider, within the bound.
No kernel may reach another device: no remote copies, remote signals or barrier semaphores. Data moves between devices by JAX's collectives and lax.ppermute only.
A program may use at most 128 MiB of HBM per device.

v0:
```python
import jax
import jax.numpy as jnp
from jax import lax
from jax.sharding import PartitionSpec as P

score_factor = 32 ** (-0.5)


def from_behind(shard, axis, by):
    size = lax.axis_size(axis)
    return lax.ppermute(shard, axis, [(i, (i + by) % size) for i in range(size)])


def window_layout():
    tokens = jnp.arange(144, dtype=jnp.int32)
    level = tokens // 72
    row_in = tokens // 12 % 6
    column = tokens % 12
    index = (
        ((level[:, None] * 2 + level[None, :]) * 36 + row_in[:, None] * 6 + row_in[None, :]) * 23
        + column[:, None]
        - column[None, :]
        + 11
    )
    return (index.reshape(-1), row_in)


def expand_bias(bias_table, positions):
    kinds, heads, _ = bias_table.shape
    return bias_table[:, :, positions].reshape(kinds, heads, 144, 144)


def table_entries(d_bias, positions, entries):
    kinds, heads = (d_bias.shape[0], d_bias.shape[1])
    return (
        jnp.zeros((kinds, heads, entries), jnp.float32)
        .at[:, :, positions]
        .add(d_bias.reshape(kinds, heads, -1))
    )


def window_grads(q_win, k_win, v_win, o_win, bias, allowed):
    batch, count, width = q_win.shape
    heads = width // 32
    shape_four = (batch, count, heads, 32)
    q_heads = q_win.reshape(shape_four)
    k_heads = k_win.reshape(shape_four)
    v_heads = v_win.reshape(shape_four)
    o_heads = o_win.reshape(shape_four)
    scores = (
        jnp.einsum("bihd,bjhd->bhij", q_heads, k_heads, preferred_element_type=jnp.float32)
        * score_factor
        + bias[None]
    )
    scores = jnp.where(allowed[None, None], scores, -jnp.inf)
    row_max = jnp.max(scores, axis=-1, keepdims=True)
    expon = jnp.exp(scores - row_max)
    probs = expon / jnp.sum(expon, axis=-1, keepdims=True)
    probs_low = probs.astype(jnp.bfloat16)
    d_probs = jnp.einsum("bihd,bjhd->bhij", o_heads, v_heads, preferred_element_type=jnp.float32)
    delta_sum = jnp.sum(probs * d_probs, axis=-1, keepdims=True)
    d_scores = probs * (d_probs - delta_sum)
    d_low = d_scores.astype(jnp.bfloat16)
    v_grad = jnp.einsum("bhij,bihd->bjhd", probs_low, o_heads, preferred_element_type=jnp.float32)
    q_grad = (
        jnp.einsum("bhij,bjhd->bihd", d_low, k_heads, preferred_element_type=jnp.float32)
        * score_factor
    )
    k_grad = (
        jnp.einsum("bhij,bihd->bjhd", d_low, q_heads, preferred_element_type=jnp.float32)
        * score_factor
    )
    final_shape = (batch, count, width)
    return (
        q_grad.reshape(final_shape).astype(jnp.bfloat16),
        k_grad.reshape(final_shape).astype(jnp.bfloat16),
        v_grad.reshape(final_shape).astype(jnp.bfloat16),
        jnp.sum(d_scores, axis=0),
    )


def merge_backward(y_block, merge_gain, d_norm_flat):
    levels, rows, cols, width = y_block.shape
    stacked = y_block.reshape(levels, rows // 2, 2, cols // 2, 2, width).transpose(0, 1, 3, 4, 2, 5)
    stacked = stacked.reshape(levels, rows // 2, cols // 2, 4 * width).astype(jnp.float32)
    mean_value = jnp.mean(stacked, axis=-1, keepdims=True)
    centred = stacked - mean_value
    variance = jnp.mean(centred * centred, axis=-1, keepdims=True)
    inverse = lax.rsqrt(variance + 1e-05)
    normed = centred * inverse
    d_hat = d_norm_flat.reshape(normed.shape) * merge_gain
    d_stack = (
        d_hat
        - jnp.mean(d_hat, axis=-1, keepdims=True)
        - normed * jnp.mean(d_hat * normed, axis=-1, keepdims=True)
    ) * inverse
    back = d_stack.reshape(levels, rows // 2, cols // 2, 2, 2, width).transpose(0, 1, 4, 2, 3, 5)
    return back.reshape(levels, rows, cols, width).astype(jnp.bfloat16)


def to_windows(field):
    levels, rows, cols, width = field.shape
    cut = field.reshape(levels, rows // 6, 6, cols // 12, 12, width).transpose(1, 3, 0, 2, 4, 5)
    return cut.reshape(rows // 6, cols // 12, 144, width)


def from_windows(windows, levels):
    kinds, count, _, width = windows.shape
    grid = windows.reshape(kinds, count, levels, 6, 12, width).transpose(2, 0, 3, 1, 4, 5)
    return grid.reshape(levels, kinds * 6, count * 12, width)


def on_device(y_block, merge_gain, merge_weight, d_merged, q_proj, k_proj, v_proj, bias_table):
    flat_grad = d_merged.reshape(-1, d_merged.shape[-1])
    d_norm_flat = lax.dot_general(
        flat_grad,
        lax.all_gather(merge_weight, "lon", axis=0, tiled=True),
        (((1,), (1,)), ((), ())),
        preferred_element_type=jnp.float32,
    )
    d_out = merge_backward(y_block, merge_gain, d_norm_flat)
    eastern = from_behind(
        (q_proj[:, :, :6], k_proj[:, :, :6], v_proj[:, :, :6], d_out[:, :, :6]), "lon", -1
    )
    across = [
        jnp.concatenate([source[:, :, 6:], arrived], axis=2)
        for source, arrived in zip((q_proj, k_proj, v_proj, d_out), eastern)
    ]
    northern = from_behind(
        (across[0][:, :3], across[1][:, :3], across[2][:, :3], across[3][:, :3]), "lat", -1
    )
    rolled = [
        jnp.concatenate([source[:, 3:], arrived], axis=1)
        for source, arrived in zip(across, northern)
    ]
    levels = q_proj.shape[0]
    local_types = q_proj.shape[1] // 6
    positions, row_in = window_layout()
    upper = row_in >= 3
    same_group = upper[:, None] == upper[None, :]
    type_ids = lax.axis_index("lat") * local_types + jnp.arange(local_types, dtype=jnp.int32)
    last_type = local_types * lax.axis_size("lat") - 1
    allowed = jnp.logical_or(same_group[None], (type_ids != last_type)[:, None, None])
    bias = expand_bias(bias_table, positions)
    grads = jax.vmap(window_grads)(
        to_windows(rolled[0]),
        to_windows(rolled[1]),
        to_windows(rolled[2]),
        to_windows(rolled[3]),
        bias,
        allowed,
    )
    entries = bias_table.shape[2]
    summed_bias = lax.psum(grads[3], "lon")
    table_grad = table_entries(summed_bias, positions, entries)
    grids = [
        from_windows(grads[0], levels),
        from_windows(grads[1], levels),
        from_windows(grads[2], levels),
    ]
    southern = from_behind((grids[0][:, -3:], grids[1][:, -3:], grids[2][:, -3:]), "lat", 1)
    lat_fixed = [
        jnp.concatenate([arrived, source[:, :-3]], axis=1)
        for source, arrived in zip(grids, southern)
    ]
    western = from_behind(
        (lat_fixed[0][:, :, -6:], lat_fixed[1][:, :, -6:], lat_fixed[2][:, :, -6:]), "lon", 1
    )
    finished = [
        jnp.concatenate([arrived, source[:, :, :-6]], axis=2)
        for source, arrived in zip(lat_fixed, western)
    ]
    return (finished[0], finished[1], finished[2], table_grad)


def solution(mesh):
    placed = (
        P(None, "lat", "lon", None),
        P(),
        P("lon", None),
        P(None, "lat", "lon", None),
        P(None, "lat", "lon", None),
        P(None, "lat", "lon", None),
        P(None, "lat", "lon", None),
        P("lat", None, None),
    )
    return jax.shard_map(
        on_device,
        mesh=mesh,
        in_specs=placed,
        out_specs=(
            P(None, "lat", "lon", None),
            P(None, "lat", "lon", None),
            P(None, "lat", "lon", None),
            P("lat", None, None),
        ),
        check_vma=False,
    )
```

profile of v0, /device:TPU:6, one launch (start us, length us, event | category | flops | bytes accessed | tf_op | source)
XLA Modules:
  0.0 1981.5 jit_solution(9537546176183283013)
XLA Ops:
  8.0 1.8 fusion.48
  9.8 14.1 collective-permute-start.2
  23.9 1.8 fusion.51
  25.7 2.9 collective-permute-start
  28.6 1.8 fusion.49
  30.4 2.9 collective-permute-start.6
  33.9 1.1 convert.5
  37.2 1.3 reshape.355
  39.0 38.7 %gather_fusion = f32[20736,24]{1,0:T(8,128)} fusion(f32[24,3312]{0,1:T(8,128)S(1)} %bitcast.57, s32[21504]{0:T(1024)S(1)} %pad_clamp_fusion), kind=kCustom, calls=%fused_computation | custom fusion | bytes 4064256 | tf_op jit(solution)/shard_map/gather | solution.py:30
  77.7 12.0 copy.101
  89.7 1.2 fusion.36
  90.9 1.9 collective-permute-start.3
  92.9 1.2 fusion.37
  94.1 3.1 collective-permute-start.1
  97.2 1.9 fusion.35
  99.1 3.1 collective-permute-start.7
  104.3 2.5 reshape.347
  106.8 2.4 copy.114
  109.2 2.5 reshape.348
  111.7 2.4 copy.97
  114.1 3.6 add_select_fusion
  117.7 502.4 %all-gather.2.cloned.1.call-done = bf16[3072,1536]{1,0:T(8,128)(2,1)} async-done(((bf16[24,1536]{1,0:T(8,128)(2,1)}), bf16[3072,1536]{1,0:T(8,128)(2,1)}) %all-gather.2.cloned.1.call-update) | async-done | bytes 9437200 | tf_op jit(solution)/shard_map/all_gather | solution.py:117
  620.1 7.0 fusion.44
  628.0 1.8 reshape.386
  629.8 1.1 copy.109
  631.1 5.8 collective-permute-start.4
  637.0 3.1 fusion.52
  640.0 1.0 fusion.34
  641.0 2.3 collective-permute-start.5
  643.3 1.2 pad_maximum_fusion.5
  645.2 2.5 reshape.350
  647.8 1.2 pad_maximum_fusion.6
  649.7 2.6 reshape.349
  652.3 2.4 copy.112
  654.8 2.1 multiply_reduce_fusion
  658.0 3.4 copy.123
  661.4 5.1 reshape.351
  666.5 4.9 fusion.13
  671.3 2.3 copy.122
  673.7 2.5 convert_element_type.105
  676.1 1.7 fusion.45
  677.9 2.4 collective-permute-start.12
  680.3 2.1 fusion.17
  682.4 2.3 copy.116
  684.7 2.5 convert_element_type.96
  687.2 1.7 fusion.47
  688.9 3.5 collective-permute-start.8
  692.4 2.4 fusion.16
  694.9 1.5 copy.119
  697.0 2.4 collective-permute-start.10
  699.4 1.1 fusion.28
  700.5 1.9 collective-permute-start.13
  702.4 1.1 fusion.30
  703.5 1.9 collective-permute-start.9
  705.5 1.9 collective-permute-start.11
  707.4 5.6 collective-permute-done.13
  713.0 1.1 fusion.25
  715.1 1.5 collective-permute-done.9
  716.6 1.0 fusion.27
  718.5 1.3 collective-permute-done.11
  720.8 1132.8 %all-reduce.2.cloned.1.call-done = f32[1,24,20736]{2,1,0:T(8,128)} async-done(((f32[1,24,20736]{2,1,0:T(8,128)}), f32[1,24,20736]{2,1,0:T(8,128)}) %all-reduce.2.cloned.1.call-update) | async-done | bytes 1990672 | tf_op jit(solution)/shard_map/psum | solution.py:154
  1853.6 7.0 copy.124
  1860.6 112.8 %scatter_custom_fusion = f32[24,3312]{0,1:T(8,128)S(1)} fusion(s32[20736]{0:T(1024)} %copy-done.7, f32[20736,24]{1,0:T(8,128)} %copy.124, f32[]{:T(128)} %constant.68.clone.1), kind=kCustom, calls=%fused_computation.25 | custom fusion | flops 497664 | bytes 318464 | tf_op jit(solution)/shard_map/scatter-add | solution.py:38
  1973.4 1.2 copy.128
  (71 shorter events, 13.4 us)
Async XLA Ops:
  7.2 29.9 %copy-start.5 = (bf16[2,6,12,768]{3,0,2,1:T(2,128)(2,1)S(1)}, bf16[2,6,12,768]{3,0,2,1:T(2,128)(2,1)}, u32[]{:S(2)}) copy-start(bf16[2,6,12,768]{3,0,2,1:T(2,128)(2,1)} %param.8) | copy-start | bytes 663556
  7.2 31.3 %copy-start.8 = (f32[1,24,3312]{2,1,0:T(8,128)S(1)}, f32[1,24,3312]{2,1,0:T(8,128)}, u32[]{:S(2)}) copy-start(f32[1,24,3312]{2,1,0:T(8,128)} %param.15) | copy-start | bytes 953860
  7.2 612.9 %all-gather.2.cloned.1.call-start = ((), (), s32[]{:S(2)}) async-start(), calls=%async_computation | async-start | bytes 9510912 | tf_op jit(solution)/shard_map/all_gather | solution.py:117
  7.9 1845.7 %all-reduce.2.cloned.1.call-start = ((), (), s32[]{:S(2)}) async-start(), calls=%async_computation.1 | async-start | bytes 3981312 | tf_op jit(solution)/shard_map/psum | solution.py:154
  9.8 80.0 %collective-permute-start.2 = (bf16[2,6,6,768]{3,0,2,1:T(2,128)(2,1)}, bf16[2,6,6,768]{3,0,2,1:T(2,128)(2,1)}, u32[]{:S(2)}, u32[]{:S(2)}) collective-permute-start(bf16[2,6,6,768]{3,0,2,1:T(2,128)(2,1)} %get-tuple-element.31), channel_id=1, source_target_pairs={{0,508},{4,0},{8,4},{12,8},{16,12},{20,16},{24,20},{28,24},{32,28}... | collective-permute-start | bytes 331784 | tf_op jit(solution)/shard_map/ppermute | solution.py:11
  25.7 67.2 %collective-permute-start = (bf16[2,6,6,768]{3,0,2,1:T(2,128)(2,1)}, bf16[2,6,6,768]{3,0,2,1:T(2,128)(2,1)}, u32[]{:S(2)}, u32[]{:S(2)}) collective-permute-start(bf16[2,6,6,768]{3,0,2,1:T(2,128)(2,1)} %get-tuple-element.43), channel_id=1, source_target_pairs={{0,508},{4,0},{8,4},{12,8},{16,12},{20,16},{24,20},{28,24},{32,28}... | collective-permute-start | bytes 331784 | tf_op jit(solution)/shard_map/ppermute | solution.py:11
  30.4 66.8 %collective-permute-start.6 = (bf16[2,6,6,768]{3,0,2,1:T(2,128)(2,1)}, bf16[2,6,6,768]{3,0,2,1:T(2,128)(2,1)}, u32[]{:S(2)}, u32[]{:S(2)}) collective-permute-start(bf16[2,6,6,768]{3,0,2,1:T(2,128)(2,1)} %get-tuple-element.35), channel_id=1, source_target_pairs={{0,508},{4,0},{8,4},{12,8},{16,12},{20,16},{24,20},{28,24},{32,28}... | collective-permute-start | bytes 331784 | tf_op jit(solution)/shard_map/ppermute | solution.py:11
  36.3 0.9 copy-start.7
  90.9 11.3 collective-permute-start.3
  94.1 9.2 collective-permute-start.1
  99.1 544.2 %collective-permute-start.7 = (bf16[2,3,12,768]{3,0,2,1:T(2,128)(2,1)}, bf16[2,3,12,768]{3,0,2,1:T(2,128)(2,1)}, u32[]{:S(2)}, u32[]{:S(2)}) collective-permute-start(bf16[2,3,12,768]{3,0,2,1:T(2,128)(2,1)} %get-tuple-element.33), channel_id=1, source_target_pairs={{0,3},{1,0},{2,1},{3,2},{4,7},{5,4},{6,5},{7,6},{8,11},{9,8},{10,9... | collective-permute-start | bytes 331784 | tf_op jit(solution)/shard_map/ppermute | solution.py:11
  620.1 7.0 copy-start.3
  620.1 16.8 copy-start
  631.1 12.2 copy-start.6
  631.1 8.9 collective-permute-start.4
  640.0 14.7 copy-start.1
  641.0 6.7 collective-permute-start.5
  654.8 2.4 copy-start.2
  654.8 2.4 copy-start.9
  677.9 21.6 %collective-permute-start.12 = (bf16[2,3,12,768]{3,2,1,0:T(8,128)(2,1)}, bf16[2,3,12,768]{3,2,1,0:T(8,128)(2,1)}, u32[]{:S(2)}, u32[]{:S(2)}) collective-permute-start(bf16[2,3,12,768]{3,2,1,0:T(8,128)(2,1)} %get-tuple-element.22), channel_id=1, source_target_pairs={{0,1},{1,2},{2,3},{3,0},{4,5},{5,6},{6,7},{7,4},{8,9},{9,10},{10,1... | collective-permute-start | bytes 331784 | tf_op jit(solution)/shard_map/ppermute | solution.py:11
  688.9 13.5 collective-permute-start.8
  694.9 21.7 %copy-start.4 = (bf16[2,3,12,768]{3,2,1,0:T(8,128)(2,1)S(1)}, bf16[2,3,12,768]{3,2,1,0:T(8,128)(2,1)}, u32[]{:S(2)}) copy-start(bf16[2,3,12,768]{3,2,1,0:T(8,128)(2,1)} %get-tuple-element.27) | copy-start | bytes 331780
  697.0 8.4 collective-permute-start.10
  700.5 12.6 collective-permute-start.13
  703.5 13.1 collective-permute-start.9
  705.5 14.3 collective-permute-start.11
Sparse Core Ops, SparseCore 0:
  10.1 609.9 all-gather.1
  666.6 1186.9 all-reduce.1
where the time goes:
time: 1980 us
  waiting for transfers between devices  1640 us (83%)
  other arithmetic  133 us (7%)
  local copies, waits for them, and re-layouts  117 us (6%)
  starting transfers between devices  50.3 us (3%)
  matrix products  22 us (1%)
    psum x1, waiting for transfers between devices, on_device(): summed_bias = lax.psum(grads[3], 'lon')  1130 us
    all_gather x1, waiting for transfers between devices, on_device(): lax.all_gather(merge_weight, 'lon', axis=0, tiled=True)  502 us
    scatter-add x1, other arithmetic, table_entries(): return jnp.zeros((kinds, heads, entries), jnp.float32).at[:, :, positions...  113 us
    ppermute x14, starting transfers between devices, from_behind(): lax.ppermute(shard, axis, [(i, (i + by) % size) for i in range(size)])  50.2 us
  transfers between devices with their start and end apart: 16, of which 5 were waited for; matrix products, arithmetic and copies ran while one was open for 7% of the time, Pallas kernels for 0%

commit v1 on v0

v1 whole, which is shorter than its diff:
```python
import jax
import jax.numpy as jnp
import numpy as np
from jax import lax
from jax.experimental import pallas as pl
from jax.experimental.pallas import tpu as pltpu
from jax.sharding import PartitionSpec as P

NX, NY, NZ = 2, 4, 16
LAT = 4
HEADS = 24
ROWS = 12
PAD = 16
TOK = ROWS * PAD
SEG = 32
WIDE = ROWS * SEG
GROUPS = 6
LOW = -1e30
VMEM = 56 * 1024 * 1024
score_factor = 32 ** (-0.5)

z_groups = [[a * NZ + z for z in range(NZ)] for a in range(NX * NY)]
y_groups = [[(x * NY + y) * NZ + z for y in range(NY)] for x in range(NX) for z in range(NZ)]
xy_groups = [[a * NZ + z for a in range(NX * NY)] for z in range(NZ)]
x_lat_groups = [
    [(x * NY * NZ + b) * LAT + l for x in range(NX) for l in range(LAT)] for b in range(NY * NZ)
]


def layout_constants():
    tokens = np.arange(TOK)
    row, col = tokens // PAD, tokens % PAD
    real = col < 12
    sums = np.zeros((TOK, WIDE), np.float32)
    sums[tokens[real], (row * SEG + 11 - col)[real]] = 1
    spread = np.zeros((WIDE, TOK), np.float32)
    spread[(row * SEG + 11 + col)[real], tokens[real]] = 1
    quarter = np.zeros((256, 256), np.float32)
    back = np.zeros((TOK, 256), np.float32)
    for level in range(2):
        for pr in range(4):
            for pc in range(6):
                for di in range(2):
                    for dj in range(2):
                        spot = (di + 2 * dj) * 64 + (level * 4 + pr) * 8 + pc
                        fine_row, fine_col = 2 * pr + di, 2 * pc + dj
                        quarter[spot, (level * 8 + fine_row) * PAD + fine_col] = 1
                        if 1 <= fine_row <= 6:
                            back[(level * 6 + fine_row - 1) * PAD + fine_col, spot] = 1
    order = np.zeros((384, 384), np.float32)
    for l in range(3):
        for z in range(NZ):
            for i in range(8):
                order[l * 128 + z * 8 + i, z * 24 + l * 8 + i] = 1
    return [jnp.asarray(a, jnp.bfloat16) for a in (sums, spread, quarter, back, order)]


def dot(a, b, dims=((1,), (0,))):
    return lax.dot_general(a, b, (dims, ((), ())), preferred_element_type=jnp.float32)


def head_mask(h):
    lanes = lax.broadcasted_iota(jnp.int32, (1, 128), 1)
    return (lanes // 32) == h


def by_head(block):
    return jnp.concatenate(
        [jnp.where(head_mask(h), block, jnp.zeros_like(block)) for h in range(4)], axis=0
    )


def probs_kernel(qkv_ref, table_ref, spread_ref, mask_ref, p_ref):
    table = table_ref[0]
    wide = jnp.broadcast_to(table[:, None, :], (4 * ROWS, PAD, WIDE))
    wide = jnp.concatenate(
        [
            pltpu.roll(wide[:, :, s * 128 : (s + 1) * 128], 0, 2, stride=1, stride_axis=1)
            for s in range(3)
        ],
        axis=2,
    ).reshape(4 * TOK, WIDE)
    high = wide.astype(jnp.bfloat16)
    low = (wide - high.astype(jnp.float32)).astype(jnp.bfloat16)
    bias = dot(high, spread_ref[...]) + dot(low, spread_ref[...])
    scores = dot(by_head(qkv_ref[0]), qkv_ref[1], ((1,), (1,))) * score_factor + bias
    scores = (scores.reshape(4, TOK, TOK) + mask_ref[...][None]).reshape(4 * TOK, TOK)
    expon = jnp.exp(scores - jnp.max(scores, axis=-1, keepdims=True))
    p_ref[0] = expon / jnp.sum(expon, axis=-1, keepdims=True)


def norm_kernel(y_ref, quarter_ref, normed_ref, inverse_ref):
    fields = dot(quarter_ref[...], y_ref[...])
    parts = [fields[q * 64 : (q + 1) * 64] for q in range(4)]
    mean = jnp.sum(parts[0] + parts[1] + parts[2] + parts[3], axis=-1, keepdims=True) / 3072
    parts = [part - mean for part in parts]
    squares = [part * part for part in parts]
    variance = (
        jnp.sum(squares[0] + squares[1] + squares[2] + squares[3], axis=-1, keepdims=True) / 3072
    )
    inverse = lax.rsqrt(variance + 1e-05)
    for q in range(4):
        normed_ref[q] = parts[q] * inverse
    inverse_ref[...] = jnp.broadcast_to(inverse, (64, 128))


def merge_kernel(x_ref, w_ref, out_ref, acc_ref):
    acc_ref[...] = dot(x_ref[...], w_ref[...], ((1,), (1,)))
    for x in range(NX):
        for l in range(LAT):
            for level in range(2):
                own = ((x * LAT + l) * 6 + level * 3) * 8
                below = ((x * LAT + (l + 1) % LAT) * 6 + level * 3) * 8
                out_ref[x * LAT + l, level * 32 : level * 32 + 16] = acc_ref[
                    own + 8 : own + 24
                ].astype(jnp.bfloat16)
                out_ref[x * LAT + l, level * 32 + 16 : level * 32 + 32] = acc_ref[
                    below : below + 16
                ].astype(jnp.bfloat16)


def grads_kernel(
    recv_ref,
    order_ref,
    normed_ref,
    inverse_ref,
    gain_ref,
    back_ref,
    sums_ref,
    qkv_ref,
    p_ref,
    grads_ref,
    table_ref,
    o_ref,
    sum_ref,
):
    g = pl.program_id(0)

    @pl.when(g == 0)
    def _():
        pieces = [
            jnp.concatenate(
                [recv_ref[x * LAT + l, :, y * 128 : (y + 1) * 128] for l in range(3)], axis=1
            )
            for x in range(NX)
            for y in range(NY)
        ]
        d_norm = dot(jnp.concatenate(pieces, axis=0), order_ref[...])
        hats = []
        for q in range(4):
            left = d_norm[(2 * q) * 64 : (2 * q + 1) * 64]
            right = d_norm[(2 * q + 1) * 64 : (2 * q + 2) * 64]
            hats.append(jnp.concatenate([left, right], axis=1) * gain_ref[q])
        mean = jnp.sum(hats[0] + hats[1] + hats[2] + hats[3], axis=-1, keepdims=True) / 3072
        cross = [hats[q] * normed_ref[q] for q in range(4)]
        along = jnp.sum(cross[0] + cross[1] + cross[2] + cross[3], axis=-1, keepdims=True) / 3072
        inverse = inverse_ref[:, 0:1]
        stack = [(hats[q] - mean - normed_ref[q] * along) * inverse for q in range(4)]
        d_out = dot(back_ref[...], jnp.concatenate(stack, axis=0).astype(jnp.bfloat16))
        d_out = d_out.astype(jnp.bfloat16)
        for s in range(GROUPS):
            o_ref[s] = d_out[:, s * 128 : (s + 1) * 128]

    o_win = o_ref[g]
    q_win, k_win, v_win = qkv_ref[0], qkv_ref[1], qkv_ref[2]
    probs = p_ref[0]
    d_probs = dot(by_head(o_win), v_win, ((1,), (1,)))
    delta = jnp.sum(probs * d_probs, axis=-1, keepdims=True)
    d_low = (probs * (d_probs - delta)).astype(jnp.bfloat16)
    p_low = probs.astype(jnp.bfloat16)

    spread = dot(d_low, sums_ref[...]).reshape(4 * ROWS, PAD, WIDE)
    sums = [
        jnp.sum(
            pltpu.roll(spread[:, :, s * 128 : (s + 1) * 128], 0, 2, stride=1, stride_axis=1), axis=1
        )
        for s in range(3)
    ]
    sum_ref[g] = jnp.concatenate(sums, axis=1)

    q_all = dot(d_low, k_win)
    q_grad = jnp.zeros((TOK, 128), jnp.float32)
    for h in range(4):
        q_grad = jnp.where(head_mask(h), q_all[h * TOK : (h + 1) * TOK], q_grad)
    grads_ref[0] = (q_grad * score_factor).astype(jnp.bfloat16)

    q_turn = q_win.astype(jnp.float32).T.astype(jnp.bfloat16)
    o_turn = o_win.astype(jnp.float32).T.astype(jnp.bfloat16)
    k_parts, v_parts = [], []
    for h in range(4):
        rows = slice(h * 32, (h + 1) * 32)
        k_parts.append(dot(q_turn[rows], d_low[h * TOK : (h + 1) * TOK]))
        v_parts.append(dot(o_turn[rows], p_low[h * TOK : (h + 1) * TOK]))
    k_grad = jnp.concatenate(k_parts, axis=0).T
    v_grad = jnp.concatenate(v_parts, axis=0).T
    grads_ref[1] = (k_grad * score_factor).astype(jnp.bfloat16)
    grads_ref[2] = v_grad.astype(jnp.bfloat16)

    @pl.when(g == GROUPS - 1)
    def _():
        whole = jnp.concatenate([sum_ref[s] for s in range(GROUPS)], axis=0)
        for part in range(8):
            table_ref[part, 0:36] = whole[part * 36 : (part + 1) * 36]
            table_ref[part, 36:40] = jnp.zeros((4, WIDE), jnp.float32)


def whole_spec(shape):
    return pl.BlockSpec(shape, lambda *_: (0,) * len(shape))


def window_probs(qkv, table, spread, mask):
    return pl.pallas_call(
        probs_kernel,
        grid=(GROUPS,),
        in_specs=[
            pl.BlockSpec((3, TOK, 128), lambda g: (0, 0, g)),
            pl.BlockSpec((1, 4 * ROWS, WIDE), lambda g: (g, 0, 0)),
            whole_spec((WIDE, TOK)),
            whole_spec((TOK, TOK)),
        ],
        out_specs=pl.BlockSpec((1, 4 * TOK, TOK), lambda g: (g, 0, 0)),
        out_shape=jax.ShapeDtypeStruct((GROUPS, 4 * TOK, TOK), jnp.float32),
        compiler_params=pltpu.CompilerParams(vmem_limit_bytes=VMEM),
        name="window_probs",
    )(qkv, table, spread, mask)


def normalise(y_rows, quarter):
    return pl.pallas_call(
        norm_kernel,
        out_shape=(
            jax.ShapeDtypeStruct((4, 64, 768), jnp.float32),
            jax.ShapeDtypeStruct((64, 128), jnp.float32),
        ),
        compiler_params=pltpu.CompilerParams(vmem_limit_bytes=VMEM),
        name="normalise",
    )(y_rows, quarter)


def merge_product(rows, weight):
    return pl.pallas_call(
        merge_kernel,
        out_shape=jax.ShapeDtypeStruct((8, 64, 512), jnp.bfloat16),
        scratch_shapes=[pltpu.VMEM((384, 512), jnp.float32)],
        compiler_params=pltpu.CompilerParams(vmem_limit_bytes=VMEM),
        name="merge_product",
    )(rows, weight)


def window_grads(recv, order, normed, inverse, gain, back, sums, qkv, probs):
    return pl.pallas_call(
        grads_kernel,
        grid=(GROUPS,),
        in_specs=[
            whole_spec((8, 64, 512)),
            whole_spec((384, 384)),
            whole_spec((4, 64, 768)),
            whole_spec((64, 128)),
            whole_spec((4, 1, 768)),
            whole_spec((TOK, 256)),
            whole_spec((TOK, WIDE)),
            pl.BlockSpec((3, TOK, 128), lambda g: (0, 0, g)),
            pl.BlockSpec((1, 4 * TOK, TOK), lambda g: (g, 0, 0)),
        ],
        out_specs=(
            pl.BlockSpec((3, TOK, 128), lambda g: (0, 0, g)),
            whole_spec((8, 40, WIDE)),
        ),
        out_shape=(
            jax.ShapeDtypeStruct((3, TOK, 768), jnp.bfloat16),
            jax.ShapeDtypeStruct((8, 40, WIDE), jnp.float32),
        ),
        scratch_shapes=[
            pltpu.VMEM((GROUPS, TOK, 128), jnp.bfloat16),
            pltpu.VMEM((GROUPS, 4 * ROWS, WIDE), jnp.float32),
        ],
        compiler_params=pltpu.CompilerParams(vmem_limit_bytes=VMEM),
        name="window_grads",
    )(recv, order, normed, inverse, gain, back, sums, qkv, probs)


def from_behind(shard, axis, by):
    size = lax.axis_size(axis)
    return lax.ppermute(shard, axis, [(i, (i + by) % size) for i in range(size)])


def swap(shard, axis, groups):
    return lax.all_to_all(shard, axis, 0, 0, tiled=True, axis_index_groups=groups)


def share(shard, count, axis, groups):
    return swap(jnp.broadcast_to(shard[None], (count,) + shard.shape), axis, groups)


def on_device(y_block, merge_gain, merge_weight, d_merged, q_proj, k_proj, v_proj, bias_table):
    sums, spread, quarter, back, order = layout_constants()
    lat = lax.axis_index("lat")

    mine = lax.dynamic_slice_in_dim(merge_weight, jnp.minimum(lat, 2) * 8, 8, axis=0)
    weight = share(mine, NZ, "lon", z_groups).reshape(NZ * 8, -1)
    weight = share(weight, NY, "lon", y_groups).reshape(NY * NZ * 8, -1)

    eastern_d = from_behind(d_merged[:, :, :3], "lon", -1)
    eastern = from_behind(
        jnp.stack([q_proj[:, :, :6], k_proj[:, :, :6], v_proj[:, :, :6], y_block[:, :, :6]]),
        "lon",
        -1,
    )
    d_rows = jnp.concatenate(
        [d_merged[:, :, 3:], eastern_d, jnp.zeros_like(d_merged[:, :, :2])], axis=2
    )
    d_rows = share(d_rows.reshape(48, -1), 8, ("lon", "lat"), x_lat_groups).reshape(384, -1)

    across = jnp.concatenate(
        [
            jnp.stack([q_proj[:, :, 6:], k_proj[:, :, 6:], v_proj[:, :, 6:], y_block[:, :, 6:]]),
            eastern,
            jnp.zeros_like(eastern[:, :, :, :4]),
        ],
        axis=3,
    )
    qkv_south = from_behind(across[:3, :, :3], "lat", -1)
    y_south = from_behind(across[3, :, :4], "lat", -1)
    qkv = jnp.concatenate([across[:3, :, 3:], qkv_south], axis=2).reshape(3, TOK, 768)
    y_rows = jnp.concatenate([across[3, :, 2:], y_south], axis=1).reshape(256, 768)

    table = bias_table.reshape(HEADS, 2, 2, 6, 6, 23).transpose(0, 1, 3, 2, 4, 5)[..., ::-1]
    table = jnp.pad(table, ((0, 0),) * 5 + ((0, SEG - 23),)).reshape(GROUPS, 4 * ROWS, WIDE)
    tokens = jnp.arange(TOK, dtype=jnp.int32)
    upper = tokens // PAD % 6 >= 3
    allowed = jnp.logical_or(upper[:, None] == upper[None, :], lat != LAT - 1)
    allowed = jnp.logical_and(allowed, (tokens % PAD < 12)[None, :])
    mask = jnp.where(allowed, 0.0, LOW)

    probs = window_probs(qkv, table, spread, mask)
    normed, inverse = normalise(y_rows, quarter)

    parts = merge_product(d_rows, weight)
    recv = swap(parts, ("lon", "lat"), x_lat_groups)
    grads, table_part = window_grads(
        recv, order, normed, inverse, merge_gain.reshape(4, 1, 768), back, sums, qkv, probs
    )

    table_part = jnp.sum(swap(table_part, "lon", xy_groups), axis=0).astype(jnp.bfloat16)
    table_part = share(table_part, NZ, "lon", z_groups).astype(jnp.float32)
    table_part = jnp.sum(table_part, axis=0).astype(jnp.bfloat16)
    table_sum = share(table_part, 8, "lon", xy_groups)[:, :36].astype(jnp.float32)
    table_sum = table_sum.reshape(HEADS, 2, 6, 2, 6, SEG)[..., :23].transpose(0, 1, 3, 2, 4, 5)
    table_grad = table_sum.reshape(bias_table.shape)

    grid = grads.reshape(3, 2, 6, PAD, 768)[:, :, :, :12]
    southern = from_behind(grid[:, :, 3:], "lat", 1)
    fixed = jnp.concatenate([southern, grid[:, :, :3]], axis=2)
    western = from_behind(fixed[:, :, :, 6:], "lon", 1)
    finished = jnp.concatenate([western, fixed[:, :, :, :6]], axis=3)
    return (finished[0], finished[1], finished[2], table_grad)


def solution(mesh):
    placed = (
        P(None, "lat", "lon", None),
        P(),
        P("lon", None),
        P(None, "lat", "lon", None),
        P(None, "lat", "lon", None),
        P(None, "lat", "lon", None),
        P(None, "lat", "lon", None),
        P("lat", None, None),
    )
    return jax.shard_map(
        on_device,
        mesh=mesh,
        in_specs=placed,
        out_specs=(
            P(None, "lat", "lon", None),
            P(None, "lat", "lon", None),
            P(None, "lat", "lon", None),
            P("lat", None, None),
        ),
        check_vma=False,
    )
```

time: 1980 us -> 197 us (0.10)
  waiting for transfers between devices: 1640 us -> 53.1 us
  other arithmetic: 133 us -> 8.81 us
  local copies, waits for them, and re-layouts: 117 us -> 24.6 us
  Pallas kernels: 0 us -> 24.5 us
  matrix products: 22 us -> 0 us
  starting transfers between devices: 50.3 us -> 70.4 us
    psum x1 -> x0, waiting for transfers between devices: 1130 us -> none  [on_device(): summed_bias = lax.psum(grads[3], 'lon')]
    all_gather x1 -> x0, waiting for transfers between devices: 502 us -> none  [on_device(): lax.all_gather(merge_weight, 'lon', axis=0, tiled=True)]
    scatter-add x1 -> x0, other arithmetic: 113 us -> none  [table_entries(): return jnp.zeros((kinds, heads, entries), jnp.float32).at[:, :, positions...]
    all_to_all x0 -> x6, waiting for transfers between devices: none -> 43.2 us  [swap(): lax.all_to_all(shard, axis, 0, 0, tiled=True, axis_index_groups=groups)]
    gather x1 -> x0, local copies, waits for them, and re-layouts: 38.7 us -> none  [expand_bias(): return bias_table[:, :, positions].reshape(kinds, heads, 144, 144)]
    all_to_all x0 -> x6, starting transfers between devices: none -> 37.4 us  [swap(): lax.all_to_all(shard, axis, 0, 0, tiled=True, axis_index_groups=groups)]
    another operation x8 -> x2, local copies, waits for them, and re-layouts: 29.3 us -> 1.29 us  [on_device(): jnp.stack([q_proj[:, :, 6:], k_proj[:, :, 6:], v_proj[:, :, 6:], y_block[...]
    pallas_call x0 -> x4, Pallas kernels: none -> 24.5 us  [the longest x1 10.2 us: window_grads(): pl.pallas_call(grads_kernel, grid=(GROUPS,), in_specs=[whole_spec((8, 64,...]
  transfers between devices with their start and end apart: 16 -> 12, of which waited for: 5 -> 7; matrix products, arithmetic and copies ran while one was open for 7% -> 13% of each run, Pallas kernels for 0% -> 7%
where the time goes in v1:
time: 197 us; the launch traced here: 195 us
  starting transfers between devices  70.4 us (36%)
  waiting for transfers between devices  53.1 us (27%)
  local copies, waits for them, and re-layouts  24.6 us (12%)
  Pallas kernels  24.5 us (12%)
  blocking collectives  13.1 us (7%)
  other arithmetic  8.81 us (4%)
    all_to_all x6, waiting for transfers between devices, swap(): lax.all_to_all(shard, axis, 0, 0, tiled=True, axis_index_groups=groups)  43.2 us
    all_to_all x6, starting transfers between devices, swap(): lax.all_to_all(shard, axis, 0, 0, tiled=True, axis_index_groups=groups)  37.4 us
    ppermute x6, starting transfers between devices, from_behind(): lax.ppermute(shard, axis, [(i, (i + by) % size) for i in range(size)])  33.1 us
    all_to_all x1, blocking collectives, swap(): lax.all_to_all(shard, axis, 0, 0, tiled=True, axis_index_groups=groups)  13.1 us
    pallas_call x1, Pallas kernels, window_grads(): pl.pallas_call(grads_kernel, grid=(GROUPS,), in_specs=[whole_spec((8, 64,...  10.2 us
    ppermute x6, waiting for transfers between devices, from_behind(): lax.ppermute(shard, axis, [(i, (i + by) % size) for i in range(size)])  9.86 us
    pallas_call x1, Pallas kernels, window_probs(): pl.pallas_call(probs_kernel, grid=(GROUPS,), in_specs=[pl.BlockSpec((3, T...  8.49 us
    broadcast_in_dim x5, local copies, waits for them, and re-layouts, share(): jnp.broadcast_to(shard[None], (count,) + shard.shape)  4.78 us
  transfers between devices with their start and end apart: 12, of which 7 were waited for; matrix products, arithmetic and copies ran while one was open for 13% of the time, Pallas kernels for 7%

profile of v1, /device:TPU:6, one launch (start us, length us, event | category | flops | bytes accessed | tf_op | source)
XLA Modules:
  0.0 195.5 jit_solution(18426791309236623855)
XLA Ops:
  0.6 0.0 copy-start
  0.6 1.0 fusion.13
  1.6 14.1 %collective-permute-start = (bf16[2,3,3,1536]{3,2,1,0:T(4,128)(2,1)S(1)}, bf16[2,3,3,1536]{3,2,1,0:T(4,128)(2,1)S(1)}, u32[]{:S(2)}, u32[]{:S(2)}) collective-permute-start(bf16[2,3,3,1536]{3,2,1,0:T(4,128)(2,1)S(1)} %copy.39), channel_id=1, source_target_pairs={{0,508},{4,0},{8,4},{12,8},{16,12},{20,16},{24,20},{28,24},{32,28}... | collective-permute-start | bytes 165896 | tf_op jit(solution)/shard_map/ppermute | solution.py:284
  15.8 0.1 pad.23.clone
  15.9 1.8 collective-permute-done
  17.7 0.1 maximum_maximum_fusion.1
  17.8 1.1 broadcast_in_dim.51
  19.0 5.1 %all-to-all-start = ((bf16[8,48,1536]{2,1,0:T(8,128)(2,1)}), bf16[8,48,1536]{2,1,0:T(8,128)(2,1)S(1)}, u32[]{:S(2)}, u32[]{:S(2)}) async-start(bf16[8,48,1536]{2,1,0:T(8,128)(2,1)} %broadcast_in_dim.51), calls=%async_computation | async-start | bytes 2359296 | tf_op jit(solution)/shard_map/all_to_all | solution.py:288
  24.2 14.6 %all-to-all-done = bf16[8,48,1536]{2,1,0:T(8,128)(2,1)S(1)} async-done(((bf16[8,48,1536]{2,1,0:T(8,128)(2,1)}), bf16[8,48,1536]{2,1,0:T(8,128)(2,1)S(1)}, u32[]{:S(2)}, u32[]{:S(2)}) %all-to-all-start) | async-done | bytes 1179680 | tf_op jit(solution)/shard_map/all_to_all | solution.py:288
  38.8 0.8 broadcast_in_dim.52
  39.6 5.0 %all-to-all-start.1 = ((bf16[16,8,1536]{2,1,0:T(8,128)(2,1)}), bf16[16,8,1536]{2,1,0:T(8,128)(2,1)S(1)}, u32[]{:S(2)}, u32[]{:S(2)}) async-start(bf16[16,8,1536]{2,1,0:T(8,128)(2,1)} %broadcast_in_dim.52), calls=%async_computation.1 | async-start | bytes 786432 | tf_op jit(solution)/shard_map/all_to_all | solution.py:288
  44.6 0.0 copy-start.7
  44.6 0.3 slice_bitcast_fusion.6
  45.0 1.0 slice_bitcast_fusion.8
  46.0 1.6 pad_maximum_fusion.1
  47.6 8.1 %collective-permute-start.1 = (bf16[4,2,6,6,768]{4,1,3,2,0:T(2,128)(2,1)}, bf16[4,2,6,6,768]{4,1,3,2,0:T(2,128)(2,1)S(1)}, u32[]{:S(2)}, u32[]{:S(2)}) collective-permute-start(bf16[4,2,6,6,768]{4,1,3,2,0:T(2,128)(2,1)} %pad_maximum_fusion.1), channel_id=1, source_target_pairs={{0,508},{4,0},{8,4},{12,8},{16,12},{20,16},{24,20},{28,24},{32,28}... | collective-permute-start | bytes 1327112 | tf_op jit(solution)/shard_map/ppermute | solution.py:284
  55.7 0.1 pad.16.clone
  55.7 3.0 %reshape.104 = f32[24,2,2,6,6,23]{5,4,3,2,1,0:T(8,128)} reshape(f32[1,24,3312]{2,1,0:T(8,128)S(1)} %copy-done.7) | data formatting | bytes 635904 | tf_op jit(solution)/shard_map/reshape | solution.py:327
  58.7 3.7 %rev.3 = f32[24,2,6,2,6,23]{5,4,2,3,1,0:T(8,128)S(1)} reverse(f32[24,2,6,2,6,23]{5,4,2,3,1,0:T(8,128)} %bitcast.38), dimensions={5} | reverse | bytes 635904 | tf_op jit(solution)/shard_map/rev | solution.py:327
  62.5 0.2 copy.42
  62.7 0.3 pad.4.clone
  62.9 1.5 reshape.105.table_ref
  64.4 3.4 %all-to-all-done.1 = bf16[16,8,1536]{2,1,0:T(8,128)(2,1)S(1)} async-done(((bf16[16,8,1536]{2,1,0:T(8,128)(2,1)}), bf16[16,8,1536]{2,1,0:T(8,128)(2,1)S(1)}, u32[]{:S(2)}, u32[]{:S(2)}) %all-to-all-start.1) | async-done | bytes 393248 | tf_op jit(solution)/shard_map/all_to_all | solution.py:288
  67.9 1.3 broadcast_in_dim.54
  69.2 4.6 %all-to-all-start.2 = ((bf16[4,128,1536]{2,1,0:T(8,128)(2,1)}), bf16[4,128,1536]{2,1,0:T(8,128)(2,1)S(1)}, u32[]{:S(2)}, u32[]{:S(2)}) async-start(bf16[4,128,1536]{2,1,0:T(8,128)(2,1)} %broadcast_in_dim.54), calls=%async_computation.2 | async-start | bytes 3145728 | tf_op jit(solution)/shard_map/all_to_all | solution.py:288
  73.8 1.7 maximum_maximum_fusion
  75.5 0.7 fusion.10
  76.3 1.9 collective-permute-start.3
  78.2 0.3 slice_bitcast_fusion.1
  78.4 3.2 %collective-permute-start.2 = (bf16[2,4,16,768]{3,0,2,1:T(2,128)(2,1)S(1)}, bf16[2,4,16,768]{3,0,2,1:T(2,128)(2,1)}, u32[]{:S(2)}, u32[]{:S(2)}) collective-permute-start(bf16[2,4,16,768]{3,0,2,1:T(2,128)(2,1)S(1)} %get-tuple-element.15), channel_id=1, source_target_pairs={{0,3},{1,0},{2,1},{3,2},{4,7},{5,4},{6,5},{7,6},{8,11},{9,8},{10,9... | collective-permute-start | bytes 589832 | tf_op jit(solution)/shard_map/ppermute | solution.py:284
  81.7 7.7 %all-to-all-done.2 = bf16[4,128,1536]{2,1,0:T(8,128)(2,1)S(1)} async-done(((bf16[4,128,1536]{2,1,0:T(8,128)(2,1)}), bf16[4,128,1536]{2,1,0:T(8,128)(2,1)S(1)}, u32[]{:S(2)}, u32[]{:S(2)}) %all-to-all-start.2) | async-done | bytes 1572896 | tf_op jit(solution)/shard_map/all_to_all | solution.py:288
  89.4 1.2 copy-done.1
  90.5 3.4 %merge_product.1 = bf16[8,64,512]{2,1,0:T(8,128)(2,1)} custom-call(bf16[384,1536]{1,0:T(8,128)(2,1)} %bitcast.42, bf16[512,1536]{1,0:T(8,128)(2,1)} %bitcast.41), custom_call_target="tpu_custom_call" | custom-call | tf_op jit(solution)/shard_map/merge_product/pallas_call | solution.py:241
  93.9 4.8 %all-to-all-start.3 = ((bf16[8,64,512]{2,1,0:T(8,128)(2,1)}), bf16[8,64,512]{2,1,0:T(8,128)(2,1)S(1)}, u32[]{:S(2)}, u32[]{:S(2)}) async-start(bf16[8,64,512]{2,1,0:T(8,128)(2,1)} %merge_product.1), calls=%async_computation.3 | async-start | bytes 1048576 | tf_op jit(solution)/shard_map/all_to_all | solution.py:288
  98.7 0.8 and_select_fusion.mask_ref
  99.5 1.4 pad_maximum_fusion.2
  101.0 0.8 copy.32
  101.7 2.4 %normalise.1 = (f32[4,64,768]{2,1,0:T(8,128)}, f32[64,128]{1,0:T(8,128)}) custom-call(bf16[256,768]{1,0:T(8,128)(2,1)} %bitcast.43, bf16[256,256]{1,0:T(8,128)(2,1)} %constant.78.clone.quarter_ref), custom_call_target="tpu_custom_call" | custom-call | tf_op jit(solution)/shard_map/normalise/pallas_call | solution.py:229
  104.2 1.1 pad_maximum_fusion
  105.3 1.0 copy.33
  106.4 8.5 %window_probs.1.p_ref = f32[6,768,192]{2,1,0:T(8,128)} custom-call(bf16[3,192,768]{2,1,0:T(8,128)(2,1)} %bitcast.39, f32[6,48,384]{2,1,0:T(8,128)} %reshape.105.table_ref, bf16[384,192]{1,0:T(8,128)(2,1)} %constant.77.clone.spread_ref, f32[192,192]{1,0:T(8,128)} %and_select_fusion.mask_ref), custom_call_target="tpu_custom_call" | custom-call | tf_op jit(solution)/shard_map/window_probs/pallas_call | solution.py:212
  114.9 0.8 copy-done.3
  115.7 10.2 %window_grads.1 = (bf16[3,192,768]{2,1,0:T(8,128)(2,1)}, f32[8,40,384]{2,1,0:T(8,128)}) custom-call(bf16[8,64,512]{2,1,0:T(8,128)(2,1)} %copy-done.3, bf16[384,384]{1,0:T(8,128)(2,1)} %constant.80.clone.order_ref, f32[4,64,768]{2,1,0:T(8,128)} %get-tuple-element.8.normed_ref, f32[64,128]{1,0:T(8,128)} %get-tuple-element.9.inverse_ref, ...), custom_call_target="tpu_custom_call" | custom-call | tf_op jit(solution)/shard_map/window_grads/pallas_call | solution.py:251
  125.8 13.1 %all_to_all.35 = f32[8,40,384]{2,1,0:T(8,128)S(1)} all-to-all(f32[8,40,384]{2,1,0:T(8,128)} %get-tuple-element.11), channel_id=1, replica_groups={{0,64,128,192,256,320,384,448},{4,68,132,196,260,324,388,452},{8,72,136..., dimensions={0} | all-to-all | bytes 983040 | tf_op jit(solution)/shard_map/all_to_all | solution.py:288
  139.0 0.8 broadcast_in_dim.58
  139.8 11.5 %all-to-all-start.5 = ((bf16[16,40,384]{2,1,0:T(8,128)(2,1)}), bf16[16,40,384]{2,1,0:T(8,128)(2,1)S(1)}, u32[]{:S(2)}, u32[]{:S(2)}) async-start(bf16[16,40,384]{2,1,0:T(8,128)(2,1)} %broadcast_in_dim.58), calls=%async_computation.5 | async-start | bytes 983040 | tf_op jit(solution)/shard_map/all_to_all | solution.py:288
  151.3 0.1 fusion.11
  151.4 0.3 copy.40
  151.6 1.9 collective-permute-start.4
  153.6 8.0 %collective-permute-done.4 = bf16[3,2,3,12,768]{4,1,3,2,0:T(2,128)(2,1)S(1)} collective-permute-done((bf16[3,2,3,12,768]{4,1,3,2,0:T(2,128)(2,1)S(1)}, bf16[3,2,3,12,768]{4,1,3,2,0:T(2,128)(2,1)S(1)}, u32[]{:S(2)}, u32[]{:S(2)}) %collective-permute-start.4) | collective-permute-done | bytes 331808 | tf_op jit(solution)/shard_map/ppermute | solution.py:284
  161.6 0.2 constant_dynamic-update-slice_fusion
  161.8 0.3 copy_dynamic-update-slice_fusion
  162.1 0.5 fusion.12
  162.6 3.8 %collective-permute-start.5 = (bf16[3,2,6,6,768]{4,1,3,2,0:T(2,128)(2,1)S(1)}, bf16[3,2,6,6,768]{4,1,3,2,0:T(2,128)(2,1)S(1)}, u32[]{:S(2)}, u32[]{:S(2)}) collective-permute-start(bf16[3,2,6,6,768]{4,1,3,2,0:T(2,128)(2,1)S(1)} %get-tuple-element.21), channel_id=1, source_target_pairs={{0,4},{4,8},{8,12},{12,16},{16,20},{20,24},{24,28},{28,32},{32,36}... | collective-permute-start | bytes 995336 | tf_op jit(solution)/shard_map/ppermute | solution.py:284
  166.4 13.3 %all-to-all-done.5 = bf16[16,40,384]{2,1,0:T(8,128)(2,1)S(1)} async-done(((bf16[16,40,384]{2,1,0:T(8,128)(2,1)}), bf16[16,40,384]{2,1,0:T(8,128)(2,1)S(1)}, u32[]{:S(2)}, u32[]{:S(2)}) %all-to-all-start.5) | async-done | bytes 491552 | tf_op jit(solution)/shard_map/all_to_all | solution.py:288
  179.7 0.1 reduce_sum.22
  179.8 0.7 broadcast_in_dim.59
  180.5 6.4 %all-to-all-start.6 = ((bf16[8,40,384]{2,1,0:T(8,128)(2,1)}), bf16[8,40,384]{2,1,0:T(8,128)(2,1)S(1)}, u32[]{:S(2)}, u32[]{:S(2)}) async-start(bf16[8,40,384]{2,1,0:T(8,128)(2,1)} %broadcast_in_dim.59), calls=%async_computation.6 | async-start | bytes 491520 | tf_op jit(solution)/shard_map/all_to_all | solution.py:288
  186.9 1.6 fusion.2
  188.5 4.1 %all-to-all-done.6 = bf16[8,40,384]{2,1,0:T(8,128)(2,1)S(1)} async-done(((bf16[8,40,384]{2,1,0:T(8,128)(2,1)}), bf16[8,40,384]{2,1,0:T(8,128)(2,1)S(1)}, u32[]{:S(2)}, u32[]{:S(2)}) %all-to-all-start.6) | async-done | bytes 245792 | tf_op jit(solution)/shard_map/all_to_all | solution.py:288
  192.6 0.9 reshape.107
  193.5 0.3 convert_bitcast_fusion
  193.8 0.2 copy.37
  194.0 1.5 reshape.111
  (32 shorter events, 0.2 us)
Async XLA Ops:
  0.6 23.5 %copy-start = (bf16[24,1536]{1,0:T(8,128)(2,1)S(1)}, bf16[24,1536]{1,0:T(8,128)(2,1)}, u32[]{:S(2)}) copy-start(bf16[24,1536]{1,0:T(8,128)(2,1)} %param.15) | copy-start | bytes 221188
  1.6 16.1 %collective-permute-start = (bf16[2,3,3,1536]{3,2,1,0:T(4,128)(2,1)S(1)}, bf16[2,3,3,1536]{3,2,1,0:T(4,128)(2,1)S(1)}, u32[]{:S(2)}, u32[]{:S(2)}) collective-permute-start(bf16[2,3,3,1536]{3,2,1,0:T(4,128)(2,1)S(1)} %copy.39), channel_id=1, source_target_pairs={{0,508},{4,0},{8,4},{12,8},{16,12},{20,16},{24,20},{28,24},{32,28}... | collective-permute-start | bytes 165896 | tf_op jit(solution)/shard_map/ppermute | solution.py:284
  19.0 19.8 %all-to-all-start = ((bf16[8,48,1536]{2,1,0:T(8,128)(2,1)}), bf16[8,48,1536]{2,1,0:T(8,128)(2,1)S(1)}, u32[]{:S(2)}, u32[]{:S(2)}) async-start(bf16[8,48,1536]{2,1,0:T(8,128)(2,1)} %broadcast_in_dim.51), calls=%async_computation | async-start | bytes 2359296 | tf_op jit(solution)/shard_map/all_to_all | solution.py:288
  24.1 20.5 %copy-start.8 = (bf16[2,6,12,768]{3,0,2,1:T(2,128)(2,1)S(1)}, bf16[2,6,12,768]{3,0,2,1:T(2,128)(2,1)}, u32[]{:S(2)}) copy-start(bf16[2,6,12,768]{3,0,2,1:T(2,128)(2,1)} %param.13) | copy-start | bytes 663556
  24.1 20.5 %copy-start.9 = (bf16[2,6,12,768]{3,0,2,1:T(2,128)(2,1)S(1)}, bf16[2,6,12,768]{3,0,2,1:T(2,128)(2,1)}, u32[]{:S(2)}) copy-start(bf16[2,6,12,768]{3,0,2,1:T(2,128)(2,1)} %param.19) | copy-start | bytes 663556
  24.1 20.9 %copy-start.10 = (bf16[2,6,12,768]{3,0,2,1:T(2,128)(2,1)S(1)}, bf16[2,6,12,768]{3,0,2,1:T(2,128)(2,1)}, u32[]{:S(2)}) copy-start(bf16[2,6,12,768]{3,0,2,1:T(2,128)(2,1)} %param.18) | copy-start | bytes 663556
  24.1 20.9 %copy-start.11 = (bf16[2,6,12,768]{3,0,2,1:T(2,128)(2,1)S(1)}, bf16[2,6,12,768]{3,0,2,1:T(2,128)(2,1)}, u32[]{:S(2)}) copy-start(bf16[2,6,12,768]{3,0,2,1:T(2,128)(2,1)} %param.17) | copy-start | bytes 663556
  38.8 7.2 %copy-start.2 = (bf16[8,48,1536]{2,1,0:T(8,128)(2,1)}, bf16[8,48,1536]{2,1,0:T(8,128)(2,1)S(1)}, u32[]{:S(2)}) copy-start(bf16[8,48,1536]{2,1,0:T(8,128)(2,1)S(1)} %all-to-all-done) | copy-start | bytes 3538948
  39.6 28.3 %all-to-all-start.1 = ((bf16[16,8,1536]{2,1,0:T(8,128)(2,1)}), bf16[16,8,1536]{2,1,0:T(8,128)(2,1)S(1)}, u32[]{:S(2)}, u32[]{:S(2)}) async-start(bf16[16,8,1536]{2,1,0:T(8,128)(2,1)} %broadcast_in_dim.52), calls=%async_computation.1 | async-start | bytes 786432 | tf_op jit(solution)/shard_map/all_to_all | solution.py:288
  44.6 11.1 %copy-start.7 = (f32[1,24,3312]{2,1,0:T(8,128)S(1)}, f32[1,24,3312]{2,1,0:T(8,128)}, u32[]{:S(2)}) copy-start(f32[1,24,3312]{2,1,0:T(8,128)} %param.20) | copy-start | bytes 953860
  47.6 26.2 %collective-permute-start.1 = (bf16[4,2,6,6,768]{4,1,3,2,0:T(2,128)(2,1)}, bf16[4,2,6,6,768]{4,1,3,2,0:T(2,128)(2,1)S(1)}, u32[]{:S(2)}, u32[]{:S(2)}) collective-permute-start(bf16[4,2,6,6,768]{4,1,3,2,0:T(2,128)(2,1)} %pad_maximum_fusion.1), channel_id=1, source_target_pairs={{0,508},{4,0},{8,4},{12,8},{16,12},{20,16},{24,20},{28,24},{32,28}... | collective-permute-start | bytes 1327112 | tf_op jit(solution)/shard_map/ppermute | solution.py:284
  69.2 4.6 %copy-start.5 = (bf16[1,2,6,6,768]{4,1,3,2,0:T(2,128)(2,1)S(1)}, bf16[1,2,6,6,768]{4,1,3,2,0:T(2,128)(2,1)}, u32[]{:S(2)}) copy-start(bf16[1,2,6,6,768]{4,1,3,2,0:T(2,128)(2,1)} %get-tuple-element.25) | copy-start | bytes 331780
  69.2 4.6 %copy-start.6 = (bf16[1,2,6,6,768]{4,1,3,2,0:T(2,128)(2,1)S(1)}, bf16[1,2,6,6,768]{4,1,3,2,0:T(2,128)(2,1)}, u32[]{:S(2)}) copy-start(bf16[1,2,6,6,768]{4,1,3,2,0:T(2,128)(2,1)} %get-tuple-element.36) | copy-start | bytes 331780
  69.2 20.2 %all-to-all-start.2 = ((bf16[4,128,1536]{2,1,0:T(8,128)(2,1)}), bf16[4,128,1536]{2,1,0:T(8,128)(2,1)S(1)}, u32[]{:S(2)}, u32[]{:S(2)}) async-start(bf16[4,128,1536]{2,1,0:T(8,128)(2,1)} %broadcast_in_dim.54), calls=%async_computation.2 | async-start | bytes 3145728 | tf_op jit(solution)/shard_map/all_to_all | solution.py:288
  76.3 27.9 %collective-permute-start.3 = (bf16[3,2,3,16,768]{4,1,3,2,0:T(2,128)(2,1)S(1)}, bf16[3,2,3,16,768]{4,1,3,2,0:T(2,128)(2,1)S(1)}, u32[]{:S(2)}, u32[]{:S(2)}) collective-permute-start(bf16[3,2,3,16,768]{4,1,3,2,0:T(2,128)(2,1)S(1)} %get-tuple-element.13), channel_id=1, source_target_pairs={{0,3},{1,0},{2,1},{3,2},{4,7},{5,4},{6,5},{7,6},{8,11},{9,8},{10,9... | collective-permute-start | bytes 1327112 | tf_op jit(solution)/shard_map/ppermute | solution.py:284
  78.4 21.1 %collective-permute-start.2 = (bf16[2,4,16,768]{3,0,2,1:T(2,128)(2,1)S(1)}, bf16[2,4,16,768]{3,0,2,1:T(2,128)(2,1)}, u32[]{:S(2)}, u32[]{:S(2)}) collective-permute-start(bf16[2,4,16,768]{3,0,2,1:T(2,128)(2,1)S(1)} %get-tuple-element.15), channel_id=1, source_target_pairs={{0,3},{1,0},{2,1},{3,2},{4,7},{5,4},{6,5},{7,6},{8,11},{9,8},{10,9... | collective-permute-start | bytes 589832 | tf_op jit(solution)/shard_map/ppermute | solution.py:284
  89.4 1.2 copy-start.1
  93.9 20.9 %all-to-all-start.3 = ((bf16[8,64,512]{2,1,0:T(8,128)(2,1)}), bf16[8,64,512]{2,1,0:T(8,128)(2,1)S(1)}, u32[]{:S(2)}, u32[]{:S(2)}) async-start(bf16[8,64,512]{2,1,0:T(8,128)(2,1)} %merge_product.1), calls=%async_computation.3 | async-start | bytes 1048576 | tf_op jit(solution)/shard_map/all_to_all | solution.py:288
  114.9 0.8 copy-start.3
  138.9 12.3 %copy-start.4 = (bf16[3,192,768]{2,1,0:T(8,128)(2,1)S(1)}, bf16[3,192,768]{2,1,0:T(8,128)(2,1)}, u32[]{:S(2)}) copy-start(bf16[3,192,768]{2,1,0:T(8,128)(2,1)} %get-tuple-element.10) | copy-start | bytes 2654212
  139.8 39.9 %all-to-all-start.5 = ((bf16[16,40,384]{2,1,0:T(8,128)(2,1)}), bf16[16,40,384]{2,1,0:T(8,128)(2,1)S(1)}, u32[]{:S(2)}, u32[]{:S(2)}) async-start(bf16[16,40,384]{2,1,0:T(8,128)(2,1)} %broadcast_in_dim.58), calls=%async_computation.5 | async-start | bytes 983040 | tf_op jit(solution)/shard_map/all_to_all | solution.py:288
  151.6 9.9 %collective-permute-start.4 = (bf16[3,2,3,12,768]{4,1,3,2,0:T(2,128)(2,1)S(1)}, bf16[3,2,3,12,768]{4,1,3,2,0:T(2,128)(2,1)S(1)}, u32[]{:S(2)}, u32[]{:S(2)}) collective-permute-start(bf16[3,2,3,12,768]{4,1,3,2,0:T(2,128)(2,1)S(1)} %copy.40), channel_id=1, source_target_pairs={{0,1},{1,2},{2,3},{3,0},{4,5},{5,6},{6,7},{7,4},{8,9},{9,10},{10,1... | collective-permute-start | bytes 995336 | tf_op jit(solution)/shard_map/ppermute | solution.py:284
  162.6 24.3 %collective-permute-start.5 = (bf16[3,2,6,6,768]{4,1,3,2,0:T(2,128)(2,1)S(1)}, bf16[3,2,6,6,768]{4,1,3,2,0:T(2,128)(2,1)S(1)}, u32[]{:S(2)}, u32[]{:S(2)}) collective-permute-start(bf16[3,2,6,6,768]{4,1,3,2,0:T(2,128)(2,1)S(1)} %get-tuple-element.21), channel_id=1, source_target_pairs={{0,4},{4,8},{8,12},{12,16},{16,20},{20,24},{24,28},{28,32},{32,36}... | collective-permute-start | bytes 995336 | tf_op jit(solution)/shard_map/ppermute | solution.py:284
  180.5 12.1 %all-to-all-start.6 = ((bf16[8,40,384]{2,1,0:T(8,128)(2,1)}), bf16[8,40,384]{2,1,0:T(8,128)(2,1)S(1)}, u32[]{:S(2)}, u32[]{:S(2)}) async-start(bf16[8,40,384]{2,1,0:T(8,128)(2,1)} %broadcast_in_dim.59), calls=%async_computation.6 | async-start | bytes 491520 | tf_op jit(solution)/shard_map/all_to_all | solution.py:288

commit v2 on v1

v2 whole, which is shorter than its diff:
```python
import jax
import jax.numpy as jnp
import numpy as np
from jax import lax
from jax.experimental import pallas as pl
from jax.experimental.pallas import tpu as pltpu
from jax.sharding import PartitionSpec as P

NX, NY, NZ = 2, 4, 16
LAT = 4
HEADS = 24
ROWS = 12
PAD = 16
TOK = ROWS * PAD
SEG = 32
WIDE = ROWS * SEG
GROUPS = 6
LOW = -1e30
VMEM = 56 * 1024 * 1024
score_factor = 32 ** (-0.5)

z_groups = [[a * NZ + z for z in range(NZ)] for a in range(NX * NY)]
y_groups = [[(x * NY + y) * NZ + z for y in range(NY)] for x in range(NX) for z in range(NZ)]
near_groups = [
    [a * NZ + 2 * pair + e for a in range(NX * NY) for e in range(2)] for pair in range(NZ // 2)
]
far_groups = [
    [a * NZ + 2 * pair + e for pair in range(NZ // 2)] for a in range(NX * NY) for e in range(2)
]
x_lat_groups = [
    [(x * NY * NZ + b) * LAT + l for x in range(NX) for l in range(LAT)] for b in range(NY * NZ)
]


def layout_constants():
    tokens = np.arange(TOK)
    row, col = tokens // PAD, tokens % PAD
    real = col < 12
    sums = np.zeros((TOK, WIDE), np.float32)
    sums[tokens[real], (row * SEG + 11 - col)[real]] = 1
    spread = np.zeros((WIDE, TOK), np.float32)
    spread[(row * SEG + 11 + col)[real], tokens[real]] = 1
    quarter = np.zeros((256, 256), np.float32)
    back = np.zeros((TOK, 256), np.float32)
    for level in range(2):
        for pr in range(4):
            for pc in range(6):
                for di in range(2):
                    for dj in range(2):
                        spot = (di + 2 * dj) * 64 + (level * 4 + pr) * 8 + pc
                        fine_row, fine_col = 2 * pr + di, 2 * pc + dj
                        quarter[spot, (level * 8 + fine_row) * PAD + fine_col] = 1
                        if 1 <= fine_row <= 6:
                            back[(level * 6 + fine_row - 1) * PAD + fine_col, spot] = 1
    shuffle = np.zeros((512, 384), np.float32)
    order = np.zeros((512, 384), np.float32)
    for l in range(4):
        for z in range(NZ):
            for i in range(6):
                shuffle[l * 128 + z * 6 + i, z * 24 + l * 6 + i] = 1
                order[l * 128 + z * 6 + i, z * 24 + l * 6 + i] = 1
    open_up = np.zeros((2, 138, WIDE), np.float32)
    for half in range(2):
        for r in range(6):
            for d in range(23):
                open_up[half, r * 23 + d, half * 192 + r * SEG + 22 - d] = 1
    all_of = (sums, spread, quarter, back, order, shuffle, open_up)
    return [jnp.asarray(a, jnp.bfloat16) for a in all_of]


def dot(a, b, dims=((1,), (0,))):
    return lax.dot_general(a, b, (dims, ((), ())), preferred_element_type=jnp.float32)


def head_mask(h):
    lanes = lax.broadcasted_iota(jnp.int32, (1, 128), 1)
    return (lanes // 32) == h


def by_head(block):
    return jnp.concatenate(
        [jnp.where(head_mask(h), block, jnp.zeros_like(block)) for h in range(4)], axis=0
    )


def split_dot(values, matrix):
    high = values.astype(jnp.bfloat16)
    low = (values - high.astype(jnp.float32)).astype(jnp.bfloat16)
    return dot(high, matrix) + dot(low, matrix)


def window(north_ref, south_ref, which):
    pieces = []
    for level in range(2):
        pieces.append(north_ref[which, level].reshape(48, 128))
        pieces.append(south_ref[which, level, 0:3].reshape(48, 128))
    return jnp.concatenate(pieces, axis=0)


def pack_kernel(lat_ref, w_ref, out_ref):
    first = lat_ref[0] * 6
    to = lax.broadcasted_iota(jnp.int32, (24, 24), 0)
    source = lax.broadcasted_iota(jnp.int32, (24, 24), 1)
    total = jnp.zeros((24, 384), jnp.float32)
    for part in range(4):
        pick = jnp.logical_and(to // 6 == part, source == first + to - part * 6)
        pick = jnp.where(pick, 1.0, 0.0).astype(jnp.bfloat16)
        total += dot(pick, w_ref[:, part * 384 : (part + 1) * 384])
    packed = total.astype(jnp.bfloat16)
    for z in range(NZ):
        out_ref[z] = packed


def bias_kernel(table_ref, open_ref, spread_ref, mask_ref, bias_ref, wide_ref):
    @pl.when(pl.program_id(0) == 0)
    def _():
        halves = []
        for half in range(2):
            pieces = []
            for a in range(ROWS):
                first = (a // 6 * 2 + half) * 828 + a % 6 * 138
                pieces.append(table_ref[0, :, first : first + 138])
            halves.append(split_dot(jnp.concatenate(pieces, axis=0), open_ref[half]))
        for s in range(3):
            wide_ref[s] = (halves[0] + halves[1])[:, s * 128 : (s + 1) * 128]

    first = pl.program_id(0) * 4
    pieces = []
    for s in range(3):
        table = jnp.concatenate(
            [wide_ref[s, pl.ds(first + h, ROWS, stride=HEADS), :] for h in range(4)], axis=0
        )
        table = jnp.broadcast_to(table[:, None, :], (4 * ROWS, PAD, 128))
        pieces.append(pltpu.roll(table, 0, 2, stride=1, stride_axis=1))
    wide = jnp.concatenate(pieces, axis=2).reshape(4 * TOK, WIDE)
    bias = split_dot(wide, spread_ref[...]).reshape(4, TOK, TOK) + mask_ref[...][None]
    bias_ref[0] = bias.reshape(4 * TOK, TOK)


def probs_kernel(north_ref, south_ref, bias_ref, p_ref):
    q_win, k_win = window(north_ref, south_ref, 0), window(north_ref, south_ref, 1)
    scores = dot(by_head(q_win), k_win, ((1,), (1,))) * score_factor + bias_ref[0]
    expon = jnp.exp(scores - jnp.max(scores, axis=-1, keepdims=True))
    p_ref[0] = expon * (1.0 / jnp.sum(expon, axis=-1, keepdims=True))


def norm_kernel(a_ref, b_ref, south_ref, quarter_ref, normed_ref, inverse_ref):
    pieces = []
    for level in range(2):
        pieces.append(a_ref[0, level].reshape(32, 768))
        pieces.append(b_ref[0, level].reshape(32, 768))
        pieces.append(south_ref[0, level].reshape(64, 768))
    fields = dot(quarter_ref[...], jnp.concatenate(pieces, axis=0))
    parts = [fields[q * 64 : (q + 1) * 64] for q in range(4)]
    mean = jnp.sum(parts[0] + parts[1] + parts[2] + parts[3], axis=-1, keepdims=True) / 3072
    parts = [part - mean for part in parts]
    squares = [part * part for part in parts]
    variance = (
        jnp.sum(squares[0] + squares[1] + squares[2] + squares[3], axis=-1, keepdims=True) / 3072
    )
    inverse = lax.rsqrt(variance + 1e-05)
    for q in range(4):
        normed_ref[q] = parts[q] * inverse
    inverse_ref[...] = jnp.broadcast_to(inverse, (64, 128))


def merge_kernel(spot_ref, near_ref, far_ref, w_ref, shuffle_ref, out_ref, acc_ref):
    weights = [dot(shuffle_ref[...], w_ref[y]).astype(jnp.bfloat16) for y in range(NY)]
    near, far = None, None
    for part in range(4):
        rows, columns = slice(part * 128, part * 128 + 128), slice(part * 384, part * 384 + 384)
        weight = jnp.concatenate([weights[y][rows] for y in range(NY)], axis=0)
        near_part = dot(near_ref[:, columns], weight, ((1,), (1,)))
        far_part = dot(far_ref[:, columns], weight, ((1,), (1,)))
        near = near_part if part == 0 else near + near_part
        far = far_part if part == 0 else far + far_part
    acc_ref[:192] = near
    acc_ref[192:] = far
    for x in range(NX):
        for l in range(LAT):
            for level in range(2):
                own = pl.multiple_of(spot_ref[x * LAT + l] + level * 24 + 8, 8)
                below = pl.multiple_of(spot_ref[x * LAT + (l + 1) % LAT] + level * 24, 8)
                out_ref[x * LAT + l, level * 32 : level * 32 + 16] = acc_ref[
                    pl.ds(own, 16)
                ].astype(jnp.bfloat16)
                out_ref[x * LAT + l, level * 32 + 16 : level * 32 + 32] = acc_ref[
                    pl.ds(below, 16)
                ].astype(jnp.bfloat16)


def scores_kernel(
    recv_ref,
    order_ref,
    normed_ref,
    inverse_ref,
    gain_ref,
    back_ref,
    sums_ref,
    north_ref,
    south_ref,
    p_ref,
    o_out_ref,
    d_ref,
    table_ref,
    o_ref,
    sum_ref,
):
    g = pl.program_id(0)

    @pl.when(g == 0)
    def _():
        pieces = [
            jnp.concatenate(
                [recv_ref[x * LAT + l, :, y * 128 : (y + 1) * 128] for l in range(LAT)], axis=1
            )
            for x in range(NX)
            for y in range(NY)
        ]
        d_norm = dot(jnp.concatenate(pieces, axis=0), order_ref[...])
        hats = []
        for q in range(4):
            left = d_norm[(2 * q) * 64 : (2 * q + 1) * 64]
            right = d_norm[(2 * q + 1) * 64 : (2 * q + 2) * 64]
            hats.append(jnp.concatenate([left, right], axis=1) * gain_ref[q])
        mean = jnp.sum(hats[0] + hats[1] + hats[2] + hats[3], axis=-1, keepdims=True) / 3072
        cross = [hats[q] * normed_ref[q] for q in range(4)]
        along = jnp.sum(cross[0] + cross[1] + cross[2] + cross[3], axis=-1, keepdims=True) / 3072
        inverse = inverse_ref[:, 0:1]
        stack = [(hats[q] - mean - normed_ref[q] * along) * inverse for q in range(4)]
        d_out = dot(back_ref[...], jnp.concatenate(stack, axis=0).astype(jnp.bfloat16))
        d_out = d_out.astype(jnp.bfloat16)
        for s in range(GROUPS):
            o_ref[s] = d_out[:, s * 128 : (s + 1) * 128]

    o_win = o_ref[g]
    o_out_ref[0] = o_win
    probs = p_ref[0]
    d_probs = dot(by_head(o_win), window(north_ref, south_ref, 0), ((1,), (1,)))
    delta = jnp.sum(probs * d_probs, axis=-1, keepdims=True)
    d_low = (probs * (d_probs - delta)).astype(jnp.bfloat16)
    d_ref[0] = d_low

    spread = dot(d_low, sums_ref[...]).reshape(4 * ROWS, PAD, WIDE)
    sums = [
        jnp.sum(
            pltpu.roll(spread[:, :, s * 128 : (s + 1) * 128], 0, 2, stride=1, stride_axis=1), axis=1
        )
        for s in range(3)
    ]
    sum_ref[g] = jnp.concatenate(sums, axis=1)

    @pl.when(g == GROUPS - 1)
    def _():
        whole = jnp.concatenate([sum_ref[s] for s in range(GROUPS)], axis=0)
        for part in range(16):
            table_ref[part, 0:18] = whole[part * 18 : (part + 1) * 18]
            table_ref[part, 18:24] = jnp.zeros((6, WIDE), jnp.float32)


def grads_kernel(north_ref, south_ref, o_ref, d_ref, p_ref, grads_ref):
    q_win, k_win = window(north_ref, south_ref, 0), window(north_ref, south_ref, 1)
    o_win = o_ref[0]
    d_low = d_ref[0]
    p_low = p_ref[0].astype(jnp.bfloat16)
    q_all = dot(d_low, k_win)
    q_grad = jnp.zeros((TOK, 128), jnp.float32)
    for h in range(4):
        q_grad = jnp.where(head_mask(h), q_all[h * TOK : (h + 1) * TOK], q_grad)
    grads_ref[0] = (q_grad * score_factor).astype(jnp.bfloat16)

    q_turn = q_win.astype(jnp.float32).T.astype(jnp.bfloat16)
    o_turn = o_win.astype(jnp.float32).T.astype(jnp.bfloat16)
    k_parts, v_parts = [], []
    for h in range(4):
        rows = slice(h * 32, (h + 1) * 32)
        k_parts.append(dot(q_turn[rows], d_low[h * TOK : (h + 1) * TOK]))
        v_parts.append(dot(o_turn[rows], p_low[h * TOK : (h + 1) * TOK]))
    k_grad = jnp.concatenate(k_parts, axis=0).T
    v_grad = jnp.concatenate(v_parts, axis=0).T
    grads_ref[1] = (k_grad * score_factor).astype(jnp.bfloat16)
    grads_ref[2] = v_grad.astype(jnp.bfloat16)


def whole_spec(shape):
    return pl.BlockSpec(shape, lambda *_: (0,) * len(shape))


def north_spec(first, count):
    return pl.BlockSpec((count, 2, 3, PAD, 128), lambda g: (first // count, 0, 1, 0, g))


def south_spec(first, count):
    return pl.BlockSpec((count, 2, 4, PAD, 128), lambda g: (first // count, 0, 0, 0, g))


def group_spec(rows, columns):
    return pl.BlockSpec((1, rows, columns), lambda g: (g, 0, 0))


params = pltpu.CompilerParams(vmem_limit_bytes=VMEM)
smem = pl.BlockSpec(memory_space=pltpu.SMEM)
vmem = pl.BlockSpec(memory_space=pltpu.VMEM)


def pack_weight(lat, weight):
    return pl.pallas_call(
        pack_kernel,
        in_specs=[smem, vmem],
        out_specs=vmem,
        out_shape=jax.ShapeDtypeStruct((NZ, 24, 384), jnp.bfloat16),
        compiler_params=params,
        name="pack_weight",
    )(lat, weight)


def window_bias(table, open_up, spread, mask):
    return pl.pallas_call(
        bias_kernel,
        grid=(GROUPS,),
        in_specs=[
            whole_spec((1, HEADS, 3312)),
            whole_spec((2, 138, WIDE)),
            whole_spec((WIDE, TOK)),
            whole_spec((TOK, TOK)),
        ],
        out_specs=group_spec(4 * TOK, TOK),
        out_shape=jax.ShapeDtypeStruct((GROUPS, 4 * TOK, TOK), jnp.float32),
        scratch_shapes=[pltpu.VMEM((3, ROWS * HEADS, 128), jnp.float32)],
        compiler_params=params,
        name="window_bias",
    )(table, open_up, spread, mask)


def window_probs(across, south, bias):
    return pl.pallas_call(
        probs_kernel,
        grid=(GROUPS,),
        in_specs=[north_spec(0, 2), south_spec(0, 2), group_spec(4 * TOK, TOK)],
        out_specs=group_spec(4 * TOK, TOK),
        out_shape=jax.ShapeDtypeStruct((GROUPS, 4 * TOK, TOK), jnp.float32),
        compiler_params=params,
        name="window_probs",
    )(across, south, bias)


def normalise(across, south, quarter):
    return pl.pallas_call(
        norm_kernel,
        grid=(1,),
        in_specs=[
            pl.BlockSpec((1, 2, 2, PAD, 768), lambda g: (3, 0, 1, 0, 0)),
            pl.BlockSpec((1, 2, 2, PAD, 768), lambda g: (3, 0, 2, 0, 0)),
            pl.BlockSpec((1, 2, 4, PAD, 768), lambda g: (3, 0, 0, 0, 0)),
            whole_spec((256, 256)),
        ],
        out_specs=(whole_spec((4, 64, 768)), whole_spec((64, 128))),
        out_shape=(
            jax.ShapeDtypeStruct((4, 64, 768), jnp.float32),
            jax.ShapeDtypeStruct((64, 128), jnp.float32),
        ),
        compiler_params=params,
        name="normalise",
    )(across, across, south, quarter)


def merge_product(spots, near, far, weight, shuffle):
    return pl.pallas_call(
        merge_kernel,
        in_specs=[smem, vmem, vmem, vmem, vmem],
        out_specs=vmem,
        out_shape=jax.ShapeDtypeStruct((8, 64, 512), jnp.bfloat16),
        scratch_shapes=[pltpu.VMEM((384, 512), jnp.float32)],
        compiler_params=params,
        name="merge_product",
    )(spots, near, far, weight, shuffle)


def score_grads(recv, order, normed, inverse, gain, back, sums, across, south, probs):
    return pl.pallas_call(
        scores_kernel,
        grid=(GROUPS,),
        in_specs=[
            whole_spec((8, 64, 512)),
            whole_spec((512, 384)),
            whole_spec((4, 64, 768)),
            whole_spec((64, 128)),
            whole_spec((4, 1, 768)),
            whole_spec((TOK, 256)),
            whole_spec((TOK, WIDE)),
            north_spec(2, 1),
            south_spec(2, 1),
            group_spec(4 * TOK, TOK),
        ],
        out_specs=(
            group_spec(TOK, 128),
            group_spec(4 * TOK, TOK),
            whole_spec((16, 24, WIDE)),
        ),
        out_shape=(
            jax.ShapeDtypeStruct((GROUPS, TOK, 128), jnp.bfloat16),
            jax.ShapeDtypeStruct((GROUPS, 4 * TOK, TOK), jnp.bfloat16),
            jax.ShapeDtypeStruct((16, 24, WIDE), jnp.float32),
        ),
        scratch_shapes=[
            pltpu.VMEM((GROUPS, TOK, 128), jnp.bfloat16),
            pltpu.VMEM((GROUPS, 4 * ROWS, WIDE), jnp.float32),
        ],
        compiler_params=params,
        name="score_grads",
    )(recv, order, normed, inverse, gain, back, sums, across, south, probs)


def window_grads(across, south, o_win, d_low, probs):
    return pl.pallas_call(
        grads_kernel,
        grid=(GROUPS,),
        in_specs=[
            north_spec(0, 2),
            south_spec(0, 2),
            group_spec(TOK, 128),
            group_spec(4 * TOK, TOK),
            group_spec(4 * TOK, TOK),
        ],
        out_specs=pl.BlockSpec((3, TOK, 128), lambda g: (0, 0, g)),
        out_shape=jax.ShapeDtypeStruct((3, TOK, 768), jnp.bfloat16),
        compiler_params=params,
        name="window_grads",
    )(across, south, o_win, d_low, probs)


def from_behind(shard, axis, by):
    size = lax.axis_size(axis)
    return lax.ppermute(shard, axis, [(i, (i + by) % size) for i in range(size)])


def partner(shard, axis, bit):
    return lax.ppermute(shard, axis, [(i, i ^ bit) for i in range(lax.axis_size(axis))])


def swap(shard, axis, groups):
    return lax.all_to_all(shard, axis, 0, 0, tiled=True, axis_index_groups=groups)


def share(shard, count, axis, groups):
    return swap(jnp.broadcast_to(shard[None], (count,) + shard.shape), axis, groups)


def on_device(y_block, merge_gain, merge_weight, d_merged, q_proj, k_proj, v_proj, bias_table):
    sums, spread, quarter, back, order, shuffle, open_up = layout_constants()
    lat = lax.axis_index("lat")

    packed = pack_weight(lat.reshape(1), merge_weight)
    weight_z = swap(packed, "lon", z_groups).reshape(NZ * 24, 384)

    tokens = jnp.arange(TOK, dtype=jnp.int32)
    upper = tokens // PAD % 6 >= 3
    allowed = jnp.logical_or(upper[:, None] == upper[None, :], lat != LAT - 1)
    allowed = jnp.logical_and(allowed, (tokens % PAD < 12)[None, :])
    bias = window_bias(bias_table, open_up, spread, jnp.where(allowed, 0.0, LOW))

    eastern_d = from_behind(d_merged[:, :, :3], "lon", -1)
    d_rows = jnp.concatenate(
        [d_merged[:, :, 3:], eastern_d, jnp.zeros_like(d_merged[:, :, :2])], axis=2
    ).reshape(48, -1)
    d_rows = jnp.concatenate([d_rows, partner(d_rows, "lat", 2)], axis=0)
    near = jnp.concatenate([d_rows, partner(d_rows, "lon", NY * NZ)], axis=0)
    far = partner(near, "lat", 1)
    me = (lax.axis_index("lon") // (NY * NZ)) * LAT + lat
    rel = jnp.bitwise_xor(jnp.arange(8, dtype=jnp.int32), me)
    spots = (rel % 2 * 4 + rel // 4 * 2 + rel // 2 % 2) * 48

    weight_z, bias, q_proj, k_proj, v_proj, y_block = lax.optimization_barrier(
        (weight_z, bias, q_proj, k_proj, v_proj, y_block)
    )
    weight = share(weight_z, NY, "lon", y_groups)
    eastern = from_behind(
        jnp.stack([q_proj[:, :, :6], k_proj[:, :, :6], v_proj[:, :, :6], y_block[:, :, :6]]),
        "lon",
        -1,
    )
    across = jnp.concatenate(
        [
            jnp.stack([q_proj[:, :, 6:], k_proj[:, :, 6:], v_proj[:, :, 6:], y_block[:, :, 6:]]),
            eastern,
            jnp.zeros_like(eastern[:, :, :, :4]),
        ],
        axis=3,
    )
    south = from_behind(across[:, :, :4], "lat", -1)

    parts = merge_product(spots, near, far, weight, shuffle)
    recv = swap(parts, ("lon", "lat"), x_lat_groups)

    south, _ = lax.optimization_barrier((south, parts))
    probs = window_probs(across, south, bias)
    normed, inverse = normalise(across, south, quarter)

    o_win, d_low, table_part = score_grads(
        recv, order, normed, inverse, merge_gain.reshape(4, 1, 768), back, sums, across, south, probs
    )

    table_part = jnp.sum(swap(table_part, "lon", near_groups), axis=0).astype(jnp.bfloat16)
    grads = window_grads(across, south, o_win, d_low, probs)
    grid = grads.reshape(3, 2, 6, PAD, 768)[:, :, :, :12]
    southern = from_behind(grid[:, :, 3:], "lat", 1)
    fixed = jnp.concatenate([southern, grid[:, :, :3]], axis=2)

    table_part = share(table_part, NZ // 2, "lon", far_groups)
    table_part, fixed = lax.optimization_barrier((table_part, fixed))
    western = from_behind(fixed[:, :, :, 6:], "lon", 1)
    finished = jnp.concatenate([western, fixed[:, :, :, :6]], axis=3)

    table_part = jnp.sum(table_part.astype(jnp.float32), axis=0).astype(jnp.bfloat16)
    table_sum = share(table_part, 16, "lon", near_groups)[:, :18].astype(jnp.float32)
    table_sum = table_sum.reshape(HEADS, 2, 6, 2, 6, SEG)[..., :23].transpose(0, 1, 3, 2, 4, 5)
    table_grad = table_sum.reshape(bias_table.shape)
    return (finished[0], finished[1], finished[2], table_grad)


def solution(mesh):
    placed = (
        P(None, "lat", "lon", None),
        P(),
        P("lon", None),
        P(None, "lat", "lon", None),
        P(None, "lat", "lon", None),
        P(None, "lat", "lon", None),
        P(None, "lat", "lon", None),
        P("lat", None, None),
    )
    return jax.shard_map(
        on_device,
        mesh=mesh,
        in_specs=placed,
        out_specs=(
            P(None, "lat", "lon", None),
            P(None, "lat", "lon", None),
            P(None, "lat", "lon", None),
            P("lat", None, None),
        ),
        check_vma=False,
    )
```

time: 197 us -> 173 us (0.88)
  Pallas kernels: 24.5 us -> 41 us
  blocking collectives: 13.1 us -> 0 us
  local copies, waits for them, and re-layouts: 24.6 us -> 11.9 us
  waiting for transfers between devices: 53.1 us -> 42.9 us
  starting transfers between devices: 70.4 us -> 67.8 us
  other arithmetic: 8.81 us -> 6.56 us
    all_to_all x6, waiting for transfers between devices: 43.2 us -> 15 us  [swap(): lax.all_to_all(shard, axis, 0, 0, tiled=True, axis_index_groups=groups)]
    pallas_call x4 -> x7, Pallas kernels: 24.5 us -> 41 us  [the longest x1 10.3 us: score_grads(): pl.pallas_call(scores_kernel, grid=(GROUPS,), in_specs=[whole_spec((8, 64...]
    all_to_all x1 -> x0, blocking collectives: 13.1 us -> none  [swap(): lax.all_to_all(shard, axis, 0, 0, tiled=True, axis_index_groups=groups)]
    ppermute x6 -> x5, waiting for transfers between devices: 9.86 us -> 22.7 us  [from_behind(): lax.ppermute(shard, axis, [(i, (i + by) % size) for i in range(size)])]
    ppermute x0 -> x3, starting transfers between devices: none -> 8.46 us  [partner(): lax.ppermute(shard, axis, [(i, i ^ bit) for i in range(lax.axis_size(axis...]
    all_to_all x6, starting transfers between devices: 37.4 us -> 29.5 us  [swap(): lax.all_to_all(shard, axis, 0, 0, tiled=True, axis_index_groups=groups)]
    ppermute x0 -> x3, waiting for transfers between devices: none -> 5.29 us  [partner(): lax.ppermute(shard, axis, [(i, i ^ bit) for i in range(lax.axis_size(axis...]
    reshape x2 -> x0, local copies, waits for them, and re-layouts: 4.46 us -> none  [the longest x1 2.97 us: on_device(): bias_table.reshape(HEADS, 2, 2, 6, 6, 23).transpose(0, 1, 3, 2, 4, 5)]
  transfers between devices with their start and end apart: 12 -> 14, of which waited for: 7 -> 7; matrix products, arithmetic and copies ran while one was open for 13% -> 6% of each run, Pallas kernels for 7% -> 18%
where the time goes in v2:
time: 173 us; the launch traced here: 171 us
  starting transfers between devices  67.8 us (39%)
  waiting for transfers between devices  42.9 us (25%)
  Pallas kernels  41 us (24%)
  local copies, waits for them, and re-layouts  11.9 us (7%)
  other arithmetic  6.56 us (4%)
    ppermute x5, starting transfers between devices, from_behind(): lax.ppermute(shard, axis, [(i, (i + by) % size) for i in range(size)])  29.8 us
    all_to_all x6, starting transfers between devices, swap(): lax.all_to_all(shard, axis, 0, 0, tiled=True, axis_index_groups=groups)  29.5 us
    ppermute x5, waiting for transfers between devices, from_behind(): lax.ppermute(shard, axis, [(i, (i + by) % size) for i in range(size)])  22.7 us
    all_to_all x6, waiting for transfers between devices, swap(): lax.all_to_all(shard, axis, 0, 0, tiled=True, axis_index_groups=groups)  15 us
    pallas_call x1, Pallas kernels, score_grads(): pl.pallas_call(scores_kernel, grid=(GROUPS,), in_specs=[whole_spec((8, 64...  10.3 us
    ppermute x3, starting transfers between devices, partner(): lax.ppermute(shard, axis, [(i, i ^ bit) for i in range(lax.axis_size(axis...  8.46 us
    pallas_call x1, Pallas kernels, window_bias(): pl.pallas_call(bias_kernel, grid=(GROUPS,), in_specs=[whole_spec((1, HEAD...  7.37 us
    pallas_call x1, Pallas kernels, window_probs(): pl.pallas_call(probs_kernel, grid=(GROUPS,), in_specs=[north_spec(0, 2),...  7.31 us
  transfers between devices with their start and end apart: 14, of which 7 were waited for; matrix products, arithmetic and copies ran while one was open for 6% of the time, Pallas kernels for 18%

profile of v2, /device:TPU:6, one launch (start us, length us, event | category | flops | bytes accessed | tf_op | source)
XLA Modules:
  0.0 171.2 jit_solution(8124089738175726453)
XLA Ops:
  0.6 0.9 fusion.17
  1.6 14.1 %collective-permute-start = (bf16[2,3,3,1536]{3,0,2,1:T(2,128)(2,1)S(1)}, bf16[2,3,3,1536]{3,0,2,1:T(2,128)(2,1)S(1)}, u32[]{:S(2)}, u32[]{:S(2)}) collective-permute-start(bf16[2,3,3,1536]{3,0,2,1:T(2,128)(2,1)S(1)} %get-tuple-element.40), channel_id=1, source_target_pairs={{0,508},{4,0},{8,4},{12,8},{16,12},{20,16},{24,20},{28,24},{32,28}... | collective-permute-start | bytes 165896 | tf_op jit(solution)/shard_map/ppermute | solution.py:434
  15.7 1.8 %pack_weight.1 = bf16[16,24,384]{2,1,0:T(8,128)(2,1)} custom-call(s32[1]{0:T(128)} %bitcast.1.lat_ref, bf16[24,1536]{1,0:T(8,128)(2,1)} %w_ref.1), custom_call_target="tpu_custom_call" | custom-call | tf_op jit(solution)/shard_map/pack_weight/pallas_call | solution.py:307
  17.5 3.6 %all-to-all-start = ((bf16[16,24,384]{2,1,0:T(8,128)(2,1)}), bf16[16,24,384]{2,1,0:T(8,128)(2,1)S(1)}, u32[]{:S(2)}, u32[]{:S(2)}) async-start(bf16[16,24,384]{2,1,0:T(8,128)(2,1)} %pack_weight.1), calls=%async_computation | async-start | bytes 589824 | tf_op jit(solution)/shard_map/all_to_all | solution.py:442
  21.0 0.1 pad.21.clone
  21.1 0.0 collective-permute-done
  21.1 0.2 maximum_maximum_fusion.1
  21.3 3.3 %collective-permute-start.1 = (bf16[48,1536]{1,0:T(8,128)(2,1)S(1)}, bf16[48,1536]{1,0:T(8,128)(2,1)S(1)}, u32[]{:S(2)}, u32[]{:S(2)}) collective-permute-start(bf16[48,1536]{1,0:T(8,128)(2,1)S(1)} %bitcast.31), channel_id=1, source_target_pairs={{0,2},{1,3},{2,0},{3,1},{4,6},{5,7},{6,4},{7,5},{8,10},{9,11},{10,... | collective-permute-start | bytes 442376 | tf_op jit(solution)/shard_map/ppermute | solution.py:438
  24.7 0.1 pad.9.clone
  24.7 5.3 %collective-permute-done.1 = bf16[48,1536]{1,0:T(8,128)(2,1)S(1)} collective-permute-done((bf16[48,1536]{1,0:T(8,128)(2,1)S(1)}, bf16[48,1536]{1,0:T(8,128)(2,1)S(1)}, u32[]{:S(2)}, u32[]{:S(2)}) %collective-permute-start.1) | collective-permute-done | bytes 147488 | tf_op jit(solution)/shard_map/ppermute | solution.py:438
  30.1 3.1 %collective-permute-start.2 = (bf16[96,1536]{1,0:T(8,128)(2,1)S(1)}, bf16[96,1536]{1,0:T(8,128)(2,1)S(1)}, u32[]{:S(2)}, u32[]{:S(2)}) collective-permute-start(bf16[96,1536]{1,0:T(8,128)(2,1)S(1)} %pad_maximum_fusion.3), channel_id=1, source_target_pairs={{0,256},{4,260},{8,264},{12,268},{16,272},{20,276},{24,280},{28,28... | collective-permute-start | bytes 884744 | tf_op jit(solution)/shard_map/ppermute | solution.py:438
  33.2 0.8 and_select_fusion.mask_ref
  34.0 7.4 %window_bias.1.bias_ref = f32[6,768,192]{2,1,0:T(8,128)} custom-call(f32[1,24,3312]{2,1,0:T(8,128)} %table_ref.1, bf16[2,138,384]{2,1,0:T(8,128)(2,1)} %constant.133.clone.open_ref, bf16[384,192]{1,0:T(8,128)(2,1)} %constant.129.clone.spread_ref, f32[192,192]{1,0:T(8,128)} %and_select_fusion.mask_ref), custom_call_target="tpu_custom_call" | custom-call | tf_op jit(solution)/shard_map/window_bias/pallas_call | solution.py:318
  41.3 0.0 collective-permute-done.2
  41.4 0.9 pad_maximum_fusion.1.near_ref
  42.2 2.0 %collective-permute-start.3 = (bf16[192,1536]{1,0:T(8,128)(2,1)}, bf16[192,1536]{1,0:T(8,128)(2,1)}, u32[]{:S(2)}, u32[]{:S(2)}) collective-permute-start(bf16[192,1536]{1,0:T(8,128)(2,1)} %pad_maximum_fusion.1.near_ref), channel_id=1, source_target_pairs={{0,1},{1,0},{2,3},{3,2},{4,5},{5,4},{6,7},{7,6},{8,9},{9,8},{10,11... | collective-permute-start | bytes 1769480 | tf_op jit(solution)/shard_map/ppermute | solution.py:438
  44.3 0.1 slice_bitcast_fusion.7
  44.4 0.1 slice_bitcast_fusion.6
  44.6 0.1 slice_bitcast_fusion.5
  44.7 0.1 slice_bitcast_fusion.4
  44.8 0.8 pad_maximum_fusion.2
  45.6 0.2 copy.60
  45.9 7.6 %collective-permute-start.4 = (bf16[4,2,6,6,768]{4,0,3,2,1:T(4,128)(2,1)S(1)}, bf16[4,2,6,6,768]{4,0,3,2,1:T(4,128)(2,1)S(1)}, u32[]{:S(2)}, u32[]{:S(2)}) collective-permute-start(bf16[4,2,6,6,768]{4,0,3,2,1:T(4,128)(2,1)S(1)} %copy.60), channel_id=1, source_target_pairs={{0,508},{4,0},{8,4},{12,8},{16,12},{20,16},{24,20},{28,24},{32,28}... | collective-permute-start | bytes 1327112 | tf_op jit(solution)/shard_map/ppermute | solution.py:434
  53.5 1.1 broadcast_in_dim.38
  54.6 3.5 %all-to-all-start.1 = ((bf16[4,384,384]{2,1,0:T(8,128)(2,1)}), bf16[4,384,384]{2,1,0:T(8,128)(2,1)S(1)}, u32[]{:S(2)}, u32[]{:S(2)}) async-start(bf16[4,384,384]{2,1,0:T(8,128)(2,1)} %broadcast_in_dim.38), calls=%async_computation.1 | async-start | bytes 2359296 | tf_op jit(solution)/shard_map/all_to_all | solution.py:442
  58.3 5.2 %collective-permute-done.4 = bf16[4,2,6,6,768]{4,0,3,2,1:T(4,128)(2,1)S(1)} collective-permute-done((bf16[4,2,6,6,768]{4,0,3,2,1:T(4,128)(2,1)S(1)}, bf16[4,2,6,6,768]{4,0,3,2,1:T(4,128)(2,1)S(1)}, u32[]{:S(2)}, u32[]{:S(2)}) %collective-permute-start.4) | collective-permute-done | bytes 442400 | tf_op jit(solution)/shard_map/ppermute | solution.py:434
  63.6 0.1 copy.61
  63.6 0.5 maximum_maximum_fusion.a_ref.b_ref.north_ref
  64.2 1.0 slice.88
  65.2 2.6 %collective-permute-start.5 = (bf16[4,2,4,16,768]{4,3,2,1,0:T(8,128)(2,1)}, bf16[4,2,4,16,768]{4,3,2,1,0:T(8,128)(2,1)S(1)}, u32[]{:S(2)}, u32[]{:S(2)}) collective-permute-start(bf16[4,2,4,16,768]{4,3,2,1,0:T(8,128)(2,1)} %slice.88), channel_id=1, source_target_pairs={{0,3},{1,0},{2,1},{3,2},{4,7},{5,4},{6,5},{7,6},{8,11},{9,8},{10,9... | collective-permute-start | bytes 2359304 | tf_op jit(solution)/shard_map/ppermute | solution.py:434
  67.9 0.5 fusion.14.spot_ref
  68.4 0.0 collective-permute-done.3.far_ref
  68.4 6.9 %all-to-all-done.1.w_ref = bf16[4,384,384]{2,1,0:T(8,128)(2,1)S(1)} async-done(((bf16[4,384,384]{2,1,0:T(8,128)(2,1)}), bf16[4,384,384]{2,1,0:T(8,128)(2,1)S(1)}, u32[]{:S(2)}, u32[]{:S(2)}) %all-to-all-start.1) | async-done | bytes 1179680 | tf_op jit(solution)/shard_map/all_to_all | solution.py:442
  75.3 1.0 copy-done.2
  76.3 4.7 %merge_product.1 = bf16[8,64,512]{2,1,0:T(8,128)(2,1)} custom-call(s32[8]{0:T(128)} %fusion.14.spot_ref, bf16[192,1536]{1,0:T(8,128)(2,1)} %pad_maximum_fusion.1.near_ref, bf16[192,1536]{1,0:T(8,128)(2,1)} %collective-permute-done.3.far_ref, bf16[4,384,384]{2,1,0:T(8,128)(2,1)} %copy-done.2, bf16[512,384]{1,0:T(8,128)(2,1)} %constant.132.clone.shuffle_ref.order_ref), custom_call_target="tpu_custom_call" | custom-call | tf_op jit(solution)/shard_map/merge_product/pallas_call | solution.py:368
  81.1 4.8 %all-to-all-start.2 = ((bf16[8,64,512]{2,1,0:T(8,128)(2,1)}), bf16[8,64,512]{2,1,0:T(8,128)(2,1)S(1)}, u32[]{:S(2)}, u32[]{:S(2)}) async-start(bf16[8,64,512]{2,1,0:T(8,128)(2,1)} %merge_product.1), calls=%async_computation.2 | async-start | bytes 1048576 | tf_op jit(solution)/shard_map/all_to_all | solution.py:442
  85.8 0.9 copy-done.1
  86.7 7.3 %window_probs.1.p_ref = f32[6,768,192]{2,1,0:T(8,128)} custom-call(bf16[4,2,6,16,768]{4,3,2,1,0:T(8,128)(2,1)} %copy-done, bf16[4,2,4,16,768]{4,3,2,1,0:T(8,128)(2,1)} %copy-done.1, f32[6,768,192]{2,1,0:T(8,128)} %window_bias.1.bias_ref), custom_call_target="tpu_custom_call" | custom-call | tf_op jit(solution)/shard_map/window_probs/pallas_call | solution.py:336
  94.0 2.5 %normalise.1 = (f32[4,64,768]{2,1,0:T(8,128)}, f32[64,128]{1,0:T(8,128)}) custom-call(bf16[4,2,6,16,768]{4,3,2,1,0:T(8,128)(2,1)} %copy-done, bf16[4,2,6,16,768]{4,3,2,1,0:T(8,128)(2,1)} %copy-done, bf16[4,2,4,16,768]{4,3,2,1,0:T(8,128)(2,1)} %copy-done.1, bf16[256,256]{1,0:T(8,128)(2,1)} %constant.130.clone.quarter_ref), custom_call_target="tpu_custom_call" | custom-call | tf_op jit(solution)/shard_map/normalise/pallas_call | solution.py:348
  96.5 0.8 copy-done.4
  97.4 10.3 %score_grads.1 = (bf16[6,192,128]{2,1,0:T(8,128)(2,1)}, bf16[6,768,192]{2,1,0:T(8,128)(2,1)}, f32[16,24,384]{2,1,0:T(8,128)}) custom-call(bf16[8,64,512]{2,1,0:T(8,128)(2,1)} %copy-done.4, bf16[512,384]{1,0:T(8,128)(2,1)} %constant.132.clone.shuffle_ref.order_ref, f32[4,64,768]{2,1,0:T(8,128)} %get-tuple-element.24.normed_ref, ...), custom_call_target="tpu_custom_call" | custom-call | tf_op jit(solution)/shard_map/score_grads/pallas_call | solution.py:380
  107.7 4.3 %all-to-all-start.3 = ((f32[16,24,384]{2,1,0:T(8,128)}), f32[16,24,384]{2,1,0:T(8,128)S(1)}, u32[]{:S(2)}, u32[]{:S(2)}) async-start(f32[16,24,384]{2,1,0:T(8,128)} %get-tuple-element.27), calls=%async_computation.3 | async-start | bytes 1179648 | tf_op jit(solution)/shard_map/all_to_all | solution.py:442
  112.0 7.0 %window_grads.1 = bf16[3,192,768]{2,1,0:T(8,128)(2,1)} custom-call(bf16[4,2,6,16,768]{4,3,2,1,0:T(8,128)(2,1)} %copy-done, bf16[4,2,4,16,768]{4,3,2,1,0:T(8,128)(2,1)} %copy-done.1, bf16[6,192,128]{2,1,0:T(8,128)(2,1)} %get-tuple-element.28.o_ref, bf16[6,768,192]{2,1,0:T(8,128)(2,1)} %get-tuple-element.29.d_ref, f32[6,768,192]{2,1,0:T(8,128)} %window_probs.1.p_ref), custom_call_target="tpu_custom_call" | custom-call | tf_op jit(solution)/shard_map/window_grads/pallas_call | solution.py:415
  119.0 3.5 %all-to-all-done.3 = f32[16,24,384]{2,1,0:T(8,128)S(1)} async-done(((f32[16,24,384]{2,1,0:T(8,128)}), f32[16,24,384]{2,1,0:T(8,128)S(1)}, u32[]{:S(2)}, u32[]{:S(2)}) %all-to-all-start.3) | async-done | bytes 589856 | tf_op jit(solution)/shard_map/all_to_all | solution.py:442
  122.5 0.7 broadcast_in_dim.40
  123.2 8.4 %all-to-all-start.4 = ((bf16[8,24,384]{2,1,0:T(8,128)(2,1)}), bf16[8,24,384]{2,1,0:T(8,128)(2,1)S(1)}, u32[]{:S(2)}, u32[]{:S(2)}) async-start(bf16[8,24,384]{2,1,0:T(8,128)(2,1)} %broadcast_in_dim.40), calls=%async_computation.4 | async-start | bytes 294912 | tf_op jit(solution)/shard_map/all_to_all | solution.py:442
  131.6 0.1 fusion.15
  131.7 0.3 copy.65
  132.0 2.1 %collective-permute-start.6 = (bf16[3,2,3,12,768]{4,1,3,2,0:T(2,128)(2,1)S(1)}, bf16[3,2,3,12,768]{4,1,3,2,0:T(2,128)(2,1)S(1)}, u32[]{:S(2)}, u32[]{:S(2)}) collective-permute-start(bf16[3,2,3,12,768]{4,1,3,2,0:T(2,128)(2,1)S(1)} %copy.65), channel_id=1, source_target_pairs={{0,1},{1,2},{2,3},{3,0},{4,5},{5,6},{6,7},{7,4},{8,9},{9,10},{10,1... | collective-permute-start | bytes 995336 | tf_op jit(solution)/shard_map/ppermute | solution.py:434
  134.1 0.3 copy.66
  134.3 7.6 %collective-permute-done.6 = bf16[3,2,3,12,768]{4,1,3,2,0:T(2,128)(2,1)S(1)} collective-permute-done((bf16[3,2,3,12,768]{4,1,3,2,0:T(2,128)(2,1)S(1)}, bf16[3,2,3,12,768]{4,1,3,2,0:T(2,128)(2,1)S(1)}, u32[]{:S(2)}, u32[]{:S(2)}) %collective-permute-start.6) | collective-permute-done | bytes 331808 | tf_op jit(solution)/shard_map/ppermute | solution.py:434
  141.9 0.9 pad_maximum_fusion
  142.8 4.6 %all-to-all-done.4 = bf16[8,24,384]{2,1,0:T(8,128)(2,1)S(1)} async-done(((bf16[8,24,384]{2,1,0:T(8,128)(2,1)}), bf16[8,24,384]{2,1,0:T(8,128)(2,1)S(1)}, u32[]{:S(2)}, u32[]{:S(2)}) %all-to-all-start.4) | async-done | bytes 147488 | tf_op jit(solution)/shard_map/all_to_all | solution.py:442
  147.4 0.7 broadcast_in_dim.41
  148.1 4.9 %all-to-all-start.5 = ((bf16[16,24,384]{2,1,0:T(8,128)(2,1)}), bf16[16,24,384]{2,1,0:T(8,128)(2,1)S(1)}, u32[]{:S(2)}, u32[]{:S(2)}) async-start(bf16[16,24,384]{2,1,0:T(8,128)(2,1)} %broadcast_in_dim.41), calls=%async_computation.5 | async-start | bytes 589824 | tf_op jit(solution)/shard_map/all_to_all | solution.py:442
  153.0 0.5 fusion.16
  153.5 3.4 %collective-permute-start.7 = (bf16[3,2,6,6,768]{4,1,3,2,0:T(2,128)(2,1)S(1)}, bf16[3,2,6,6,768]{4,1,3,2,0:T(2,128)(2,1)S(1)}, u32[]{:S(2)}, u32[]{:S(2)}) collective-permute-start(bf16[3,2,6,6,768]{4,1,3,2,0:T(2,128)(2,1)S(1)} %get-tuple-element.37), channel_id=1, source_target_pairs={{0,4},{4,8},{8,12},{12,16},{16,20},{20,24},{24,28},{28,32},{32,36}... | collective-permute-start | bytes 995336 | tf_op jit(solution)/shard_map/ppermute | solution.py:434
  156.9 9.8 %collective-permute-done.7 = bf16[3,2,6,6,768]{4,1,3,2,0:T(2,128)(2,1)S(1)} collective-permute-done((bf16[3,2,6,6,768]{4,1,3,2,0:T(2,128)(2,1)S(1)}, bf16[3,2,6,6,768]{4,1,3,2,0:T(2,128)(2,1)S(1)}, u32[]{:S(2)}, u32[]{:S(2)}) %collective-permute-start.7) | collective-permute-done | bytes 331808 | tf_op jit(solution)/shard_map/ppermute | solution.py:434
  166.7 1.6 fusion.2
  168.3 0.0 all-to-all-done.5
  168.3 0.9 reshape.93
  169.2 0.3 convert_bitcast_fusion
  169.5 0.2 copy.64
  169.7 1.5 reshape.97
  (33 shorter events, 0.5 us)
Async XLA Ops:
  1.6 19.6 %collective-permute-start = (bf16[2,3,3,1536]{3,0,2,1:T(2,128)(2,1)S(1)}, bf16[2,3,3,1536]{3,0,2,1:T(2,128)(2,1)S(1)}, u32[]{:S(2)}, u32[]{:S(2)}) collective-permute-start(bf16[2,3,3,1536]{3,0,2,1:T(2,128)(2,1)S(1)} %get-tuple-element.40), channel_id=1, source_target_pairs={{0,508},{4,0},{8,4},{12,8},{16,12},{20,16},{24,20},{28,24},{32,28}... | collective-permute-start | bytes 165896 | tf_op jit(solution)/shard_map/ppermute | solution.py:434
  17.5 26.8 %all-to-all-start = ((bf16[16,24,384]{2,1,0:T(8,128)(2,1)}), bf16[16,24,384]{2,1,0:T(8,128)(2,1)S(1)}, u32[]{:S(2)}, u32[]{:S(2)}) async-start(bf16[16,24,384]{2,1,0:T(8,128)(2,1)} %pack_weight.1), calls=%async_computation | async-start | bytes 589824 | tf_op jit(solution)/shard_map/all_to_all | solution.py:442
  21.3 8.7 %collective-permute-start.1 = (bf16[48,1536]{1,0:T(8,128)(2,1)S(1)}, bf16[48,1536]{1,0:T(8,128)(2,1)S(1)}, u32[]{:S(2)}, u32[]{:S(2)}) collective-permute-start(bf16[48,1536]{1,0:T(8,128)(2,1)S(1)} %bitcast.31), channel_id=1, source_target_pairs={{0,2},{1,3},{2,0},{3,1},{4,6},{5,7},{6,4},{7,5},{8,10},{9,11},{10,... | collective-permute-start | bytes 442376 | tf_op jit(solution)/shard_map/ppermute | solution.py:438
  30.1 11.3 %collective-permute-start.2 = (bf16[96,1536]{1,0:T(8,128)(2,1)S(1)}, bf16[96,1536]{1,0:T(8,128)(2,1)S(1)}, u32[]{:S(2)}, u32[]{:S(2)}) collective-permute-start(bf16[96,1536]{1,0:T(8,128)(2,1)S(1)} %pad_maximum_fusion.3), channel_id=1, source_target_pairs={{0,256},{4,260},{8,264},{12,268},{16,272},{20,276},{24,280},{28,28... | collective-permute-start | bytes 884744 | tf_op jit(solution)/shard_map/ppermute | solution.py:438
  41.3 2.9 %copy-start.5 = (bf16[2,6,12,768]{3,0,2,1:T(2,128)(2,1)S(1)}, bf16[2,6,12,768]{3,0,2,1:T(2,128)(2,1)}, u32[]{:S(2)}) copy-start(bf16[2,6,12,768]{3,0,2,1:T(2,128)(2,1)} %param.19) | copy-start | bytes 663556
  41.3 3.1 %copy-start.6 = (bf16[2,6,12,768]{3,0,2,1:T(2,128)(2,1)S(1)}, bf16[2,6,12,768]{3,0,2,1:T(2,128)(2,1)}, u32[]{:S(2)}) copy-start(bf16[2,6,12,768]{3,0,2,1:T(2,128)(2,1)} %param.20) | copy-start | bytes 663556
  41.3 3.2 %copy-start.7 = (bf16[2,6,12,768]{3,0,2,1:T(2,128)(2,1)S(1)}, bf16[2,6,12,768]{3,0,2,1:T(2,128)(2,1)}, u32[]{:S(2)}) copy-start(bf16[2,6,12,768]{3,0,2,1:T(2,128)(2,1)} %param.21) | copy-start | bytes 663556
  42.2 2.5 %copy-start.8 = (bf16[2,6,12,768]{3,0,2,1:T(2,128)(2,1)S(1)}, bf16[2,6,12,768]{3,0,2,1:T(2,128)(2,1)}, u32[]{:S(2)}) copy-start(bf16[2,6,12,768]{3,0,2,1:T(2,128)(2,1)} %param.15) | copy-start | bytes 663556
  42.2 26.2 %collective-permute-start.3 = (bf16[192,1536]{1,0:T(8,128)(2,1)}, bf16[192,1536]{1,0:T(8,128)(2,1)}, u32[]{:S(2)}, u32[]{:S(2)}) collective-permute-start(bf16[192,1536]{1,0:T(8,128)(2,1)} %pad_maximum_fusion.1.near_ref), channel_id=1, source_target_pairs={{0,1},{1,0},{2,3},{3,2},{4,5},{5,4},{6,7},{7,6},{8,9},{9,8},{10,11... | collective-permute-start | bytes 1769480 | tf_op jit(solution)/shard_map/ppermute | solution.py:438
  45.9 17.7 %collective-permute-start.4 = (bf16[4,2,6,6,768]{4,0,3,2,1:T(4,128)(2,1)S(1)}, bf16[4,2,6,6,768]{4,0,3,2,1:T(4,128)(2,1)S(1)}, u32[]{:S(2)}, u32[]{:S(2)}) collective-permute-start(bf16[4,2,6,6,768]{4,0,3,2,1:T(4,128)(2,1)S(1)} %copy.60), channel_id=1, source_target_pairs={{0,508},{4,0},{8,4},{12,8},{16,12},{20,16},{24,20},{28,24},{32,28}... | collective-permute-start | bytes 1327112 | tf_op jit(solution)/shard_map/ppermute | solution.py:434
  54.6 20.7 %all-to-all-start.1 = ((bf16[4,384,384]{2,1,0:T(8,128)(2,1)}), bf16[4,384,384]{2,1,0:T(8,128)(2,1)S(1)}, u32[]{:S(2)}, u32[]{:S(2)}) async-start(bf16[4,384,384]{2,1,0:T(8,128)(2,1)} %broadcast_in_dim.38), calls=%async_computation.1 | async-start | bytes 2359296 | tf_op jit(solution)/shard_map/all_to_all | solution.py:442
  64.2 16.9 %copy-start = (bf16[4,2,6,16,768]{4,3,2,1,0:T(8,128)(2,1)}, bf16[4,2,6,16,768]{4,3,2,1,0:T(8,128)(2,1)S(1)}, u32[]{:S(2)}) copy-start(bf16[4,2,6,16,768]{4,3,2,1,0:T(8,128)(2,1)S(1)} %maximum_maximum_fusion.a_ref.b_ref.north_ref) | copy-start | bytes 3538948
  65.2 20.6 %collective-permute-start.5 = (bf16[4,2,4,16,768]{4,3,2,1,0:T(8,128)(2,1)}, bf16[4,2,4,16,768]{4,3,2,1,0:T(8,128)(2,1)S(1)}, u32[]{:S(2)}, u32[]{:S(2)}) collective-permute-start(bf16[4,2,4,16,768]{4,3,2,1,0:T(8,128)(2,1)} %slice.88), channel_id=1, source_target_pairs={{0,3},{1,0},{2,1},{3,2},{4,7},{5,4},{6,5},{7,6},{8,11},{9,8},{10,9... | collective-permute-start | bytes 2359304 | tf_op jit(solution)/shard_map/ppermute | solution.py:434
  75.3 1.0 copy-start.2
  81.1 15.5 %all-to-all-start.2 = ((bf16[8,64,512]{2,1,0:T(8,128)(2,1)}), bf16[8,64,512]{2,1,0:T(8,128)(2,1)S(1)}, u32[]{:S(2)}, u32[]{:S(2)}) async-start(bf16[8,64,512]{2,1,0:T(8,128)(2,1)} %merge_product.1), calls=%async_computation.2 | async-start | bytes 1048576 | tf_op jit(solution)/shard_map/all_to_all | solution.py:442
  85.8 0.9 copy-start.1
  96.5 0.8 copy-start.4
  107.7 14.8 %all-to-all-start.3 = ((f32[16,24,384]{2,1,0:T(8,128)}), f32[16,24,384]{2,1,0:T(8,128)S(1)}, u32[]{:S(2)}, u32[]{:S(2)}) async-start(f32[16,24,384]{2,1,0:T(8,128)} %get-tuple-element.27), calls=%async_computation.3 | async-start | bytes 1179648 | tf_op jit(solution)/shard_map/all_to_all | solution.py:442
  119.0 12.6 %copy-start.3 = (bf16[3,192,768]{2,1,0:T(8,128)(2,1)S(1)}, bf16[3,192,768]{2,1,0:T(8,128)(2,1)}, u32[]{:S(2)}) copy-start(bf16[3,192,768]{2,1,0:T(8,128)(2,1)} %window_grads.1) | copy-start | bytes 2654212
  123.2 24.2 %all-to-all-start.4 = ((bf16[8,24,384]{2,1,0:T(8,128)(2,1)}), bf16[8,24,384]{2,1,0:T(8,128)(2,1)S(1)}, u32[]{:S(2)}, u32[]{:S(2)}) async-start(bf16[8,24,384]{2,1,0:T(8,128)(2,1)} %broadcast_in_dim.40), calls=%async_computation.4 | async-start | bytes 294912 | tf_op jit(solution)/shard_map/all_to_all | solution.py:442
  132.0 9.9 %collective-permute-start.6 = (bf16[3,2,3,12,768]{4,1,3,2,0:T(2,128)(2,1)S(1)}, bf16[3,2,3,12,768]{4,1,3,2,0:T(2,128)(2,1)S(1)}, u32[]{:S(2)}, u32[]{:S(2)}) collective-permute-start(bf16[3,2,3,12,768]{4,1,3,2,0:T(2,128)(2,1)S(1)} %copy.65), channel_id=1, source_target_pairs={{0,1},{1,2},{2,3},{3,0},{4,5},{5,6},{6,7},{7,4},{8,9},{9,10},{10,1... | collective-permute-start | bytes 995336 | tf_op jit(solution)/shard_map/ppermute | solution.py:434
  148.1 20.2 %all-to-all-start.5 = ((bf16[16,24,384]{2,1,0:T(8,128)(2,1)}), bf16[16,24,384]{2,1,0:T(8,128)(2,1)S(1)}, u32[]{:S(2)}, u32[]{:S(2)}) async-start(bf16[16,24,384]{2,1,0:T(8,128)(2,1)} %broadcast_in_dim.41), calls=%async_computation.5 | async-start | bytes 589824 | tf_op jit(solution)/shard_map/all_to_all | solution.py:442
  153.5 13.2 %collective-permute-start.7 = (bf16[3,2,6,6,768]{4,1,3,2,0:T(2,128)(2,1)S(1)}, bf16[3,2,6,6,768]{4,1,3,2,0:T(2,128)(2,1)S(1)}, u32[]{:S(2)}, u32[]{:S(2)}) collective-permute-start(bf16[3,2,6,6,768]{4,1,3,2,0:T(2,128)(2,1)S(1)} %get-tuple-element.37), channel_id=1, source_target_pairs={{0,4},{4,8},{8,12},{12,16},{16,20},{20,24},{24,28},{28,32},{32,36}... | collective-permute-start | bytes 995336 | tf_op jit(solution)/shard_map/ppermute | solution.py:434

commit v3 on v2

--- a/solution.py
+++ b/solution.py
@@ -451,14 +451,15 @@
     lat = lax.axis_index("lat")
 
     packed = pack_weight(lat.reshape(1), merge_weight)
-    weight_z = swap(packed, "lon", z_groups).reshape(NZ * 24, 384)
 
     tokens = jnp.arange(TOK, dtype=jnp.int32)
     upper = tokens // PAD % 6 >= 3
     allowed = jnp.logical_or(upper[:, None] == upper[None, :], lat != LAT - 1)
     allowed = jnp.logical_and(allowed, (tokens % PAD < 12)[None, :])
-    bias = window_bias(bias_table, open_up, spread, jnp.where(allowed, 0.0, LOW))
-
+    mask = jnp.where(allowed, 0.0, LOW)
+
+    packed, d_merged = lax.optimization_barrier((packed, d_merged))
+    weight_z = swap(packed, "lon", z_groups).reshape(NZ * 24, 384)
     eastern_d = from_behind(d_merged[:, :, :3], "lon", -1)
     d_rows = jnp.concatenate(
         [d_merged[:, :, 3:], eastern_d, jnp.zeros_like(d_merged[:, :, :2])], axis=2
@@ -470,10 +471,11 @@
     rel = jnp.bitwise_xor(jnp.arange(8, dtype=jnp.int32), me)
     spots = (rel % 2 * 4 + rel // 4 * 2 + rel // 2 % 2) * 48
 
-    weight_z, bias, q_proj, k_proj, v_proj, y_block = lax.optimization_barrier(
-        (weight_z, bias, q_proj, k_proj, v_proj, y_block)
-    )
-    weight = share(weight_z, NY, "lon", y_groups)
+    weight_z = jnp.broadcast_to(weight_z[None], (NY,) + weight_z.shape)
+    weight_z, bias_table = lax.optimization_barrier((weight_z, bias_table))
+    weight = swap(weight_z, "lon", y_groups)
+    bias = window_bias(bias_table, open_up, spread, mask)
+
     eastern = from_behind(
         jnp.stack([q_proj[:, :, :6], k_proj[:, :, :6], v_proj[:, :, :6], y_block[:, :, :6]]),
         "lon",
@@ -489,12 +491,13 @@
     )
     south = from_behind(across[:, :, :4], "lat", -1)
 
+    normed, inverse = normalise(across, south, quarter)
+    weight, bias, normed = lax.optimization_barrier((weight, bias, normed))
     parts = merge_product(spots, near, far, weight, shuffle)
     recv = swap(parts, ("lon", "lat"), x_lat_groups)
 
-    south, _ = lax.optimization_barrier((south, parts))
+    bias, _ = lax.optimization_barrier((bias, parts))
     probs = window_probs(across, south, bias)
-    normed, inverse = normalise(across, south, quarter)
 
     o_win, d_low, table_part = score_grads(
         recv, order, normed, inverse, merge_gain.reshape(4, 1, 768), back, sums, across, south, probs

time: 173 us -> 169 us (0.977)
  waiting for transfers between devices: 42.9 us -> 32.7 us
  starting transfers between devices: 67.8 us -> 73.7 us
    all_to_all x6, starting transfers between devices: 29.5 us -> 46.8 us  [swap(): lax.all_to_all(shard, axis, 0, 0, tiled=True, axis_index_groups=groups)]
    ppermute x5, starting transfers between devices: 29.8 us -> 18.5 us  [from_behind(): lax.ppermute(shard, axis, [(i, (i + by) % size) for i in range(size)])]
    all_to_all x6, waiting for transfers between devices: 15 us -> 7.51 us  [swap(): lax.all_to_all(shard, axis, 0, 0, tiled=True, axis_index_groups=groups)]
    ppermute x5, waiting for transfers between devices: 22.7 us -> 20.2 us  [from_behind(): lax.ppermute(shard, axis, [(i, (i + by) % size) for i in range(size)])]
    unnamed x20 -> x26, local copies, waits for them, and re-layouts: 3.27 us -> 4.14 us
  transfers between devices with their start and end apart: 14 -> 14, of which waited for: 7 -> 7; matrix products, arithmetic and copies ran while one was open for 6% -> 7% of each run, Pallas kernels for 18% -> 14%
where the time goes in v3:
time: 169 us; the launch traced here: 168 us
  starting transfers between devices  73.7 us (44%)
  Pallas kernels  41.1 us (24%)
  waiting for transfers between devices  32.7 us (19%)
  local copies, waits for them, and re-layouts  11.9 us (7%)
  other arithmetic  7.52 us (4%)
    all_to_all x6, starting transfers between devices, swap(): lax.all_to_all(shard, axis, 0, 0, tiled=True, axis_index_groups=groups)  46.8 us
    ppermute x5, waiting for transfers between devices, from_behind(): lax.ppermute(shard, axis, [(i, (i + by) % size) for i in range(size)])  20.2 us
    ppermute x5, starting transfers between devices, from_behind(): lax.ppermute(shard, axis, [(i, (i + by) % size) for i in range(size)])  18.5 us
    pallas_call x1, Pallas kernels, score_grads(): pl.pallas_call(scores_kernel, grid=(GROUPS,), in_specs=[whole_spec((8, 64...  10.3 us
    ppermute x3, starting transfers between devices, partner(): lax.ppermute(shard, axis, [(i, i ^ bit) for i in range(lax.axis_size(axis...  8.43 us
    all_to_all x6, waiting for transfers between devices, swap(): lax.all_to_all(shard, axis, 0, 0, tiled=True, axis_index_groups=groups)  7.51 us
    pallas_call x1, Pallas kernels, window_probs(): pl.pallas_call(probs_kernel, grid=(GROUPS,), in_specs=[north_spec(0, 2),...  7.36 us
    pallas_call x1, Pallas kernels, window_bias(): pl.pallas_call(bias_kernel, grid=(GROUPS,), in_specs=[whole_spec((1, HEAD...  7.34 us
  transfers between devices with their start and end apart: 14, of which 7 were waited for; matrix products, arithmetic and copies ran while one was open for 7% of the time, Pallas kernels for 14%

profile of v3, /device:TPU:6, one launch (start us, length us, event | category | flops | bytes accessed | tf_op | source)
XLA Modules:
  0.0 168.0 jit_solution(15714993984166156548)
XLA Ops:
  0.7 1.9 %pack_weight.1 = bf16[16,24,384]{2,1,0:T(8,128)(2,1)} custom-call(s32[1]{0:T(128)} %bitcast.lat_ref, bf16[24,1536]{1,0:T(8,128)(2,1)} %w_ref.1), custom_call_target="tpu_custom_call" | custom-call | tf_op jit(solution)/shard_map/pack_weight/pallas_call | solution.py:307
  2.5 15.2 %all-to-all-start = ((bf16[16,24,384]{2,1,0:T(8,128)(2,1)}), bf16[16,24,384]{2,1,0:T(8,128)(2,1)S(1)}, u32[]{:S(2)}, u32[]{:S(2)}) async-start(bf16[16,24,384]{2,1,0:T(8,128)(2,1)} %pack_weight.1), calls=%async_computation | async-start | bytes 589824 | tf_op jit(solution)/shard_map/all_to_all | solution.py:442
  17.7 0.9 fusion.21
  18.7 7.8 %collective-permute-start = (bf16[2,3,3,1536]{3,0,2,1:T(2,128)(2,1)S(1)}, bf16[2,3,3,1536]{3,0,2,1:T(2,128)(2,1)S(1)}, u32[]{:S(2)}, u32[]{:S(2)}) collective-permute-start(bf16[2,3,3,1536]{3,0,2,1:T(2,128)(2,1)S(1)} %get-tuple-element.50), channel_id=1, source_target_pairs={{0,508},{4,0},{8,4},{12,8},{16,12},{20,16},{24,20},{28,24},{32,28}... | collective-permute-start | bytes 165896 | tf_op jit(solution)/shard_map/ppermute | solution.py:434
  26.5 0.3 fusion.19
  26.8 0.3 fusion.17
  27.2 0.8 pad_maximum_fusion.2
  28.0 0.2 copy.60
  28.2 3.4 %collective-permute-start.4 = (bf16[4,2,6,6,768]{4,0,3,2,1:T(4,128)(2,1)S(1)}, bf16[4,2,6,6,768]{4,0,3,2,1:T(4,128)(2,1)S(1)}, u32[]{:S(2)}, u32[]{:S(2)}) collective-permute-start(bf16[4,2,6,6,768]{4,0,3,2,1:T(4,128)(2,1)S(1)} %copy.60), channel_id=1, source_target_pairs={{0,508},{4,0},{8,4},{12,8},{16,12},{20,16},{24,20},{28,24},{32,28}... | collective-permute-start | bytes 1327112 | tf_op jit(solution)/shard_map/ppermute | solution.py:434
  31.6 0.1 pad.21.clone
  31.6 2.8 %collective-permute-done = bf16[2,3,3,1536]{3,0,2,1:T(2,128)(2,1)S(1)} collective-permute-done((bf16[2,3,3,1536]{3,0,2,1:T(2,128)(2,1)S(1)}, bf16[2,3,3,1536]{3,0,2,1:T(2,128)(2,1)S(1)}, u32[]{:S(2)}, u32[]{:S(2)}) %collective-permute-start) | collective-permute-done | bytes 55328 | tf_op jit(solution)/shard_map/ppermute | solution.py:434
  34.4 0.2 maximum_maximum_fusion.1
  34.6 3.5 %collective-permute-start.1 = (bf16[48,1536]{1,0:T(8,128)(2,1)S(1)}, bf16[48,1536]{1,0:T(8,128)(2,1)S(1)}, u32[]{:S(2)}, u32[]{:S(2)}) collective-permute-start(bf16[48,1536]{1,0:T(8,128)(2,1)S(1)} %bitcast.35), channel_id=1, source_target_pairs={{0,2},{1,3},{2,0},{3,1},{4,6},{5,7},{6,4},{7,5},{8,10},{9,11},{10,... | collective-permute-start | bytes 442376 | tf_op jit(solution)/shard_map/ppermute | solution.py:438
  38.1 5.0 %collective-permute-done.1 = bf16[48,1536]{1,0:T(8,128)(2,1)S(1)} collective-permute-done((bf16[48,1536]{1,0:T(8,128)(2,1)S(1)}, bf16[48,1536]{1,0:T(8,128)(2,1)S(1)}, u32[]{:S(2)}, u32[]{:S(2)}) %collective-permute-start.1) | collective-permute-done | bytes 147488 | tf_op jit(solution)/shard_map/ppermute | solution.py:438
  43.2 2.5 %collective-permute-start.2 = (bf16[96,1536]{1,0:T(8,128)(2,1)S(1)}, bf16[96,1536]{1,0:T(8,128)(2,1)}, u32[]{:S(2)}, u32[]{:S(2)}) collective-permute-start(bf16[96,1536]{1,0:T(8,128)(2,1)S(1)} %pad_maximum_fusion.3), channel_id=1, source_target_pairs={{0,256},{4,260},{8,264},{12,268},{16,272},{20,276},{24,280},{28,28... | collective-permute-start | bytes 884744 | tf_op jit(solution)/shard_map/ppermute | solution.py:438
  45.7 0.1 pad.9.clone
  45.9 0.0 collective-permute-done.4
  45.9 0.1 copy.61
  45.9 0.0 all-to-all-done
  46.0 1.1 broadcast_in_dim.38
  47.1 5.4 %all-to-all-start.1 = ((bf16[4,384,384]{2,1,0:T(8,128)(2,1)}), bf16[4,384,384]{2,1,0:T(8,128)(2,1)S(1)}, u32[]{:S(2)}, u32[]{:S(2)}) async-start(bf16[4,384,384]{2,1,0:T(8,128)(2,1)} %broadcast_in_dim.38), calls=%async_computation.1 | async-start | bytes 2359296 | tf_op jit(solution)/shard_map/all_to_all | solution.py:442
  52.5 0.5 maximum_maximum_fusion.a_ref.b_ref.north_ref
  53.0 0.1 slice.84
  53.1 1.9 %collective-permute-start.5 = (bf16[4,2,4,16,768]{4,3,2,1,0:T(8,128)(2,1)S(1)}, bf16[4,2,4,16,768]{4,3,2,1,0:T(8,128)(2,1)S(1)}, u32[]{:S(2)}, u32[]{:S(2)}) collective-permute-start(bf16[4,2,4,16,768]{4,3,2,1,0:T(8,128)(2,1)S(1)} %slice.84), channel_id=1, source_target_pairs={{0,3},{1,0},{2,1},{3,2},{4,7},{5,4},{6,5},{7,6},{8,11},{9,8},{10,9... | collective-permute-start | bytes 2359304 | tf_op jit(solution)/shard_map/ppermute | solution.py:434
  55.0 1.8 %pad_maximum_fusion.1.near_ref = bf16[192,1536]{1,0:T(8,128)(2,1)} fusion(bf16[96,1536]{1,0:T(8,128)(2,1)} %collective-permute-done.2, bf16[48,1536]{1,0:T(8,128)(2,1)S(1)} %collective-permute-done.1, bf16[48,1536]{1,0:T(8,128)(2,1)S(1)} %bitcast.37), kind=kLoop, calls=%fused_computation.3 | loop fusion | flops 1769472 | bytes 1179648 | tf_op jit(solution)/shard_map/concatenate | solution.py:468
  56.8 2.4 %collective-permute-start.3 = (bf16[192,1536]{1,0:T(8,128)(2,1)}, bf16[192,1536]{1,0:T(8,128)(2,1)S(1)}, u32[]{:S(2)}, u32[]{:S(2)}) collective-permute-start(bf16[192,1536]{1,0:T(8,128)(2,1)} %pad_maximum_fusion.1.near_ref), channel_id=1, source_target_pairs={{0,1},{1,0},{2,3},{3,2},{4,5},{5,4},{6,7},{7,6},{8,9},{9,8},{10,11... | collective-permute-start | bytes 1769480 | tf_op jit(solution)/shard_map/ppermute | solution.py:438
  59.3 0.5 fusion.14.spot_ref
  59.8 0.8 and_select_fusion.mask_ref
  60.6 7.3 %window_bias.1.bias_ref = f32[6,768,192]{2,1,0:T(8,128)} custom-call(f32[1,24,3312]{2,1,0:T(8,128)} %table_ref, bf16[2,138,384]{2,1,0:T(8,128)(2,1)} %constant.133.clone.open_ref, bf16[384,192]{1,0:T(8,128)(2,1)} %constant.129.clone.spread_ref, f32[192,192]{1,0:T(8,128)} %and_select_fusion.mask_ref), custom_call_target="tpu_custom_call" | custom-call | tf_op jit(solution)/shard_map/window_bias/pallas_call | solution.py:318
  67.9 0.0 collective-permute-done.5.south_ref
  67.9 0.9 copy-done.1
  68.8 2.5 %normalise.1 = (f32[4,64,768]{2,1,0:T(8,128)}, f32[64,128]{1,0:T(8,128)}) custom-call(bf16[4,2,6,16,768]{4,3,2,1,0:T(8,128)(2,1)} %copy-done, bf16[4,2,6,16,768]{4,3,2,1,0:T(8,128)(2,1)} %copy-done, bf16[4,2,4,16,768]{4,3,2,1,0:T(8,128)(2,1)} %copy-done.1, bf16[256,256]{1,0:T(8,128)(2,1)} %constant.130.clone.quarter_ref), custom_call_target="tpu_custom_call" | custom-call | tf_op jit(solution)/shard_map/normalise/pallas_call | solution.py:348
  71.4 0.0 all-to-all-done.1.w_ref
  71.4 1.0 copy-done.2
  72.4 0.8 copy-done.5
  73.2 4.7 %merge_product.1 = bf16[8,64,512]{2,1,0:T(8,128)(2,1)} custom-call(s32[8]{0:T(128)} %fusion.14.spot_ref, bf16[192,1536]{1,0:T(8,128)(2,1)} %pad_maximum_fusion.1.near_ref, bf16[192,1536]{1,0:T(8,128)(2,1)} %copy-done.5, bf16[4,384,384]{2,1,0:T(8,128)(2,1)} %copy-done.2, bf16[512,384]{1,0:T(8,128)(2,1)} %constant.132.clone.shuffle_ref.order_ref), custom_call_target="tpu_custom_call" | custom-call | tf_op jit(solution)/shard_map/merge_product/pallas_call | solution.py:368
  77.9 5.2 %all-to-all-start.2 = ((bf16[8,64,512]{2,1,0:T(8,128)(2,1)}), bf16[8,64,512]{2,1,0:T(8,128)(2,1)S(1)}, u32[]{:S(2)}, u32[]{:S(2)}) async-start(bf16[8,64,512]{2,1,0:T(8,128)(2,1)} %merge_product.1), calls=%async_computation.2 | async-start | bytes 1048576 | tf_op jit(solution)/shard_map/all_to_all | solution.py:442
  83.2 7.4 %window_probs.1.p_ref = f32[6,768,192]{2,1,0:T(8,128)} custom-call(bf16[4,2,6,16,768]{4,3,2,1,0:T(8,128)(2,1)} %copy-done, bf16[4,2,4,16,768]{4,3,2,1,0:T(8,128)(2,1)} %copy-done.1, f32[6,768,192]{2,1,0:T(8,128)} %window_bias.1.bias_ref), custom_call_target="tpu_custom_call" | custom-call | tf_op jit(solution)/shard_map/window_probs/pallas_call | solution.py:336
  90.5 0.3 all-to-all-done.2.recv_ref
  90.8 0.8 copy-done.4
  91.6 10.3 %score_grads.1 = (bf16[6,192,128]{2,1,0:T(8,128)(2,1)}, bf16[6,768,192]{2,1,0:T(8,128)(2,1)}, f32[16,24,384]{2,1,0:T(8,128)}) custom-call(bf16[8,64,512]{2,1,0:T(8,128)(2,1)} %copy-done.4, bf16[512,384]{1,0:T(8,128)(2,1)} %constant.132.clone.shuffle_ref.order_ref, f32[4,64,768]{2,1,0:T(8,128)} %get-tuple-element.25.normed_ref, ...), custom_call_target="tpu_custom_call" | custom-call | tf_op jit(solution)/shard_map/score_grads/pallas_call | solution.py:380
  102.0 7.7 %all-to-all-start.3 = ((f32[16,24,384]{2,1,0:T(8,128)}), f32[16,24,384]{2,1,0:T(8,128)S(1)}, u32[]{:S(2)}, u32[]{:S(2)}) async-start(f32[16,24,384]{2,1,0:T(8,128)} %get-tuple-element.29), calls=%async_computation.3 | async-start | bytes 1179648 | tf_op jit(solution)/shard_map/all_to_all | solution.py:442
  109.6 7.0 %window_grads.1 = bf16[3,192,768]{2,1,0:T(8,128)(2,1)} custom-call(bf16[4,2,6,16,768]{4,3,2,1,0:T(8,128)(2,1)} %copy-done, bf16[4,2,4,16,768]{4,3,2,1,0:T(8,128)(2,1)} %copy-done.1, bf16[6,192,128]{2,1,0:T(8,128)(2,1)} %get-tuple-element.30.o_ref, bf16[6,768,192]{2,1,0:T(8,128)(2,1)} %get-tuple-element.31.d_ref, f32[6,768,192]{2,1,0:T(8,128)} %window_probs.1.p_ref), custom_call_target="tpu_custom_call" | custom-call | tf_op jit(solution)/shard_map/window_grads/pallas_call | solution.py:415
  116.6 3.1 %all-to-all-done.3 = f32[16,24,384]{2,1,0:T(8,128)S(1)} async-done(((f32[16,24,384]{2,1,0:T(8,128)}), f32[16,24,384]{2,1,0:T(8,128)S(1)}, u32[]{:S(2)}, u32[]{:S(2)}) %all-to-all-start.3) | async-done | bytes 589856 | tf_op jit(solution)/shard_map/all_to_all | solution.py:442
  119.7 0.7 broadcast_in_dim.42
  120.4 8.5 %all-to-all-start.4 = ((bf16[8,24,384]{2,1,0:T(8,128)(2,1)}), bf16[8,24,384]{2,1,0:T(8,128)(2,1)S(1)}, u32[]{:S(2)}, u32[]{:S(2)}) async-start(bf16[8,24,384]{2,1,0:T(8,128)(2,1)} %broadcast_in_dim.42), calls=%async_computation.4 | async-start | bytes 294912 | tf_op jit(solution)/shard_map/all_to_all | solution.py:442
  128.9 0.1 fusion.15
  129.0 0.3 copy.69
  129.3 2.1 %collective-permute-start.6 = (bf16[3,2,3,12,768]{4,1,3,2,0:T(2,128)(2,1)S(1)}, bf16[3,2,3,12,768]{4,1,3,2,0:T(2,128)(2,1)S(1)}, u32[]{:S(2)}, u32[]{:S(2)}) collective-permute-start(bf16[3,2,3,12,768]{4,1,3,2,0:T(2,128)(2,1)S(1)} %copy.69), channel_id=1, source_target_pairs={{0,1},{1,2},{2,3},{3,0},{4,5},{5,6},{6,7},{7,4},{8,9},{9,10},{10,1... | collective-permute-start | bytes 995336 | tf_op jit(solution)/shard_map/ppermute | solution.py:434
  131.4 0.3 copy.70
  131.6 7.6 %collective-permute-done.6 = bf16[3,2,3,12,768]{4,1,3,2,0:T(2,128)(2,1)S(1)} collective-permute-done((bf16[3,2,3,12,768]{4,1,3,2,0:T(2,128)(2,1)S(1)}, bf16[3,2,3,12,768]{4,1,3,2,0:T(2,128)(2,1)S(1)}, u32[]{:S(2)}, u32[]{:S(2)}) %collective-permute-start.6) | collective-permute-done | bytes 331808 | tf_op jit(solution)/shard_map/ppermute | solution.py:434
  139.2 0.9 pad_maximum_fusion
  140.1 4.1 %all-to-all-done.4 = bf16[8,24,384]{2,1,0:T(8,128)(2,1)S(1)} async-done(((bf16[8,24,384]{2,1,0:T(8,128)(2,1)}), bf16[8,24,384]{2,1,0:T(8,128)(2,1)S(1)}, u32[]{:S(2)}, u32[]{:S(2)}) %all-to-all-start.4) | async-done | bytes 147488 | tf_op jit(solution)/shard_map/all_to_all | solution.py:442
  144.2 0.7 broadcast_in_dim.43
  144.9 4.8 %all-to-all-start.5 = ((bf16[16,24,384]{2,1,0:T(8,128)(2,1)}), bf16[16,24,384]{2,1,0:T(8,128)(2,1)S(1)}, u32[]{:S(2)}, u32[]{:S(2)}) async-start(bf16[16,24,384]{2,1,0:T(8,128)(2,1)} %broadcast_in_dim.43), calls=%async_computation.5 | async-start | bytes 589824 | tf_op jit(solution)/shard_map/all_to_all | solution.py:442
  149.8 0.5 fusion.16
  150.2 3.4 %collective-permute-start.7 = (bf16[3,2,6,6,768]{4,1,3,2,0:T(2,128)(2,1)S(1)}, bf16[3,2,6,6,768]{4,1,3,2,0:T(2,128)(2,1)S(1)}, u32[]{:S(2)}, u32[]{:S(2)}) collective-permute-start(bf16[3,2,6,6,768]{4,1,3,2,0:T(2,128)(2,1)S(1)} %get-tuple-element.39), channel_id=1, source_target_pairs={{0,4},{4,8},{8,12},{12,16},{16,20},{20,24},{24,28},{28,32},{32,36}... | collective-permute-start | bytes 995336 | tf_op jit(solution)/shard_map/ppermute | solution.py:434
  153.6 9.8 %collective-permute-done.7 = bf16[3,2,6,6,768]{4,1,3,2,0:T(2,128)(2,1)S(1)} collective-permute-done((bf16[3,2,6,6,768]{4,1,3,2,0:T(2,128)(2,1)S(1)}, bf16[3,2,6,6,768]{4,1,3,2,0:T(2,128)(2,1)S(1)}, u32[]{:S(2)}, u32[]{:S(2)}) %collective-permute-start.7) | collective-permute-done | bytes 331808 | tf_op jit(solution)/shard_map/ppermute | solution.py:434
  163.5 1.6 fusion.2
  165.1 0.0 all-to-all-done.5
  165.1 0.9 reshape.89
  166.0 0.3 convert_bitcast_fusion
  166.3 0.2 copy.64
  166.5 1.5 reshape.93
  (29 shorter events, 0.2 us)
Async XLA Ops:
  0.6 25.8 %copy-start.6 = (bf16[2,6,12,768]{3,0,2,1:T(2,128)(2,1)S(1)}, bf16[2,6,12,768]{3,0,2,1:T(2,128)(2,1)}, u32[]{:S(2)}) copy-start(bf16[2,6,12,768]{3,0,2,1:T(2,128)(2,1)} %param.21) | copy-start | bytes 663556
  0.6 25.8 %copy-start.7 = (bf16[2,6,12,768]{3,0,2,1:T(2,128)(2,1)S(1)}, bf16[2,6,12,768]{3,0,2,1:T(2,128)(2,1)}, u32[]{:S(2)}) copy-start(bf16[2,6,12,768]{3,0,2,1:T(2,128)(2,1)} %param.15) | copy-start | bytes 663556
  0.7 26.2 %copy-start.9 = (bf16[2,6,12,768]{3,0,2,1:T(2,128)(2,1)S(1)}, bf16[2,6,12,768]{3,0,2,1:T(2,128)(2,1)}, u32[]{:S(2)}) copy-start(bf16[2,6,12,768]{3,0,2,1:T(2,128)(2,1)} %param.20) | copy-start | bytes 663556
  0.7 26.2 %copy-start.8 = (bf16[2,6,12,768]{3,0,2,1:T(2,128)(2,1)S(1)}, bf16[2,6,12,768]{3,0,2,1:T(2,128)(2,1)}, u32[]{:S(2)}) copy-start(bf16[2,6,12,768]{3,0,2,1:T(2,128)(2,1)} %param.19) | copy-start | bytes 663556
  2.5 43.4 %all-to-all-start = ((bf16[16,24,384]{2,1,0:T(8,128)(2,1)}), bf16[16,24,384]{2,1,0:T(8,128)(2,1)S(1)}, u32[]{:S(2)}, u32[]{:S(2)}) async-start(bf16[16,24,384]{2,1,0:T(8,128)(2,1)} %pack_weight.1), calls=%async_computation | async-start | bytes 589824 | tf_op jit(solution)/shard_map/all_to_all | solution.py:442
  18.7 15.7 %collective-permute-start = (bf16[2,3,3,1536]{3,0,2,1:T(2,128)(2,1)S(1)}, bf16[2,3,3,1536]{3,0,2,1:T(2,128)(2,1)S(1)}, u32[]{:S(2)}, u32[]{:S(2)}) collective-permute-start(bf16[2,3,3,1536]{3,0,2,1:T(2,128)(2,1)S(1)} %get-tuple-element.50), channel_id=1, source_target_pairs={{0,508},{4,0},{8,4},{12,8},{16,12},{20,16},{24,20},{28,24},{32,28}... | collective-permute-start | bytes 165896 | tf_op jit(solution)/shard_map/ppermute | solution.py:434
  28.2 17.7 %collective-permute-start.4 = (bf16[4,2,6,6,768]{4,0,3,2,1:T(4,128)(2,1)S(1)}, bf16[4,2,6,6,768]{4,0,3,2,1:T(4,128)(2,1)S(1)}, u32[]{:S(2)}, u32[]{:S(2)}) collective-permute-start(bf16[4,2,6,6,768]{4,0,3,2,1:T(4,128)(2,1)S(1)} %copy.60), channel_id=1, source_target_pairs={{0,508},{4,0},{8,4},{12,8},{16,12},{20,16},{24,20},{28,24},{32,28}... | collective-permute-start | bytes 1327112 | tf_op jit(solution)/shard_map/ppermute | solution.py:434
  34.6 8.5 %collective-permute-start.1 = (bf16[48,1536]{1,0:T(8,128)(2,1)S(1)}, bf16[48,1536]{1,0:T(8,128)(2,1)S(1)}, u32[]{:S(2)}, u32[]{:S(2)}) collective-permute-start(bf16[48,1536]{1,0:T(8,128)(2,1)S(1)} %bitcast.35), channel_id=1, source_target_pairs={{0,2},{1,3},{2,0},{3,1},{4,6},{5,7},{6,4},{7,5},{8,10},{9,11},{10,... | collective-permute-start | bytes 442376 | tf_op jit(solution)/shard_map/ppermute | solution.py:438
  43.2 11.8 %collective-permute-start.2 = (bf16[96,1536]{1,0:T(8,128)(2,1)S(1)}, bf16[96,1536]{1,0:T(8,128)(2,1)}, u32[]{:S(2)}, u32[]{:S(2)}) collective-permute-start(bf16[96,1536]{1,0:T(8,128)(2,1)S(1)} %pad_maximum_fusion.3), channel_id=1, source_target_pairs={{0,256},{4,260},{8,264},{12,268},{16,272},{20,276},{24,280},{28,28... | collective-permute-start | bytes 884744 | tf_op jit(solution)/shard_map/ppermute | solution.py:438
  47.1 24.3 %all-to-all-start.1 = ((bf16[4,384,384]{2,1,0:T(8,128)(2,1)}), bf16[4,384,384]{2,1,0:T(8,128)(2,1)S(1)}, u32[]{:S(2)}, u32[]{:S(2)}) async-start(bf16[4,384,384]{2,1,0:T(8,128)(2,1)} %broadcast_in_dim.38), calls=%async_computation.1 | async-start | bytes 2359296 | tf_op jit(solution)/shard_map/all_to_all | solution.py:442
  53.0 3.8 %copy-start = (bf16[4,2,6,16,768]{4,3,2,1,0:T(8,128)(2,1)}, bf16[4,2,6,16,768]{4,3,2,1,0:T(8,128)(2,1)S(1)}, u32[]{:S(2)}) copy-start(bf16[4,2,6,16,768]{4,3,2,1,0:T(8,128)(2,1)S(1)} %maximum_maximum_fusion.a_ref.b_ref.north_ref) | copy-start | bytes 3538948
  53.1 14.9 %collective-permute-start.5 = (bf16[4,2,4,16,768]{4,3,2,1,0:T(8,128)(2,1)S(1)}, bf16[4,2,4,16,768]{4,3,2,1,0:T(8,128)(2,1)S(1)}, u32[]{:S(2)}, u32[]{:S(2)}) collective-permute-start(bf16[4,2,4,16,768]{4,3,2,1,0:T(8,128)(2,1)S(1)} %slice.84), channel_id=1, source_target_pairs={{0,3},{1,0},{2,1},{3,2},{4,7},{5,4},{6,5},{7,6},{8,11},{9,8},{10,9... | collective-permute-start | bytes 2359304 | tf_op jit(solution)/shard_map/ppermute | solution.py:434
  56.8 14.5 %collective-permute-start.3 = (bf16[192,1536]{1,0:T(8,128)(2,1)}, bf16[192,1536]{1,0:T(8,128)(2,1)S(1)}, u32[]{:S(2)}, u32[]{:S(2)}) collective-permute-start(bf16[192,1536]{1,0:T(8,128)(2,1)} %pad_maximum_fusion.1.near_ref), channel_id=1, source_target_pairs={{0,1},{1,0},{2,3},{3,2},{4,5},{5,4},{6,7},{7,6},{8,9},{9,8},{10,11... | collective-permute-start | bytes 1769480 | tf_op jit(solution)/shard_map/ppermute | solution.py:438
  67.9 0.9 copy-start.1
  71.4 1.0 copy-start.2
  72.4 0.8 copy-start.5
  77.9 12.9 %all-to-all-start.2 = ((bf16[8,64,512]{2,1,0:T(8,128)(2,1)}), bf16[8,64,512]{2,1,0:T(8,128)(2,1)S(1)}, u32[]{:S(2)}, u32[]{:S(2)}) async-start(bf16[8,64,512]{2,1,0:T(8,128)(2,1)} %merge_product.1), calls=%async_computation.2 | async-start | bytes 1048576 | tf_op jit(solution)/shard_map/all_to_all | solution.py:442
  90.8 0.8 copy-start.4
  102.0 17.7 %all-to-all-start.3 = ((f32[16,24,384]{2,1,0:T(8,128)}), f32[16,24,384]{2,1,0:T(8,128)S(1)}, u32[]{:S(2)}, u32[]{:S(2)}) async-start(f32[16,24,384]{2,1,0:T(8,128)} %get-tuple-element.29), calls=%async_computation.3 | async-start | bytes 1179648 | tf_op jit(solution)/shard_map/all_to_all | solution.py:442
  116.6 12.3 %copy-start.3 = (bf16[3,192,768]{2,1,0:T(8,128)(2,1)S(1)}, bf16[3,192,768]{2,1,0:T(8,128)(2,1)}, u32[]{:S(2)}) copy-start(bf16[3,192,768]{2,1,0:T(8,128)(2,1)} %window_grads.1) | copy-start | bytes 2654212
  120.4 23.8 %all-to-all-start.4 = ((bf16[8,24,384]{2,1,0:T(8,128)(2,1)}), bf16[8,24,384]{2,1,0:T(8,128)(2,1)S(1)}, u32[]{:S(2)}, u32[]{:S(2)}) async-start(bf16[8,24,384]{2,1,0:T(8,128)(2,1)} %broadcast_in_dim.42), calls=%async_computation.4 | async-start | bytes 294912 | tf_op jit(solution)/shard_map/all_to_all | solution.py:442
  129.3 9.9 %collective-permute-start.6 = (bf16[3,2,3,12,768]{4,1,3,2,0:T(2,128)(2,1)S(1)}, bf16[3,2,3,12,768]{4,1,3,2,0:T(2,128)(2,1)S(1)}, u32[]{:S(2)}, u32[]{:S(2)}) collective-permute-start(bf16[3,2,3,12,768]{4,1,3,2,0:T(2,128)(2,1)S(1)} %copy.69), channel_id=1, source_target_pairs={{0,1},{1,2},{2,3},{3,0},{4,5},{5,6},{6,7},{7,4},{8,9},{9,10},{10,1... | collective-permute-start | bytes 995336 | tf_op jit(solution)/shard_map/ppermute | solution.py:434
  144.9 20.1 %all-to-all-start.5 = ((bf16[16,24,384]{2,1,0:T(8,128)(2,1)}), bf16[16,24,384]{2,1,0:T(8,128)(2,1)S(1)}, u32[]{:S(2)}, u32[]{:S(2)}) async-start(bf16[16,24,384]{2,1,0:T(8,128)(2,1)} %broadcast_in_dim.43), calls=%async_computation.5 | async-start | bytes 589824 | tf_op jit(solution)/shard_map/all_to_all | solution.py:442
  150.2 13.2 %collective-permute-start.7 = (bf16[3,2,6,6,768]{4,1,3,2,0:T(2,128)(2,1)S(1)}, bf16[3,2,6,6,768]{4,1,3,2,0:T(2,128)(2,1)S(1)}, u32[]{:S(2)}, u32[]{:S(2)}) collective-permute-start(bf16[3,2,6,6,768]{4,1,3,2,0:T(2,128)(2,1)S(1)} %get-tuple-element.39), channel_id=1, source_target_pairs={{0,4},{4,8},{8,12},{12,16},{16,20},{20,24},{24,28},{28,32},{32,36}... | collective-permute-start | bytes 995336 | tf_op jit(solution)/shard_map/ppermute | solution.py:434

commit v4 on v3

--- a/solution.py
+++ b/solution.py
@@ -111,35 +111,36 @@
         out_ref[z] = packed
 
 
-def bias_kernel(table_ref, open_ref, spread_ref, mask_ref, bias_ref, wide_ref):
-    @pl.when(pl.program_id(0) == 0)
-    def _():
-        halves = []
-        for half in range(2):
-            pieces = []
-            for a in range(ROWS):
-                first = (a // 6 * 2 + half) * 828 + a % 6 * 138
-                pieces.append(table_ref[0, :, first : first + 138])
-            halves.append(split_dot(jnp.concatenate(pieces, axis=0), open_ref[half]))
+def open_kernel(table_ref, open_ref, out_ref, wide_ref):
+    halves = []
+    for half in range(2):
+        pieces = []
+        for a in range(ROWS):
+            first = (a // 6 * 2 + half) * 828 + a % 6 * 138
+            pieces.append(table_ref[0, :, first : first + 138])
+        halves.append(split_dot(jnp.concatenate(pieces, axis=0), open_ref[half]))
+    whole = halves[0] + halves[1]
+    for s in range(3):
+        wide_ref[s] = whole[:, s * 128 : (s + 1) * 128]
+    for head in range(HEADS):
+        row = head % 4 * ROWS
         for s in range(3):
-            wide_ref[s] = (halves[0] + halves[1])[:, s * 128 : (s + 1) * 128]
-
-    first = pl.program_id(0) * 4
+            out_ref[head // 4, row : row + ROWS, s * 128 : (s + 1) * 128] = wide_ref[
+                s, pl.ds(head, ROWS, stride=HEADS), :
+            ]
+
+
+def probs_kernel(north_ref, south_ref, table_ref, spread_ref, mask_ref, p_ref):
     pieces = []
     for s in range(3):
-        table = jnp.concatenate(
-            [wide_ref[s, pl.ds(first + h, ROWS, stride=HEADS), :] for h in range(4)], axis=0
-        )
+        table = table_ref[0, :, s * 128 : (s + 1) * 128]
         table = jnp.broadcast_to(table[:, None, :], (4 * ROWS, PAD, 128))
         pieces.append(pltpu.roll(table, 0, 2, stride=1, stride_axis=1))
     wide = jnp.concatenate(pieces, axis=2).reshape(4 * TOK, WIDE)
-    bias = split_dot(wide, spread_ref[...]).reshape(4, TOK, TOK) + mask_ref[...][None]
-    bias_ref[0] = bias.reshape(4 * TOK, TOK)
-
-
-def probs_kernel(north_ref, south_ref, bias_ref, p_ref):
     q_win, k_win = window(north_ref, south_ref, 0), window(north_ref, south_ref, 1)
-    scores = dot(by_head(q_win), k_win, ((1,), (1,))) * score_factor + bias_ref[0]
+    scores = dot(by_head(q_win), k_win, ((1,), (1,))) * score_factor
+    scores = scores + split_dot(wide, spread_ref[...])
+    scores = (scores.reshape(4, TOK, TOK) + mask_ref[...][None]).reshape(4 * TOK, TOK)
     expon = jnp.exp(scores - jnp.max(scores, axis=-1, keepdims=True))
     p_ref[0] = expon * (1.0 / jnp.sum(expon, axis=-1, keepdims=True))
 
@@ -314,34 +315,34 @@
     )(lat, weight)
 
 
-def window_bias(table, open_up, spread, mask):
-    return pl.pallas_call(
-        bias_kernel,
+def open_table(table, open_up):
+    return pl.pallas_call(
+        open_kernel,
+        in_specs=[vmem, vmem],
+        out_specs=vmem,
+        out_shape=jax.ShapeDtypeStruct((GROUPS, 4 * ROWS, WIDE), jnp.float32),
+        scratch_shapes=[pltpu.VMEM((3, ROWS * HEADS, 128), jnp.float32)],
+        compiler_params=params,
+        name="open_table",
+    )(table, open_up)
+
+
+def window_probs(across, south, table, spread, mask):
+    return pl.pallas_call(
+        probs_kernel,
         grid=(GROUPS,),
         in_specs=[
-            whole_spec((1, HEADS, 3312)),
-            whole_spec((2, 138, WIDE)),
+            north_spec(0, 2),
+            south_spec(0, 2),
+            group_spec(4 * ROWS, WIDE),
             whole_spec((WIDE, TOK)),
             whole_spec((TOK, TOK)),
         ],
         out_specs=group_spec(4 * TOK, TOK),
         out_shape=jax.ShapeDtypeStruct((GROUPS, 4 * TOK, TOK), jnp.float32),
-        scratch_shapes=[pltpu.VMEM((3, ROWS * HEADS, 128), jnp.float32)],
-        compiler_params=params,
-        name="window_bias",
-    )(table, open_up, spread, mask)
-
-
-def window_probs(across, south, bias):
-    return pl.pallas_call(
-        probs_kernel,
-        grid=(GROUPS,),
-        in_specs=[north_spec(0, 2), south_spec(0, 2), group_spec(4 * TOK, TOK)],
-        out_specs=group_spec(4 * TOK, TOK),
-        out_shape=jax.ShapeDtypeStruct((GROUPS, 4 * TOK, TOK), jnp.float32),
         compiler_params=params,
         name="window_probs",
-    )(across, south, bias)
+    )(across, south, table, spread, mask)
 
 
 def normalise(across, south, quarter):
@@ -471,10 +472,8 @@
     rel = jnp.bitwise_xor(jnp.arange(8, dtype=jnp.int32), me)
     spots = (rel % 2 * 4 + rel // 4 * 2 + rel // 2 % 2) * 48
 
-    weight_z = jnp.broadcast_to(weight_z[None], (NY,) + weight_z.shape)
-    weight_z, bias_table = lax.optimization_barrier((weight_z, bias_table))
-    weight = swap(weight_z, "lon", y_groups)
-    bias = window_bias(bias_table, open_up, spread, mask)
+    weight = share(weight_z, NY, "lon", y_groups)
+    table = open_table(bias_table, open_up)
 
     eastern = from_behind(
         jnp.stack([q_proj[:, :, :6], k_proj[:, :, :6], v_proj[:, :, :6], y_block[:, :, :6]]),
@@ -492,12 +491,12 @@
     south = from_behind(across[:, :, :4], "lat", -1)
 
     normed, inverse = normalise(across, south, quarter)
-    weight, bias, normed = lax.optimization_barrier((weight, bias, normed))
+    weight, table, mask, normed = lax.optimization_barrier((weight, table, mask, normed))
     parts = merge_product(spots, near, far, weight, shuffle)
     recv = swap(parts, ("lon", "lat"), x_lat_groups)
 
-    bias, _ = lax.optimization_barrier((bias, parts))
-    probs = window_probs(across, south, bias)
+    table, _ = lax.optimization_barrier((table, parts))
+    probs = window_probs(across, south, table, spread, mask)
 
     o_win, d_low, table_part = score_grads(
         recv, order, normed, inverse, merge_gain.reshape(4, 1, 768), back, sums, across, south, probs

time: 169 us -> 169 us (level)
  Pallas kernels: 41.1 us -> 37.3 us
  waiting for transfers between devices: 32.7 us -> 34.5 us
    pallas_call x1, Pallas kernels: 7.34 us -> 2.46 us  [open_table(): pl.pallas_call(open_kernel, in_specs=[vmem, vmem], out_specs=vmem, out_sh...]
  transfers between devices with their start and end apart: 14 -> 14, of which waited for: 7 -> 7; matrix products, arithmetic and copies ran while one was open for 7% -> 7% of each run, Pallas kernels for 14% -> 12%
where the time goes in v4:
time: 169 us; the launch traced here: 167 us
  starting transfers between devices  74.8 us (44%)
  Pallas kernels  37.3 us (22%)
  waiting for transfers between devices  34.5 us (20%)
  local copies, waits for them, and re-layouts  11.9 us (7%)
  other arithmetic  7.52 us (4%)
    all_to_all x6, starting transfers between devices, swap(): lax.all_to_all(shard, axis, 0, 0, tiled=True, axis_index_groups=groups)  47.8 us
    ppermute x5, waiting for transfers between devices, from_behind(): lax.ppermute(shard, axis, [(i, (i + by) % size) for i in range(size)])  21.6 us
    ppermute x5, starting transfers between devices, from_behind(): lax.ppermute(shard, axis, [(i, (i + by) % size) for i in range(size)])  18.5 us
    pallas_call x1, Pallas kernels, score_grads(): pl.pallas_call(scores_kernel, grid=(GROUPS,), in_specs=[whole_spec((8, 64...  10.3 us
    ppermute x3, starting transfers between devices, partner(): lax.ppermute(shard, axis, [(i, i ^ bit) for i in range(lax.axis_size(axis...  8.43 us
    pallas_call x1, Pallas kernels, window_probs(): pl.pallas_call(probs_kernel, grid=(GROUPS,), in_specs=[north_spec(0, 2),...  8.33 us
    all_to_all x6, waiting for transfers between devices, swap(): lax.all_to_all(shard, axis, 0, 0, tiled=True, axis_index_groups=groups)  7.86 us
    pallas_call x1, Pallas kernels, window_grads(): pl.pallas_call(grads_kernel, grid=(GROUPS,), in_specs=[north_spec(0, 2),...  6.99 us
  transfers between devices with their start and end apart: 14, of which 7 were waited for; matrix products, arithmetic and copies ran while one was open for 7% of the time, Pallas kernels for 12%

profile of v4, /device:TPU:6, one launch (start us, length us, event | category | flops | bytes accessed | tf_op | source)
XLA Modules:
  0.0 167.0 jit_solution(2488955836595192489)
XLA Ops:
  0.7 1.9 %pack_weight.1 = bf16[16,24,384]{2,1,0:T(8,128)(2,1)} custom-call(s32[1]{0:T(128)} %bitcast.lat_ref, bf16[24,1536]{1,0:T(8,128)(2,1)} %w_ref.1), custom_call_target="tpu_custom_call" | custom-call | tf_op jit(solution)/shard_map/pack_weight/pallas_call | solution.py:308
  2.5 15.2 %all-to-all-start = ((bf16[16,24,384]{2,1,0:T(8,128)(2,1)}), bf16[16,24,384]{2,1,0:T(8,128)(2,1)S(1)}, u32[]{:S(2)}, u32[]{:S(2)}) async-start(bf16[16,24,384]{2,1,0:T(8,128)(2,1)} %pack_weight.1), calls=%async_computation | async-start | bytes 589824 | tf_op jit(solution)/shard_map/all_to_all | solution.py:443
  17.7 0.9 fusion.21
  18.7 7.8 %collective-permute-start = (bf16[2,3,3,1536]{3,0,2,1:T(2,128)(2,1)S(1)}, bf16[2,3,3,1536]{3,0,2,1:T(2,128)(2,1)S(1)}, u32[]{:S(2)}, u32[]{:S(2)}) collective-permute-start(bf16[2,3,3,1536]{3,0,2,1:T(2,128)(2,1)S(1)} %get-tuple-element.48), channel_id=1, source_target_pairs={{0,508},{4,0},{8,4},{12,8},{16,12},{20,16},{24,20},{28,24},{32,28}... | collective-permute-start | bytes 165896 | tf_op jit(solution)/shard_map/ppermute | solution.py:435
  26.5 0.3 fusion.19
  26.8 0.3 fusion.17
  27.2 0.8 pad_maximum_fusion.2
  28.0 0.2 copy.60
  28.2 3.4 %collective-permute-start.4 = (bf16[4,2,6,6,768]{4,0,3,2,1:T(4,128)(2,1)S(1)}, bf16[4,2,6,6,768]{4,0,3,2,1:T(4,128)(2,1)S(1)}, u32[]{:S(2)}, u32[]{:S(2)}) collective-permute-start(bf16[4,2,6,6,768]{4,0,3,2,1:T(4,128)(2,1)S(1)} %copy.60), channel_id=1, source_target_pairs={{0,508},{4,0},{8,4},{12,8},{16,12},{20,16},{24,20},{28,24},{32,28}... | collective-permute-start | bytes 1327112 | tf_op jit(solution)/shard_map/ppermute | solution.py:435
  31.6 0.1 pad.21.clone
  31.6 2.8 %collective-permute-done = bf16[2,3,3,1536]{3,0,2,1:T(2,128)(2,1)S(1)} collective-permute-done((bf16[2,3,3,1536]{3,0,2,1:T(2,128)(2,1)S(1)}, bf16[2,3,3,1536]{3,0,2,1:T(2,128)(2,1)S(1)}, u32[]{:S(2)}, u32[]{:S(2)}) %collective-permute-start) | collective-permute-done | bytes 55328 | tf_op jit(solution)/shard_map/ppermute | solution.py:435
  34.4 0.2 maximum_maximum_fusion.1
  34.6 3.5 %collective-permute-start.1 = (bf16[48,1536]{1,0:T(8,128)(2,1)S(1)}, bf16[48,1536]{1,0:T(8,128)(2,1)S(1)}, u32[]{:S(2)}, u32[]{:S(2)}) collective-permute-start(bf16[48,1536]{1,0:T(8,128)(2,1)S(1)} %bitcast.35), channel_id=1, source_target_pairs={{0,2},{1,3},{2,0},{3,1},{4,6},{5,7},{6,4},{7,5},{8,10},{9,11},{10,... | collective-permute-start | bytes 442376 | tf_op jit(solution)/shard_map/ppermute | solution.py:439
  38.1 5.0 %collective-permute-done.1 = bf16[48,1536]{1,0:T(8,128)(2,1)S(1)} collective-permute-done((bf16[48,1536]{1,0:T(8,128)(2,1)S(1)}, bf16[48,1536]{1,0:T(8,128)(2,1)S(1)}, u32[]{:S(2)}, u32[]{:S(2)}) %collective-permute-start.1) | collective-permute-done | bytes 147488 | tf_op jit(solution)/shard_map/ppermute | solution.py:439
  43.2 2.5 %collective-permute-start.2 = (bf16[96,1536]{1,0:T(8,128)(2,1)S(1)}, bf16[96,1536]{1,0:T(8,128)(2,1)}, u32[]{:S(2)}, u32[]{:S(2)}) collective-permute-start(bf16[96,1536]{1,0:T(8,128)(2,1)S(1)} %pad_maximum_fusion.3), channel_id=1, source_target_pairs={{0,256},{4,260},{8,264},{12,268},{16,272},{20,276},{24,280},{28,28... | collective-permute-start | bytes 884744 | tf_op jit(solution)/shard_map/ppermute | solution.py:439
  45.7 0.1 pad.9.clone
  45.9 0.0 collective-permute-done.4
  45.9 0.1 copy.61
  45.9 0.0 all-to-all-done
  46.0 1.1 broadcast_in_dim.38
  47.1 5.4 %all-to-all-start.1 = ((bf16[4,384,384]{2,1,0:T(8,128)(2,1)}), bf16[4,384,384]{2,1,0:T(8,128)(2,1)S(1)}, u32[]{:S(2)}, u32[]{:S(2)}) async-start(bf16[4,384,384]{2,1,0:T(8,128)(2,1)} %broadcast_in_dim.38), calls=%async_computation.1 | async-start | bytes 2359296 | tf_op jit(solution)/shard_map/all_to_all | solution.py:443
  52.5 0.5 maximum_maximum_fusion.a_ref.b_ref.north_ref
  53.0 0.1 slice.84
  53.1 1.9 %collective-permute-start.5 = (bf16[4,2,4,16,768]{4,3,2,1,0:T(8,128)(2,1)S(1)}, bf16[4,2,4,16,768]{4,3,2,1,0:T(8,128)(2,1)S(1)}, u32[]{:S(2)}, u32[]{:S(2)}) collective-permute-start(bf16[4,2,4,16,768]{4,3,2,1,0:T(8,128)(2,1)S(1)} %slice.84), channel_id=1, source_target_pairs={{0,3},{1,0},{2,1},{3,2},{4,7},{5,4},{6,5},{7,6},{8,11},{9,8},{10,9... | collective-permute-start | bytes 2359304 | tf_op jit(solution)/shard_map/ppermute | solution.py:435
  55.0 0.0 collective-permute-done.2
  55.0 1.8 %pad_maximum_fusion.1.near_ref = bf16[192,1536]{1,0:T(8,128)(2,1)} fusion(bf16[96,1536]{1,0:T(8,128)(2,1)} %collective-permute-done.2, bf16[48,1536]{1,0:T(8,128)(2,1)S(1)} %collective-permute-done.1, bf16[48,1536]{1,0:T(8,128)(2,1)S(1)} %bitcast.37), kind=kLoop, calls=%fused_computation.3 | loop fusion | flops 1769472 | bytes 1179648 | tf_op jit(solution)/shard_map/concatenate | solution.py:469
  56.8 2.4 %collective-permute-start.3 = (bf16[192,1536]{1,0:T(8,128)(2,1)}, bf16[192,1536]{1,0:T(8,128)(2,1)S(1)}, u32[]{:S(2)}, u32[]{:S(2)}) collective-permute-start(bf16[192,1536]{1,0:T(8,128)(2,1)} %pad_maximum_fusion.1.near_ref), channel_id=1, source_target_pairs={{0,1},{1,0},{2,3},{3,2},{4,5},{5,4},{6,7},{7,6},{8,9},{9,8},{10,11... | collective-permute-start | bytes 1769480 | tf_op jit(solution)/shard_map/ppermute | solution.py:439
  59.2 2.5 %open_table.1.table_ref = f32[6,48,384]{2,1,0:T(8,128)} custom-call(f32[1,24,3312]{2,1,0:T(8,128)} %table_ref.1, bf16[2,138,384]{2,1,0:T(8,128)(2,1)} %constant.133.clone.open_ref), custom_call_target="tpu_custom_call" | custom-call | tf_op jit(solution)/shard_map/open_table/pallas_call | solution.py:319
  61.7 0.5 fusion.14.spot_ref
  62.3 0.8 and_select_fusion.mask_ref
  63.0 1.4 collective-permute-done.5.south_ref
  64.5 0.9 copy-done.1
  65.4 2.6 %normalise.1 = (f32[4,64,768]{2,1,0:T(8,128)}, f32[64,128]{1,0:T(8,128)}) custom-call(bf16[4,2,6,16,768]{4,3,2,1,0:T(8,128)(2,1)} %copy-done, bf16[4,2,6,16,768]{4,3,2,1,0:T(8,128)(2,1)} %copy-done, bf16[4,2,4,16,768]{4,3,2,1,0:T(8,128)(2,1)} %copy-done.1, bf16[256,256]{1,0:T(8,128)(2,1)} %constant.130.clone.quarter_ref), custom_call_target="tpu_custom_call" | custom-call | tf_op jit(solution)/shard_map/normalise/pallas_call | solution.py:349
  68.0 0.0 all-to-all-done.1.w_ref
  68.0 0.0 collective-permute-done.3.far_ref
  68.0 1.0 copy-done.2
  69.0 0.8 copy-done.5
  69.8 4.7 %merge_product.1 = bf16[8,64,512]{2,1,0:T(8,128)(2,1)} custom-call(s32[8]{0:T(128)} %fusion.14.spot_ref, bf16[192,1536]{1,0:T(8,128)(2,1)} %pad_maximum_fusion.1.near_ref, bf16[192,1536]{1,0:T(8,128)(2,1)} %copy-done.5, bf16[4,384,384]{2,1,0:T(8,128)(2,1)} %copy-done.2, bf16[512,384]{1,0:T(8,128)(2,1)} %constant.132.clone.shuffle_ref.order_ref), custom_call_target="tpu_custom_call" | custom-call | tf_op jit(solution)/shard_map/merge_product/pallas_call | solution.py:369
  74.6 5.5 %all-to-all-start.2 = ((bf16[8,64,512]{2,1,0:T(8,128)(2,1)}), bf16[8,64,512]{2,1,0:T(8,128)(2,1)S(1)}, u32[]{:S(2)}, u32[]{:S(2)}) async-start(bf16[8,64,512]{2,1,0:T(8,128)(2,1)} %merge_product.1), calls=%async_computation.2 | async-start | bytes 1048576 | tf_op jit(solution)/shard_map/all_to_all | solution.py:443
  80.1 8.3 %window_probs.1.p_ref = f32[6,768,192]{2,1,0:T(8,128)} custom-call(bf16[4,2,6,16,768]{4,3,2,1,0:T(8,128)(2,1)} %copy-done, bf16[4,2,4,16,768]{4,3,2,1,0:T(8,128)(2,1)} %copy-done.1, f32[6,48,384]{2,1,0:T(8,128)} %open_table.1.table_ref, bf16[384,192]{1,0:T(8,128)(2,1)} %constant.129.clone.spread_ref, f32[192,192]{1,0:T(8,128)} %and_select_fusion.mask_ref), custom_call_target="tpu_custom_call" | custom-call | tf_op jit(solution)/shard_map/window_probs/pallas_call | solution.py:331
  88.4 0.8 copy-done.4
  89.2 10.3 %score_grads.1 = (bf16[6,192,128]{2,1,0:T(8,128)(2,1)}, bf16[6,768,192]{2,1,0:T(8,128)(2,1)}, f32[16,24,384]{2,1,0:T(8,128)}) custom-call(bf16[8,64,512]{2,1,0:T(8,128)(2,1)} %copy-done.4, bf16[512,384]{1,0:T(8,128)(2,1)} %constant.132.clone.shuffle_ref.order_ref, f32[4,64,768]{2,1,0:T(8,128)} %get-tuple-element.22.normed_ref, ...), custom_call_target="tpu_custom_call" | custom-call | tf_op jit(solution)/shard_map/score_grads/pallas_call | solution.py:381
  99.6 7.6 %all-to-all-start.3 = ((f32[16,24,384]{2,1,0:T(8,128)}), f32[16,24,384]{2,1,0:T(8,128)S(1)}, u32[]{:S(2)}, u32[]{:S(2)}) async-start(f32[16,24,384]{2,1,0:T(8,128)} %get-tuple-element.27), calls=%async_computation.3 | async-start | bytes 1179648 | tf_op jit(solution)/shard_map/all_to_all | solution.py:443
  107.2 7.0 %window_grads.1 = bf16[3,192,768]{2,1,0:T(8,128)(2,1)} custom-call(bf16[4,2,6,16,768]{4,3,2,1,0:T(8,128)(2,1)} %copy-done, bf16[4,2,4,16,768]{4,3,2,1,0:T(8,128)(2,1)} %copy-done.1, bf16[6,192,128]{2,1,0:T(8,128)(2,1)} %get-tuple-element.28.o_ref, bf16[6,768,192]{2,1,0:T(8,128)(2,1)} %get-tuple-element.29.d_ref, f32[6,768,192]{2,1,0:T(8,128)} %window_probs.1.p_ref), custom_call_target="tpu_custom_call" | custom-call | tf_op jit(solution)/shard_map/window_grads/pallas_call | solution.py:416
  114.2 3.3 %all-to-all-done.3 = f32[16,24,384]{2,1,0:T(8,128)S(1)} async-done(((f32[16,24,384]{2,1,0:T(8,128)}), f32[16,24,384]{2,1,0:T(8,128)S(1)}, u32[]{:S(2)}, u32[]{:S(2)}) %all-to-all-start.3) | async-done | bytes 589856 | tf_op jit(solution)/shard_map/all_to_all | solution.py:443
  117.6 0.7 broadcast_in_dim.42
  118.2 9.4 %all-to-all-start.4 = ((bf16[8,24,384]{2,1,0:T(8,128)(2,1)}), bf16[8,24,384]{2,1,0:T(8,128)(2,1)S(1)}, u32[]{:S(2)}, u32[]{:S(2)}) async-start(bf16[8,24,384]{2,1,0:T(8,128)(2,1)} %broadcast_in_dim.42), calls=%async_computation.4 | async-start | bytes 294912 | tf_op jit(solution)/shard_map/all_to_all | solution.py:443
  127.7 0.1 fusion.15
  127.8 0.3 copy.69
  128.0 2.1 %collective-permute-start.6 = (bf16[3,2,3,12,768]{4,1,3,2,0:T(2,128)(2,1)S(1)}, bf16[3,2,3,12,768]{4,1,3,2,0:T(2,128)(2,1)S(1)}, u32[]{:S(2)}, u32[]{:S(2)}) collective-permute-start(bf16[3,2,3,12,768]{4,1,3,2,0:T(2,128)(2,1)S(1)} %copy.69), channel_id=1, source_target_pairs={{0,1},{1,2},{2,3},{3,0},{4,5},{5,6},{6,7},{7,4},{8,9},{9,10},{10,1... | collective-permute-start | bytes 995336 | tf_op jit(solution)/shard_map/ppermute | solution.py:435
  130.1 0.3 copy.70
  130.4 7.6 %collective-permute-done.6 = bf16[3,2,3,12,768]{4,1,3,2,0:T(2,128)(2,1)S(1)} collective-permute-done((bf16[3,2,3,12,768]{4,1,3,2,0:T(2,128)(2,1)S(1)}, bf16[3,2,3,12,768]{4,1,3,2,0:T(2,128)(2,1)S(1)}, u32[]{:S(2)}, u32[]{:S(2)}) %collective-permute-start.6) | collective-permute-done | bytes 331808 | tf_op jit(solution)/shard_map/ppermute | solution.py:435
  138.0 0.9 pad_maximum_fusion
  138.8 4.5 %all-to-all-done.4 = bf16[8,24,384]{2,1,0:T(8,128)(2,1)S(1)} async-done(((bf16[8,24,384]{2,1,0:T(8,128)(2,1)}), bf16[8,24,384]{2,1,0:T(8,128)(2,1)S(1)}, u32[]{:S(2)}, u32[]{:S(2)}) %all-to-all-start.4) | async-done | bytes 147488 | tf_op jit(solution)/shard_map/all_to_all | solution.py:443
  143.4 0.7 broadcast_in_dim.43
  144.1 4.7 %all-to-all-start.5 = ((bf16[16,24,384]{2,1,0:T(8,128)(2,1)}), bf16[16,24,384]{2,1,0:T(8,128)(2,1)S(1)}, u32[]{:S(2)}, u32[]{:S(2)}) async-start(bf16[16,24,384]{2,1,0:T(8,128)(2,1)} %broadcast_in_dim.43), calls=%async_computation.5 | async-start | bytes 589824 | tf_op jit(solution)/shard_map/all_to_all | solution.py:443
  148.8 0.5 fusion.16
  149.3 3.4 %collective-permute-start.7 = (bf16[3,2,6,6,768]{4,1,3,2,0:T(2,128)(2,1)S(1)}, bf16[3,2,6,6,768]{4,1,3,2,0:T(2,128)(2,1)S(1)}, u32[]{:S(2)}, u32[]{:S(2)}) collective-permute-start(bf16[3,2,6,6,768]{4,1,3,2,0:T(2,128)(2,1)S(1)} %get-tuple-element.37), channel_id=1, source_target_pairs={{0,4},{4,8},{8,12},{12,16},{16,20},{20,24},{24,28},{28,32},{32,36}... | collective-permute-start | bytes 995336 | tf_op jit(solution)/shard_map/ppermute | solution.py:435
  152.6 9.8 %collective-permute-done.7 = bf16[3,2,6,6,768]{4,1,3,2,0:T(2,128)(2,1)S(1)} collective-permute-done((bf16[3,2,6,6,768]{4,1,3,2,0:T(2,128)(2,1)S(1)}, bf16[3,2,6,6,768]{4,1,3,2,0:T(2,128)(2,1)S(1)}, u32[]{:S(2)}, u32[]{:S(2)}) %collective-permute-start.7) | collective-permute-done | bytes 331808 | tf_op jit(solution)/shard_map/ppermute | solution.py:435
  162.5 1.6 fusion.2
  164.1 0.9 reshape.89
  165.0 0.3 convert_bitcast_fusion
  165.3 0.2 copy.64
  165.5 1.5 reshape.93
  (29 shorter events, 0.2 us)
Async XLA Ops:
  0.6 25.8 %copy-start.6 = (bf16[2,6,12,768]{3,0,2,1:T(2,128)(2,1)S(1)}, bf16[2,6,12,768]{3,0,2,1:T(2,128)(2,1)}, u32[]{:S(2)}) copy-start(bf16[2,6,12,768]{3,0,2,1:T(2,128)(2,1)} %param.21) | copy-start | bytes 663556
  0.6 25.8 %copy-start.7 = (bf16[2,6,12,768]{3,0,2,1:T(2,128)(2,1)S(1)}, bf16[2,6,12,768]{3,0,2,1:T(2,128)(2,1)}, u32[]{:S(2)}) copy-start(bf16[2,6,12,768]{3,0,2,1:T(2,128)(2,1)} %param.15) | copy-start | bytes 663556
  0.7 26.2 %copy-start.9 = (bf16[2,6,12,768]{3,0,2,1:T(2,128)(2,1)S(1)}, bf16[2,6,12,768]{3,0,2,1:T(2,128)(2,1)}, u32[]{:S(2)}) copy-start(bf16[2,6,12,768]{3,0,2,1:T(2,128)(2,1)} %param.20) | copy-start | bytes 663556
  0.7 26.2 %copy-start.8 = (bf16[2,6,12,768]{3,0,2,1:T(2,128)(2,1)S(1)}, bf16[2,6,12,768]{3,0,2,1:T(2,128)(2,1)}, u32[]{:S(2)}) copy-start(bf16[2,6,12,768]{3,0,2,1:T(2,128)(2,1)} %param.19) | copy-start | bytes 663556
  2.5 43.4 %all-to-all-start = ((bf16[16,24,384]{2,1,0:T(8,128)(2,1)}), bf16[16,24,384]{2,1,0:T(8,128)(2,1)S(1)}, u32[]{:S(2)}, u32[]{:S(2)}) async-start(bf16[16,24,384]{2,1,0:T(8,128)(2,1)} %pack_weight.1), calls=%async_computation | async-start | bytes 589824 | tf_op jit(solution)/shard_map/all_to_all | solution.py:443
  18.7 15.7 %collective-permute-start = (bf16[2,3,3,1536]{3,0,2,1:T(2,128)(2,1)S(1)}, bf16[2,3,3,1536]{3,0,2,1:T(2,128)(2,1)S(1)}, u32[]{:S(2)}, u32[]{:S(2)}) collective-permute-start(bf16[2,3,3,1536]{3,0,2,1:T(2,128)(2,1)S(1)} %get-tuple-element.48), channel_id=1, source_target_pairs={{0,508},{4,0},{8,4},{12,8},{16,12},{20,16},{24,20},{28,24},{32,28}... | collective-permute-start | bytes 165896 | tf_op jit(solution)/shard_map/ppermute | solution.py:435
  28.2 17.7 %collective-permute-start.4 = (bf16[4,2,6,6,768]{4,0,3,2,1:T(4,128)(2,1)S(1)}, bf16[4,2,6,6,768]{4,0,3,2,1:T(4,128)(2,1)S(1)}, u32[]{:S(2)}, u32[]{:S(2)}) collective-permute-start(bf16[4,2,6,6,768]{4,0,3,2,1:T(4,128)(2,1)S(1)} %copy.60), channel_id=1, source_target_pairs={{0,508},{4,0},{8,4},{12,8},{16,12},{20,16},{24,20},{28,24},{32,28}... | collective-permute-start | bytes 1327112 | tf_op jit(solution)/shard_map/ppermute | solution.py:435
  34.6 8.5 %collective-permute-start.1 = (bf16[48,1536]{1,0:T(8,128)(2,1)S(1)}, bf16[48,1536]{1,0:T(8,128)(2,1)S(1)}, u32[]{:S(2)}, u32[]{:S(2)}) collective-permute-start(bf16[48,1536]{1,0:T(8,128)(2,1)S(1)} %bitcast.35), channel_id=1, source_target_pairs={{0,2},{1,3},{2,0},{3,1},{4,6},{5,7},{6,4},{7,5},{8,10},{9,11},{10,... | collective-permute-start | bytes 442376 | tf_op jit(solution)/shard_map/ppermute | solution.py:439
  43.2 11.8 %collective-permute-start.2 = (bf16[96,1536]{1,0:T(8,128)(2,1)S(1)}, bf16[96,1536]{1,0:T(8,128)(2,1)}, u32[]{:S(2)}, u32[]{:S(2)}) collective-permute-start(bf16[96,1536]{1,0:T(8,128)(2,1)S(1)} %pad_maximum_fusion.3), channel_id=1, source_target_pairs={{0,256},{4,260},{8,264},{12,268},{16,272},{20,276},{24,280},{28,28... | collective-permute-start | bytes 884744 | tf_op jit(solution)/shard_map/ppermute | solution.py:439
  47.1 20.9 %all-to-all-start.1 = ((bf16[4,384,384]{2,1,0:T(8,128)(2,1)}), bf16[4,384,384]{2,1,0:T(8,128)(2,1)S(1)}, u32[]{:S(2)}, u32[]{:S(2)}) async-start(bf16[4,384,384]{2,1,0:T(8,128)(2,1)} %broadcast_in_dim.38), calls=%async_computation.1 | async-start | bytes 2359296 | tf_op jit(solution)/shard_map/all_to_all | solution.py:443
  53.0 3.8 %copy-start = (bf16[4,2,6,16,768]{4,3,2,1,0:T(8,128)(2,1)}, bf16[4,2,6,16,768]{4,3,2,1,0:T(8,128)(2,1)S(1)}, u32[]{:S(2)}) copy-start(bf16[4,2,6,16,768]{4,3,2,1,0:T(8,128)(2,1)S(1)} %maximum_maximum_fusion.a_ref.b_ref.north_ref) | copy-start | bytes 3538948
  53.1 11.4 %collective-permute-start.5 = (bf16[4,2,4,16,768]{4,3,2,1,0:T(8,128)(2,1)S(1)}, bf16[4,2,4,16,768]{4,3,2,1,0:T(8,128)(2,1)S(1)}, u32[]{:S(2)}, u32[]{:S(2)}) collective-permute-start(bf16[4,2,4,16,768]{4,3,2,1,0:T(8,128)(2,1)S(1)} %slice.84), channel_id=1, source_target_pairs={{0,3},{1,0},{2,1},{3,2},{4,7},{5,4},{6,5},{7,6},{8,11},{9,8},{10,9... | collective-permute-start | bytes 2359304 | tf_op jit(solution)/shard_map/ppermute | solution.py:435
  56.8 11.2 %collective-permute-start.3 = (bf16[192,1536]{1,0:T(8,128)(2,1)}, bf16[192,1536]{1,0:T(8,128)(2,1)S(1)}, u32[]{:S(2)}, u32[]{:S(2)}) collective-permute-start(bf16[192,1536]{1,0:T(8,128)(2,1)} %pad_maximum_fusion.1.near_ref), channel_id=1, source_target_pairs={{0,1},{1,0},{2,3},{3,2},{4,5},{5,4},{6,7},{7,6},{8,9},{9,8},{10,11... | collective-permute-start | bytes 1769480 | tf_op jit(solution)/shard_map/ppermute | solution.py:439
  64.5 0.9 copy-start.1
  68.0 1.0 copy-start.2
  69.0 0.8 copy-start.5
  74.6 13.9 %all-to-all-start.2 = ((bf16[8,64,512]{2,1,0:T(8,128)(2,1)}), bf16[8,64,512]{2,1,0:T(8,128)(2,1)S(1)}, u32[]{:S(2)}, u32[]{:S(2)}) async-start(bf16[8,64,512]{2,1,0:T(8,128)(2,1)} %merge_product.1), calls=%async_computation.2 | async-start | bytes 1048576 | tf_op jit(solution)/shard_map/all_to_all | solution.py:443
  88.4 0.8 copy-start.4
  99.6 18.0 %all-to-all-start.3 = ((f32[16,24,384]{2,1,0:T(8,128)}), f32[16,24,384]{2,1,0:T(8,128)S(1)}, u32[]{:S(2)}, u32[]{:S(2)}) async-start(f32[16,24,384]{2,1,0:T(8,128)} %get-tuple-element.27), calls=%async_computation.3 | async-start | bytes 1179648 | tf_op jit(solution)/shard_map/all_to_all | solution.py:443
  114.2 13.5 %copy-start.3 = (bf16[3,192,768]{2,1,0:T(8,128)(2,1)S(1)}, bf16[3,192,768]{2,1,0:T(8,128)(2,1)}, u32[]{:S(2)}) copy-start(bf16[3,192,768]{2,1,0:T(8,128)(2,1)} %window_grads.1) | copy-start | bytes 2654212
  118.2 25.1 %all-to-all-start.4 = ((bf16[8,24,384]{2,1,0:T(8,128)(2,1)}), bf16[8,24,384]{2,1,0:T(8,128)(2,1)S(1)}, u32[]{:S(2)}, u32[]{:S(2)}) async-start(bf16[8,24,384]{2,1,0:T(8,128)(2,1)} %broadcast_in_dim.42), calls=%async_computation.4 | async-start | bytes 294912 | tf_op jit(solution)/shard_map/all_to_all | solution.py:443
  128.0 9.9 %collective-permute-start.6 = (bf16[3,2,3,12,768]{4,1,3,2,0:T(2,128)(2,1)S(1)}, bf16[3,2,3,12,768]{4,1,3,2,0:T(2,128)(2,1)S(1)}, u32[]{:S(2)}, u32[]{:S(2)}) collective-permute-start(bf16[3,2,3,12,768]{4,1,3,2,0:T(2,128)(2,1)S(1)} %copy.69), channel_id=1, source_target_pairs={{0,1},{1,2},{2,3},{3,0},{4,5},{5,6},{6,7},{7,4},{8,9},{9,10},{10,1... | collective-permute-start | bytes 995336 | tf_op jit(solution)/shard_map/ppermute | solution.py:435
  144.1 20.0 %all-to-all-start.5 = ((bf16[16,24,384]{2,1,0:T(8,128)(2,1)}), bf16[16,24,384]{2,1,0:T(8,128)(2,1)S(1)}, u32[]{:S(2)}, u32[]{:S(2)}) async-start(bf16[16,24,384]{2,1,0:T(8,128)(2,1)} %broadcast_in_dim.43), calls=%async_computation.5 | async-start | bytes 589824 | tf_op jit(solution)/shard_map/all_to_all | solution.py:443
  149.3 13.2 %collective-permute-start.7 = (bf16[3,2,6,6,768]{4,1,3,2,0:T(2,128)(2,1)S(1)}, bf16[3,2,6,6,768]{4,1,3,2,0:T(2,128)(2,1)S(1)}, u32[]{:S(2)}, u32[]{:S(2)}) collective-permute-start(bf16[3,2,6,6,768]{4,1,3,2,0:T(2,128)(2,1)S(1)} %get-tuple-element.37), channel_id=1, source_target_pairs={{0,4},{4,8},{8,12},{12,16},{16,20},{20,24},{24,28},{28,32},{32,36}... | collective-permute-start | bytes 995336 | tf_op jit(solution)/shard_map/ppermute | solution.py:435

commit v5 on v4

--- a/solution.py
+++ b/solution.py
@@ -16,7 +16,7 @@
 WIDE = ROWS * SEG
 GROUPS = 6
 LOW = -1e30
-VMEM = 56 * 1024 * 1024
+VMEM = 12 * 1024 * 1024
 score_factor = 32 ** (-0.5)
 
 z_groups = [[a * NZ + z for z in range(NZ)] for a in range(NX * NY)]
@@ -488,15 +488,16 @@
         ],
         axis=3,
     )
-    south = from_behind(across[:, :, :4], "lat", -1)
-
-    normed, inverse = normalise(across, south, quarter)
-    weight, table, mask, normed = lax.optimization_barrier((weight, table, mask, normed))
+    south = from_behind(across[:, :, :4, :12], "lat", -1)
+    south = jnp.pad(south, ((0, 0), (0, 0), (0, 0), (0, 4), (0, 0)))
+
+    weight, table, mask = lax.optimization_barrier((weight, table, mask))
     parts = merge_product(spots, near, far, weight, shuffle)
     recv = swap(parts, ("lon", "lat"), x_lat_groups)
 
-    table, _ = lax.optimization_barrier((table, parts))
+    south, _ = lax.optimization_barrier((south, parts))
     probs = window_probs(across, south, table, spread, mask)
+    normed, inverse = normalise(across, south, quarter)
 
     o_win, d_low, table_part = score_grads(
         recv, order, normed, inverse, merge_gain.reshape(4, 1, 768), back, sums, across, south, probs

time: 169 us -> 164 us (0.970)
  local copies, waits for them, and re-layouts: 11.9 us -> 32.2 us
  Pallas kernels: 37.3 us -> 21.5 us
  starting transfers between devices: 74.8 us -> 68.7 us
  waiting for transfers between devices: 34.5 us -> 31.7 us
    all_to_all x6, starting transfers between devices: 47.8 us -> 30.2 us  [swap(): lax.all_to_all(shard, axis, 0, 0, tiled=True, axis_index_groups=groups)]
    unnamed x26 -> x60, local copies, waits for them, and re-layouts: 4.16 us -> 20.4 us
    ppermute x5, starting transfers between devices: 18.5 us -> 30.1 us  [from_behind(): lax.ppermute(shard, axis, [(i, (i + by) % size) for i in range(size)])]
    pallas_call x1, Pallas kernels: 6.99 us -> 3.03 us  [window_grads(): pl.pallas_call(grads_kernel, grid=(GROUPS,), in_specs=[north_spec(0, 2),...]
    ppermute x5, waiting for transfers between devices: 21.6 us -> 18 us  [from_behind(): lax.ppermute(shard, axis, [(i, (i + by) % size) for i in range(size)])]
    pallas_call x1, Pallas kernels: 10.3 us -> 6.86 us  [score_grads(): pl.pallas_call(scores_kernel, grid=(GROUPS,), in_specs=[whole_spec((8, 64...]
    ppermute x1 -> x2, local copies, waits for them, and re-layouts: 0.06 us -> 3.08 us  [from_behind(): lax.ppermute(shard, axis, [(i, (i + by) % size) for i in range(size)])]
    concatenate x1 -> x2, other arithmetic: 0.53 us -> 3.1 us  [on_device(): jnp.concatenate([jnp.stack([q_proj[:, :, 6:], k_proj[:, :, 6:], v_proj[:,...]
  transfers between devices with their start and end apart: 14 -> 14, of which waited for: 7 -> 7; matrix products, arithmetic and copies ran while one was open for 7% -> 9% of each run, Pallas kernels for 12% -> 8%
where the time goes in v5:
time: 164 us; the launch traced here: 162 us
  starting transfers between devices  68.7 us (42%)
  local copies, waits for them, and re-layouts  32.2 us (20%)
  waiting for transfers between devices  31.7 us (19%)
  Pallas kernels  21.5 us (13%)
  other arithmetic  7.12 us (4%)
    all_to_all x6, starting transfers between devices, swap(): lax.all_to_all(shard, axis, 0, 0, tiled=True, axis_index_groups=groups)  30.2 us
    ppermute x5, starting transfers between devices, from_behind(): lax.ppermute(shard, axis, [(i, (i + by) % size) for i in range(size)])  30.1 us
    unnamed x60, local copies, waits for them, and re-layouts  20.4 us
    ppermute x5, waiting for transfers between devices, from_behind(): lax.ppermute(shard, axis, [(i, (i + by) % size) for i in range(size)])  18 us
    all_to_all x6, waiting for transfers between devices, swap(): lax.all_to_all(shard, axis, 0, 0, tiled=True, axis_index_groups=groups)  8.67 us
    ppermute x3, starting transfers between devices, partner(): lax.ppermute(shard, axis, [(i, i ^ bit) for i in range(lax.axis_size(axis...  8.33 us
    pallas_call x1, Pallas kernels, score_grads(): pl.pallas_call(scores_kernel, grid=(GROUPS,), in_specs=[whole_spec((8, 64...  6.86 us
    pallas_call x1, Pallas kernels, window_probs(): pl.pallas_call(probs_kernel, grid=(GROUPS,), in_specs=[north_spec(0, 2),...  5.99 us
  transfers between devices with their start and end apart: 14, of which 7 were waited for; matrix products, arithmetic and copies ran while one was open for 9% of the time, Pallas kernels for 8%

profile of v5, /device:TPU:6, one launch (start us, length us, event | category | flops | bytes accessed | tf_op | source)
XLA Modules:
  0.0 162.4 jit_solution(17866459168809349205)
XLA Ops:
  0.6 0.9 copy-done.17
  1.5 0.9 pack_weight.1
  2.4 0.9 fusion.21
  3.4 14.1 %collective-permute-start = (bf16[2,3,3,1536]{3,0,2,1:T(2,128)(2,1)S(1)}, bf16[2,3,3,1536]{3,0,2,1:T(2,128)(2,1)S(1)}, u32[]{:S(2)}, u32[]{:S(2)}) collective-permute-start(bf16[2,3,3,1536]{3,0,2,1:T(2,128)(2,1)S(1)} %get-tuple-element.46), channel_id=1, source_target_pairs={{0,508},{4,0},{8,4},{12,8},{16,12},{20,16},{24,20},{28,24},{32,28}... | collective-permute-start | bytes 165896 | tf_op jit(solution)/shard_map/ppermute | solution.py:435
  17.5 3.6 %all-to-all-start = ((bf16[16,24,384]{2,1,0:T(8,128)(2,1)}), bf16[16,24,384]{2,1,0:T(8,128)(2,1)S(1)}, u32[]{:S(2)}, u32[]{:S(2)}) async-start(bf16[16,24,384]{2,1,0:T(8,128)(2,1)} %pack_weight.1), calls=%async_computation | async-start | bytes 589824 | tf_op jit(solution)/shard_map/all_to_all | solution.py:443
  21.4 3.3 %collective-permute-start.1 = (bf16[48,1536]{1,0:T(8,128)(2,1)S(1)}, bf16[48,1536]{1,0:T(8,128)(2,1)S(1)}, u32[]{:S(2)}, u32[]{:S(2)}) collective-permute-start(bf16[48,1536]{1,0:T(8,128)(2,1)S(1)} %bitcast.36), channel_id=1, source_target_pairs={{0,2},{1,3},{2,0},{3,1},{4,6},{5,7},{6,4},{7,5},{8,10},{9,11},{10,... | collective-permute-start | bytes 442376 | tf_op jit(solution)/shard_map/ppermute | solution.py:439
  24.7 0.3 fusion.19
  25.0 5.0 %collective-permute-done.1 = bf16[48,1536]{1,0:T(8,128)(2,1)S(1)} collective-permute-done((bf16[48,1536]{1,0:T(8,128)(2,1)S(1)}, bf16[48,1536]{1,0:T(8,128)(2,1)S(1)}, u32[]{:S(2)}, u32[]{:S(2)}) %collective-permute-start.1) | collective-permute-done | bytes 147488 | tf_op jit(solution)/shard_map/ppermute | solution.py:439
  30.1 3.1 %collective-permute-start.2 = (bf16[96,1536]{1,0:T(8,128)(2,1)S(1)}, bf16[96,1536]{1,0:T(8,128)(2,1)S(1)}, u32[]{:S(2)}, u32[]{:S(2)}) collective-permute-start(bf16[96,1536]{1,0:T(8,128)(2,1)S(1)} %pad_maximum_fusion.7), channel_id=1, source_target_pairs={{0,256},{4,260},{8,264},{12,268},{16,272},{20,276},{24,280},{28,28... | collective-permute-start | bytes 884744 | tf_op jit(solution)/shard_map/ppermute | solution.py:439
  33.2 0.3 fusion.17
  33.5 0.8 pad_maximum_fusion.6
  34.5 7.6 %collective-permute-start.4 = (bf16[4,2,6,6,768]{4,0,3,2,1:T(4,128)(2,1)S(1)}, bf16[4,2,6,6,768]{4,0,3,2,1:T(4,128)(2,1)}, u32[]{:S(2)}, u32[]{:S(2)}) collective-permute-start(bf16[4,2,6,6,768]{4,0,3,2,1:T(4,128)(2,1)S(1)} %copy.63), channel_id=1, source_target_pairs={{0,508},{4,0},{8,4},{12,8},{16,12},{20,16},{24,20},{28,24},{32,28}... | collective-permute-start | bytes 1327112 | tf_op jit(solution)/shard_map/ppermute | solution.py:435
  42.1 1.2 broadcast_in_dim.38
  43.3 3.5 %all-to-all-start.1 = ((bf16[4,384,384]{2,1,0:T(8,128)(2,1)}), bf16[4,384,384]{2,1,0:T(8,128)(2,1)S(1)}, u32[]{:S(2)}, u32[]{:S(2)}) async-start(bf16[4,384,384]{2,1,0:T(8,128)(2,1)} %broadcast_in_dim.38), calls=%async_computation.1 | async-start | bytes 2359296 | tf_op jit(solution)/shard_map/all_to_all | solution.py:443
  46.9 1.9 %collective-permute-start.3 = (bf16[192,1536]{1,0:T(8,128)(2,1)S(1)}, bf16[192,1536]{1,0:T(8,128)(2,1)S(1)}, u32[]{:S(2)}, u32[]{:S(2)}) collective-permute-start(bf16[192,1536]{1,0:T(8,128)(2,1)S(1)} %pad_maximum_fusion.5.near_ref), channel_id=1, source_target_pairs={{0,1},{1,0},{2,3},{3,2},{4,5},{5,4},{6,7},{7,6},{8,9},{9,8},{10,11... | collective-permute-start | bytes 1769480 | tf_op jit(solution)/shard_map/ppermute | solution.py:439
  49.0 0.6 collective-permute-done.4
  49.6 1.9 %copy.64 = bf16[4,2,6,6,768]{4,3,2,1,0:T(8,128)(2,1)} copy(bf16[4,2,6,6,768]{4,0,3,2,1:T(4,128)(2,1)} %collective-permute-done.4) | data formatting | bytes 884736 | tf_op jit(solution)/shard_map/ppermute | solution.py:435
  51.5 1.3 pad_maximum_fusion
  52.7 1.1 copy.66
  53.9 2.9 %collective-permute-start.5 = (bf16[4,2,4,12,768]{4,2,3,1,0:T(4,128)(2,1)}, bf16[4,2,4,12,768]{4,2,3,1,0:T(4,128)(2,1)}, u32[]{:S(2)}, u32[]{:S(2)}) collective-permute-start(bf16[4,2,4,12,768]{4,2,3,1,0:T(4,128)(2,1)} %copy.66), channel_id=1, source_target_pairs={{0,3},{1,0},{2,1},{3,2},{4,7},{5,4},{6,5},{7,6},{8,11},{9,8},{10,9... | collective-permute-start | bytes 1769480 | tf_op jit(solution)/shard_map/ppermute | solution.py:435
  57.0 1.0 copy-done.9
  57.9 0.9 copy-done.12
  58.8 0.6 open_table.1.table_ref
  59.5 1.8 %all-to-all-done.1.w_ref = bf16[4,384,384]{2,1,0:T(8,128)(2,1)S(1)} async-done(((bf16[4,384,384]{2,1,0:T(8,128)(2,1)}), bf16[4,384,384]{2,1,0:T(8,128)(2,1)S(1)}, u32[]{:S(2)}, u32[]{:S(2)}) %all-to-all-start.1) | async-done | bytes 1179680 | tf_op jit(solution)/shard_map/all_to_all | solution.py:443
  61.3 3.5 %merge_product.1 = bf16[8,64,512]{2,1,0:T(8,128)(2,1)} custom-call(s32[8]{0:T(128)S(1)} %fusion.14.spot_ref, bf16[192,1536]{1,0:T(8,128)(2,1)S(1)} %pad_maximum_fusion.5.near_ref, bf16[192,1536]{1,0:T(8,128)(2,1)S(1)} %collective-permute-done.3.far_ref, bf16[4,384,384]{2,1,0:T(8,128)(2,1)S(1)} %all-to-all-done.1.w_ref, bf16[512,384]{1,0:T(8,128)(2,1)S(1)} %copy-done.5), custom_call_target="tpu_custom_call" | custom-call | tf_op jit(solution)/shard_map/merge_product/pallas_call | solution.py:369
  64.9 4.8 %all-to-all-start.2 = ((bf16[8,64,512]{2,1,0:T(8,128)(2,1)}), bf16[8,64,512]{2,1,0:T(8,128)(2,1)S(1)}, u32[]{:S(2)}, u32[]{:S(2)}) async-start(bf16[8,64,512]{2,1,0:T(8,128)(2,1)} %merge_product.1), calls=%async_computation.2 | async-start | bytes 1048576 | tf_op jit(solution)/shard_map/all_to_all | solution.py:443
  69.7 1.8 %maximum_maximum_fusion.a_ref.b_ref.north_ref = bf16[4,2,6,16,768]{4,3,2,1,0:T(8,128)(2,1)S(1)} fusion(bf16[4,2,6,6,768]{4,3,2,1,0:T(8,128)(2,1)} %copy.64, bf16[1,2,6,6,768]{4,3,2,1,0:T(8,128)(2,1)} %bitcast.42, bf16[1,2,6,6,768]{4,3,2,1,0:T(8,128)(2,1)} %bitcast.40, bf16[1,2,6,6,768]{4,3,2,1,0:T(8,128)(2,1)} %bitcast.46, ...), kind=kLoop, calls=%fused_computation.1 | loop fusion | flops 7077888 | bytes 2064416 | tf_op jit(solution)/shard_map/concatenate | solution.py:483
  71.6 1.2 copy.67
  72.9 0.5 normalise.1
  73.4 0.9 copy-done.6
  74.4 6.0 %window_probs.1.p_ref = f32[6,768,192]{2,1,0:T(8,128)S(1)} custom-call(bf16[4,2,6,16,768]{4,3,2,1,0:T(8,128)(2,1)S(1)} %maximum_maximum_fusion.a_ref.b_ref.north_ref, bf16[4,2,4,16,768]{4,3,2,1,0:T(8,128)(2,1)S(1)} %pad.4.south_ref, f32[6,48,384]{2,1,0:T(8,128)S(1)} %open_table.1.table_ref, bf16[384,192]{1,0:T(8,128)(2,1)S(1)} %copy-done.13, ...), custom_call_target="tpu_custom_call" | custom-call | tf_op jit(solution)/shard_map/window_probs/pallas_call | solution.py:331
  80.4 2.1 %copy-done = f32[6,768,192]{2,1,0:T(8,128)} copy-done((f32[6,768,192]{2,1,0:T(8,128)}, f32[6,768,192]{2,1,0:T(8,128)S(1)}, u32[]{:S(2)}) %copy-start) | copy-done | bytes 3538968
  82.5 2.3 %copy-done.1 = f32[6,768,192]{2,1,0:T(8,128)S(1)} copy-done((f32[6,768,192]{2,1,0:T(8,128)S(1)}, f32[6,768,192]{2,1,0:T(8,128)}, u32[]{:S(2)}) %copy-start.1) | copy-done | bytes 3538968
  84.9 1.1 copy-done.7
  86.0 0.9 copy-done.14
  86.9 0.9 copy-done.16
  87.8 0.7 copy-done.18
  88.5 6.9 %score_grads.1 = (bf16[6,192,128]{2,1,0:T(8,128)(2,1)S(1)}, bf16[6,768,192]{2,1,0:T(8,128)(2,1)S(1)}, f32[16,24,384]{2,1,0:T(8,128)S(1)}) custom-call(bf16[8,64,512]{2,1,0:T(8,128)(2,1)S(1)} %all-to-all-done.2.recv_ref, bf16[512,384]{1,0:T(8,128)(2,1)S(1)} %copy-done.5, f32[4,64,768]{2,1,0:T(8,128)S(1)} %copy-done.7, ...), custom_call_target="tpu_custom_call" | custom-call | tf_op jit(solution)/shard_map/score_grads/pallas_call | solution.py:381
  95.4 1.4 copy-done.3
  96.8 0.9 copy-done.8
  97.7 0.7 copy-done.10
  98.4 5.6 %all-to-all-start.3 = ((f32[16,24,384]{2,1,0:T(8,128)}), f32[16,24,384]{2,1,0:T(8,128)S(1)}, u32[]{:S(2)}, u32[]{:S(2)}) async-start(f32[16,24,384]{2,1,0:T(8,128)} %copy-done.8), calls=%async_computation.3 | async-start | bytes 1179648 | tf_op jit(solution)/shard_map/all_to_all | solution.py:443
  103.9 2.3 %copy-done.2 = f32[6,768,192]{2,1,0:T(8,128)S(1)} copy-done((f32[6,768,192]{2,1,0:T(8,128)S(1)}, f32[6,768,192]{2,1,0:T(8,128)}, u32[]{:S(2)}) %copy-start.2) | copy-done | bytes 3538968
  106.3 1.7 %copy-done.4 = bf16[6,768,192]{2,1,0:T(8,128)(2,1)S(1)} copy-done((bf16[6,768,192]{2,1,0:T(8,128)(2,1)S(1)}, bf16[6,768,192]{2,1,0:T(8,128)(2,1)}, u32[]{:S(2)}) %copy-start.4) | copy-done | bytes 1769496
  107.9 1.0 copy-done.11
  108.9 3.0 %window_grads.1 = bf16[3,192,768]{2,1,0:T(8,128)(2,1)S(1)} custom-call(bf16[4,2,6,16,768]{4,3,2,1,0:T(8,128)(2,1)S(1)} %maximum_maximum_fusion.a_ref.b_ref.north_ref, bf16[4,2,4,16,768]{4,3,2,1,0:T(8,128)(2,1)S(1)} %pad.4.south_ref, bf16[6,192,128]{2,1,0:T(8,128)(2,1)S(1)} %copy-done.11, bf16[6,768,192]{2,1,0:T(8,128)(2,1)S(1)} %copy-done.4, ...), custom_call_target="tpu_custom_call" | custom-call | tf_op jit(solution)/shard_map/window_grads/pallas_call | solution.py:416
  111.9 2.3 %all-to-all-done.3 = f32[16,24,384]{2,1,0:T(8,128)S(1)} async-done(((f32[16,24,384]{2,1,0:T(8,128)}), f32[16,24,384]{2,1,0:T(8,128)S(1)}, u32[]{:S(2)}, u32[]{:S(2)}) %all-to-all-start.3) | async-done | bytes 589856 | tf_op jit(solution)/shard_map/all_to_all | solution.py:443
  114.3 0.7 broadcast_in_dim.42
  115.0 8.1 %all-to-all-start.4 = ((bf16[8,24,384]{2,1,0:T(8,128)(2,1)}), bf16[8,24,384]{2,1,0:T(8,128)(2,1)S(1)}, u32[]{:S(2)}, u32[]{:S(2)}) async-start(bf16[8,24,384]{2,1,0:T(8,128)(2,1)} %broadcast_in_dim.42), calls=%async_computation.4 | async-start | bytes 294912 | tf_op jit(solution)/shard_map/all_to_all | solution.py:443
  123.2 0.3 copy.75
  123.4 2.1 %collective-permute-start.6 = (bf16[3,2,3,12,768]{4,1,3,2,0:T(2,128)(2,1)S(1)}, bf16[3,2,3,12,768]{4,1,3,2,0:T(2,128)(2,1)S(1)}, u32[]{:S(2)}, u32[]{:S(2)}) collective-permute-start(bf16[3,2,3,12,768]{4,1,3,2,0:T(2,128)(2,1)S(1)} %copy.75), channel_id=1, source_target_pairs={{0,1},{1,2},{2,3},{3,0},{4,5},{5,6},{6,7},{7,4},{8,9},{9,10},{10,1... | collective-permute-start | bytes 995336 | tf_op jit(solution)/shard_map/ppermute | solution.py:435
  125.5 0.3 copy.76
  125.8 7.6 %collective-permute-done.6 = bf16[3,2,3,12,768]{4,1,3,2,0:T(2,128)(2,1)S(1)} collective-permute-done((bf16[3,2,3,12,768]{4,1,3,2,0:T(2,128)(2,1)S(1)}, bf16[3,2,3,12,768]{4,1,3,2,0:T(2,128)(2,1)S(1)}, u32[]{:S(2)}, u32[]{:S(2)}) %collective-permute-start.6) | collective-permute-done | bytes 331808 | tf_op jit(solution)/shard_map/ppermute | solution.py:435
  133.4 0.9 pad_maximum_fusion.4
  134.2 4.5 %all-to-all-done.4 = bf16[8,24,384]{2,1,0:T(8,128)(2,1)S(1)} async-done(((bf16[8,24,384]{2,1,0:T(8,128)(2,1)}), bf16[8,24,384]{2,1,0:T(8,128)(2,1)S(1)}, u32[]{:S(2)}, u32[]{:S(2)}) %all-to-all-start.4) | async-done | bytes 147488 | tf_op jit(solution)/shard_map/all_to_all | solution.py:443
  138.8 0.7 broadcast_in_dim.43
  139.5 4.7 %all-to-all-start.5 = ((bf16[16,24,384]{2,1,0:T(8,128)(2,1)}), bf16[16,24,384]{2,1,0:T(8,128)(2,1)S(1)}, u32[]{:S(2)}, u32[]{:S(2)}) async-start(bf16[16,24,384]{2,1,0:T(8,128)(2,1)} %broadcast_in_dim.43), calls=%async_computation.5 | async-start | bytes 589824 | tf_op jit(solution)/shard_map/all_to_all | solution.py:443
  144.2 0.5 fusion.16
  144.7 3.4 %collective-permute-start.7 = (bf16[3,2,6,6,768]{4,1,3,2,0:T(2,128)(2,1)S(1)}, bf16[3,2,6,6,768]{4,1,3,2,0:T(2,128)(2,1)S(1)}, u32[]{:S(2)}, u32[]{:S(2)}) collective-permute-start(bf16[3,2,6,6,768]{4,1,3,2,0:T(2,128)(2,1)S(1)} %get-tuple-element.35), channel_id=1, source_target_pairs={{0,4},{4,8},{8,12},{12,16},{16,20},{20,24},{24,28},{28,32},{32,36}... | collective-permute-start | bytes 995336 | tf_op jit(solution)/shard_map/ppermute | solution.py:435
  148.0 9.8 %collective-permute-done.7 = bf16[3,2,6,6,768]{4,1,3,2,0:T(2,128)(2,1)S(1)} collective-permute-done((bf16[3,2,6,6,768]{4,1,3,2,0:T(2,128)(2,1)S(1)}, bf16[3,2,6,6,768]{4,1,3,2,0:T(2,128)(2,1)S(1)}, u32[]{:S(2)}, u32[]{:S(2)}) %collective-permute-start.7) | collective-permute-done | bytes 331808 | tf_op jit(solution)/shard_map/ppermute | solution.py:435
  157.9 1.6 fusion.2
  159.5 0.9 reshape.89
  160.4 0.3 convert_bitcast_fusion
  160.9 1.5 reshape.93
  (66 shorter events, 1.3 us)
Async XLA Ops:
  0.6 0.9 copy-start.17
  1.5 23.2 %copy-start.23 = (bf16[2,6,12,768]{3,0,2,1:T(2,128)(2,1)S(1)}, bf16[2,6,12,768]{3,0,2,1:T(2,128)(2,1)}, u32[]{:S(2)}) copy-start(bf16[2,6,12,768]{3,0,2,1:T(2,128)(2,1)} %param.21) | copy-start | bytes 663556
  1.5 23.2 %copy-start.24 = (bf16[2,6,12,768]{3,0,2,1:T(2,128)(2,1)S(1)}, bf16[2,6,12,768]{3,0,2,1:T(2,128)(2,1)}, u32[]{:S(2)}) copy-start(bf16[2,6,12,768]{3,0,2,1:T(2,128)(2,1)} %param.15) | copy-start | bytes 663556
  1.5 31.7 %copy-start.25 = (bf16[2,6,12,768]{3,0,2,1:T(2,128)(2,1)S(1)}, bf16[2,6,12,768]{3,0,2,1:T(2,128)(2,1)}, u32[]{:S(2)}) copy-start(bf16[2,6,12,768]{3,0,2,1:T(2,128)(2,1)} %param.19) | copy-start | bytes 663556
  1.5 31.7 %copy-start.26 = (bf16[2,6,12,768]{3,0,2,1:T(2,128)(2,1)S(1)}, bf16[2,6,12,768]{3,0,2,1:T(2,128)(2,1)}, u32[]{:S(2)}) copy-start(bf16[2,6,12,768]{3,0,2,1:T(2,128)(2,1)} %param.20) | copy-start | bytes 663556
  3.4 17.8 %collective-permute-start = (bf16[2,3,3,1536]{3,0,2,1:T(2,128)(2,1)S(1)}, bf16[2,3,3,1536]{3,0,2,1:T(2,128)(2,1)S(1)}, u32[]{:S(2)}, u32[]{:S(2)}) collective-permute-start(bf16[2,3,3,1536]{3,0,2,1:T(2,128)(2,1)S(1)} %get-tuple-element.46), channel_id=1, source_target_pairs={{0,508},{4,0},{8,4},{12,8},{16,12},{20,16},{24,20},{28,24},{32,28}... | collective-permute-start | bytes 165896 | tf_op jit(solution)/shard_map/ppermute | solution.py:435
  17.5 24.6 %all-to-all-start = ((bf16[16,24,384]{2,1,0:T(8,128)(2,1)}), bf16[16,24,384]{2,1,0:T(8,128)(2,1)S(1)}, u32[]{:S(2)}, u32[]{:S(2)}) async-start(bf16[16,24,384]{2,1,0:T(8,128)(2,1)} %pack_weight.1), calls=%async_computation | async-start | bytes 589824 | tf_op jit(solution)/shard_map/all_to_all | solution.py:443
  21.4 8.7 %collective-permute-start.1 = (bf16[48,1536]{1,0:T(8,128)(2,1)S(1)}, bf16[48,1536]{1,0:T(8,128)(2,1)S(1)}, u32[]{:S(2)}, u32[]{:S(2)}) collective-permute-start(bf16[48,1536]{1,0:T(8,128)(2,1)S(1)} %bitcast.36), channel_id=1, source_target_pairs={{0,2},{1,3},{2,0},{3,1},{4,6},{5,7},{6,4},{7,5},{8,10},{9,11},{10,... | collective-permute-start | bytes 442376 | tf_op jit(solution)/shard_map/ppermute | solution.py:439
  30.1 16.8 %collective-permute-start.2 = (bf16[96,1536]{1,0:T(8,128)(2,1)S(1)}, bf16[96,1536]{1,0:T(8,128)(2,1)S(1)}, u32[]{:S(2)}, u32[]{:S(2)}) collective-permute-start(bf16[96,1536]{1,0:T(8,128)(2,1)S(1)} %pad_maximum_fusion.7), channel_id=1, source_target_pairs={{0,256},{4,260},{8,264},{12,268},{16,272},{20,276},{24,280},{28,28... | collective-permute-start | bytes 884744 | tf_op jit(solution)/shard_map/ppermute | solution.py:439
  34.5 15.0 %collective-permute-start.4 = (bf16[4,2,6,6,768]{4,0,3,2,1:T(4,128)(2,1)S(1)}, bf16[4,2,6,6,768]{4,0,3,2,1:T(4,128)(2,1)}, u32[]{:S(2)}, u32[]{:S(2)}) collective-permute-start(bf16[4,2,6,6,768]{4,0,3,2,1:T(4,128)(2,1)S(1)} %copy.63), channel_id=1, source_target_pairs={{0,508},{4,0},{8,4},{12,8},{16,12},{20,16},{24,20},{28,24},{32,28}... | collective-permute-start | bytes 1327112 | tf_op jit(solution)/shard_map/ppermute | solution.py:435
  43.3 18.0 %all-to-all-start.1 = ((bf16[4,384,384]{2,1,0:T(8,128)(2,1)}), bf16[4,384,384]{2,1,0:T(8,128)(2,1)S(1)}, u32[]{:S(2)}, u32[]{:S(2)}) async-start(bf16[4,384,384]{2,1,0:T(8,128)(2,1)} %broadcast_in_dim.38), calls=%async_computation.1 | async-start | bytes 2359296 | tf_op jit(solution)/shard_map/all_to_all | solution.py:443
  46.9 14.4 %collective-permute-start.3 = (bf16[192,1536]{1,0:T(8,128)(2,1)S(1)}, bf16[192,1536]{1,0:T(8,128)(2,1)S(1)}, u32[]{:S(2)}, u32[]{:S(2)}) collective-permute-start(bf16[192,1536]{1,0:T(8,128)(2,1)S(1)} %pad_maximum_fusion.5.near_ref), channel_id=1, source_target_pairs={{0,1},{1,0},{2,3},{3,2},{4,5},{5,4},{6,7},{7,6},{8,9},{9,8},{10,11... | collective-permute-start | bytes 1769480 | tf_op jit(solution)/shard_map/ppermute | solution.py:439
  48.9 2.6 %copy-start.19 = (bf16[2,6,6,768]{3,2,1,0:T(8,128)(2,1)}, bf16[2,6,6,768]{3,2,1,0:T(8,128)(2,1)S(1)}, u32[]{:S(2)}) copy-start(bf16[2,6,6,768]{3,2,1,0:T(8,128)(2,1)S(1)} %copy.82) | copy-start | bytes 331780
  48.9 2.6 %copy-start.20 = (bf16[2,6,6,768]{3,2,1,0:T(8,128)(2,1)}, bf16[2,6,6,768]{3,2,1,0:T(8,128)(2,1)S(1)}, u32[]{:S(2)}) copy-start(bf16[2,6,6,768]{3,2,1,0:T(8,128)(2,1)S(1)} %copy.81) | copy-start | bytes 331780
  48.9 2.5 %copy-start.21 = (bf16[2,6,6,768]{3,2,1,0:T(8,128)(2,1)}, bf16[2,6,6,768]{3,2,1,0:T(8,128)(2,1)S(1)}, u32[]{:S(2)}) copy-start(bf16[2,6,6,768]{3,2,1,0:T(8,128)(2,1)S(1)} %copy.84) | copy-start | bytes 331780
  49.0 2.5 %copy-start.22 = (bf16[2,6,6,768]{3,2,1,0:T(8,128)(2,1)}, bf16[2,6,6,768]{3,2,1,0:T(8,128)(2,1)S(1)}, u32[]{:S(2)}) copy-start(bf16[2,6,6,768]{3,2,1,0:T(8,128)(2,1)S(1)} %copy.83) | copy-start | bytes 331780
  52.7 8.6 %copy-start.5 = (bf16[512,384]{1,0:T(8,128)(2,1)S(1)}, bf16[512,384]{1,0:T(8,128)(2,1)}, u32[]{:S(2)}) copy-start(bf16[512,384]{1,0:T(8,128)(2,1)} %constant.134.clone.shuffle_ref.order_ref) | copy-start | bytes 1179652
  53.9 17.7 %collective-permute-start.5 = (bf16[4,2,4,12,768]{4,2,3,1,0:T(4,128)(2,1)}, bf16[4,2,4,12,768]{4,2,3,1,0:T(4,128)(2,1)}, u32[]{:S(2)}, u32[]{:S(2)}) collective-permute-start(bf16[4,2,4,12,768]{4,2,3,1,0:T(4,128)(2,1)} %copy.66), channel_id=1, source_target_pairs={{0,3},{1,0},{2,1},{3,2},{4,7},{5,4},{6,5},{7,6},{8,11},{9,8},{10,9... | collective-permute-start | bytes 1769480 | tf_op jit(solution)/shard_map/ppermute | solution.py:435
  56.9 1.0 copy-start.9
  57.9 0.9 copy-start.12
  64.9 17.6 %all-to-all-start.2 = ((bf16[8,64,512]{2,1,0:T(8,128)(2,1)}), bf16[8,64,512]{2,1,0:T(8,128)(2,1)S(1)}, u32[]{:S(2)}, u32[]{:S(2)}) async-start(bf16[8,64,512]{2,1,0:T(8,128)(2,1)} %merge_product.1), calls=%async_computation.2 | async-start | bytes 1048576 | tf_op jit(solution)/shard_map/all_to_all | solution.py:443
  71.6 1.3 copy-start.15
  72.9 1.5 copy-start.13
  73.4 0.9 copy-start.6
  80.4 2.2 %copy-start = (f32[6,768,192]{2,1,0:T(8,128)}, f32[6,768,192]{2,1,0:T(8,128)S(1)}, u32[]{:S(2)}) copy-start(f32[6,768,192]{2,1,0:T(8,128)S(1)} %window_probs.1.p_ref) | copy-start | bytes 10616836
  82.5 2.3 %copy-start.1 = (f32[6,768,192]{2,1,0:T(8,128)S(1)}, f32[6,768,192]{2,1,0:T(8,128)}, u32[]{:S(2)}) copy-start(f32[6,768,192]{2,1,0:T(8,128)} %copy-done) | copy-start | bytes 10616836
  84.9 1.1 copy-start.7
  86.0 0.9 copy-start.14
  86.9 0.9 copy-start.16
  87.8 0.7 copy-start.18
  95.4 1.4 copy-start.3
  96.8 0.9 copy-start.8
  97.7 0.7 copy-start.10
  98.4 15.9 %all-to-all-start.3 = ((f32[16,24,384]{2,1,0:T(8,128)}), f32[16,24,384]{2,1,0:T(8,128)S(1)}, u32[]{:S(2)}, u32[]{:S(2)}) async-start(f32[16,24,384]{2,1,0:T(8,128)} %copy-done.8), calls=%async_computation.3 | async-start | bytes 1179648 | tf_op jit(solution)/shard_map/all_to_all | solution.py:443
  103.9 2.3 %copy-start.2 = (f32[6,768,192]{2,1,0:T(8,128)S(1)}, f32[6,768,192]{2,1,0:T(8,128)}, u32[]{:S(2)}) copy-start(f32[6,768,192]{2,1,0:T(8,128)} %copy-done) | copy-start | bytes 10616836
  106.3 1.7 %copy-start.4 = (bf16[6,768,192]{2,1,0:T(8,128)(2,1)S(1)}, bf16[6,768,192]{2,1,0:T(8,128)(2,1)}, u32[]{:S(2)}) copy-start(bf16[6,768,192]{2,1,0:T(8,128)(2,1)} %copy-done.3) | copy-start | bytes 5308420
  107.9 1.0 copy-start.11
  115.0 23.8 %all-to-all-start.4 = ((bf16[8,24,384]{2,1,0:T(8,128)(2,1)}), bf16[8,24,384]{2,1,0:T(8,128)(2,1)S(1)}, u32[]{:S(2)}, u32[]{:S(2)}) async-start(bf16[8,24,384]{2,1,0:T(8,128)(2,1)} %broadcast_in_dim.42), calls=%async_computation.4 | async-start | bytes 294912 | tf_op jit(solution)/shard_map/all_to_all | solution.py:443
  123.4 9.9 %collective-permute-start.6 = (bf16[3,2,3,12,768]{4,1,3,2,0:T(2,128)(2,1)S(1)}, bf16[3,2,3,12,768]{4,1,3,2,0:T(2,128)(2,1)S(1)}, u32[]{:S(2)}, u32[]{:S(2)}) collective-permute-start(bf16[3,2,3,12,768]{4,1,3,2,0:T(2,128)(2,1)S(1)} %copy.75), channel_id=1, source_target_pairs={{0,1},{1,2},{2,3},{3,0},{4,5},{5,6},{6,7},{7,4},{8,9},{9,10},{10,1... | collective-permute-start | bytes 995336 | tf_op jit(solution)/shard_map/ppermute | solution.py:435
  139.5 20.0 %all-to-all-start.5 = ((bf16[16,24,384]{2,1,0:T(8,128)(2,1)}), bf16[16,24,384]{2,1,0:T(8,128)(2,1)S(1)}, u32[]{:S(2)}, u32[]{:S(2)}) async-start(bf16[16,24,384]{2,1,0:T(8,128)(2,1)} %broadcast_in_dim.43), calls=%async_computation.5 | async-start | bytes 589824 | tf_op jit(solution)/shard_map/all_to_all | solution.py:443
  144.7 13.2 %collective-permute-start.7 = (bf16[3,2,6,6,768]{4,1,3,2,0:T(2,128)(2,1)S(1)}, bf16[3,2,6,6,768]{4,1,3,2,0:T(2,128)(2,1)S(1)}, u32[]{:S(2)}, u32[]{:S(2)}) collective-permute-start(bf16[3,2,6,6,768]{4,1,3,2,0:T(2,128)(2,1)S(1)} %get-tuple-element.35), channel_id=1, source_target_pairs={{0,4},{4,8},{8,12},{12,16},{16,20},{20,24},{24,28},{28,32},{32,36}... | collective-permute-start | bytes 995336 | tf_op jit(solution)/shard_map/ppermute | solution.py:435

commit v6 on v5

--- a/solution.py
+++ b/solution.py
@@ -15,8 +15,11 @@
 SEG = 32
 WIDE = ROWS * SEG
 GROUPS = 6
+PER = 3
+STEPS = GROUPS // PER
 LOW = -1e30
-VMEM = 12 * 1024 * 1024
+SMALL = 12 * 1024 * 1024
+LARGE = 56 * 1024 * 1024
 score_factor = 32 ** (-0.5)
 
 z_groups = [[a * NZ + z for z in range(NZ)] for a in range(NX * NY)]
@@ -89,11 +92,12 @@
     return dot(high, matrix) + dot(low, matrix)
 
 
-def window(north_ref, south_ref, which):
+def window(north_ref, south_ref, which, group):
+    lanes = slice(group * 128, (group + 1) * 128)
     pieces = []
     for level in range(2):
-        pieces.append(north_ref[which, level].reshape(48, 128))
-        pieces.append(south_ref[which, level, 0:3].reshape(48, 128))
+        pieces.append(north_ref[which, level, :, :, lanes].reshape(48, 128))
+        pieces.append(south_ref[which, level, 0:3, :, lanes].reshape(48, 128))
     return jnp.concatenate(pieces, axis=0)
 
 
@@ -131,18 +135,21 @@
 
 
 def probs_kernel(north_ref, south_ref, table_ref, spread_ref, mask_ref, p_ref):
-    pieces = []
-    for s in range(3):
-        table = table_ref[0, :, s * 128 : (s + 1) * 128]
-        table = jnp.broadcast_to(table[:, None, :], (4 * ROWS, PAD, 128))
-        pieces.append(pltpu.roll(table, 0, 2, stride=1, stride_axis=1))
-    wide = jnp.concatenate(pieces, axis=2).reshape(4 * TOK, WIDE)
-    q_win, k_win = window(north_ref, south_ref, 0), window(north_ref, south_ref, 1)
-    scores = dot(by_head(q_win), k_win, ((1,), (1,))) * score_factor
-    scores = scores + split_dot(wide, spread_ref[...])
-    scores = (scores.reshape(4, TOK, TOK) + mask_ref[...][None]).reshape(4 * TOK, TOK)
-    expon = jnp.exp(scores - jnp.max(scores, axis=-1, keepdims=True))
-    p_ref[0] = expon * (1.0 / jnp.sum(expon, axis=-1, keepdims=True))
+    for group in range(PER):
+        pieces = []
+        for s in range(3):
+            table = table_ref[group, :, s * 128 : (s + 1) * 128]
+            table = jnp.broadcast_to(table[:, None, :], (4 * ROWS, PAD, 128))
+            pieces.append(pltpu.roll(table, 0, 2, stride=1, stride_axis=1))
+        wide = jnp.concatenate(pieces, axis=2).reshape(4 * TOK, WIDE)
+        q_win = window(north_ref, south_ref, 0, group)
+        k_win = window(north_ref, south_ref, 1, group)
+        scores = dot(by_head(q_win), k_win, ((1,), (1,))) * score_factor
+        scores = scores + split_dot(wide, spread_ref[...])
+        scores = (scores.reshape(4, TOK, TOK) + mask_ref[...][None]).reshape(4 * TOK, TOK)
+        expon = jnp.exp(scores - jnp.max(scores, axis=-1, keepdims=True))
+        probs = expon * (1.0 / jnp.sum(expon, axis=-1, keepdims=True))
+        p_ref[group] = probs.astype(jnp.bfloat16)
 
 
 def norm_kernel(a_ref, b_ref, south_ref, quarter_ref, normed_ref, inverse_ref):
@@ -234,24 +241,23 @@
         for s in range(GROUPS):
             o_ref[s] = d_out[:, s * 128 : (s + 1) * 128]
 
-    o_win = o_ref[g]
-    o_out_ref[0] = o_win
-    probs = p_ref[0]
-    d_probs = dot(by_head(o_win), window(north_ref, south_ref, 0), ((1,), (1,)))
-    delta = jnp.sum(probs * d_probs, axis=-1, keepdims=True)
-    d_low = (probs * (d_probs - delta)).astype(jnp.bfloat16)
-    d_ref[0] = d_low
-
-    spread = dot(d_low, sums_ref[...]).reshape(4 * ROWS, PAD, WIDE)
-    sums = [
-        jnp.sum(
-            pltpu.roll(spread[:, :, s * 128 : (s + 1) * 128], 0, 2, stride=1, stride_axis=1), axis=1
-        )
-        for s in range(3)
-    ]
-    sum_ref[g] = jnp.concatenate(sums, axis=1)
-
-    @pl.when(g == GROUPS - 1)
+    for group in range(PER):
+        o_win = o_ref[g * PER + group]
+        o_out_ref[group] = o_win
+        probs = p_ref[group].astype(jnp.float32)
+        v_win = window(north_ref, south_ref, 0, group)
+        d_probs = dot(by_head(o_win), v_win, ((1,), (1,)))
+        delta = jnp.sum(probs * d_probs, axis=-1, keepdims=True)
+        d_low = (probs * (d_probs - delta)).astype(jnp.bfloat16)
+        d_ref[group] = d_low
+
+        spread = dot(d_low, sums_ref[...]).reshape(4 * ROWS, PAD, WIDE)
+        for s in range(3):
+            lanes = slice(s * 128, (s + 1) * 128)
+            turned = pltpu.roll(spread[:, :, lanes], 0, 2, stride=1, stride_axis=1)
+            sum_ref[g * PER + group, :, lanes] = jnp.sum(turned, axis=1)
+
+    @pl.when(g == STEPS - 1)
     def _():
         whole = jnp.concatenate([sum_ref[s] for s in range(GROUPS)], axis=0)
         for part in range(16):
@@ -260,27 +266,28 @@
 
 
 def grads_kernel(north_ref, south_ref, o_ref, d_ref, p_ref, grads_ref):
-    q_win, k_win = window(north_ref, south_ref, 0), window(north_ref, south_ref, 1)
-    o_win = o_ref[0]
-    d_low = d_ref[0]
-    p_low = p_ref[0].astype(jnp.bfloat16)
-    q_all = dot(d_low, k_win)
-    q_grad = jnp.zeros((TOK, 128), jnp.float32)
-    for h in range(4):
-        q_grad = jnp.where(head_mask(h), q_all[h * TOK : (h + 1) * TOK], q_grad)
-    grads_ref[0] = (q_grad * score_factor).astype(jnp.bfloat16)
-
-    q_turn = q_win.astype(jnp.float32).T.astype(jnp.bfloat16)
-    o_turn = o_win.astype(jnp.float32).T.astype(jnp.bfloat16)
-    k_parts, v_parts = [], []
-    for h in range(4):
-        rows = slice(h * 32, (h + 1) * 32)
-        k_parts.append(dot(q_turn[rows], d_low[h * TOK : (h + 1) * TOK]))
-        v_parts.append(dot(o_turn[rows], p_low[h * TOK : (h + 1) * TOK]))
-    k_grad = jnp.concatenate(k_parts, axis=0).T
-    v_grad = jnp.concatenate(v_parts, axis=0).T
-    grads_ref[1] = (k_grad * score_factor).astype(jnp.bfloat16)
-    grads_ref[2] = v_grad.astype(jnp.bfloat16)
+    for group in range(PER):
+        lanes = slice(group * 128, (group + 1) * 128)
+        q_win = window(north_ref, south_ref, 0, group)
+        k_win = window(north_ref, south_ref, 1, group)
+        o_win, d_low, p_low = o_ref[group], d_ref[group], p_ref[group]
+        q_all = dot(d_low, k_win)
+        q_grad = jnp.zeros((TOK, 128), jnp.float32)
+        for h in range(4):
+            q_grad = jnp.where(head_mask(h), q_all[h * TOK : (h + 1) * TOK], q_grad)
+        grads_ref[0, :, lanes] = (q_grad * score_factor).astype(jnp.bfloat16)
+
+        q_turn = q_win.astype(jnp.float32).T.astype(jnp.bfloat16)
+        o_turn = o_win.astype(jnp.float32).T.astype(jnp.bfloat16)
+        k_parts, v_parts = [], []
+        for h in range(4):
+            rows = slice(h * 32, (h + 1) * 32)
+            k_parts.append(dot(q_turn[rows], d_low[h * TOK : (h + 1) * TOK]))
+            v_parts.append(dot(o_turn[rows], p_low[h * TOK : (h + 1) * TOK]))
+        k_grad = jnp.concatenate(k_parts, axis=0).T
+        v_grad = jnp.concatenate(v_parts, axis=0).T
+        grads_ref[1, :, lanes] = (k_grad * score_factor).astype(jnp.bfloat16)
+        grads_ref[2, :, lanes] = v_grad.astype(jnp.bfloat16)
 
 
 def whole_spec(shape):
@@ -288,18 +295,19 @@
 
 
 def north_spec(first, count):
-    return pl.BlockSpec((count, 2, 3, PAD, 128), lambda g: (first // count, 0, 1, 0, g))
+    return pl.BlockSpec((count, 2, 3, PAD, PER * 128), lambda g: (first // count, 0, 1, 0, g))
 
 
 def south_spec(first, count):
-    return pl.BlockSpec((count, 2, 4, PAD, 128), lambda g: (first // count, 0, 0, 0, g))
+    return pl.BlockSpec((count, 2, 4, PAD, PER * 128), lambda g: (first // count, 0, 0, 0, g))
 
 
 def group_spec(rows, columns):
-    return pl.BlockSpec((1, rows, columns), lambda g: (g, 0, 0))
-
-
-params = pltpu.CompilerParams(vmem_limit_bytes=VMEM)
+    return pl.BlockSpec((PER, rows, columns), lambda g: (g, 0, 0))
+
+
+params = pltpu.CompilerParams(vmem_limit_bytes=SMALL)
+large = pltpu.CompilerParams(vmem_limit_bytes=LARGE)
 smem = pl.BlockSpec(memory_space=pltpu.SMEM)
 vmem = pl.BlockSpec(memory_space=pltpu.VMEM)
 
@@ -330,7 +338,7 @@
 def window_probs(across, south, table, spread, mask):
     return pl.pallas_call(
         probs_kernel,
-        grid=(GROUPS,),
+        grid=(STEPS,),
         in_specs=[
             north_spec(0, 2),
             south_spec(0, 2),
@@ -339,8 +347,8 @@
             whole_spec((TOK, TOK)),
         ],
         out_specs=group_spec(4 * TOK, TOK),
-        out_shape=jax.ShapeDtypeStruct((GROUPS, 4 * TOK, TOK), jnp.float32),
-        compiler_params=params,
+        out_shape=jax.ShapeDtypeStruct((GROUPS, 4 * TOK, TOK), jnp.bfloat16),
+        compiler_params=large,
         name="window_probs",
     )(across, south, table, spread, mask)
 
@@ -380,7 +388,7 @@
 def score_grads(recv, order, normed, inverse, gain, back, sums, across, south, probs):
     return pl.pallas_call(
         scores_kernel,
-        grid=(GROUPS,),
+        grid=(STEPS,),
         in_specs=[
             whole_spec((8, 64, 512)),
             whole_spec((512, 384)),
@@ -407,7 +415,7 @@
             pltpu.VMEM((GROUPS, TOK, 128), jnp.bfloat16),
             pltpu.VMEM((GROUPS, 4 * ROWS, WIDE), jnp.float32),
         ],
-        compiler_params=params,
+        compiler_params=large,
         name="score_grads",
     )(recv, order, normed, inverse, gain, back, sums, across, south, probs)
 
@@ -415,7 +423,7 @@
 def window_grads(across, south, o_win, d_low, probs):
     return pl.pallas_call(
         grads_kernel,
-        grid=(GROUPS,),
+        grid=(STEPS,),
         in_specs=[
             north_spec(0, 2),
             south_spec(0, 2),
@@ -423,9 +431,9 @@
             group_spec(4 * TOK, TOK),
             group_spec(4 * TOK, TOK),
         ],
-        out_specs=pl.BlockSpec((3, TOK, 128), lambda g: (0, 0, g)),
+        out_specs=pl.BlockSpec((3, TOK, PER * 128), lambda g: (0, 0, g)),
         out_shape=jax.ShapeDtypeStruct((3, TOK, 768), jnp.bfloat16),
-        compiler_params=params,
+        compiler_params=large,
         name="window_grads",
     )(across, south, o_win, d_low, probs)
 

time: 164 us -> 158 us (0.963)
  local copies, waits for them, and re-layouts: 32.2 us -> 17.4 us
  Pallas kernels: 21.5 us -> 26.6 us
  waiting for transfers between devices: 31.7 us -> 35.1 us
    unnamed x60 -> x52, local copies, waits for them, and re-layouts: 20.4 us -> 5.91 us
    pallas_call x3, Pallas kernels: 15.9 us -> 21 us  [the longest x1 9.33 us: score_grads(): pl.pallas_call(scores_kernel, grid=(STEPS,), in_specs=[whole_spec((8, 64,...]
    all_to_all x6, waiting for transfers between devices: 8.67 us -> 12.7 us  [swap(): lax.all_to_all(shard, axis, 0, 0, tiled=True, axis_index_groups=groups)]
  transfers between devices with their start and end apart: 14 -> 14, of which waited for: 7 -> 6; matrix products, arithmetic and copies ran while one was open for 9% -> 9% of each run, Pallas kernels for 8% -> 10%
where the time goes in v6:
time: 158 us; the launch traced here: 157 us
  starting transfers between devices  68.7 us (43%)
  waiting for transfers between devices  35.1 us (22%)
  Pallas kernels  26.6 us (17%)
  local copies, waits for them, and re-layouts  17.4 us (11%)
  other arithmetic  7.51 us (5%)
    ppermute x5, starting transfers between devices, from_behind(): lax.ppermute(shard, axis, [(i, (i + by) % size) for i in range(size)])  30.7 us
    all_to_all x6, starting transfers between devices, swap(): lax.all_to_all(shard, axis, 0, 0, tiled=True, axis_index_groups=groups)  29.7 us
    ppermute x5, waiting for transfers between devices, from_behind(): lax.ppermute(shard, axis, [(i, (i + by) % size) for i in range(size)])  17.4 us
    all_to_all x6, waiting for transfers between devices, swap(): lax.all_to_all(shard, axis, 0, 0, tiled=True, axis_index_groups=groups)  12.7 us
    pallas_call x1, Pallas kernels, score_grads(): pl.pallas_call(scores_kernel, grid=(STEPS,), in_specs=[whole_spec((8, 64,...  9.33 us
    ppermute x3, starting transfers between devices, partner(): lax.ppermute(shard, axis, [(i, i ^ bit) for i in range(lax.axis_size(axis...  8.34 us
    pallas_call x1, Pallas kernels, window_probs(): pl.pallas_call(probs_kernel, grid=(STEPS,), in_specs=[north_spec(0, 2), s...  7.18 us
    unnamed x52, local copies, waits for them, and re-layouts  5.91 us
  transfers between devices with their start and end apart: 14, of which 6 were waited for; matrix products, arithmetic and copies ran while one was open for 9% of the time, Pallas kernels for 10%

profile of v6, /device:TPU:6, one launch (start us, length us, event | category | flops | bytes accessed | tf_op | source)
XLA Modules:
  0.0 156.5 jit_solution(16849409607353209579)
XLA Ops:
  0.6 0.9 copy-done.8
  1.5 0.9 pack_weight.1
  2.4 0.9 fusion.21
  3.4 14.1 %collective-permute-start = (bf16[2,3,3,1536]{3,0,2,1:T(2,128)(2,1)S(1)}, bf16[2,3,3,1536]{3,0,2,1:T(2,128)(2,1)S(1)}, u32[]{:S(2)}, u32[]{:S(2)}) collective-permute-start(bf16[2,3,3,1536]{3,0,2,1:T(2,128)(2,1)S(1)} %get-tuple-element.46), channel_id=1, source_target_pairs={{0,508},{4,0},{8,4},{12,8},{16,12},{20,16},{24,20},{28,24},{32,28}... | collective-permute-start | bytes 165896 | tf_op jit(solution)/shard_map/ppermute | solution.py:443
  17.5 3.6 %all-to-all-start = ((bf16[16,24,384]{2,1,0:T(8,128)(2,1)}), bf16[16,24,384]{2,1,0:T(8,128)(2,1)S(1)}, u32[]{:S(2)}, u32[]{:S(2)}) async-start(bf16[16,24,384]{2,1,0:T(8,128)(2,1)} %pack_weight.1), calls=%async_computation | async-start | bytes 589824 | tf_op jit(solution)/shard_map/all_to_all | solution.py:451
  21.1 0.1 pad.31.clone
  21.1 0.2 maximum_maximum_fusion.1
  21.4 3.3 %collective-permute-start.1 = (bf16[48,1536]{1,0:T(8,128)(2,1)S(1)}, bf16[48,1536]{1,0:T(8,128)(2,1)S(1)}, u32[]{:S(2)}, u32[]{:S(2)}) collective-permute-start(bf16[48,1536]{1,0:T(8,128)(2,1)S(1)} %bitcast.35), channel_id=1, source_target_pairs={{0,2},{1,3},{2,0},{3,1},{4,6},{5,7},{6,4},{7,5},{8,10},{9,11},{10,... | collective-permute-start | bytes 442376 | tf_op jit(solution)/shard_map/ppermute | solution.py:447
  24.7 0.3 fusion.19
  25.0 5.0 %collective-permute-done.1 = bf16[48,1536]{1,0:T(8,128)(2,1)S(1)} collective-permute-done((bf16[48,1536]{1,0:T(8,128)(2,1)S(1)}, bf16[48,1536]{1,0:T(8,128)(2,1)S(1)}, u32[]{:S(2)}, u32[]{:S(2)}) %collective-permute-start.1) | collective-permute-done | bytes 147488 | tf_op jit(solution)/shard_map/ppermute | solution.py:447
  30.1 3.1 %collective-permute-start.2 = (bf16[96,1536]{1,0:T(8,128)(2,1)S(1)}, bf16[96,1536]{1,0:T(8,128)(2,1)}, u32[]{:S(2)}, u32[]{:S(2)}) collective-permute-start(bf16[96,1536]{1,0:T(8,128)(2,1)S(1)} %pad_maximum_fusion.7), channel_id=1, source_target_pairs={{0,256},{4,260},{8,264},{12,268},{16,272},{20,276},{24,280},{28,28... | collective-permute-start | bytes 884744 | tf_op jit(solution)/shard_map/ppermute | solution.py:447
  33.2 0.3 fusion.17
  33.5 0.8 pad_maximum_fusion.6
  34.3 0.2 copy.63
  34.5 7.6 %collective-permute-start.4 = (bf16[4,2,6,6,768]{4,0,3,2,1:T(4,128)(2,1)S(1)}, bf16[4,2,6,6,768]{4,0,3,2,1:T(4,128)(2,1)}, u32[]{:S(2)}, u32[]{:S(2)}) collective-permute-start(bf16[4,2,6,6,768]{4,0,3,2,1:T(4,128)(2,1)S(1)} %copy.63), channel_id=1, source_target_pairs={{0,508},{4,0},{8,4},{12,8},{16,12},{20,16},{24,20},{28,24},{32,28}... | collective-permute-start | bytes 1327112 | tf_op jit(solution)/shard_map/ppermute | solution.py:443
  42.1 1.2 broadcast_in_dim.38
  43.3 3.5 %all-to-all-start.1 = ((bf16[4,384,384]{2,1,0:T(8,128)(2,1)}), bf16[4,384,384]{2,1,0:T(8,128)(2,1)S(1)}, u32[]{:S(2)}, u32[]{:S(2)}) async-start(bf16[4,384,384]{2,1,0:T(8,128)(2,1)} %broadcast_in_dim.38), calls=%async_computation.1 | async-start | bytes 2359296 | tf_op jit(solution)/shard_map/all_to_all | solution.py:451
  46.9 1.0 pad_maximum_fusion.5.near_ref
  47.9 1.9 %collective-permute-start.3 = (bf16[192,1536]{1,0:T(8,128)(2,1)S(1)}, bf16[192,1536]{1,0:T(8,128)(2,1)S(1)}, u32[]{:S(2)}, u32[]{:S(2)}) collective-permute-start(bf16[192,1536]{1,0:T(8,128)(2,1)S(1)} %pad_maximum_fusion.5.near_ref), channel_id=1, source_target_pairs={{0,1},{1,0},{2,3},{3,2},{4,5},{5,4},{6,7},{7,6},{8,9},{9,8},{10,11... | collective-permute-start | bytes 1769480 | tf_op jit(solution)/shard_map/ppermute | solution.py:447
  50.0 1.1 copy.64
  51.2 0.8 copy-done.10
  52.0 0.3 pad_maximum_fusion
  52.2 0.0 copy-start.3
  52.2 1.1 copy.66
  53.4 3.4 %collective-permute-start.5 = (bf16[4,2,4,12,768]{4,2,3,1,0:T(4,128)(2,1)}, bf16[4,2,4,12,768]{4,2,3,1,0:T(4,128)(2,1)}, u32[]{:S(2)}, u32[]{:S(2)}) collective-permute-start(bf16[4,2,4,12,768]{4,2,3,1,0:T(4,128)(2,1)} %copy.66), channel_id=1, source_target_pairs={{0,3},{1,0},{2,1},{3,2},{4,7},{5,4},{6,5},{7,6},{8,11},{9,8},{10,9... | collective-permute-start | bytes 1769480 | tf_op jit(solution)/shard_map/ppermute | solution.py:443
  56.8 0.8 and_select_fusion.mask_ref
  57.6 0.6 open_table.1.table_ref
  58.2 0.8 copy-done.2
  59.0 2.3 %all-to-all-done.1.w_ref = bf16[4,384,384]{2,1,0:T(8,128)(2,1)S(1)} async-done(((bf16[4,384,384]{2,1,0:T(8,128)(2,1)}), bf16[4,384,384]{2,1,0:T(8,128)(2,1)S(1)}, u32[]{:S(2)}, u32[]{:S(2)}) %all-to-all-start.1) | async-done | bytes 1179680 | tf_op jit(solution)/shard_map/all_to_all | solution.py:451
  61.3 3.6 %merge_product.1 = bf16[8,64,512]{2,1,0:T(8,128)(2,1)} custom-call(s32[8]{0:T(128)S(1)} %fusion.14.spot_ref, bf16[192,1536]{1,0:T(8,128)(2,1)S(1)} %pad_maximum_fusion.5.near_ref, bf16[192,1536]{1,0:T(8,128)(2,1)S(1)} %collective-permute-done.3.far_ref, bf16[4,384,384]{2,1,0:T(8,128)(2,1)S(1)} %all-to-all-done.1.w_ref, bf16[512,384]{1,0:T(8,128)(2,1)S(1)} %copy-done.3), custom_call_target="tpu_custom_call" | custom-call | tf_op jit(solution)/shard_map/merge_product/pallas_call | solution.py:377
  64.9 4.8 %all-to-all-start.2 = ((bf16[8,64,512]{2,1,0:T(8,128)(2,1)}), bf16[8,64,512]{2,1,0:T(8,128)(2,1)S(1)}, u32[]{:S(2)}, u32[]{:S(2)}) async-start(bf16[8,64,512]{2,1,0:T(8,128)(2,1)} %merge_product.1), calls=%async_computation.2 | async-start | bytes 1048576 | tf_op jit(solution)/shard_map/all_to_all | solution.py:451
  69.7 0.1 pad.19.clone
  69.8 1.6 %maximum_maximum_fusion.a_ref.b_ref.north_ref = bf16[4,2,6,16,768]{4,3,2,1,0:T(8,128)(2,1)S(1)} fusion(bf16[4,2,6,6,768]{4,3,2,1,0:T(8,128)(2,1)S(1)} %copy-done.11, bf16[1,2,6,6,768]{4,3,2,1,0:T(8,128)(2,1)} %bitcast.41, bf16[1,2,6,6,768]{4,3,2,1,0:T(8,128)(2,1)S(1)} %bitcast.39, bf16[1,2,6,6,768]{4,3,2,1,0:T(8,128)(2,1)} %bitcast.45, ...), kind=kLoop, calls=%fused_computation.1 | loop fusion | flops 7077888 | bytes 2064416 | tf_op jit(solution)/shard_map/concatenate | solution.py:491
  71.4 1.6 %copy.67 = bf16[4,2,4,12,768]{4,3,2,1,0:T(8,128)(2,1)S(1)} copy(bf16[4,2,4,12,768]{4,2,3,1,0:T(4,128)(2,1)} %collective-permute-done.5) | data formatting | bytes 1179648 | tf_op jit(solution)/shard_map/ppermute | solution.py:443
  73.0 0.1 pad.4.south_ref
  73.1 0.5 normalise.1
  73.7 0.3 copy-done.1
  74.0 1.0 copy-done.4
  75.0 0.6 copy-done.9
  75.6 7.2 %window_probs.1.p_ref = bf16[6,768,192]{2,1,0:T(8,128)(2,1)} custom-call(bf16[4,2,6,16,768]{4,3,2,1,0:T(8,128)(2,1)} %copy-done, bf16[4,2,4,16,768]{4,3,2,1,0:T(8,128)(2,1)} %copy-done.1, f32[6,48,384]{2,1,0:T(8,128)} %copy-done.2, bf16[384,192]{1,0:T(8,128)(2,1)} %constant.131.clone.spread_ref, f32[192,192]{1,0:T(8,128)} %and_select_fusion.mask_ref), custom_call_target="tpu_custom_call" | custom-call | tf_op jit(solution)/shard_map/window_probs/pallas_call | solution.py:339
  82.8 0.9 copy-done.13
  83.7 9.3 %score_grads.1 = (bf16[6,192,128]{2,1,0:T(8,128)(2,1)}, bf16[6,768,192]{2,1,0:T(8,128)(2,1)}, f32[16,24,384]{2,1,0:T(8,128)}) custom-call(bf16[8,64,512]{2,1,0:T(8,128)(2,1)} %copy-done.13, bf16[512,384]{1,0:T(8,128)(2,1)} %constant.134.clone.shuffle_ref.order_ref, f32[4,64,768]{2,1,0:T(8,128)} %copy-done.4, f32[64,128]{1,0:T(8,128)} %copy-done.9, ...), custom_call_target="tpu_custom_call" | custom-call | tf_op jit(solution)/shard_map/score_grads/pallas_call | solution.py:389
  93.0 5.1 %all-to-all-start.3 = ((f32[16,24,384]{2,1,0:T(8,128)}), f32[16,24,384]{2,1,0:T(8,128)S(1)}, u32[]{:S(2)}, u32[]{:S(2)}) async-start(f32[16,24,384]{2,1,0:T(8,128)} %get-tuple-element.25), calls=%async_computation.3 | async-start | bytes 1179648 | tf_op jit(solution)/shard_map/all_to_all | solution.py:451
  98.1 4.5 %window_grads.1 = bf16[3,192,768]{2,1,0:T(8,128)(2,1)} custom-call(bf16[4,2,6,16,768]{4,3,2,1,0:T(8,128)(2,1)} %copy-done, bf16[4,2,4,16,768]{4,3,2,1,0:T(8,128)(2,1)} %copy-done.1, bf16[6,192,128]{2,1,0:T(8,128)(2,1)} %get-tuple-element.26.o_ref, bf16[6,768,192]{2,1,0:T(8,128)(2,1)} %get-tuple-element.27.d_ref, bf16[6,768,192]{2,1,0:T(8,128)(2,1)} %window_probs.1.p_ref), custom_call_target="tpu_custom_call" | custom-call | tf_op jit(solution)/shard_map/window_grads/pallas_call | solution.py:424
  102.6 5.8 %all-to-all-done.3 = f32[16,24,384]{2,1,0:T(8,128)S(1)} async-done(((f32[16,24,384]{2,1,0:T(8,128)}), f32[16,24,384]{2,1,0:T(8,128)S(1)}, u32[]{:S(2)}, u32[]{:S(2)}) %all-to-all-start.3) | async-done | bytes 589856 | tf_op jit(solution)/shard_map/all_to_all | solution.py:451
  108.4 0.7 broadcast_in_dim.42
  109.1 8.1 %all-to-all-start.4 = ((bf16[8,24,384]{2,1,0:T(8,128)(2,1)}), bf16[8,24,384]{2,1,0:T(8,128)(2,1)S(1)}, u32[]{:S(2)}, u32[]{:S(2)}) async-start(bf16[8,24,384]{2,1,0:T(8,128)(2,1)} %broadcast_in_dim.42), calls=%async_computation.4 | async-start | bytes 294912 | tf_op jit(solution)/shard_map/all_to_all | solution.py:451
  117.2 0.1 fusion.15
  117.3 0.3 copy.75
  117.6 1.9 %collective-permute-start.6 = (bf16[3,2,3,12,768]{4,1,3,2,0:T(2,128)(2,1)S(1)}, bf16[3,2,3,12,768]{4,1,3,2,0:T(2,128)(2,1)S(1)}, u32[]{:S(2)}, u32[]{:S(2)}) collective-permute-start(bf16[3,2,3,12,768]{4,1,3,2,0:T(2,128)(2,1)S(1)} %copy.75), channel_id=1, source_target_pairs={{0,1},{1,2},{2,3},{3,0},{4,5},{5,6},{6,7},{7,4},{8,9},{9,10},{10,1... | collective-permute-start | bytes 995336 | tf_op jit(solution)/shard_map/ppermute | solution.py:443
  119.5 0.3 copy.76
  119.8 7.7 %collective-permute-done.6 = bf16[3,2,3,12,768]{4,1,3,2,0:T(2,128)(2,1)S(1)} collective-permute-done((bf16[3,2,3,12,768]{4,1,3,2,0:T(2,128)(2,1)S(1)}, bf16[3,2,3,12,768]{4,1,3,2,0:T(2,128)(2,1)S(1)}, u32[]{:S(2)}, u32[]{:S(2)}) %collective-permute-start.6) | collective-permute-done | bytes 331808 | tf_op jit(solution)/shard_map/ppermute | solution.py:443
  127.5 0.9 pad_maximum_fusion.4
  128.4 4.5 %all-to-all-done.4 = bf16[8,24,384]{2,1,0:T(8,128)(2,1)S(1)} async-done(((bf16[8,24,384]{2,1,0:T(8,128)(2,1)}), bf16[8,24,384]{2,1,0:T(8,128)(2,1)S(1)}, u32[]{:S(2)}, u32[]{:S(2)}) %all-to-all-start.4) | async-done | bytes 147488 | tf_op jit(solution)/shard_map/all_to_all | solution.py:451
  133.0 0.7 broadcast_in_dim.43
  133.7 4.7 %all-to-all-start.5 = ((bf16[16,24,384]{2,1,0:T(8,128)(2,1)}), bf16[16,24,384]{2,1,0:T(8,128)(2,1)S(1)}, u32[]{:S(2)}, u32[]{:S(2)}) async-start(bf16[16,24,384]{2,1,0:T(8,128)(2,1)} %broadcast_in_dim.43), calls=%async_computation.5 | async-start | bytes 589824 | tf_op jit(solution)/shard_map/all_to_all | solution.py:451
  138.4 0.5 fusion.16
  138.8 3.6 %collective-permute-start.7 = (bf16[3,2,6,6,768]{4,1,3,2,0:T(2,128)(2,1)S(1)}, bf16[3,2,6,6,768]{4,1,3,2,0:T(2,128)(2,1)S(1)}, u32[]{:S(2)}, u32[]{:S(2)}) collective-permute-start(bf16[3,2,6,6,768]{4,1,3,2,0:T(2,128)(2,1)S(1)} %get-tuple-element.35), channel_id=1, source_target_pairs={{0,4},{4,8},{8,12},{12,16},{16,20},{20,24},{24,28},{28,32},{32,36}... | collective-permute-start | bytes 995336 | tf_op jit(solution)/shard_map/ppermute | solution.py:443
  142.4 9.6 %collective-permute-done.7 = bf16[3,2,6,6,768]{4,1,3,2,0:T(2,128)(2,1)S(1)} collective-permute-done((bf16[3,2,6,6,768]{4,1,3,2,0:T(2,128)(2,1)S(1)}, bf16[3,2,6,6,768]{4,1,3,2,0:T(2,128)(2,1)S(1)}, u32[]{:S(2)}, u32[]{:S(2)}) %collective-permute-start.7) | collective-permute-done | bytes 331808 | tf_op jit(solution)/shard_map/ppermute | solution.py:443
  152.1 1.6 %fusion.2 = (bf16[2,6,12,768]{3,0,2,1:T(2,128)(2,1)}, bf16[2,6,12,768]{3,0,2,1:T(2,128)(2,1)}, bf16[2,6,12,768]{3,0,2,1:T(2,128)(2,1)}) fusion(bf16[3,2,6,6,768]{4,1,3,2,0:T(2,128)(2,1)S(1)} %get-tuple-element.36, bf16[3,2,6,6,768]{4,1,3,2,0:T(2,128)(2,1)S(1)} %collective-permute-done.7), kind=kLoop, calls=%fused_computation.17 | loop fusion | flops 331776 | bytes 1327104 | tf_op jit(solution)/shard_map/squeeze | solution.py:529
  153.7 0.9 reshape.89
  154.5 0.3 convert_bitcast_fusion
  154.8 0.2 copy.70
  155.0 1.5 reshape.93
  (58 shorter events, 0.3 us)
Async XLA Ops:
  0.6 0.9 copy-start.8
  1.5 23.2 %copy-start.19 = (bf16[2,6,12,768]{3,0,2,1:T(2,128)(2,1)S(1)}, bf16[2,6,12,768]{3,0,2,1:T(2,128)(2,1)}, u32[]{:S(2)}) copy-start(bf16[2,6,12,768]{3,0,2,1:T(2,128)(2,1)} %param.21) | copy-start | bytes 663556
  1.5 23.2 %copy-start.20 = (bf16[2,6,12,768]{3,0,2,1:T(2,128)(2,1)S(1)}, bf16[2,6,12,768]{3,0,2,1:T(2,128)(2,1)}, u32[]{:S(2)}) copy-start(bf16[2,6,12,768]{3,0,2,1:T(2,128)(2,1)} %param.15) | copy-start | bytes 663556
  1.5 31.7 %copy-start.21 = (bf16[2,6,12,768]{3,0,2,1:T(2,128)(2,1)S(1)}, bf16[2,6,12,768]{3,0,2,1:T(2,128)(2,1)}, u32[]{:S(2)}) copy-start(bf16[2,6,12,768]{3,0,2,1:T(2,128)(2,1)} %param.19) | copy-start | bytes 663556
  1.5 31.7 %copy-start.22 = (bf16[2,6,12,768]{3,0,2,1:T(2,128)(2,1)S(1)}, bf16[2,6,12,768]{3,0,2,1:T(2,128)(2,1)}, u32[]{:S(2)}) copy-start(bf16[2,6,12,768]{3,0,2,1:T(2,128)(2,1)} %param.20) | copy-start | bytes 663556
  3.4 17.8 %collective-permute-start = (bf16[2,3,3,1536]{3,0,2,1:T(2,128)(2,1)S(1)}, bf16[2,3,3,1536]{3,0,2,1:T(2,128)(2,1)S(1)}, u32[]{:S(2)}, u32[]{:S(2)}) collective-permute-start(bf16[2,3,3,1536]{3,0,2,1:T(2,128)(2,1)S(1)} %get-tuple-element.46), channel_id=1, source_target_pairs={{0,508},{4,0},{8,4},{12,8},{16,12},{20,16},{24,20},{28,24},{32,28}... | collective-permute-start | bytes 165896 | tf_op jit(solution)/shard_map/ppermute | solution.py:443
  17.5 24.6 %all-to-all-start = ((bf16[16,24,384]{2,1,0:T(8,128)(2,1)}), bf16[16,24,384]{2,1,0:T(8,128)(2,1)S(1)}, u32[]{:S(2)}, u32[]{:S(2)}) async-start(bf16[16,24,384]{2,1,0:T(8,128)(2,1)} %pack_weight.1), calls=%async_computation | async-start | bytes 589824 | tf_op jit(solution)/shard_map/all_to_all | solution.py:451
  21.4 8.7 %collective-permute-start.1 = (bf16[48,1536]{1,0:T(8,128)(2,1)S(1)}, bf16[48,1536]{1,0:T(8,128)(2,1)S(1)}, u32[]{:S(2)}, u32[]{:S(2)}) collective-permute-start(bf16[48,1536]{1,0:T(8,128)(2,1)S(1)} %bitcast.35), channel_id=1, source_target_pairs={{0,2},{1,3},{2,0},{3,1},{4,6},{5,7},{6,4},{7,5},{8,10},{9,11},{10,... | collective-permute-start | bytes 442376 | tf_op jit(solution)/shard_map/ppermute | solution.py:447
  30.1 16.8 %collective-permute-start.2 = (bf16[96,1536]{1,0:T(8,128)(2,1)S(1)}, bf16[96,1536]{1,0:T(8,128)(2,1)}, u32[]{:S(2)}, u32[]{:S(2)}) collective-permute-start(bf16[96,1536]{1,0:T(8,128)(2,1)S(1)} %pad_maximum_fusion.7), channel_id=1, source_target_pairs={{0,256},{4,260},{8,264},{12,268},{16,272},{20,276},{24,280},{28,28... | collective-permute-start | bytes 884744 | tf_op jit(solution)/shard_map/ppermute | solution.py:447
  34.5 15.5 %collective-permute-start.4 = (bf16[4,2,6,6,768]{4,0,3,2,1:T(4,128)(2,1)S(1)}, bf16[4,2,6,6,768]{4,0,3,2,1:T(4,128)(2,1)}, u32[]{:S(2)}, u32[]{:S(2)}) collective-permute-start(bf16[4,2,6,6,768]{4,0,3,2,1:T(4,128)(2,1)S(1)} %copy.63), channel_id=1, source_target_pairs={{0,508},{4,0},{8,4},{12,8},{16,12},{20,16},{24,20},{28,24},{32,28}... | collective-permute-start | bytes 1327112 | tf_op jit(solution)/shard_map/ppermute | solution.py:443
  43.3 18.0 %all-to-all-start.1 = ((bf16[4,384,384]{2,1,0:T(8,128)(2,1)}), bf16[4,384,384]{2,1,0:T(8,128)(2,1)S(1)}, u32[]{:S(2)}, u32[]{:S(2)}) async-start(bf16[4,384,384]{2,1,0:T(8,128)(2,1)} %broadcast_in_dim.38), calls=%async_computation.1 | async-start | bytes 2359296 | tf_op jit(solution)/shard_map/all_to_all | solution.py:451
  47.9 13.5 %collective-permute-start.3 = (bf16[192,1536]{1,0:T(8,128)(2,1)S(1)}, bf16[192,1536]{1,0:T(8,128)(2,1)S(1)}, u32[]{:S(2)}, u32[]{:S(2)}) collective-permute-start(bf16[192,1536]{1,0:T(8,128)(2,1)S(1)} %pad_maximum_fusion.5.near_ref), channel_id=1, source_target_pairs={{0,1},{1,0},{2,3},{3,2},{4,5},{5,4},{6,7},{7,6},{8,9},{9,8},{10,11... | collective-permute-start | bytes 1769480 | tf_op jit(solution)/shard_map/ppermute | solution.py:447
  49.8 1.3 copy-start.14
  49.9 1.3 copy-start.16
  49.9 1.3 copy-start.17
  49.9 1.2 copy-start.18
  51.1 0.8 copy-start.10
  52.0 5.6 %copy-start.5 = (f32[1,24,3312]{2,1,0:T(8,128)S(1)}, f32[1,24,3312]{2,1,0:T(8,128)}, u32[]{:S(2)}) copy-start(f32[1,24,3312]{2,1,0:T(8,128)} %table_ref.1) | copy-start | bytes 953860
  52.0 5.6 %copy-start.6 = (bf16[2,138,384]{2,1,0:T(8,128)(2,1)S(1)}, bf16[2,138,384]{2,1,0:T(8,128)(2,1)}, u32[]{:S(2)}) copy-start(bf16[2,138,384]{2,1,0:T(8,128)(2,1)} %constant.135.clone.open_ref) | copy-start | bytes 635908
  52.2 9.1 %copy-start.3 = (bf16[512,384]{1,0:T(8,128)(2,1)S(1)}, bf16[512,384]{1,0:T(8,128)(2,1)}, u32[]{:S(2)}) copy-start(bf16[512,384]{1,0:T(8,128)(2,1)} %constant.134.clone.shuffle_ref.order_ref) | copy-start | bytes 1179652
  53.4 18.0 %collective-permute-start.5 = (bf16[4,2,4,12,768]{4,2,3,1,0:T(4,128)(2,1)}, bf16[4,2,4,12,768]{4,2,3,1,0:T(4,128)(2,1)}, u32[]{:S(2)}, u32[]{:S(2)}) collective-permute-start(bf16[4,2,4,12,768]{4,2,3,1,0:T(4,128)(2,1)} %copy.66), channel_id=1, source_target_pairs={{0,3},{1,0},{2,1},{3,2},{4,7},{5,4},{6,5},{7,6},{8,11},{9,8},{10,9... | collective-permute-start | bytes 1769480 | tf_op jit(solution)/shard_map/ppermute | solution.py:443
  58.2 0.8 copy-start.2
  59.0 10.8 %copy-start.11 = (bf16[4,2,6,6,768]{4,3,2,1,0:T(8,128)(2,1)S(1)}, bf16[4,2,6,6,768]{4,3,2,1,0:T(8,128)(2,1)}, u32[]{:S(2)}) copy-start(bf16[4,2,6,6,768]{4,3,2,1,0:T(8,128)(2,1)} %copy-done.10) | copy-start | bytes 1327108
  59.0 10.7 %copy-start.15 = (bf16[2,6,6,768]{3,2,1,0:T(8,128)(2,1)S(1)}, bf16[2,6,6,768]{3,2,1,0:T(8,128)(2,1)}, u32[]{:S(2)}) copy-start(bf16[2,6,6,768]{3,2,1,0:T(8,128)(2,1)} %copy-done.14) | copy-start | bytes 331780
  64.9 17.9 %all-to-all-start.2 = ((bf16[8,64,512]{2,1,0:T(8,128)(2,1)}), bf16[8,64,512]{2,1,0:T(8,128)(2,1)S(1)}, u32[]{:S(2)}, u32[]{:S(2)}) async-start(bf16[8,64,512]{2,1,0:T(8,128)(2,1)} %merge_product.1), calls=%async_computation.2 | async-start | bytes 1048576 | tf_op jit(solution)/shard_map/all_to_all | solution.py:451
  71.4 2.3 %copy-start = (bf16[4,2,6,16,768]{4,3,2,1,0:T(8,128)(2,1)}, bf16[4,2,6,16,768]{4,3,2,1,0:T(8,128)(2,1)S(1)}, u32[]{:S(2)}) copy-start(bf16[4,2,6,16,768]{4,3,2,1,0:T(8,128)(2,1)S(1)} %maximum_maximum_fusion.a_ref.b_ref.north_ref) | copy-start | bytes 3538948
  71.4 1.7 %copy-start.7 = (bf16[256,256]{1,0:T(8,128)(2,1)S(1)}, bf16[256,256]{1,0:T(8,128)(2,1)}, u32[]{:S(2)}) copy-start(bf16[256,256]{1,0:T(8,128)(2,1)} %constant.132.clone.quarter_ref) | copy-start | bytes 393220
  73.1 0.9 copy-start.1
  74.0 1.0 copy-start.4
  75.0 0.6 copy-start.9
  82.8 0.9 copy-start.13
  93.0 15.4 %all-to-all-start.3 = ((f32[16,24,384]{2,1,0:T(8,128)}), f32[16,24,384]{2,1,0:T(8,128)S(1)}, u32[]{:S(2)}, u32[]{:S(2)}) async-start(f32[16,24,384]{2,1,0:T(8,128)} %get-tuple-element.25), calls=%async_computation.3 | async-start | bytes 1179648 | tf_op jit(solution)/shard_map/all_to_all | solution.py:451
  102.6 14.7 %copy-start.12 = (bf16[3,192,768]{2,1,0:T(8,128)(2,1)S(1)}, bf16[3,192,768]{2,1,0:T(8,128)(2,1)}, u32[]{:S(2)}) copy-start(bf16[3,192,768]{2,1,0:T(8,128)(2,1)} %window_grads.1) | copy-start | bytes 2654212
  109.1 23.8 %all-to-all-start.4 = ((bf16[8,24,384]{2,1,0:T(8,128)(2,1)}), bf16[8,24,384]{2,1,0:T(8,128)(2,1)S(1)}, u32[]{:S(2)}, u32[]{:S(2)}) async-start(bf16[8,24,384]{2,1,0:T(8,128)(2,1)} %broadcast_in_dim.42), calls=%async_computation.4 | async-start | bytes 294912 | tf_op jit(solution)/shard_map/all_to_all | solution.py:451
  117.6 9.9 %collective-permute-start.6 = (bf16[3,2,3,12,768]{4,1,3,2,0:T(2,128)(2,1)S(1)}, bf16[3,2,3,12,768]{4,1,3,2,0:T(2,128)(2,1)S(1)}, u32[]{:S(2)}, u32[]{:S(2)}) collective-permute-start(bf16[3,2,3,12,768]{4,1,3,2,0:T(2,128)(2,1)S(1)} %copy.75), channel_id=1, source_target_pairs={{0,1},{1,2},{2,3},{3,0},{4,5},{5,6},{6,7},{7,4},{8,9},{9,10},{10,1... | collective-permute-start | bytes 995336 | tf_op jit(solution)/shard_map/ppermute | solution.py:443
  133.7 20.0 %all-to-all-start.5 = ((bf16[16,24,384]{2,1,0:T(8,128)(2,1)}), bf16[16,24,384]{2,1,0:T(8,128)(2,1)S(1)}, u32[]{:S(2)}, u32[]{:S(2)}) async-start(bf16[16,24,384]{2,1,0:T(8,128)(2,1)} %broadcast_in_dim.43), calls=%async_computation.5 | async-start | bytes 589824 | tf_op jit(solution)/shard_map/all_to_all | solution.py:451
  138.8 13.2 %collective-permute-start.7 = (bf16[3,2,6,6,768]{4,1,3,2,0:T(2,128)(2,1)S(1)}, bf16[3,2,6,6,768]{4,1,3,2,0:T(2,128)(2,1)S(1)}, u32[]{:S(2)}, u32[]{:S(2)}) collective-permute-start(bf16[3,2,6,6,768]{4,1,3,2,0:T(2,128)(2,1)S(1)} %get-tuple-element.35), channel_id=1, source_target_pairs={{0,4},{4,8},{8,12},{12,16},{16,20},{20,24},{24,28},{28,32},{32,36}... | collective-permute-start | bytes 995336 | tf_op jit(solution)/shard_map/ppermute | solution.py:443

commit v7 on v6

--- a/solution.py
+++ b/solution.py
@@ -17,6 +17,7 @@
 GROUPS = 6
 PER = 3
 STEPS = GROUPS // PER
+SHARE = 7
 LOW = -1e30
 SMALL = 12 * 1024 * 1024
 LARGE = 56 * 1024 * 1024
@@ -67,7 +68,11 @@
         for r in range(6):
             for d in range(23):
                 open_up[half, r * 23 + d, half * 192 + r * SEG + 22 - d] = 1
-    all_of = (sums, spread, quarter, back, order, shuffle, open_up)
+    close = np.zeros((WIDE, 512), np.float32)
+    for b in range(ROWS):
+        for d in range(23):
+            close[b * SEG + d, b // 6 * 256 + b % 6 * 23 + d] = 1
+    all_of = (sums, spread, quarter, back, order, shuffle, open_up, close)
     return [jnp.asarray(a, jnp.bfloat16) for a in all_of]
 
 
@@ -197,6 +202,13 @@
                 ].astype(jnp.bfloat16)
 
 
+def score_grad(probs, o_win, v_win):
+    d_probs = dot(by_head(o_win), v_win, ((1,), (1,)))
+    probs = probs.astype(jnp.float32)
+    delta = jnp.sum(probs * d_probs, axis=-1, keepdims=True)
+    return (probs * (d_probs - delta)).astype(jnp.bfloat16)
+
+
 def scores_kernel(
     recv_ref,
     order_ref,
@@ -209,7 +221,6 @@
     south_ref,
     p_ref,
     o_out_ref,
-    d_ref,
     table_ref,
     o_ref,
     sum_ref,
@@ -244,13 +255,7 @@
     for group in range(PER):
         o_win = o_ref[g * PER + group]
         o_out_ref[group] = o_win
-        probs = p_ref[group].astype(jnp.float32)
-        v_win = window(north_ref, south_ref, 0, group)
-        d_probs = dot(by_head(o_win), v_win, ((1,), (1,)))
-        delta = jnp.sum(probs * d_probs, axis=-1, keepdims=True)
-        d_low = (probs * (d_probs - delta)).astype(jnp.bfloat16)
-        d_ref[group] = d_low
-
+        d_low = score_grad(p_ref[group], o_win, window(north_ref, south_ref, 0, group))
         spread = dot(d_low, sums_ref[...]).reshape(4 * ROWS, PAD, WIDE)
         for s in range(3):
             lanes = slice(s * 128, (s + 1) * 128)
@@ -260,17 +265,42 @@
     @pl.when(g == STEPS - 1)
     def _():
         whole = jnp.concatenate([sum_ref[s] for s in range(GROUPS)], axis=0)
+        tiles = [
+            whole[r * 8 : (r + 1) * 8, s * 128 : (s + 1) * 128] for s in range(3) for r in range(36)
+        ]
+        tiles += [jnp.zeros((8, 128), jnp.float32)] * (16 * SHARE - len(tiles))
         for part in range(16):
-            table_ref[part, 0:18] = whole[part * 18 : (part + 1) * 18]
-            table_ref[part, 18:24] = jnp.zeros((6, WIDE), jnp.float32)
-
-
-def grads_kernel(north_ref, south_ref, o_ref, d_ref, p_ref, grads_ref):
+            chunk = jnp.concatenate(tiles[part * SHARE : (part + 1) * SHARE], axis=0)
+            table_ref[part] = chunk.astype(jnp.bfloat16)
+
+
+def close_kernel(parts_ref, close_ref, out_ref, wide_ref):
+    for part in range(16):
+        chunk = parts_ref[part].astype(jnp.float32)
+        for k in range(SHARE):
+            s, r = divmod(part * SHARE + k, 36)
+            if s < 3:
+                wide_ref[s, r * 8 : (r + 1) * 8] = chunk[k * 8 : (k + 1) * 8]
+    rows = []
+    for a in range(ROWS):
+        lanes = [wide_ref[s, pl.ds(a, HEADS, stride=ROWS), :] for s in range(3)]
+        rows.append(jnp.concatenate(lanes, axis=1))
+    dense = dot(jnp.concatenate(rows, axis=0).astype(jnp.bfloat16), close_ref[...])
+    for a in range(ROWS):
+        for half in range(2):
+            first = (a // 6 * 2 + half) * 828 + a % 6 * 138
+            out_ref[0, :, first : first + 138] = dense[
+                a * HEADS : (a + 1) * HEADS, half * 256 : half * 256 + 138
+            ]
+
+
+def grads_kernel(north_ref, south_ref, o_ref, p_ref, grads_ref):
     for group in range(PER):
         lanes = slice(group * 128, (group + 1) * 128)
         q_win = window(north_ref, south_ref, 0, group)
         k_win = window(north_ref, south_ref, 1, group)
-        o_win, d_low, p_low = o_ref[group], d_ref[group], p_ref[group]
+        o_win, p_low = o_ref[group], p_ref[group]
+        d_low = score_grad(p_low, o_win, window(north_ref, south_ref, 2, group))
         q_all = dot(d_low, k_win)
         q_grad = jnp.zeros((TOK, 128), jnp.float32)
         for h in range(4):
@@ -403,13 +433,11 @@
         ],
         out_specs=(
             group_spec(TOK, 128),
-            group_spec(4 * TOK, TOK),
-            whole_spec((16, 24, WIDE)),
+            whole_spec((16, 8 * SHARE, 128)),
         ),
         out_shape=(
             jax.ShapeDtypeStruct((GROUPS, TOK, 128), jnp.bfloat16),
-            jax.ShapeDtypeStruct((GROUPS, 4 * TOK, TOK), jnp.bfloat16),
-            jax.ShapeDtypeStruct((16, 24, WIDE), jnp.float32),
+            jax.ShapeDtypeStruct((16, 8 * SHARE, 128), jnp.bfloat16),
         ),
         scratch_shapes=[
             pltpu.VMEM((GROUPS, TOK, 128), jnp.bfloat16),
@@ -420,22 +448,33 @@
     )(recv, order, normed, inverse, gain, back, sums, across, south, probs)
 
 
-def window_grads(across, south, o_win, d_low, probs):
+def close_table(parts, close):
+    return pl.pallas_call(
+        close_kernel,
+        in_specs=[vmem, vmem],
+        out_specs=vmem,
+        out_shape=jax.ShapeDtypeStruct((1, HEADS, 3312), jnp.float32),
+        scratch_shapes=[pltpu.VMEM((3, ROWS * HEADS, 128), jnp.float32)],
+        compiler_params=params,
+        name="close_table",
+    )(parts, close)
+
+
+def window_grads(across, south, o_win, probs):
     return pl.pallas_call(
         grads_kernel,
         grid=(STEPS,),
         in_specs=[
-            north_spec(0, 2),
-            south_spec(0, 2),
+            north_spec(0, 3),
+            south_spec(0, 3),
             group_spec(TOK, 128),
-            group_spec(4 * TOK, TOK),
             group_spec(4 * TOK, TOK),
         ],
         out_specs=pl.BlockSpec((3, TOK, PER * 128), lambda g: (0, 0, g)),
         out_shape=jax.ShapeDtypeStruct((3, TOK, 768), jnp.bfloat16),
         compiler_params=large,
         name="window_grads",
-    )(across, south, o_win, d_low, probs)
+    )(across, south, o_win, probs)
 
 
 def from_behind(shard, axis, by):
@@ -456,7 +495,7 @@
 
 
 def on_device(y_block, merge_gain, merge_weight, d_merged, q_proj, k_proj, v_proj, bias_table):
-    sums, spread, quarter, back, order, shuffle, open_up = layout_constants()
+    sums, spread, quarter, back, order, shuffle, open_up, close = layout_constants()
     lat = lax.axis_index("lat")
 
     packed = pack_weight(lat.reshape(1), merge_weight)
@@ -496,23 +535,23 @@
         ],
         axis=3,
     )
-    south = from_behind(across[:, :, :4, :12], "lat", -1)
-    south = jnp.pad(south, ((0, 0), (0, 0), (0, 0), (0, 4), (0, 0)))
+    south = from_behind(across[:, :, :4], "lat", -1)
 
     weight, table, mask = lax.optimization_barrier((weight, table, mask))
     parts = merge_product(spots, near, far, weight, shuffle)
     recv = swap(parts, ("lon", "lat"), x_lat_groups)
 
-    south, _ = lax.optimization_barrier((south, parts))
+    table, quarter, _ = lax.optimization_barrier((table, quarter, parts))
     probs = window_probs(across, south, table, spread, mask)
     normed, inverse = normalise(across, south, quarter)
 
-    o_win, d_low, table_part = score_grads(
+    o_win, table_part = score_grads(
         recv, order, normed, inverse, merge_gain.reshape(4, 1, 768), back, sums, across, south, probs
     )
 
-    table_part = jnp.sum(swap(table_part, "lon", near_groups), axis=0).astype(jnp.bfloat16)
-    grads = window_grads(across, south, o_win, d_low, probs)
+    table_part = swap(table_part, "lon", near_groups).astype(jnp.float32)
+    table_part = jnp.sum(table_part, axis=0).astype(jnp.bfloat16)
+    grads = window_grads(across, south, o_win, probs)
     grid = grads.reshape(3, 2, 6, PAD, 768)[:, :, :, :12]
     southern = from_behind(grid[:, :, 3:], "lat", 1)
     fixed = jnp.concatenate([southern, grid[:, :, :3]], axis=2)
@@ -523,9 +562,7 @@
     finished = jnp.concatenate([western, fixed[:, :, :, :6]], axis=3)
 
     table_part = jnp.sum(table_part.astype(jnp.float32), axis=0).astype(jnp.bfloat16)
-    table_sum = share(table_part, 16, "lon", near_groups)[:, :18].astype(jnp.float32)
-    table_sum = table_sum.reshape(HEADS, 2, 6, 2, 6, SEG)[..., :23].transpose(0, 1, 3, 2, 4, 5)
-    table_grad = table_sum.reshape(bias_table.shape)
+    table_grad = close_table(share(table_part, 16, "lon", near_groups), close)
     return (finished[0], finished[1], finished[2], table_grad)
 
 

time: 158 us -> 156 us (0.987)
  waiting for transfers between devices: 35.1 us -> 30.5 us
  starting transfers between devices: 68.7 us -> 72.7 us
  local copies, waits for them, and re-layouts: 17.4 us -> 13.7 us
  Pallas kernels: 26.6 us -> 28.9 us
    all_to_all x6, waiting for transfers between devices: 12.7 us -> 18.4 us  [swap(): lax.all_to_all(shard, axis, 0, 0, tiled=True, axis_index_groups=groups)]
    ppermute x5, waiting for transfers between devices: 17.4 us -> 12.1 us  [from_behind(): lax.ppermute(shard, axis, [(i, (i + by) % size) for i in range(size)])]
    ppermute x3, waiting for transfers between devices: 5.04 us -> 0.01 us  [partner(): lax.ppermute(shard, axis, [(i, i ^ bit) for i in range(lax.axis_size(axis...]
    all_to_all x6, starting transfers between devices: 29.7 us -> 33.8 us  [swap(): lax.all_to_all(shard, axis, 0, 0, tiled=True, axis_index_groups=groups)]
    pallas_call x1 -> x2, Pallas kernels: 4.48 us -> 7.48 us  [the longest x1 6.3 us: window_grads(): pl.pallas_call(grads_kernel, grid=(STEPS,), in_specs=[north_spec(0, 3), s...]
    ppermute x2 -> x1, local copies, waits for them, and re-layouts: 2.77 us -> 0.06 us  [from_behind(): lax.ppermute(shard, axis, [(i, (i + by) % size) for i in range(size)])]
    reshape x3 -> x0, local copies, waits for them, and re-layouts: 2.55 us -> none  [the longest x2 1.69 us: on_device(): table_grad = table_sum.reshape(bias_table.shape)]
    unnamed x52 -> x40, local copies, waits for them, and re-layouts: 5.91 us -> 6.64 us
  transfers between devices with their start and end apart: 14 -> 14, of which waited for: 6 -> 5; matrix products, arithmetic and copies ran while one was open for 9% -> 9% of each run, Pallas kernels for 10% -> 12%
where the time goes in v7:
time: 156 us; the launch traced here: 154 us
  starting transfers between devices  72.7 us (47%)
  waiting for transfers between devices  30.5 us (20%)
  Pallas kernels  28.9 us (19%)
  local copies, waits for them, and re-layouts  13.7 us (9%)
  other arithmetic  7.43 us (5%)
    all_to_all x6, starting transfers between devices, swap(): lax.all_to_all(shard, axis, 0, 0, tiled=True, axis_index_groups=groups)  33.8 us
    ppermute x5, starting transfers between devices, from_behind(): lax.ppermute(shard, axis, [(i, (i + by) % size) for i in range(size)])  29.7 us
    all_to_all x6, waiting for transfers between devices, swap(): lax.all_to_all(shard, axis, 0, 0, tiled=True, axis_index_groups=groups)  18.4 us
    ppermute x5, waiting for transfers between devices, from_behind(): lax.ppermute(shard, axis, [(i, (i + by) % size) for i in range(size)])  12.1 us
    ppermute x3, starting transfers between devices, partner(): lax.ppermute(shard, axis, [(i, i ^ bit) for i in range(lax.axis_size(axis...  9.21 us
    pallas_call x1, Pallas kernels, score_grads(): pl.pallas_call(scores_kernel, grid=(STEPS,), in_specs=[whole_spec((8, 64,...  8.69 us
    pallas_call x1, Pallas kernels, window_probs(): pl.pallas_call(probs_kernel, grid=(STEPS,), in_specs=[north_spec(0, 2), s...  7.17 us
    unnamed x40, local copies, waits for them, and re-layouts  6.64 us
  transfers between devices with their start and end apart: 14, of which 5 were waited for; matrix products, arithmetic and copies ran while one was open for 9% of the time, Pallas kernels for 12%

profile of v7, /device:TPU:6, one launch (start us, length us, event | category | flops | bytes accessed | tf_op | source)
XLA Modules:
  0.0 154.2 jit_solution(10030112583895946994)
XLA Ops:
  0.6 0.9 copy-done.10
  1.5 0.9 pack_weight.1
  2.4 0.9 fusion.21
  3.4 14.1 %collective-permute-start = (bf16[2,3,3,1536]{3,0,2,1:T(2,128)(2,1)S(1)}, bf16[2,3,3,1536]{3,0,2,1:T(2,128)(2,1)S(1)}, u32[]{:S(2)}, u32[]{:S(2)}) collective-permute-start(bf16[2,3,3,1536]{3,0,2,1:T(2,128)(2,1)S(1)} %get-tuple-element.46), channel_id=1, source_target_pairs={{0,508},{4,0},{8,4},{12,8},{16,12},{20,16},{24,20},{28,24},{32,28}... | collective-permute-start | bytes 165896 | tf_op jit(solution)/shard_map/ppermute | solution.py:482
  17.5 3.6 %all-to-all-start = ((bf16[16,24,384]{2,1,0:T(8,128)(2,1)}), bf16[16,24,384]{2,1,0:T(8,128)(2,1)S(1)}, u32[]{:S(2)}, u32[]{:S(2)}) async-start(bf16[16,24,384]{2,1,0:T(8,128)(2,1)} %pack_weight.1), calls=%async_computation | async-start | bytes 589824 | tf_op jit(solution)/shard_map/all_to_all | solution.py:490
  21.1 0.3 fusion.17
  21.4 0.3 fusion.19
  21.7 0.1 pad.21.clone
  21.8 0.0 collective-permute-done
  21.8 0.2 maximum_maximum_fusion.1
  22.0 3.3 %collective-permute-start.1 = (bf16[48,1536]{1,0:T(8,128)(2,1)S(1)}, bf16[48,1536]{1,0:T(8,128)(2,1)S(1)}, u32[]{:S(2)}, u32[]{:S(2)}) collective-permute-start(bf16[48,1536]{1,0:T(8,128)(2,1)S(1)} %bitcast.32), channel_id=1, source_target_pairs={{0,2},{1,3},{2,0},{3,1},{4,6},{5,7},{6,4},{7,5},{8,10},{9,11},{10,... | collective-permute-start | bytes 442376 | tf_op jit(solution)/shard_map/ppermute | solution.py:486
  25.4 0.8 pad_maximum_fusion.2
  26.2 0.2 copy.48
  26.3 6.9 %collective-permute-start.4 = (bf16[4,2,6,6,768]{4,0,3,2,1:T(4,128)(2,1)S(1)}, bf16[4,2,6,6,768]{4,0,3,2,1:T(4,128)(2,1)S(1)}, u32[]{:S(2)}, u32[]{:S(2)}) collective-permute-start(bf16[4,2,6,6,768]{4,0,3,2,1:T(4,128)(2,1)S(1)} %copy.48), channel_id=1, source_target_pairs={{0,508},{4,0},{8,4},{12,8},{16,12},{20,16},{24,20},{28,24},{32,28}... | collective-permute-start | bytes 1327112 | tf_op jit(solution)/shard_map/ppermute | solution.py:482
  33.2 0.0 collective-permute-done.1
  33.2 0.7 pad_maximum_fusion.3
  34.0 4.0 %collective-permute-start.2 = (bf16[96,1536]{1,0:T(8,128)(2,1)}, bf16[96,1536]{1,0:T(8,128)(2,1)}, u32[]{:S(2)}, u32[]{:S(2)}) collective-permute-start(bf16[96,1536]{1,0:T(8,128)(2,1)} %pad_maximum_fusion.3), channel_id=1, source_target_pairs={{0,256},{4,260},{8,264},{12,268},{16,272},{20,276},{24,280},{28,28... | collective-permute-start | bytes 884744 | tf_op jit(solution)/shard_map/ppermute | solution.py:486
  38.0 2.3 %all-to-all-done = bf16[16,24,384]{2,1,0:T(8,128)(2,1)S(1)} async-done(((bf16[16,24,384]{2,1,0:T(8,128)(2,1)}), bf16[16,24,384]{2,1,0:T(8,128)(2,1)S(1)}, u32[]{:S(2)}, u32[]{:S(2)}) %all-to-all-start) | async-done | bytes 294944 | tf_op jit(solution)/shard_map/all_to_all | solution.py:490
  40.3 1.1 broadcast_in_dim.38
  41.4 4.6 %all-to-all-start.1 = ((bf16[4,384,384]{2,1,0:T(8,128)(2,1)}), bf16[4,384,384]{2,1,0:T(8,128)(2,1)S(1)}, u32[]{:S(2)}, u32[]{:S(2)}) async-start(bf16[4,384,384]{2,1,0:T(8,128)(2,1)} %broadcast_in_dim.38), calls=%async_computation.1 | async-start | bytes 2359296 | tf_op jit(solution)/shard_map/all_to_all | solution.py:490
  46.2 0.1 pad.9.clone
  46.3 0.6 open_table.1.table_ref
  46.9 0.8 copy-done.3
  47.7 0.0 collective-permute-done.4
  47.7 0.1 copy.49
  47.8 1.8 %pad_maximum_fusion.1.near_ref = bf16[192,1536]{1,0:T(8,128)(2,1)} fusion(bf16[96,1536]{1,0:T(8,128)(2,1)} %collective-permute-done.2, bf16[48,1536]{1,0:T(8,128)(2,1)S(1)} %collective-permute-done.1, bf16[48,1536]{1,0:T(8,128)(2,1)S(1)} %bitcast.34), kind=kLoop, calls=%fused_computation.2 | loop fusion | flops 1769472 | bytes 1179648 | tf_op jit(solution)/shard_map/concatenate | solution.py:516
  49.6 1.9 %collective-permute-start.3 = (bf16[192,1536]{1,0:T(8,128)(2,1)}, bf16[192,1536]{1,0:T(8,128)(2,1)}, u32[]{:S(2)}, u32[]{:S(2)}) collective-permute-start(bf16[192,1536]{1,0:T(8,128)(2,1)} %pad_maximum_fusion.1.near_ref), channel_id=1, source_target_pairs={{0,1},{1,0},{2,3},{3,2},{4,5},{5,4},{6,7},{7,6},{8,9},{9,8},{10,11... | collective-permute-start | bytes 1769480 | tf_op jit(solution)/shard_map/ppermute | solution.py:486
  51.5 0.5 maximum_maximum_fusion.a_ref.b_ref.north_ref
  52.1 0.0 copy-start.4
  52.1 1.0 slice.75
  53.0 3.4 %collective-permute-start.5 = (bf16[4,2,4,16,768]{4,3,2,1,0:T(8,128)(2,1)}, bf16[4,2,4,16,768]{4,3,2,1,0:T(8,128)(2,1)S(1)}, u32[]{:S(2)}, u32[]{:S(2)}) collective-permute-start(bf16[4,2,4,16,768]{4,3,2,1,0:T(8,128)(2,1)} %slice.75), channel_id=1, source_target_pairs={{0,3},{1,0},{2,1},{3,2},{4,7},{5,4},{6,5},{7,6},{8,11},{9,8},{10,9... | collective-permute-start | bytes 2359304 | tf_op jit(solution)/shard_map/ppermute | solution.py:482
  56.5 0.8 and_select_fusion.mask_ref
  57.2 0.6 all-to-all-done.1.w_ref
  57.8 3.5 %merge_product.1 = bf16[8,64,512]{2,1,0:T(8,128)(2,1)S(1)} custom-call(s32[8]{0:T(128)S(1)} %fusion.14.spot_ref, bf16[192,1536]{1,0:T(8,128)(2,1)} %pad_maximum_fusion.1.near_ref, bf16[192,1536]{1,0:T(8,128)(2,1)} %collective-permute-done.3.far_ref, bf16[4,384,384]{2,1,0:T(8,128)(2,1)S(1)} %all-to-all-done.1.w_ref, bf16[512,384]{1,0:T(8,128)(2,1)S(1)} %copy-done.4), custom_call_target="tpu_custom_call" | custom-call | tf_op jit(solution)/shard_map/merge_product/pallas_call | solution.py:407
  61.3 0.8 copy-done.2
  62.1 5.5 %all-to-all-start.2 = ((bf16[8,64,512]{2,1,0:T(8,128)(2,1)}), bf16[8,64,512]{2,1,0:T(8,128)(2,1)S(1)}, u32[]{:S(2)}, u32[]{:S(2)}) async-start(bf16[8,64,512]{2,1,0:T(8,128)(2,1)} %copy-done.2), calls=%async_computation.2 | async-start | bytes 1048576 | tf_op jit(solution)/shard_map/all_to_all | solution.py:490
  67.6 0.0 copy-start.9
  67.6 0.9 copy-done.9
  68.5 0.5 normalise.1
  69.0 0.4 copy-done.1
  69.4 0.9 copy-done.5
  70.3 0.6 copy-done.11
  70.9 7.2 %window_probs.1.p_ref = bf16[6,768,192]{2,1,0:T(8,128)(2,1)} custom-call(bf16[4,2,6,16,768]{4,3,2,1,0:T(8,128)(2,1)} %copy-done, bf16[4,2,4,16,768]{4,3,2,1,0:T(8,128)(2,1)} %copy-done.1, f32[6,48,384]{2,1,0:T(8,128)} %copy-done.3, bf16[384,192]{1,0:T(8,128)(2,1)} %constant.132.clone.spread_ref, f32[192,192]{1,0:T(8,128)} %and_select_fusion.mask_ref), custom_call_target="tpu_custom_call" | custom-call | tf_op jit(solution)/shard_map/window_probs/pallas_call | solution.py:369
  78.1 0.0 all-to-all-done.2.recv_ref
  78.1 0.8 copy-done.12
  78.9 8.7 %score_grads.1 = (bf16[6,192,128]{2,1,0:T(8,128)(2,1)}, bf16[16,56,128]{2,1,0:T(8,128)(2,1)}) custom-call(bf16[8,64,512]{2,1,0:T(8,128)(2,1)} %copy-done.12, bf16[512,384]{1,0:T(8,128)(2,1)} %constant.135.clone.shuffle_ref.order_ref, f32[4,64,768]{2,1,0:T(8,128)} %copy-done.5, f32[64,128]{1,0:T(8,128)} %copy-done.11, f32[4,1,768]{2,1,0:T(1,128)} %bitcast.40, ...), custom_call_target="tpu_custom_call" | custom-call | tf_op jit(solution)/shard_map/score_grads/pallas_call | solution.py:419
  87.6 7.4 %all-to-all-start.3 = ((bf16[16,56,128]{2,1,0:T(8,128)(2,1)}), bf16[16,56,128]{2,1,0:T(8,128)(2,1)S(1)}, u32[]{:S(2)}, u32[]{:S(2)}) async-start(bf16[16,56,128]{2,1,0:T(8,128)(2,1)} %get-tuple-element.26), calls=%async_computation.3 | async-start | bytes 458752 | tf_op jit(solution)/shard_map/all_to_all | solution.py:490
  95.0 6.3 %window_grads.1 = bf16[3,192,768]{2,1,0:T(8,128)(2,1)} custom-call(bf16[4,2,6,16,768]{4,3,2,1,0:T(8,128)(2,1)} %copy-done, bf16[4,2,4,16,768]{4,3,2,1,0:T(8,128)(2,1)} %copy-done.1, bf16[6,192,128]{2,1,0:T(8,128)(2,1)} %get-tuple-element.27.o_ref, bf16[6,768,192]{2,1,0:T(8,128)(2,1)} %window_probs.1.p_ref), custom_call_target="tpu_custom_call" | custom-call | tf_op jit(solution)/shard_map/window_grads/pallas_call | solution.py:464
  101.3 1.2 fusion.15
  102.5 0.3 copy.56
  102.8 1.9 %collective-permute-start.6 = (bf16[3,2,3,12,768]{4,1,3,2,0:T(2,128)(2,1)S(1)}, bf16[3,2,3,12,768]{4,1,3,2,0:T(2,128)(2,1)S(1)}, u32[]{:S(2)}, u32[]{:S(2)}) collective-permute-start(bf16[3,2,3,12,768]{4,1,3,2,0:T(2,128)(2,1)S(1)} %copy.56), channel_id=1, source_target_pairs={{0,1},{1,2},{2,3},{3,0},{4,5},{5,6},{6,7},{7,4},{8,9},{9,10},{10,1... | collective-permute-start | bytes 995336 | tf_op jit(solution)/shard_map/ppermute | solution.py:482
  104.8 0.7 broadcast_in_dim.42
  105.5 6.9 %all-to-all-start.4 = ((bf16[8,56,128]{2,1,0:T(8,128)(2,1)}), bf16[8,56,128]{2,1,0:T(8,128)(2,1)S(1)}, u32[]{:S(2)}, u32[]{:S(2)}) async-start(bf16[8,56,128]{2,1,0:T(8,128)(2,1)} %broadcast_in_dim.42), calls=%async_computation.4 | async-start | bytes 229376 | tf_op jit(solution)/shard_map/all_to_all | solution.py:490
  112.4 0.3 copy.57
  112.6 0.1 collective-permute-done.6
  112.7 0.9 pad_maximum_fusion
  113.6 15.5 %all-to-all-done.4 = bf16[8,56,128]{2,1,0:T(8,128)(2,1)S(1)} async-done(((bf16[8,56,128]{2,1,0:T(8,128)(2,1)}), bf16[8,56,128]{2,1,0:T(8,128)(2,1)S(1)}, u32[]{:S(2)}, u32[]{:S(2)}) %all-to-all-start.4) | async-done | bytes 114720 | tf_op jit(solution)/shard_map/all_to_all | solution.py:490
  129.1 0.7 broadcast_in_dim.43
  129.8 5.7 %all-to-all-start.5 = ((bf16[16,56,128]{2,1,0:T(8,128)(2,1)}), bf16[16,56,128]{2,1,0:T(8,128)(2,1)S(1)}, u32[]{:S(2)}, u32[]{:S(2)}) async-start(bf16[16,56,128]{2,1,0:T(8,128)(2,1)} %broadcast_in_dim.43), calls=%async_computation.5 | async-start | bytes 458752 | tf_op jit(solution)/shard_map/all_to_all | solution.py:490
  135.6 0.5 fusion.16
  136.0 3.4 %collective-permute-start.7 = (bf16[3,2,6,6,768]{4,1,3,2,0:T(2,128)(2,1)S(1)}, bf16[3,2,6,6,768]{4,1,3,2,0:T(2,128)(2,1)S(1)}, u32[]{:S(2)}, u32[]{:S(2)}) collective-permute-start(bf16[3,2,6,6,768]{4,1,3,2,0:T(2,128)(2,1)S(1)} %get-tuple-element.35), channel_id=1, source_target_pairs={{0,4},{4,8},{8,12},{12,16},{16,20},{20,24},{24,28},{28,32},{32,36}... | collective-permute-start | bytes 995336 | tf_op jit(solution)/shard_map/ppermute | solution.py:482
  139.4 11.9 %collective-permute-done.7 = bf16[3,2,6,6,768]{4,1,3,2,0:T(2,128)(2,1)S(1)} collective-permute-done((bf16[3,2,6,6,768]{4,1,3,2,0:T(2,128)(2,1)S(1)}, bf16[3,2,6,6,768]{4,1,3,2,0:T(2,128)(2,1)S(1)}, u32[]{:S(2)}, u32[]{:S(2)}) %collective-permute-start.7) | collective-permute-done | bytes 331808 | tf_op jit(solution)/shard_map/ppermute | solution.py:482
  151.3 1.6 %fusion.2 = (bf16[2,6,12,768]{3,0,2,1:T(2,128)(2,1)}, bf16[2,6,12,768]{3,0,2,1:T(2,128)(2,1)}, bf16[2,6,12,768]{3,0,2,1:T(2,128)(2,1)}) fusion(bf16[3,2,6,6,768]{4,1,3,2,0:T(2,128)(2,1)S(1)} %get-tuple-element.36, bf16[3,2,6,6,768]{4,1,3,2,0:T(2,128)(2,1)S(1)} %collective-permute-done.7), kind=kLoop, calls=%fused_computation.12 | loop fusion | flops 331776 | bytes 1327104 | tf_op jit(solution)/shard_map/squeeze | solution.py:566
  153.0 1.2 close_table.1
  (40 shorter events, 0.3 us)
Async XLA Ops:
  0.6 0.9 copy-start.10
  1.5 19.5 %copy-start.13 = (bf16[2,6,12,768]{3,0,2,1:T(2,128)(2,1)S(1)}, bf16[2,6,12,768]{3,0,2,1:T(2,128)(2,1)}, u32[]{:S(2)}) copy-start(bf16[2,6,12,768]{3,0,2,1:T(2,128)(2,1)} %param.20) | copy-start | bytes 663556
  1.5 19.6 %copy-start.14 = (bf16[2,6,12,768]{3,0,2,1:T(2,128)(2,1)S(1)}, bf16[2,6,12,768]{3,0,2,1:T(2,128)(2,1)}, u32[]{:S(2)}) copy-start(bf16[2,6,12,768]{3,0,2,1:T(2,128)(2,1)} %param.21) | copy-start | bytes 663556
  1.5 19.9 %copy-start.15 = (bf16[2,6,12,768]{3,0,2,1:T(2,128)(2,1)S(1)}, bf16[2,6,12,768]{3,0,2,1:T(2,128)(2,1)}, u32[]{:S(2)}) copy-start(bf16[2,6,12,768]{3,0,2,1:T(2,128)(2,1)} %param.22) | copy-start | bytes 663556
  1.5 19.9 %copy-start.16 = (bf16[2,6,12,768]{3,0,2,1:T(2,128)(2,1)S(1)}, bf16[2,6,12,768]{3,0,2,1:T(2,128)(2,1)}, u32[]{:S(2)}) copy-start(bf16[2,6,12,768]{3,0,2,1:T(2,128)(2,1)} %param.16) | copy-start | bytes 663556
  3.4 18.5 %collective-permute-start = (bf16[2,3,3,1536]{3,0,2,1:T(2,128)(2,1)S(1)}, bf16[2,3,3,1536]{3,0,2,1:T(2,128)(2,1)S(1)}, u32[]{:S(2)}, u32[]{:S(2)}) collective-permute-start(bf16[2,3,3,1536]{3,0,2,1:T(2,128)(2,1)S(1)} %get-tuple-element.46), channel_id=1, source_target_pairs={{0,508},{4,0},{8,4},{12,8},{16,12},{20,16},{24,20},{28,24},{32,28}... | collective-permute-start | bytes 165896 | tf_op jit(solution)/shard_map/ppermute | solution.py:482
  17.5 22.8 %all-to-all-start = ((bf16[16,24,384]{2,1,0:T(8,128)(2,1)}), bf16[16,24,384]{2,1,0:T(8,128)(2,1)S(1)}, u32[]{:S(2)}, u32[]{:S(2)}) async-start(bf16[16,24,384]{2,1,0:T(8,128)(2,1)} %pack_weight.1), calls=%async_computation | async-start | bytes 589824 | tf_op jit(solution)/shard_map/all_to_all | solution.py:490
  22.0 11.2 %collective-permute-start.1 = (bf16[48,1536]{1,0:T(8,128)(2,1)S(1)}, bf16[48,1536]{1,0:T(8,128)(2,1)S(1)}, u32[]{:S(2)}, u32[]{:S(2)}) collective-permute-start(bf16[48,1536]{1,0:T(8,128)(2,1)S(1)} %bitcast.32), channel_id=1, source_target_pairs={{0,2},{1,3},{2,0},{3,1},{4,6},{5,7},{6,4},{7,5},{8,10},{9,11},{10,... | collective-permute-start | bytes 442376 | tf_op jit(solution)/shard_map/ppermute | solution.py:486
  26.3 21.3 %collective-permute-start.4 = (bf16[4,2,6,6,768]{4,0,3,2,1:T(4,128)(2,1)S(1)}, bf16[4,2,6,6,768]{4,0,3,2,1:T(4,128)(2,1)S(1)}, u32[]{:S(2)}, u32[]{:S(2)}) collective-permute-start(bf16[4,2,6,6,768]{4,0,3,2,1:T(4,128)(2,1)S(1)} %copy.48), channel_id=1, source_target_pairs={{0,508},{4,0},{8,4},{12,8},{16,12},{20,16},{24,20},{28,24},{32,28}... | collective-permute-start | bytes 1327112 | tf_op jit(solution)/shard_map/ppermute | solution.py:482
  34.0 13.8 %collective-permute-start.2 = (bf16[96,1536]{1,0:T(8,128)(2,1)}, bf16[96,1536]{1,0:T(8,128)(2,1)}, u32[]{:S(2)}, u32[]{:S(2)}) collective-permute-start(bf16[96,1536]{1,0:T(8,128)(2,1)} %pad_maximum_fusion.3), channel_id=1, source_target_pairs={{0,256},{4,260},{8,264},{12,268},{16,272},{20,276},{24,280},{28,28... | collective-permute-start | bytes 884744 | tf_op jit(solution)/shard_map/ppermute | solution.py:486
  41.4 4.9 %copy-start.7 = (f32[1,24,3312]{2,1,0:T(8,128)S(1)}, f32[1,24,3312]{2,1,0:T(8,128)}, u32[]{:S(2)}) copy-start(f32[1,24,3312]{2,1,0:T(8,128)} %table_ref.1) | copy-start | bytes 953860
  41.4 4.9 %copy-start.8 = (bf16[2,138,384]{2,1,0:T(8,128)(2,1)S(1)}, bf16[2,138,384]{2,1,0:T(8,128)(2,1)}, u32[]{:S(2)}) copy-start(bf16[2,138,384]{2,1,0:T(8,128)(2,1)} %constant.136.clone.open_ref) | copy-start | bytes 635908
  41.4 16.4 %all-to-all-start.1 = ((bf16[4,384,384]{2,1,0:T(8,128)(2,1)}), bf16[4,384,384]{2,1,0:T(8,128)(2,1)S(1)}, u32[]{:S(2)}, u32[]{:S(2)}) async-start(bf16[4,384,384]{2,1,0:T(8,128)(2,1)} %broadcast_in_dim.38), calls=%async_computation.1 | async-start | bytes 2359296 | tf_op jit(solution)/shard_map/all_to_all | solution.py:490
  46.9 0.8 copy-start.3
  49.6 8.2 %collective-permute-start.3 = (bf16[192,1536]{1,0:T(8,128)(2,1)}, bf16[192,1536]{1,0:T(8,128)(2,1)}, u32[]{:S(2)}, u32[]{:S(2)}) collective-permute-start(bf16[192,1536]{1,0:T(8,128)(2,1)} %pad_maximum_fusion.1.near_ref), channel_id=1, source_target_pairs={{0,1},{1,0},{2,3},{3,2},{4,5},{5,4},{6,7},{7,6},{8,9},{9,8},{10,11... | collective-permute-start | bytes 1769480 | tf_op jit(solution)/shard_map/ppermute | solution.py:486
  52.0 15.6 %copy-start = (bf16[4,2,6,16,768]{4,3,2,1,0:T(8,128)(2,1)}, bf16[4,2,6,16,768]{4,3,2,1,0:T(8,128)(2,1)S(1)}, u32[]{:S(2)}) copy-start(bf16[4,2,6,16,768]{4,3,2,1,0:T(8,128)(2,1)S(1)} %maximum_maximum_fusion.a_ref.b_ref.north_ref) | copy-start | bytes 3538948
  52.1 5.8 %copy-start.4 = (bf16[512,384]{1,0:T(8,128)(2,1)S(1)}, bf16[512,384]{1,0:T(8,128)(2,1)}, u32[]{:S(2)}) copy-start(bf16[512,384]{1,0:T(8,128)(2,1)} %constant.135.clone.shuffle_ref.order_ref) | copy-start | bytes 1179652
  53.0 14.6 %collective-permute-start.5 = (bf16[4,2,4,16,768]{4,3,2,1,0:T(8,128)(2,1)}, bf16[4,2,4,16,768]{4,3,2,1,0:T(8,128)(2,1)S(1)}, u32[]{:S(2)}, u32[]{:S(2)}) collective-permute-start(bf16[4,2,4,16,768]{4,3,2,1,0:T(8,128)(2,1)} %slice.75), channel_id=1, source_target_pairs={{0,3},{1,0},{2,1},{3,2},{4,7},{5,4},{6,5},{7,6},{8,11},{9,8},{10,9... | collective-permute-start | bytes 2359304 | tf_op jit(solution)/shard_map/ppermute | solution.py:482
  61.3 0.8 copy-start.2
  62.1 16.0 %all-to-all-start.2 = ((bf16[8,64,512]{2,1,0:T(8,128)(2,1)}), bf16[8,64,512]{2,1,0:T(8,128)(2,1)S(1)}, u32[]{:S(2)}, u32[]{:S(2)}) async-start(bf16[8,64,512]{2,1,0:T(8,128)(2,1)} %copy-done.2), calls=%async_computation.2 | async-start | bytes 1048576 | tf_op jit(solution)/shard_map/all_to_all | solution.py:490
  67.6 0.9 copy-start.9
  68.5 0.9 copy-start.1
  69.4 0.9 copy-start.5
  70.3 0.6 copy-start.11
  78.1 0.8 copy-start.12
  87.6 17.1 %all-to-all-start.3 = ((bf16[16,56,128]{2,1,0:T(8,128)(2,1)}), bf16[16,56,128]{2,1,0:T(8,128)(2,1)S(1)}, u32[]{:S(2)}, u32[]{:S(2)}) async-start(bf16[16,56,128]{2,1,0:T(8,128)(2,1)} %get-tuple-element.26), calls=%async_computation.3 | async-start | bytes 458752 | tf_op jit(solution)/shard_map/all_to_all | solution.py:490
  102.8 9.9 %collective-permute-start.6 = (bf16[3,2,3,12,768]{4,1,3,2,0:T(2,128)(2,1)S(1)}, bf16[3,2,3,12,768]{4,1,3,2,0:T(2,128)(2,1)S(1)}, u32[]{:S(2)}, u32[]{:S(2)}) collective-permute-start(bf16[3,2,3,12,768]{4,1,3,2,0:T(2,128)(2,1)S(1)} %copy.56), channel_id=1, source_target_pairs={{0,1},{1,2},{2,3},{3,0},{4,5},{5,6},{6,7},{7,4},{8,9},{9,10},{10,1... | collective-permute-start | bytes 995336 | tf_op jit(solution)/shard_map/ppermute | solution.py:482
  105.5 23.6 %all-to-all-start.4 = ((bf16[8,56,128]{2,1,0:T(8,128)(2,1)}), bf16[8,56,128]{2,1,0:T(8,128)(2,1)S(1)}, u32[]{:S(2)}, u32[]{:S(2)}) async-start(bf16[8,56,128]{2,1,0:T(8,128)(2,1)} %broadcast_in_dim.42), calls=%async_computation.4 | async-start | bytes 229376 | tf_op jit(solution)/shard_map/all_to_all | solution.py:490
  129.8 23.1 %all-to-all-start.5 = ((bf16[16,56,128]{2,1,0:T(8,128)(2,1)}), bf16[16,56,128]{2,1,0:T(8,128)(2,1)S(1)}, u32[]{:S(2)}, u32[]{:S(2)}) async-start(bf16[16,56,128]{2,1,0:T(8,128)(2,1)} %broadcast_in_dim.43), calls=%async_computation.5 | async-start | bytes 458752 | tf_op jit(solution)/shard_map/all_to_all | solution.py:490
  135.5 17.4 %copy-start.6 = (bf16[384,512]{1,0:T(8,128)(2,1)S(1)}, bf16[384,512]{1,0:T(8,128)(2,1)}, u32[]{:S(2)}) copy-start(bf16[384,512]{1,0:T(8,128)(2,1)} %constant.137.clone.close_ref) | copy-start | bytes 1179652
  136.0 15.3 %collective-permute-start.7 = (bf16[3,2,6,6,768]{4,1,3,2,0:T(2,128)(2,1)S(1)}, bf16[3,2,6,6,768]{4,1,3,2,0:T(2,128)(2,1)S(1)}, u32[]{:S(2)}, u32[]{:S(2)}) collective-permute-start(bf16[3,2,6,6,768]{4,1,3,2,0:T(2,128)(2,1)S(1)} %get-tuple-element.35), channel_id=1, source_target_pairs={{0,4},{4,8},{8,12},{12,16},{16,20},{20,24},{24,28},{28,32},{32,36}... | collective-permute-start | bytes 995336 | tf_op jit(solution)/shard_map/ppermute | solution.py:482

commit v8 on v7

--- a/solution.py
+++ b/solution.py
@@ -541,7 +541,7 @@
     parts = merge_product(spots, near, far, weight, shuffle)
     recv = swap(parts, ("lon", "lat"), x_lat_groups)
 
-    table, quarter, _ = lax.optimization_barrier((table, quarter, parts))
+    south, _ = lax.optimization_barrier((south, parts))
     probs = window_probs(across, south, table, spread, mask)
     normed, inverse = normalise(across, south, quarter)
 
@@ -553,14 +553,12 @@
     table_part = jnp.sum(table_part, axis=0).astype(jnp.bfloat16)
     grads = window_grads(across, south, o_win, probs)
     grid = grads.reshape(3, 2, 6, PAD, 768)[:, :, :, :12]
-    southern = from_behind(grid[:, :, 3:], "lat", 1)
-    fixed = jnp.concatenate([southern, grid[:, :, :3]], axis=2)
+    western = from_behind(grid[:, :, :, 6:], "lon", 1)
+    fixed = jnp.concatenate([western, grid[:, :, :, :6]], axis=3)
+    southern = from_behind(fixed[:, :, 3:], "lat", 1)
+    finished = jnp.concatenate([southern, fixed[:, :, :3]], axis=2)
 
     table_part = share(table_part, NZ // 2, "lon", far_groups)
-    table_part, fixed = lax.optimization_barrier((table_part, fixed))
-    western = from_behind(fixed[:, :, :, 6:], "lon", 1)
-    finished = jnp.concatenate([western, fixed[:, :, :, :6]], axis=3)
-
     table_part = jnp.sum(table_part.astype(jnp.float32), axis=0).astype(jnp.bfloat16)
     table_grad = close_table(share(table_part, 16, "lon", near_groups), close)
     return (finished[0], finished[1], finished[2], table_grad)

time: 156 us -> 151 us (0.968)
  waiting for transfers between devices: 30.5 us -> 26.6 us
    all_to_all x6, waiting for transfers between devices: 18.4 us -> 13.4 us  [swap(): lax.all_to_all(shard, axis, 0, 0, tiled=True, axis_index_groups=groups)]
where the time goes in v8:
time: 151 us; the launch traced here: 150 us
  starting transfers between devices  72.3 us (48%)
  Pallas kernels  28.9 us (19%)
  waiting for transfers between devices  26.6 us (18%)
  local copies, waits for them, and re-layouts  14.2 us (9%)
  other arithmetic  6.57 us (4%)
    all_to_all x6, starting transfers between devices, swap(): lax.all_to_all(shard, axis, 0, 0, tiled=True, axis_index_groups=groups)  33.4 us
    ppermute x5, starting transfers between devices, from_behind(): lax.ppermute(shard, axis, [(i, (i + by) % size) for i in range(size)])  29.7 us
    all_to_all x6, waiting for transfers between devices, swap(): lax.all_to_all(shard, axis, 0, 0, tiled=True, axis_index_groups=groups)  13.4 us
    ppermute x5, waiting for transfers between devices, from_behind(): lax.ppermute(shard, axis, [(i, (i + by) % size) for i in range(size)])  13.2 us
    ppermute x3, starting transfers between devices, partner(): lax.ppermute(shard, axis, [(i, i ^ bit) for i in range(lax.axis_size(axis...  9.21 us
    pallas_call x1, Pallas kernels, score_grads(): pl.pallas_call(scores_kernel, grid=(STEPS,), in_specs=[whole_spec((8, 64,...  8.69 us
    pallas_call x1, Pallas kernels, window_probs(): pl.pallas_call(probs_kernel, grid=(STEPS,), in_specs=[north_spec(0, 2), s...  7.17 us
    unnamed x40, local copies, waits for them, and re-layouts  6.62 us
  transfers between devices with their start and end apart: 14, of which 5 were waited for; matrix products, arithmetic and copies ran while one was open for 9% of the time, Pallas kernels for 12%

profile of v8, /device:TPU:6, one launch (start us, length us, event | category | flops | bytes accessed | tf_op | source)
XLA Modules:
  0.0 149.7 jit_solution(16169626609515918011)
XLA Ops:
  0.6 0.9 copy-done.10
  1.5 0.9 pack_weight.1
  2.4 0.9 fusion.21
  3.4 14.1 %collective-permute-start.2 = (bf16[2,3,3,1536]{3,0,2,1:T(2,128)(2,1)S(1)}, bf16[2,3,3,1536]{3,0,2,1:T(2,128)(2,1)S(1)}, u32[]{:S(2)}, u32[]{:S(2)}) collective-permute-start(bf16[2,3,3,1536]{3,0,2,1:T(2,128)(2,1)S(1)} %get-tuple-element.40), channel_id=1, source_target_pairs={{0,508},{4,0},{8,4},{12,8},{16,12},{20,16},{24,20},{28,24},{32,28}... | collective-permute-start | bytes 165896 | tf_op jit(solution)/shard_map/ppermute | solution.py:482
  17.5 3.6 %all-to-all-start = ((bf16[16,24,384]{2,1,0:T(8,128)(2,1)}), bf16[16,24,384]{2,1,0:T(8,128)(2,1)S(1)}, u32[]{:S(2)}, u32[]{:S(2)}) async-start(bf16[16,24,384]{2,1,0:T(8,128)(2,1)} %pack_weight.1), calls=%async_computation | async-start | bytes 589824 | tf_op jit(solution)/shard_map/all_to_all | solution.py:490
  21.1 0.3 fusion.17
  21.4 0.3 fusion.19
  21.7 0.1 pad.9.clone
  21.8 0.2 maximum_maximum_fusion.1
  22.0 3.3 %collective-permute-start.3 = (bf16[48,1536]{1,0:T(8,128)(2,1)S(1)}, bf16[48,1536]{1,0:T(8,128)(2,1)S(1)}, u32[]{:S(2)}, u32[]{:S(2)}) collective-permute-start(bf16[48,1536]{1,0:T(8,128)(2,1)S(1)} %bitcast.32), channel_id=1, source_target_pairs={{0,2},{1,3},{2,0},{3,1},{4,6},{5,7},{6,4},{7,5},{8,10},{9,11},{10,... | collective-permute-start | bytes 442376 | tf_op jit(solution)/shard_map/ppermute | solution.py:486
  25.4 0.8 pad_maximum_fusion.1
  26.2 0.2 copy.56
  26.3 6.9 %collective-permute-start = (bf16[4,2,6,6,768]{4,0,3,2,1:T(4,128)(2,1)S(1)}, bf16[4,2,6,6,768]{4,0,3,2,1:T(4,128)(2,1)S(1)}, u32[]{:S(2)}, u32[]{:S(2)}) collective-permute-start(bf16[4,2,6,6,768]{4,0,3,2,1:T(4,128)(2,1)S(1)} %copy.56), channel_id=1, source_target_pairs={{0,508},{4,0},{8,4},{12,8},{16,12},{20,16},{24,20},{28,24},{32,28}... | collective-permute-start | bytes 1327112 | tf_op jit(solution)/shard_map/ppermute | solution.py:482
  33.2 0.7 pad_maximum_fusion.2
  34.0 4.0 %collective-permute-start.4 = (bf16[96,1536]{1,0:T(8,128)(2,1)}, bf16[96,1536]{1,0:T(8,128)(2,1)}, u32[]{:S(2)}, u32[]{:S(2)}) collective-permute-start(bf16[96,1536]{1,0:T(8,128)(2,1)} %pad_maximum_fusion.2), channel_id=1, source_target_pairs={{0,256},{4,260},{8,264},{12,268},{16,272},{20,276},{24,280},{28,28... | collective-permute-start | bytes 884744 | tf_op jit(solution)/shard_map/ppermute | solution.py:486
  38.0 2.3 %all-to-all-done = bf16[16,24,384]{2,1,0:T(8,128)(2,1)S(1)} async-done(((bf16[16,24,384]{2,1,0:T(8,128)(2,1)}), bf16[16,24,384]{2,1,0:T(8,128)(2,1)S(1)}, u32[]{:S(2)}, u32[]{:S(2)}) %all-to-all-start) | async-done | bytes 294944 | tf_op jit(solution)/shard_map/all_to_all | solution.py:490
  40.3 1.1 broadcast_in_dim.39
  41.4 4.6 %all-to-all-start.1 = ((bf16[4,384,384]{2,1,0:T(8,128)(2,1)}), bf16[4,384,384]{2,1,0:T(8,128)(2,1)S(1)}, u32[]{:S(2)}, u32[]{:S(2)}) async-start(bf16[4,384,384]{2,1,0:T(8,128)(2,1)} %broadcast_in_dim.39), calls=%async_computation.1 | async-start | bytes 2359296 | tf_op jit(solution)/shard_map/all_to_all | solution.py:490
  46.2 0.1 pad.15.clone
  46.3 0.6 open_table.1.table_ref
  46.9 0.8 copy-done.3
  47.7 0.0 collective-permute-done
  47.7 0.1 copy.57
  47.8 1.8 %pad_maximum_fusion.near_ref = bf16[192,1536]{1,0:T(8,128)(2,1)} fusion(bf16[96,1536]{1,0:T(8,128)(2,1)} %collective-permute-done.4, bf16[48,1536]{1,0:T(8,128)(2,1)S(1)} %collective-permute-done.3, bf16[48,1536]{1,0:T(8,128)(2,1)S(1)} %bitcast.34), kind=kLoop, calls=%fused_computation.1 | loop fusion | flops 1769472 | bytes 1179648 | tf_op jit(solution)/shard_map/concatenate | solution.py:516
  49.6 1.9 %collective-permute-start.5 = (bf16[192,1536]{1,0:T(8,128)(2,1)}, bf16[192,1536]{1,0:T(8,128)(2,1)}, u32[]{:S(2)}, u32[]{:S(2)}) collective-permute-start(bf16[192,1536]{1,0:T(8,128)(2,1)} %pad_maximum_fusion.near_ref), channel_id=1, source_target_pairs={{0,1},{1,0},{2,3},{3,2},{4,5},{5,4},{6,7},{7,6},{8,9},{9,8},{10,11... | collective-permute-start | bytes 1769480 | tf_op jit(solution)/shard_map/ppermute | solution.py:486
  51.5 0.5 maximum_maximum_fusion.a_ref.b_ref.north_ref
  52.1 0.0 copy-start.4
  52.1 1.0 slice.75
  53.0 3.4 %collective-permute-start.1 = (bf16[4,2,4,16,768]{4,3,2,1,0:T(8,128)(2,1)}, bf16[4,2,4,16,768]{4,3,2,1,0:T(8,128)(2,1)S(1)}, u32[]{:S(2)}, u32[]{:S(2)}) collective-permute-start(bf16[4,2,4,16,768]{4,3,2,1,0:T(8,128)(2,1)} %slice.75), channel_id=1, source_target_pairs={{0,3},{1,0},{2,1},{3,2},{4,7},{5,4},{6,5},{7,6},{8,11},{9,8},{10,9... | collective-permute-start | bytes 2359304 | tf_op jit(solution)/shard_map/ppermute | solution.py:482
  56.5 0.8 and_select_fusion.mask_ref
  57.2 0.6 all-to-all-done.1.w_ref
  57.8 3.5 %merge_product.1 = bf16[8,64,512]{2,1,0:T(8,128)(2,1)S(1)} custom-call(s32[8]{0:T(128)S(1)} %fusion.14.spot_ref, bf16[192,1536]{1,0:T(8,128)(2,1)} %pad_maximum_fusion.near_ref, bf16[192,1536]{1,0:T(8,128)(2,1)} %collective-permute-done.5.far_ref, bf16[4,384,384]{2,1,0:T(8,128)(2,1)S(1)} %all-to-all-done.1.w_ref, bf16[512,384]{1,0:T(8,128)(2,1)S(1)} %copy-done.4), custom_call_target="tpu_custom_call" | custom-call | tf_op jit(solution)/shard_map/merge_product/pallas_call | solution.py:407
  61.3 0.8 copy-done.2
  62.1 5.5 %all-to-all-start.2 = ((bf16[8,64,512]{2,1,0:T(8,128)(2,1)}), bf16[8,64,512]{2,1,0:T(8,128)(2,1)S(1)}, u32[]{:S(2)}, u32[]{:S(2)}) async-start(bf16[8,64,512]{2,1,0:T(8,128)(2,1)} %copy-done.2), calls=%async_computation.2 | async-start | bytes 1048576 | tf_op jit(solution)/shard_map/all_to_all | solution.py:490
  67.6 0.0 copy-start.9
  67.6 0.9 copy-done.9
  68.5 0.5 normalise.1
  69.0 0.4 copy-done.1
  69.4 0.9 copy-done.5
  70.3 0.6 copy-done.11
  70.9 7.2 %window_probs.1.p_ref = bf16[6,768,192]{2,1,0:T(8,128)(2,1)} custom-call(bf16[4,2,6,16,768]{4,3,2,1,0:T(8,128)(2,1)} %copy-done, bf16[4,2,4,16,768]{4,3,2,1,0:T(8,128)(2,1)} %copy-done.1, f32[6,48,384]{2,1,0:T(8,128)} %copy-done.3, bf16[384,192]{1,0:T(8,128)(2,1)} %constant.132.clone.spread_ref, f32[192,192]{1,0:T(8,128)} %and_select_fusion.mask_ref), custom_call_target="tpu_custom_call" | custom-call | tf_op jit(solution)/shard_map/window_probs/pallas_call | solution.py:369
  78.1 0.0 all-to-all-done.2.recv_ref
  78.1 0.8 copy-done.12
  78.9 8.7 %score_grads.1 = (bf16[6,192,128]{2,1,0:T(8,128)(2,1)}, bf16[16,56,128]{2,1,0:T(8,128)(2,1)}) custom-call(bf16[8,64,512]{2,1,0:T(8,128)(2,1)} %copy-done.12, bf16[512,384]{1,0:T(8,128)(2,1)} %constant.135.clone.shuffle_ref.order_ref, f32[4,64,768]{2,1,0:T(8,128)} %copy-done.5, f32[64,128]{1,0:T(8,128)} %copy-done.11, f32[4,1,768]{2,1,0:T(1,128)} %bitcast.40, ...), custom_call_target="tpu_custom_call" | custom-call | tf_op jit(solution)/shard_map/score_grads/pallas_call | solution.py:419
  87.6 7.4 %all-to-all-start.3 = ((bf16[16,56,128]{2,1,0:T(8,128)(2,1)}), bf16[16,56,128]{2,1,0:T(8,128)(2,1)S(1)}, u32[]{:S(2)}, u32[]{:S(2)}) async-start(bf16[16,56,128]{2,1,0:T(8,128)(2,1)} %get-tuple-element.23), calls=%async_computation.3 | async-start | bytes 458752 | tf_op jit(solution)/shard_map/all_to_all | solution.py:490
  95.0 6.3 %window_grads.1 = bf16[3,192,768]{2,1,0:T(8,128)(2,1)} custom-call(bf16[4,2,6,16,768]{4,3,2,1,0:T(8,128)(2,1)} %copy-done, bf16[4,2,4,16,768]{4,3,2,1,0:T(8,128)(2,1)} %copy-done.1, bf16[6,192,128]{2,1,0:T(8,128)(2,1)} %get-tuple-element.22.o_ref, bf16[6,768,192]{2,1,0:T(8,128)(2,1)} %window_probs.1.p_ref), custom_call_target="tpu_custom_call" | custom-call | tf_op jit(solution)/shard_map/window_grads/pallas_call | solution.py:464
  101.3 1.5 fusion.15
  102.8 0.3 copy.65
  103.1 3.4 %collective-permute-start.6 = (bf16[3,2,6,6,768]{4,1,3,2,0:T(2,128)(2,1)S(1)}, bf16[3,2,6,6,768]{4,1,3,2,0:T(2,128)(2,1)S(1)}, u32[]{:S(2)}, u32[]{:S(2)}) collective-permute-start(bf16[3,2,6,6,768]{4,1,3,2,0:T(2,128)(2,1)S(1)} %copy.65), channel_id=1, source_target_pairs={{0,4},{4,8},{8,12},{12,16},{16,20},{20,24},{24,28},{28,32},{32,36}... | collective-permute-start | bytes 995336 | tf_op jit(solution)/shard_map/ppermute | solution.py:482
  106.5 0.7 broadcast_in_dim.42
  107.2 6.6 %all-to-all-start.4 = ((bf16[8,56,128]{2,1,0:T(8,128)(2,1)}), bf16[8,56,128]{2,1,0:T(8,128)(2,1)S(1)}, u32[]{:S(2)}, u32[]{:S(2)}) async-start(bf16[8,56,128]{2,1,0:T(8,128)(2,1)} %broadcast_in_dim.42), calls=%async_computation.4 | async-start | bytes 229376 | tf_op jit(solution)/shard_map/all_to_all | solution.py:490
  113.7 5.2 %collective-permute-done.6 = bf16[3,2,6,6,768]{4,1,3,2,0:T(2,128)(2,1)S(1)} collective-permute-done((bf16[3,2,6,6,768]{4,1,3,2,0:T(2,128)(2,1)S(1)}, bf16[3,2,6,6,768]{4,1,3,2,0:T(2,128)(2,1)S(1)}, u32[]{:S(2)}, u32[]{:S(2)}) %collective-permute-start.6) | collective-permute-done | bytes 331808 | tf_op jit(solution)/shard_map/ppermute | solution.py:482
  118.9 0.2 constant_dynamic-update-slice_fusion
  119.2 10.5 %all-to-all-done.4 = bf16[8,56,128]{2,1,0:T(8,128)(2,1)S(1)} async-done(((bf16[8,56,128]{2,1,0:T(8,128)(2,1)}), bf16[8,56,128]{2,1,0:T(8,128)(2,1)S(1)}, u32[]{:S(2)}, u32[]{:S(2)}) %all-to-all-start.4) | async-done | bytes 114720 | tf_op jit(solution)/shard_map/all_to_all | solution.py:490
  129.7 0.7 broadcast_in_dim.43
  130.4 5.7 %all-to-all-start.5 = ((bf16[16,56,128]{2,1,0:T(8,128)(2,1)}), bf16[16,56,128]{2,1,0:T(8,128)(2,1)S(1)}, u32[]{:S(2)}, u32[]{:S(2)}) async-start(bf16[16,56,128]{2,1,0:T(8,128)(2,1)} %broadcast_in_dim.43), calls=%async_computation.5 | async-start | bytes 458752 | tf_op jit(solution)/shard_map/all_to_all | solution.py:490
  136.1 0.3 copy_dynamic-update-slice_fusion
  136.4 0.0 copy-start.6
  136.4 0.5 fusion.16
  136.9 1.9 %collective-permute-start.7 = (bf16[3,2,3,12,768]{4,1,3,2,0:T(2,128)(2,1)S(1)}, bf16[3,2,3,12,768]{4,1,3,2,0:T(2,128)(2,1)S(1)}, u32[]{:S(2)}, u32[]{:S(2)}) collective-permute-start(bf16[3,2,3,12,768]{4,1,3,2,0:T(2,128)(2,1)S(1)} %get-tuple-element.29), channel_id=1, source_target_pairs={{0,1},{1,2},{2,3},{3,0},{4,5},{5,6},{6,7},{7,4},{8,9},{9,10},{10,1... | collective-permute-start | bytes 995336 | tf_op jit(solution)/shard_map/ppermute | solution.py:482
  138.8 8.0 %collective-permute-done.7 = bf16[3,2,3,12,768]{4,1,3,2,0:T(2,128)(2,1)S(1)} collective-permute-done((bf16[3,2,3,12,768]{4,1,3,2,0:T(2,128)(2,1)S(1)}, bf16[3,2,3,12,768]{4,1,3,2,0:T(2,128)(2,1)S(1)}, u32[]{:S(2)}, u32[]{:S(2)}) %collective-permute-start.7) | collective-permute-done | bytes 331808 | tf_op jit(solution)/shard_map/ppermute | solution.py:482
  146.9 1.6 %fusion.2 = (bf16[2,6,12,768]{3,0,2,1:T(2,128)(2,1)}, bf16[2,6,12,768]{3,0,2,1:T(2,128)(2,1)}, bf16[2,6,12,768]{3,0,2,1:T(2,128)(2,1)}) fusion(bf16[3,2,3,12,768]{4,1,3,2,0:T(2,128)(2,1)S(1)} %get-tuple-element.30, bf16[3,2,3,12,768]{4,1,3,2,0:T(2,128)(2,1)S(1)} %collective-permute-done.7), kind=kLoop, calls=%fused_computation.12 | loop fusion | flops 331776 | bytes 1327104 | tf_op jit(solution)/shard_map/squeeze | solution.py:564
  148.5 0.0 all-to-all-done.5.parts_ref
  148.5 1.2 close_table.1
  (40 shorter events, 0.3 us)
Async XLA Ops:
  0.6 0.9 copy-start.10
  1.5 19.5 %copy-start.13 = (bf16[2,6,12,768]{3,0,2,1:T(2,128)(2,1)S(1)}, bf16[2,6,12,768]{3,0,2,1:T(2,128)(2,1)}, u32[]{:S(2)}) copy-start(bf16[2,6,12,768]{3,0,2,1:T(2,128)(2,1)} %param.20) | copy-start | bytes 663556
  1.5 19.6 %copy-start.14 = (bf16[2,6,12,768]{3,0,2,1:T(2,128)(2,1)S(1)}, bf16[2,6,12,768]{3,0,2,1:T(2,128)(2,1)}, u32[]{:S(2)}) copy-start(bf16[2,6,12,768]{3,0,2,1:T(2,128)(2,1)} %param.21) | copy-start | bytes 663556
  1.5 19.9 %copy-start.15 = (bf16[2,6,12,768]{3,0,2,1:T(2,128)(2,1)S(1)}, bf16[2,6,12,768]{3,0,2,1:T(2,128)(2,1)}, u32[]{:S(2)}) copy-start(bf16[2,6,12,768]{3,0,2,1:T(2,128)(2,1)} %param.22) | copy-start | bytes 663556
  1.5 19.9 %copy-start.16 = (bf16[2,6,12,768]{3,0,2,1:T(2,128)(2,1)S(1)}, bf16[2,6,12,768]{3,0,2,1:T(2,128)(2,1)}, u32[]{:S(2)}) copy-start(bf16[2,6,12,768]{3,0,2,1:T(2,128)(2,1)} %param.16) | copy-start | bytes 663556
  3.4 18.5 %collective-permute-start.2 = (bf16[2,3,3,1536]{3,0,2,1:T(2,128)(2,1)S(1)}, bf16[2,3,3,1536]{3,0,2,1:T(2,128)(2,1)S(1)}, u32[]{:S(2)}, u32[]{:S(2)}) collective-permute-start(bf16[2,3,3,1536]{3,0,2,1:T(2,128)(2,1)S(1)} %get-tuple-element.40), channel_id=1, source_target_pairs={{0,508},{4,0},{8,4},{12,8},{16,12},{20,16},{24,20},{28,24},{32,28}... | collective-permute-start | bytes 165896 | tf_op jit(solution)/shard_map/ppermute | solution.py:482
  17.5 22.8 %all-to-all-start = ((bf16[16,24,384]{2,1,0:T(8,128)(2,1)}), bf16[16,24,384]{2,1,0:T(8,128)(2,1)S(1)}, u32[]{:S(2)}, u32[]{:S(2)}) async-start(bf16[16,24,384]{2,1,0:T(8,128)(2,1)} %pack_weight.1), calls=%async_computation | async-start | bytes 589824 | tf_op jit(solution)/shard_map/all_to_all | solution.py:490
  22.0 11.2 %collective-permute-start.3 = (bf16[48,1536]{1,0:T(8,128)(2,1)S(1)}, bf16[48,1536]{1,0:T(8,128)(2,1)S(1)}, u32[]{:S(2)}, u32[]{:S(2)}) collective-permute-start(bf16[48,1536]{1,0:T(8,128)(2,1)S(1)} %bitcast.32), channel_id=1, source_target_pairs={{0,2},{1,3},{2,0},{3,1},{4,6},{5,7},{6,4},{7,5},{8,10},{9,11},{10,... | collective-permute-start | bytes 442376 | tf_op jit(solution)/shard_map/ppermute | solution.py:486
  26.3 21.3 %collective-permute-start = (bf16[4,2,6,6,768]{4,0,3,2,1:T(4,128)(2,1)S(1)}, bf16[4,2,6,6,768]{4,0,3,2,1:T(4,128)(2,1)S(1)}, u32[]{:S(2)}, u32[]{:S(2)}) collective-permute-start(bf16[4,2,6,6,768]{4,0,3,2,1:T(4,128)(2,1)S(1)} %copy.56), channel_id=1, source_target_pairs={{0,508},{4,0},{8,4},{12,8},{16,12},{20,16},{24,20},{28,24},{32,28}... | collective-permute-start | bytes 1327112 | tf_op jit(solution)/shard_map/ppermute | solution.py:482
  34.0 13.8 %collective-permute-start.4 = (bf16[96,1536]{1,0:T(8,128)(2,1)}, bf16[96,1536]{1,0:T(8,128)(2,1)}, u32[]{:S(2)}, u32[]{:S(2)}) collective-permute-start(bf16[96,1536]{1,0:T(8,128)(2,1)} %pad_maximum_fusion.2), channel_id=1, source_target_pairs={{0,256},{4,260},{8,264},{12,268},{16,272},{20,276},{24,280},{28,28... | collective-permute-start | bytes 884744 | tf_op jit(solution)/shard_map/ppermute | solution.py:486
  41.4 4.9 %copy-start.7 = (f32[1,24,3312]{2,1,0:T(8,128)S(1)}, f32[1,24,3312]{2,1,0:T(8,128)}, u32[]{:S(2)}) copy-start(f32[1,24,3312]{2,1,0:T(8,128)} %table_ref.1) | copy-start | bytes 953860
  41.4 4.9 %copy-start.8 = (bf16[2,138,384]{2,1,0:T(8,128)(2,1)S(1)}, bf16[2,138,384]{2,1,0:T(8,128)(2,1)}, u32[]{:S(2)}) copy-start(bf16[2,138,384]{2,1,0:T(8,128)(2,1)} %constant.136.clone.open_ref) | copy-start | bytes 635908
  41.4 16.4 %all-to-all-start.1 = ((bf16[4,384,384]{2,1,0:T(8,128)(2,1)}), bf16[4,384,384]{2,1,0:T(8,128)(2,1)S(1)}, u32[]{:S(2)}, u32[]{:S(2)}) async-start(bf16[4,384,384]{2,1,0:T(8,128)(2,1)} %broadcast_in_dim.39), calls=%async_computation.1 | async-start | bytes 2359296 | tf_op jit(solution)/shard_map/all_to_all | solution.py:490
  46.9 0.8 copy-start.3
  49.6 8.2 %collective-permute-start.5 = (bf16[192,1536]{1,0:T(8,128)(2,1)}, bf16[192,1536]{1,0:T(8,128)(2,1)}, u32[]{:S(2)}, u32[]{:S(2)}) collective-permute-start(bf16[192,1536]{1,0:T(8,128)(2,1)} %pad_maximum_fusion.near_ref), channel_id=1, source_target_pairs={{0,1},{1,0},{2,3},{3,2},{4,5},{5,4},{6,7},{7,6},{8,9},{9,8},{10,11... | collective-permute-start | bytes 1769480 | tf_op jit(solution)/shard_map/ppermute | solution.py:486
  52.0 15.6 %copy-start = (bf16[4,2,6,16,768]{4,3,2,1,0:T(8,128)(2,1)}, bf16[4,2,6,16,768]{4,3,2,1,0:T(8,128)(2,1)S(1)}, u32[]{:S(2)}) copy-start(bf16[4,2,6,16,768]{4,3,2,1,0:T(8,128)(2,1)S(1)} %maximum_maximum_fusion.a_ref.b_ref.north_ref) | copy-start | bytes 3538948
  52.1 5.8 %copy-start.4 = (bf16[512,384]{1,0:T(8,128)(2,1)S(1)}, bf16[512,384]{1,0:T(8,128)(2,1)}, u32[]{:S(2)}) copy-start(bf16[512,384]{1,0:T(8,128)(2,1)} %constant.135.clone.shuffle_ref.order_ref) | copy-start | bytes 1179652
  53.0 14.6 %collective-permute-start.1 = (bf16[4,2,4,16,768]{4,3,2,1,0:T(8,128)(2,1)}, bf16[4,2,4,16,768]{4,3,2,1,0:T(8,128)(2,1)S(1)}, u32[]{:S(2)}, u32[]{:S(2)}) collective-permute-start(bf16[4,2,4,16,768]{4,3,2,1,0:T(8,128)(2,1)} %slice.75), channel_id=1, source_target_pairs={{0,3},{1,0},{2,1},{3,2},{4,7},{5,4},{6,5},{7,6},{8,11},{9,8},{10,9... | collective-permute-start | bytes 2359304 | tf_op jit(solution)/shard_map/ppermute | solution.py:482
  61.3 0.8 copy-start.2
  62.1 16.0 %all-to-all-start.2 = ((bf16[8,64,512]{2,1,0:T(8,128)(2,1)}), bf16[8,64,512]{2,1,0:T(8,128)(2,1)S(1)}, u32[]{:S(2)}, u32[]{:S(2)}) async-start(bf16[8,64,512]{2,1,0:T(8,128)(2,1)} %copy-done.2), calls=%async_computation.2 | async-start | bytes 1048576 | tf_op jit(solution)/shard_map/all_to_all | solution.py:490
  67.6 0.9 copy-start.9
  68.5 0.9 copy-start.1
  69.4 0.9 copy-start.5
  70.3 0.6 copy-start.11
  78.1 0.8 copy-start.12
  87.6 18.9 %all-to-all-start.3 = ((bf16[16,56,128]{2,1,0:T(8,128)(2,1)}), bf16[16,56,128]{2,1,0:T(8,128)(2,1)S(1)}, u32[]{:S(2)}, u32[]{:S(2)}) async-start(bf16[16,56,128]{2,1,0:T(8,128)(2,1)} %get-tuple-element.23), calls=%async_computation.3 | async-start | bytes 458752 | tf_op jit(solution)/shard_map/all_to_all | solution.py:490
  103.1 15.8 %collective-permute-start.6 = (bf16[3,2,6,6,768]{4,1,3,2,0:T(2,128)(2,1)S(1)}, bf16[3,2,6,6,768]{4,1,3,2,0:T(2,128)(2,1)S(1)}, u32[]{:S(2)}, u32[]{:S(2)}) collective-permute-start(bf16[3,2,6,6,768]{4,1,3,2,0:T(2,128)(2,1)S(1)} %copy.65), channel_id=1, source_target_pairs={{0,4},{4,8},{8,12},{12,16},{16,20},{20,24},{24,28},{28,32},{32,36}... | collective-permute-start | bytes 995336 | tf_op jit(solution)/shard_map/ppermute | solution.py:482
  107.2 22.5 %all-to-all-start.4 = ((bf16[8,56,128]{2,1,0:T(8,128)(2,1)}), bf16[8,56,128]{2,1,0:T(8,128)(2,1)S(1)}, u32[]{:S(2)}, u32[]{:S(2)}) async-start(bf16[8,56,128]{2,1,0:T(8,128)(2,1)} %broadcast_in_dim.42), calls=%async_computation.4 | async-start | bytes 229376 | tf_op jit(solution)/shard_map/all_to_all | solution.py:490
  130.4 18.1 %all-to-all-start.5 = ((bf16[16,56,128]{2,1,0:T(8,128)(2,1)}), bf16[16,56,128]{2,1,0:T(8,128)(2,1)S(1)}, u32[]{:S(2)}, u32[]{:S(2)}) async-start(bf16[16,56,128]{2,1,0:T(8,128)(2,1)} %broadcast_in_dim.43), calls=%async_computation.5 | async-start | bytes 458752 | tf_op jit(solution)/shard_map/all_to_all | solution.py:490
  136.4 12.0 %copy-start.6 = (bf16[384,512]{1,0:T(8,128)(2,1)S(1)}, bf16[384,512]{1,0:T(8,128)(2,1)}, u32[]{:S(2)}) copy-start(bf16[384,512]{1,0:T(8,128)(2,1)} %constant.137.clone.close_ref) | copy-start | bytes 1179652
  136.9 9.9 %collective-permute-start.7 = (bf16[3,2,3,12,768]{4,1,3,2,0:T(2,128)(2,1)S(1)}, bf16[3,2,3,12,768]{4,1,3,2,0:T(2,128)(2,1)S(1)}, u32[]{:S(2)}, u32[]{:S(2)}) collective-permute-start(bf16[3,2,3,12,768]{4,1,3,2,0:T(2,128)(2,1)S(1)} %get-tuple-element.29), channel_id=1, source_target_pairs={{0,1},{1,2},{2,3},{3,0},{4,5},{5,6},{6,7},{7,4},{8,9},{9,10},{10,1... | collective-permute-start | bytes 995336 | tf_op jit(solution)/shard_map/ppermute | solution.py:482

commit v9 on v8

--- a/solution.py
+++ b/solution.py
@@ -157,7 +157,7 @@
         p_ref[group] = probs.astype(jnp.bfloat16)
 
 
-def norm_kernel(a_ref, b_ref, south_ref, quarter_ref, normed_ref, inverse_ref):
+def normalise(a_ref, b_ref, south_ref, quarter_ref):
     pieces = []
     for level in range(2):
         pieces.append(a_ref[0, level].reshape(32, 768))
@@ -172,9 +172,7 @@
         jnp.sum(squares[0] + squares[1] + squares[2] + squares[3], axis=-1, keepdims=True) / 3072
     )
     inverse = lax.rsqrt(variance + 1e-05)
-    for q in range(4):
-        normed_ref[q] = parts[q] * inverse
-    inverse_ref[...] = jnp.broadcast_to(inverse, (64, 128))
+    return [part * inverse for part in parts], inverse
 
 
 def merge_kernel(spot_ref, near_ref, far_ref, w_ref, shuffle_ref, out_ref, acc_ref):
@@ -212,8 +210,10 @@
 def scores_kernel(
     recv_ref,
     order_ref,
-    normed_ref,
-    inverse_ref,
+    y_a_ref,
+    y_b_ref,
+    y_south_ref,
+    quarter_ref,
     gain_ref,
     back_ref,
     sums_ref,
@@ -222,56 +222,47 @@
     p_ref,
     o_out_ref,
     table_ref,
-    o_ref,
-    sum_ref,
 ):
-    g = pl.program_id(0)
-
-    @pl.when(g == 0)
-    def _():
-        pieces = [
-            jnp.concatenate(
-                [recv_ref[x * LAT + l, :, y * 128 : (y + 1) * 128] for l in range(LAT)], axis=1
-            )
-            for x in range(NX)
-            for y in range(NY)
-        ]
-        d_norm = dot(jnp.concatenate(pieces, axis=0), order_ref[...])
-        hats = []
-        for q in range(4):
-            left = d_norm[(2 * q) * 64 : (2 * q + 1) * 64]
-            right = d_norm[(2 * q + 1) * 64 : (2 * q + 2) * 64]
-            hats.append(jnp.concatenate([left, right], axis=1) * gain_ref[q])
-        mean = jnp.sum(hats[0] + hats[1] + hats[2] + hats[3], axis=-1, keepdims=True) / 3072
-        cross = [hats[q] * normed_ref[q] for q in range(4)]
-        along = jnp.sum(cross[0] + cross[1] + cross[2] + cross[3], axis=-1, keepdims=True) / 3072
-        inverse = inverse_ref[:, 0:1]
-        stack = [(hats[q] - mean - normed_ref[q] * along) * inverse for q in range(4)]
-        d_out = dot(back_ref[...], jnp.concatenate(stack, axis=0).astype(jnp.bfloat16))
-        d_out = d_out.astype(jnp.bfloat16)
-        for s in range(GROUPS):
-            o_ref[s] = d_out[:, s * 128 : (s + 1) * 128]
-
-    for group in range(PER):
-        o_win = o_ref[g * PER + group]
+    pieces = [
+        jnp.concatenate(
+            [recv_ref[x * LAT + l, :, y * 128 : (y + 1) * 128] for l in range(LAT)], axis=1
+        )
+        for x in range(NX)
+        for y in range(NY)
+    ]
+    d_norm = dot(jnp.concatenate(pieces, axis=0), order_ref[...])
+    hats = []
+    for q in range(4):
+        left = d_norm[(2 * q) * 64 : (2 * q + 1) * 64]
+        right = d_norm[(2 * q + 1) * 64 : (2 * q + 2) * 64]
+        hats.append(jnp.concatenate([left, right], axis=1) * gain_ref[q])
+    mean = jnp.sum(hats[0] + hats[1] + hats[2] + hats[3], axis=-1, keepdims=True) / 3072
+    normed, inverse = normalise(y_a_ref, y_b_ref, y_south_ref, quarter_ref)
+    cross = [hats[q] * normed[q] for q in range(4)]
+    along = jnp.sum(cross[0] + cross[1] + cross[2] + cross[3], axis=-1, keepdims=True) / 3072
+    stack = [(hats[q] - mean - normed[q] * along) * inverse for q in range(4)]
+    d_out = dot(back_ref[...], jnp.concatenate(stack, axis=0).astype(jnp.bfloat16))
+    d_out = d_out.astype(jnp.bfloat16)
+
+    sums = [[], [], []]
+    for group in range(GROUPS):
+        o_win = d_out[:, group * 128 : (group + 1) * 128]
         o_out_ref[group] = o_win
         d_low = score_grad(p_ref[group], o_win, window(north_ref, south_ref, 0, group))
         spread = dot(d_low, sums_ref[...]).reshape(4 * ROWS, PAD, WIDE)
         for s in range(3):
-            lanes = slice(s * 128, (s + 1) * 128)
-            turned = pltpu.roll(spread[:, :, lanes], 0, 2, stride=1, stride_axis=1)
-            sum_ref[g * PER + group, :, lanes] = jnp.sum(turned, axis=1)
-
-    @pl.when(g == STEPS - 1)
-    def _():
-        whole = jnp.concatenate([sum_ref[s] for s in range(GROUPS)], axis=0)
-        tiles = [
-            whole[r * 8 : (r + 1) * 8, s * 128 : (s + 1) * 128] for s in range(3) for r in range(36)
-        ]
-        tiles += [jnp.zeros((8, 128), jnp.float32)] * (16 * SHARE - len(tiles))
-        for part in range(16):
-            chunk = jnp.concatenate(tiles[part * SHARE : (part + 1) * SHARE], axis=0)
-            table_ref[part] = chunk.astype(jnp.bfloat16)
+            part = spread[:, :, s * 128 : (s + 1) * 128]
+            turned = pltpu.roll(part, 0, 2, stride=1, stride_axis=1)
+            sums[s].append(jnp.sum(turned, axis=1))
+
+    tiles = []
+    for s in range(3):
+        whole = jnp.concatenate(sums[s], axis=0)
+        tiles += [whole[r * 8 : (r + 1) * 8] for r in range(36)]
+    tiles += [jnp.zeros((8, 128), jnp.float32)] * (16 * SHARE - len(tiles))
+    for part in range(16):
+        chunk = jnp.concatenate(tiles[part * SHARE : (part + 1) * SHARE], axis=0)
+        table_ref[part] = chunk.astype(jnp.bfloat16)
 
 
 def close_kernel(parts_ref, close_ref, out_ref, wide_ref):
@@ -383,26 +374,6 @@
     )(across, south, table, spread, mask)
 
 
-def normalise(across, south, quarter):
-    return pl.pallas_call(
-        norm_kernel,
-        grid=(1,),
-        in_specs=[
-            pl.BlockSpec((1, 2, 2, PAD, 768), lambda g: (3, 0, 1, 0, 0)),
-            pl.BlockSpec((1, 2, 2, PAD, 768), lambda g: (3, 0, 2, 0, 0)),
-            pl.BlockSpec((1, 2, 4, PAD, 768), lambda g: (3, 0, 0, 0, 0)),
-            whole_spec((256, 256)),
-        ],
-        out_specs=(whole_spec((4, 64, 768)), whole_spec((64, 128))),
-        out_shape=(
-            jax.ShapeDtypeStruct((4, 64, 768), jnp.float32),
-            jax.ShapeDtypeStruct((64, 128), jnp.float32),
-        ),
-        compiler_params=params,
-        name="normalise",
-    )(across, across, south, quarter)
-
-
 def merge_product(spots, near, far, weight, shuffle):
     return pl.pallas_call(
         merge_kernel,
@@ -415,37 +386,35 @@
     )(spots, near, far, weight, shuffle)
 
 
-def score_grads(recv, order, normed, inverse, gain, back, sums, across, south, probs):
+def score_grads(recv, order, quarter, gain, back, sums, across, south, probs):
     return pl.pallas_call(
         scores_kernel,
-        grid=(STEPS,),
+        grid=(1,),
         in_specs=[
             whole_spec((8, 64, 512)),
             whole_spec((512, 384)),
-            whole_spec((4, 64, 768)),
-            whole_spec((64, 128)),
+            pl.BlockSpec((1, 2, 2, PAD, 768), lambda g: (3, 0, 1, 0, 0)),
+            pl.BlockSpec((1, 2, 2, PAD, 768), lambda g: (3, 0, 2, 0, 0)),
+            pl.BlockSpec((1, 2, 4, PAD, 768), lambda g: (3, 0, 0, 0, 0)),
+            whole_spec((256, 256)),
             whole_spec((4, 1, 768)),
             whole_spec((TOK, 256)),
             whole_spec((TOK, WIDE)),
-            north_spec(2, 1),
-            south_spec(2, 1),
-            group_spec(4 * TOK, TOK),
+            pl.BlockSpec((1, 2, 3, PAD, 768), lambda g: (2, 0, 1, 0, 0)),
+            pl.BlockSpec((1, 2, 4, PAD, 768), lambda g: (2, 0, 0, 0, 0)),
+            whole_spec((GROUPS, 4 * TOK, TOK)),
         ],
         out_specs=(
-            group_spec(TOK, 128),
+            whole_spec((GROUPS, TOK, 128)),
             whole_spec((16, 8 * SHARE, 128)),
         ),
         out_shape=(
             jax.ShapeDtypeStruct((GROUPS, TOK, 128), jnp.bfloat16),
             jax.ShapeDtypeStruct((16, 8 * SHARE, 128), jnp.bfloat16),
         ),
-        scratch_shapes=[
-            pltpu.VMEM((GROUPS, TOK, 128), jnp.bfloat16),
-            pltpu.VMEM((GROUPS, 4 * ROWS, WIDE), jnp.float32),
-        ],
         compiler_params=large,
         name="score_grads",
-    )(recv, order, normed, inverse, gain, back, sums, across, south, probs)
+    )(recv, order, across, across, south, quarter, gain, back, sums, across, south, probs)
 
 
 def close_table(parts, close):
@@ -543,10 +512,10 @@
 
     south, _ = lax.optimization_barrier((south, parts))
     probs = window_probs(across, south, table, spread, mask)
-    normed, inverse = normalise(across, south, quarter)
-
+
+    gain = merge_gain.reshape(4, 1, 768)
     o_win, table_part = score_grads(
-        recv, order, normed, inverse, merge_gain.reshape(4, 1, 768), back, sums, across, south, probs
+        recv, order, quarter, gain, back, sums, across, south, probs
     )
 
     table_part = swap(table_part, "lon", near_groups).astype(jnp.float32)
@@ -555,11 +524,12 @@
     grid = grads.reshape(3, 2, 6, PAD, 768)[:, :, :, :12]
     western = from_behind(grid[:, :, :, 6:], "lon", 1)
     fixed = jnp.concatenate([western, grid[:, :, :, :6]], axis=3)
+
+    table_part = share(table_part, NZ // 2, "lon", far_groups)
+    table_part, fixed = lax.optimization_barrier((table_part, fixed))
     southern = from_behind(fixed[:, :, 3:], "lat", 1)
+    table_part = jnp.sum(table_part.astype(jnp.float32), axis=0).astype(jnp.bfloat16)
     finished = jnp.concatenate([southern, fixed[:, :, :3]], axis=2)
-
-    table_part = share(table_part, NZ // 2, "lon", far_groups)
-    table_part = jnp.sum(table_part.astype(jnp.float32), axis=0).astype(jnp.bfloat16)
     table_grad = close_table(share(table_part, 16, "lon", near_groups), close)
     return (finished[0], finished[1], finished[2], table_grad)
 

time: 151 us -> 147 us (0.974)
  local copies, waits for them, and re-layouts: 14.2 us -> 11.2 us
    unnamed x40 -> x34, local copies, waits for them, and re-layouts: 6.62 us -> 3.94 us
    pallas_call x2 -> x1, Pallas kernels: 9.21 us -> 7.88 us  [score_grads(): pl.pallas_call(scores_kernel, grid=(1,), in_specs=[whole_spec((8, 64, 512...]
where the time goes in v9:
time: 147 us; the launch traced here: 145 us
  starting transfers between devices  72.6 us (49%)
  Pallas kernels  27.7 us (19%)
  waiting for transfers between devices  25.9 us (18%)
  local copies, waits for them, and re-layouts  11.2 us (8%)
  other arithmetic  7.12 us (5%)
    all_to_all x6, starting transfers between devices, swap(): lax.all_to_all(shard, axis, 0, 0, tiled=True, axis_index_groups=groups)  33.7 us
    ppermute x5, starting transfers between devices, from_behind(): lax.ppermute(shard, axis, [(i, (i + by) % size) for i in range(size)])  29.7 us
    ppermute x5, waiting for transfers between devices, from_behind(): lax.ppermute(shard, axis, [(i, (i + by) % size) for i in range(size)])  13.9 us
    all_to_all x6, waiting for transfers between devices, swap(): lax.all_to_all(shard, axis, 0, 0, tiled=True, axis_index_groups=groups)  12 us
    ppermute x3, starting transfers between devices, partner(): lax.ppermute(shard, axis, [(i, i ^ bit) for i in range(lax.axis_size(axis...  9.22 us
    pallas_call x1, Pallas kernels, score_grads(): pl.pallas_call(scores_kernel, grid=(1,), in_specs=[whole_spec((8, 64, 512...  7.88 us
    pallas_call x1, Pallas kernels, window_probs(): pl.pallas_call(probs_kernel, grid=(STEPS,), in_specs=[north_spec(0, 2), s...  7.18 us
    pallas_call x1, Pallas kernels, window_grads(): pl.pallas_call(grads_kernel, grid=(STEPS,), in_specs=[north_spec(0, 3), s...  6.33 us
  transfers between devices with their start and end apart: 14, of which 5 were waited for; matrix products, arithmetic and copies ran while one was open for 9% of the time, Pallas kernels for 12%

profile of v9, /device:TPU:6, one launch (start us, length us, event | category | flops | bytes accessed | tf_op | source)
XLA Modules:
  0.0 145.5 jit_solution(4810456489378532308)
XLA Ops:
  0.6 0.9 copy-done.5
  1.5 0.9 pack_weight.1
  2.4 0.9 fusion.21
  3.4 14.1 %collective-permute-start = (bf16[2,3,3,1536]{3,0,2,1:T(2,128)(2,1)S(1)}, bf16[2,3,3,1536]{3,0,2,1:T(2,128)(2,1)S(1)}, u32[]{:S(2)}, u32[]{:S(2)}) collective-permute-start(bf16[2,3,3,1536]{3,0,2,1:T(2,128)(2,1)S(1)} %get-tuple-element.40), channel_id=1, source_target_pairs={{0,508},{4,0},{8,4},{12,8},{16,12},{20,16},{24,20},{28,24},{32,28}... | collective-permute-start | bytes 165896 | tf_op jit(solution)/shard_map/ppermute | solution.py:451
  17.5 3.6 %all-to-all-start = ((bf16[16,24,384]{2,1,0:T(8,128)(2,1)}), bf16[16,24,384]{2,1,0:T(8,128)(2,1)S(1)}, u32[]{:S(2)}, u32[]{:S(2)}) async-start(bf16[16,24,384]{2,1,0:T(8,128)(2,1)} %pack_weight.1), calls=%async_computation | async-start | bytes 589824 | tf_op jit(solution)/shard_map/all_to_all | solution.py:459
  21.1 0.3 fusion.19
  21.4 0.3 fusion.17
  21.8 0.1 pad.21.clone
  21.8 0.0 collective-permute-done
  21.8 0.2 maximum_maximum_fusion.1
  22.1 3.3 %collective-permute-start.1 = (bf16[48,1536]{1,0:T(8,128)(2,1)S(1)}, bf16[48,1536]{1,0:T(8,128)(2,1)S(1)}, u32[]{:S(2)}, u32[]{:S(2)}) collective-permute-start(bf16[48,1536]{1,0:T(8,128)(2,1)S(1)} %bitcast.32), channel_id=1, source_target_pairs={{0,2},{1,3},{2,0},{3,1},{4,6},{5,7},{6,4},{7,5},{8,10},{9,11},{10,... | collective-permute-start | bytes 442376 | tf_op jit(solution)/shard_map/ppermute | solution.py:455
  25.4 0.8 pad_maximum_fusion.2
  26.2 0.2 copy.48
  26.4 6.9 %collective-permute-start.4 = (bf16[4,2,6,6,768]{4,0,3,2,1:T(4,128)(2,1)S(1)}, bf16[4,2,6,6,768]{4,0,3,2,1:T(4,128)(2,1)S(1)}, u32[]{:S(2)}, u32[]{:S(2)}) collective-permute-start(bf16[4,2,6,6,768]{4,0,3,2,1:T(4,128)(2,1)S(1)} %copy.48), channel_id=1, source_target_pairs={{0,508},{4,0},{8,4},{12,8},{16,12},{20,16},{24,20},{28,24},{32,28}... | collective-permute-start | bytes 1327112 | tf_op jit(solution)/shard_map/ppermute | solution.py:451
  33.2 0.0 collective-permute-done.1
  33.2 0.7 pad_maximum_fusion.3
  34.0 4.0 %collective-permute-start.2 = (bf16[96,1536]{1,0:T(8,128)(2,1)}, bf16[96,1536]{1,0:T(8,128)(2,1)}, u32[]{:S(2)}, u32[]{:S(2)}) collective-permute-start(bf16[96,1536]{1,0:T(8,128)(2,1)} %pad_maximum_fusion.3), channel_id=1, source_target_pairs={{0,256},{4,260},{8,264},{12,268},{16,272},{20,276},{24,280},{28,28... | collective-permute-start | bytes 884744 | tf_op jit(solution)/shard_map/ppermute | solution.py:455
  38.0 2.3 %all-to-all-done = bf16[16,24,384]{2,1,0:T(8,128)(2,1)S(1)} async-done(((bf16[16,24,384]{2,1,0:T(8,128)(2,1)}), bf16[16,24,384]{2,1,0:T(8,128)(2,1)S(1)}, u32[]{:S(2)}, u32[]{:S(2)}) %all-to-all-start) | async-done | bytes 294944 | tf_op jit(solution)/shard_map/all_to_all | solution.py:459
  40.3 1.1 broadcast_in_dim.38
  41.4 4.6 %all-to-all-start.1 = ((bf16[4,384,384]{2,1,0:T(8,128)(2,1)}), bf16[4,384,384]{2,1,0:T(8,128)(2,1)S(1)}, u32[]{:S(2)}, u32[]{:S(2)}) async-start(bf16[4,384,384]{2,1,0:T(8,128)(2,1)} %broadcast_in_dim.38), calls=%async_computation.1 | async-start | bytes 2359296 | tf_op jit(solution)/shard_map/all_to_all | solution.py:459
  46.0 0.5 fusion.7
  46.7 0.1 pad.9.clone
  46.8 0.6 open_table.1.table_ref
  47.4 0.8 copy-done
  48.2 0.0 collective-permute-done.4
  48.2 0.1 copy.49
  48.2 0.0 collective-permute-done.2
  48.2 1.0 pad_maximum_fusion.1.near_ref
  49.2 1.9 %collective-permute-start.3 = (bf16[192,1536]{1,0:T(8,128)(2,1)S(1)}, bf16[192,1536]{1,0:T(8,128)(2,1)S(1)}, u32[]{:S(2)}, u32[]{:S(2)}) collective-permute-start(bf16[192,1536]{1,0:T(8,128)(2,1)S(1)} %pad_maximum_fusion.1.near_ref), channel_id=1, source_target_pairs={{0,1},{1,0},{2,3},{3,2},{4,5},{5,4},{6,7},{7,6},{8,9},{9,8},{10,11... | collective-permute-start | bytes 1769480 | tf_op jit(solution)/shard_map/ppermute | solution.py:455
  51.2 0.5 maximum_maximum_fusion.north_ref.y_a_ref.y_b_ref
  51.7 0.0 copy-start.13
  51.7 0.0 copy-start.1
  51.7 0.9 slice.75
  52.7 3.4 %collective-permute-start.5 = (bf16[4,2,4,16,768]{4,3,2,1,0:T(8,128)(2,1)}, bf16[4,2,4,16,768]{4,3,2,1,0:T(8,128)(2,1)S(1)}, u32[]{:S(2)}, u32[]{:S(2)}) collective-permute-start(bf16[4,2,4,16,768]{4,3,2,1,0:T(8,128)(2,1)} %slice.75), channel_id=1, source_target_pairs={{0,3},{1,0},{2,1},{3,2},{4,7},{5,4},{6,5},{7,6},{8,11},{9,8},{10,9... | collective-permute-start | bytes 2359304 | tf_op jit(solution)/shard_map/ppermute | solution.py:451
  56.1 0.8 and_select_fusion.mask_ref
  56.9 0.9 all-to-all-done.1.w_ref
  57.9 0.0 collective-permute-done.3.far_ref
  57.9 3.6 %merge_product.1 = bf16[8,64,512]{2,1,0:T(8,128)(2,1)} custom-call(s32[8]{0:T(128)S(1)} %fusion.14.spot_ref, bf16[192,1536]{1,0:T(8,128)(2,1)S(1)} %pad_maximum_fusion.1.near_ref, bf16[192,1536]{1,0:T(8,128)(2,1)S(1)} %collective-permute-done.3.far_ref, bf16[4,384,384]{2,1,0:T(8,128)(2,1)S(1)} %all-to-all-done.1.w_ref, bf16[512,384]{1,0:T(8,128)(2,1)S(1)} %copy-done.1), custom_call_target="tpu_custom_call" | custom-call | tf_op jit(solution)/shard_map/merge_product/pallas_call | solution.py:378
  61.4 5.5 %all-to-all-start.2 = ((bf16[8,64,512]{2,1,0:T(8,128)(2,1)}), bf16[8,64,512]{2,1,0:T(8,128)(2,1)S(1)}, u32[]{:S(2)}, u32[]{:S(2)}) async-start(bf16[8,64,512]{2,1,0:T(8,128)(2,1)} %merge_product.1), calls=%async_computation.2 | async-start | bytes 1048576 | tf_op jit(solution)/shard_map/all_to_all | solution.py:459
  66.9 0.0 collective-permute-done.5.south_ref.y_south_ref
  67.0 0.9 copy-done.7
  67.8 7.2 %window_probs.1.p_ref = bf16[6,768,192]{2,1,0:T(8,128)(2,1)} custom-call(bf16[4,2,6,16,768]{4,3,2,1,0:T(8,128)(2,1)} %copy-done.6, bf16[4,2,4,16,768]{4,3,2,1,0:T(8,128)(2,1)} %copy-done.7, f32[6,48,384]{2,1,0:T(8,128)} %copy-done, bf16[384,192]{1,0:T(8,128)(2,1)} %constant.132.clone.spread_ref, f32[192,192]{1,0:T(8,128)} %and_select_fusion.mask_ref), custom_call_target="tpu_custom_call" | custom-call | tf_op jit(solution)/shard_map/window_probs/pallas_call | solution.py:360
  75.0 0.0 all-to-all-done.2.recv_ref
  75.0 0.8 copy-done.8
  75.8 7.9 %score_grads.1 = (bf16[6,192,128]{2,1,0:T(8,128)(2,1)}, bf16[16,56,128]{2,1,0:T(8,128)(2,1)}) custom-call(bf16[8,64,512]{2,1,0:T(8,128)(2,1)} %copy-done.8, bf16[512,384]{1,0:T(8,128)(2,1)} %constant.135.clone.shuffle_ref.order_ref, bf16[4,2,6,16,768]{4,3,2,1,0:T(8,128)(2,1)} %copy-done.6, bf16[4,2,6,16,768]{4,3,2,1,0:T(8,128)(2,1)} %copy-done.6, ...), custom_call_target="tpu_custom_call" | custom-call | tf_op jit(solution)/shard_map/score_grads/pallas_call | solution.py:390
  83.7 7.4 %all-to-all-start.3 = ((bf16[16,56,128]{2,1,0:T(8,128)(2,1)}), bf16[16,56,128]{2,1,0:T(8,128)(2,1)S(1)}, u32[]{:S(2)}, u32[]{:S(2)}) async-start(bf16[16,56,128]{2,1,0:T(8,128)(2,1)} %get-tuple-element.20), calls=%async_computation.3 | async-start | bytes 458752 | tf_op jit(solution)/shard_map/all_to_all | solution.py:459
  91.1 6.3 %window_grads.1 = bf16[3,192,768]{2,1,0:T(8,128)(2,1)} custom-call(bf16[4,2,6,16,768]{4,3,2,1,0:T(8,128)(2,1)} %copy-done.6, bf16[4,2,4,16,768]{4,3,2,1,0:T(8,128)(2,1)} %copy-done.7, bf16[6,192,128]{2,1,0:T(8,128)(2,1)} %get-tuple-element.21.o_ref, bf16[6,768,192]{2,1,0:T(8,128)(2,1)} %window_probs.1.p_ref), custom_call_target="tpu_custom_call" | custom-call | tf_op jit(solution)/shard_map/window_grads/pallas_call | solution.py:433
  97.4 1.4 fusion.15
  98.8 0.3 copy.56
  99.1 3.4 %collective-permute-start.6 = (bf16[3,2,6,6,768]{4,1,3,2,0:T(2,128)(2,1)S(1)}, bf16[3,2,6,6,768]{4,1,3,2,0:T(2,128)(2,1)S(1)}, u32[]{:S(2)}, u32[]{:S(2)}) collective-permute-start(bf16[3,2,6,6,768]{4,1,3,2,0:T(2,128)(2,1)S(1)} %copy.56), channel_id=1, source_target_pairs={{0,4},{4,8},{8,12},{12,16},{16,20},{20,24},{24,28},{28,32},{32,36}... | collective-permute-start | bytes 995336 | tf_op jit(solution)/shard_map/ppermute | solution.py:451
  102.5 0.0 all-to-all-done.3
  102.5 0.7 broadcast_in_dim.42
  103.2 6.5 %all-to-all-start.4 = ((bf16[8,56,128]{2,1,0:T(8,128)(2,1)}), bf16[8,56,128]{2,1,0:T(8,128)(2,1)S(1)}, u32[]{:S(2)}, u32[]{:S(2)}) async-start(bf16[8,56,128]{2,1,0:T(8,128)(2,1)} %broadcast_in_dim.42), calls=%async_computation.4 | async-start | bytes 229376 | tf_op jit(solution)/shard_map/all_to_all | solution.py:459
  109.8 0.3 copy.57
  110.0 5.8 %collective-permute-done.6 = bf16[3,2,6,6,768]{4,1,3,2,0:T(2,128)(2,1)S(1)} collective-permute-done((bf16[3,2,6,6,768]{4,1,3,2,0:T(2,128)(2,1)S(1)}, bf16[3,2,6,6,768]{4,1,3,2,0:T(2,128)(2,1)S(1)}, u32[]{:S(2)}, u32[]{:S(2)}) %collective-permute-start.6) | collective-permute-done | bytes 331808 | tf_op jit(solution)/shard_map/ppermute | solution.py:451
  115.8 0.9 pad_maximum_fusion
  116.7 8.8 %all-to-all-done.4 = bf16[8,56,128]{2,1,0:T(8,128)(2,1)S(1)} async-done(((bf16[8,56,128]{2,1,0:T(8,128)(2,1)}), bf16[8,56,128]{2,1,0:T(8,128)(2,1)S(1)}, u32[]{:S(2)}, u32[]{:S(2)}) %all-to-all-start.4) | async-done | bytes 114720 | tf_op jit(solution)/shard_map/all_to_all | solution.py:459
  125.5 0.7 broadcast_in_dim.43
  126.2 6.0 %all-to-all-start.5 = ((bf16[16,56,128]{2,1,0:T(8,128)(2,1)}), bf16[16,56,128]{2,1,0:T(8,128)(2,1)S(1)}, u32[]{:S(2)}, u32[]{:S(2)}) async-start(bf16[16,56,128]{2,1,0:T(8,128)(2,1)} %broadcast_in_dim.43), calls=%async_computation.5 | async-start | bytes 458752 | tf_op jit(solution)/shard_map/all_to_all | solution.py:459
  132.3 0.5 fusion.16
  132.7 1.9 %collective-permute-start.7 = (bf16[3,2,3,12,768]{4,1,3,2,0:T(2,128)(2,1)S(1)}, bf16[3,2,3,12,768]{4,1,3,2,0:T(2,128)(2,1)S(1)}, u32[]{:S(2)}, u32[]{:S(2)}) collective-permute-start(bf16[3,2,3,12,768]{4,1,3,2,0:T(2,128)(2,1)S(1)} %get-tuple-element.29), channel_id=1, source_target_pairs={{0,1},{1,2},{2,3},{3,0},{4,5},{5,6},{6,7},{7,4},{8,9},{9,10},{10,1... | collective-permute-start | bytes 995336 | tf_op jit(solution)/shard_map/ppermute | solution.py:451
  134.7 8.0 %collective-permute-done.7 = bf16[3,2,3,12,768]{4,1,3,2,0:T(2,128)(2,1)S(1)} collective-permute-done((bf16[3,2,3,12,768]{4,1,3,2,0:T(2,128)(2,1)S(1)}, bf16[3,2,3,12,768]{4,1,3,2,0:T(2,128)(2,1)S(1)}, u32[]{:S(2)}, u32[]{:S(2)}) %collective-permute-start.7) | collective-permute-done | bytes 331808 | tf_op jit(solution)/shard_map/ppermute | solution.py:451
  142.7 1.6 %fusion.2 = (bf16[2,6,12,768]{3,0,2,1:T(2,128)(2,1)}, bf16[2,6,12,768]{3,0,2,1:T(2,128)(2,1)}, bf16[2,6,12,768]{3,0,2,1:T(2,128)(2,1)}) fusion(bf16[3,2,3,12,768]{4,1,3,2,0:T(2,128)(2,1)S(1)} %get-tuple-element.30, bf16[3,2,3,12,768]{4,1,3,2,0:T(2,128)(2,1)S(1)} %collective-permute-done.7), kind=kLoop, calls=%fused_computation.12 | loop fusion | flops 331776 | bytes 1327104 | tf_op jit(solution)/shard_map/squeeze | solution.py:534
  144.3 1.2 close_table.1
  (33 shorter events, 0.2 us)
Async XLA Ops:
  0.6 0.9 copy-start.5
  1.5 19.5 %copy-start.9 = (bf16[2,6,12,768]{3,0,2,1:T(2,128)(2,1)S(1)}, bf16[2,6,12,768]{3,0,2,1:T(2,128)(2,1)}, u32[]{:S(2)}) copy-start(bf16[2,6,12,768]{3,0,2,1:T(2,128)(2,1)} %param.22) | copy-start | bytes 663556
  1.5 19.5 %copy-start.10 = (bf16[2,6,12,768]{3,0,2,1:T(2,128)(2,1)S(1)}, bf16[2,6,12,768]{3,0,2,1:T(2,128)(2,1)}, u32[]{:S(2)}) copy-start(bf16[2,6,12,768]{3,0,2,1:T(2,128)(2,1)} %param.16) | copy-start | bytes 663556
  1.5 19.9 %copy-start.11 = (bf16[2,6,12,768]{3,0,2,1:T(2,128)(2,1)S(1)}, bf16[2,6,12,768]{3,0,2,1:T(2,128)(2,1)}, u32[]{:S(2)}) copy-start(bf16[2,6,12,768]{3,0,2,1:T(2,128)(2,1)} %param.20) | copy-start | bytes 663556
  1.5 19.9 %copy-start.12 = (bf16[2,6,12,768]{3,0,2,1:T(2,128)(2,1)S(1)}, bf16[2,6,12,768]{3,0,2,1:T(2,128)(2,1)}, u32[]{:S(2)}) copy-start(bf16[2,6,12,768]{3,0,2,1:T(2,128)(2,1)} %param.21) | copy-start | bytes 663556
  3.4 18.5 %collective-permute-start = (bf16[2,3,3,1536]{3,0,2,1:T(2,128)(2,1)S(1)}, bf16[2,3,3,1536]{3,0,2,1:T(2,128)(2,1)S(1)}, u32[]{:S(2)}, u32[]{:S(2)}) collective-permute-start(bf16[2,3,3,1536]{3,0,2,1:T(2,128)(2,1)S(1)} %get-tuple-element.40), channel_id=1, source_target_pairs={{0,508},{4,0},{8,4},{12,8},{16,12},{20,16},{24,20},{28,24},{32,28}... | collective-permute-start | bytes 165896 | tf_op jit(solution)/shard_map/ppermute | solution.py:451
  17.5 22.8 %all-to-all-start = ((bf16[16,24,384]{2,1,0:T(8,128)(2,1)}), bf16[16,24,384]{2,1,0:T(8,128)(2,1)S(1)}, u32[]{:S(2)}, u32[]{:S(2)}) async-start(bf16[16,24,384]{2,1,0:T(8,128)(2,1)} %pack_weight.1), calls=%async_computation | async-start | bytes 589824 | tf_op jit(solution)/shard_map/all_to_all | solution.py:459
  22.1 11.2 %collective-permute-start.1 = (bf16[48,1536]{1,0:T(8,128)(2,1)S(1)}, bf16[48,1536]{1,0:T(8,128)(2,1)S(1)}, u32[]{:S(2)}, u32[]{:S(2)}) collective-permute-start(bf16[48,1536]{1,0:T(8,128)(2,1)S(1)} %bitcast.32), channel_id=1, source_target_pairs={{0,2},{1,3},{2,0},{3,1},{4,6},{5,7},{6,4},{7,5},{8,10},{9,11},{10,... | collective-permute-start | bytes 442376 | tf_op jit(solution)/shard_map/ppermute | solution.py:455
  26.4 21.8 %collective-permute-start.4 = (bf16[4,2,6,6,768]{4,0,3,2,1:T(4,128)(2,1)S(1)}, bf16[4,2,6,6,768]{4,0,3,2,1:T(4,128)(2,1)S(1)}, u32[]{:S(2)}, u32[]{:S(2)}) collective-permute-start(bf16[4,2,6,6,768]{4,0,3,2,1:T(4,128)(2,1)S(1)} %copy.48), channel_id=1, source_target_pairs={{0,508},{4,0},{8,4},{12,8},{16,12},{20,16},{24,20},{28,24},{32,28}... | collective-permute-start | bytes 1327112 | tf_op jit(solution)/shard_map/ppermute | solution.py:451
  34.0 14.2 %collective-permute-start.2 = (bf16[96,1536]{1,0:T(8,128)(2,1)}, bf16[96,1536]{1,0:T(8,128)(2,1)}, u32[]{:S(2)}, u32[]{:S(2)}) collective-permute-start(bf16[96,1536]{1,0:T(8,128)(2,1)} %pad_maximum_fusion.3), channel_id=1, source_target_pairs={{0,256},{4,260},{8,264},{12,268},{16,272},{20,276},{24,280},{28,28... | collective-permute-start | bytes 884744 | tf_op jit(solution)/shard_map/ppermute | solution.py:455
  41.4 5.3 %copy-start.3 = (f32[1,24,3312]{2,1,0:T(8,128)S(1)}, f32[1,24,3312]{2,1,0:T(8,128)}, u32[]{:S(2)}) copy-start(f32[1,24,3312]{2,1,0:T(8,128)} %table_ref.1) | copy-start | bytes 953860
  41.4 5.3 %copy-start.4 = (bf16[2,138,384]{2,1,0:T(8,128)(2,1)S(1)}, bf16[2,138,384]{2,1,0:T(8,128)(2,1)}, u32[]{:S(2)}) copy-start(bf16[2,138,384]{2,1,0:T(8,128)(2,1)} %constant.136.clone.open_ref) | copy-start | bytes 635908
  41.4 16.4 %all-to-all-start.1 = ((bf16[4,384,384]{2,1,0:T(8,128)(2,1)}), bf16[4,384,384]{2,1,0:T(8,128)(2,1)S(1)}, u32[]{:S(2)}, u32[]{:S(2)}) async-start(bf16[4,384,384]{2,1,0:T(8,128)(2,1)} %broadcast_in_dim.38), calls=%async_computation.1 | async-start | bytes 2359296 | tf_op jit(solution)/shard_map/all_to_all | solution.py:459
  47.4 0.8 copy-start
  49.2 8.6 %collective-permute-start.3 = (bf16[192,1536]{1,0:T(8,128)(2,1)S(1)}, bf16[192,1536]{1,0:T(8,128)(2,1)S(1)}, u32[]{:S(2)}, u32[]{:S(2)}) collective-permute-start(bf16[192,1536]{1,0:T(8,128)(2,1)S(1)} %pad_maximum_fusion.1.near_ref), channel_id=1, source_target_pairs={{0,1},{1,0},{2,3},{3,2},{4,5},{5,4},{6,7},{7,6},{8,9},{9,8},{10,11... | collective-permute-start | bytes 1769480 | tf_op jit(solution)/shard_map/ppermute | solution.py:455
  51.7 4.4 %copy-start.6 = (bf16[4,2,6,16,768]{4,3,2,1,0:T(8,128)(2,1)}, bf16[4,2,6,16,768]{4,3,2,1,0:T(8,128)(2,1)S(1)}, u32[]{:S(2)}) copy-start(bf16[4,2,6,16,768]{4,3,2,1,0:T(8,128)(2,1)S(1)} %maximum_maximum_fusion.north_ref.y_a_ref.y_b_ref) | copy-start | bytes 3538948
  51.7 4.4 %copy-start.13 = (pred[192]{0:T(512)(128)(4,1)S(1)}, pred[192]{0:T(512)(128)(4,1)}, u32[]{:S(2)}) copy-start(pred[192]{0:T(512)(128)(4,1)} %get-tuple-element.41) | copy-start | bytes 580
  51.7 6.1 %copy-start.1 = (bf16[512,384]{1,0:T(8,128)(2,1)S(1)}, bf16[512,384]{1,0:T(8,128)(2,1)}, u32[]{:S(2)}) copy-start(bf16[512,384]{1,0:T(8,128)(2,1)} %constant.135.clone.shuffle_ref.order_ref) | copy-start | bytes 1179652
  52.7 14.3 %collective-permute-start.5 = (bf16[4,2,4,16,768]{4,3,2,1,0:T(8,128)(2,1)}, bf16[4,2,4,16,768]{4,3,2,1,0:T(8,128)(2,1)S(1)}, u32[]{:S(2)}, u32[]{:S(2)}) collective-permute-start(bf16[4,2,4,16,768]{4,3,2,1,0:T(8,128)(2,1)} %slice.75), channel_id=1, source_target_pairs={{0,3},{1,0},{2,1},{3,2},{4,7},{5,4},{6,5},{7,6},{8,11},{9,8},{10,9... | collective-permute-start | bytes 2359304 | tf_op jit(solution)/shard_map/ppermute | solution.py:451
  61.4 13.6 %all-to-all-start.2 = ((bf16[8,64,512]{2,1,0:T(8,128)(2,1)}), bf16[8,64,512]{2,1,0:T(8,128)(2,1)S(1)}, u32[]{:S(2)}, u32[]{:S(2)}) async-start(bf16[8,64,512]{2,1,0:T(8,128)(2,1)} %merge_product.1), calls=%async_computation.2 | async-start | bytes 1048576 | tf_op jit(solution)/shard_map/all_to_all | solution.py:459
  66.9 0.9 copy-start.7
  75.0 0.8 copy-start.8
  83.7 18.8 %all-to-all-start.3 = ((bf16[16,56,128]{2,1,0:T(8,128)(2,1)}), bf16[16,56,128]{2,1,0:T(8,128)(2,1)S(1)}, u32[]{:S(2)}, u32[]{:S(2)}) async-start(bf16[16,56,128]{2,1,0:T(8,128)(2,1)} %get-tuple-element.20), calls=%async_computation.3 | async-start | bytes 458752 | tf_op jit(solution)/shard_map/all_to_all | solution.py:459
  99.1 16.7 %collective-permute-start.6 = (bf16[3,2,6,6,768]{4,1,3,2,0:T(2,128)(2,1)S(1)}, bf16[3,2,6,6,768]{4,1,3,2,0:T(2,128)(2,1)S(1)}, u32[]{:S(2)}, u32[]{:S(2)}) collective-permute-start(bf16[3,2,6,6,768]{4,1,3,2,0:T(2,128)(2,1)S(1)} %copy.56), channel_id=1, source_target_pairs={{0,4},{4,8},{8,12},{12,16},{16,20},{20,24},{24,28},{28,32},{32,36}... | collective-permute-start | bytes 995336 | tf_op jit(solution)/shard_map/ppermute | solution.py:451
  103.2 22.3 %all-to-all-start.4 = ((bf16[8,56,128]{2,1,0:T(8,128)(2,1)}), bf16[8,56,128]{2,1,0:T(8,128)(2,1)S(1)}, u32[]{:S(2)}, u32[]{:S(2)}) async-start(bf16[8,56,128]{2,1,0:T(8,128)(2,1)} %broadcast_in_dim.42), calls=%async_computation.4 | async-start | bytes 229376 | tf_op jit(solution)/shard_map/all_to_all | solution.py:459
  126.2 18.0 %all-to-all-start.5 = ((bf16[16,56,128]{2,1,0:T(8,128)(2,1)}), bf16[16,56,128]{2,1,0:T(8,128)(2,1)S(1)}, u32[]{:S(2)}, u32[]{:S(2)}) async-start(bf16[16,56,128]{2,1,0:T(8,128)(2,1)} %broadcast_in_dim.43), calls=%async_computation.5 | async-start | bytes 458752 | tf_op jit(solution)/shard_map/all_to_all | solution.py:459
  132.3 12.0 %copy-start.2 = (bf16[384,512]{1,0:T(8,128)(2,1)S(1)}, bf16[384,512]{1,0:T(8,128)(2,1)}, u32[]{:S(2)}) copy-start(bf16[384,512]{1,0:T(8,128)(2,1)} %constant.137.clone.close_ref) | copy-start | bytes 1179652
  132.7 9.9 %collective-permute-start.7 = (bf16[3,2,3,12,768]{4,1,3,2,0:T(2,128)(2,1)S(1)}, bf16[3,2,3,12,768]{4,1,3,2,0:T(2,128)(2,1)S(1)}, u32[]{:S(2)}, u32[]{:S(2)}) collective-permute-start(bf16[3,2,3,12,768]{4,1,3,2,0:T(2,128)(2,1)S(1)} %get-tuple-element.29), channel_id=1, source_target_pairs={{0,1},{1,2},{2,3},{3,0},{4,5},{5,6},{6,7},{7,4},{8,9},{9,10},{10,1... | collective-permute-start | bytes 995336 | tf_op jit(solution)/shard_map/ppermute | solution.py:451

commit v10 on v9

--- a/solution.py
+++ b/solution.py
@@ -40,10 +40,11 @@
     tokens = np.arange(TOK)
     row, col = tokens // PAD, tokens % PAD
     real = col < 12
-    sums = np.zeros((TOK, WIDE), np.float32)
-    sums[tokens[real], (row * SEG + 11 - col)[real]] = 1
-    spread = np.zeros((WIDE, TOK), np.float32)
-    spread[(row * SEG + 11 + col)[real], tokens[real]] = 1
+    sums = np.zeros((2, TOK, WIDE), np.float32)
+    spread = np.zeros((2, WIDE, TOK), np.float32)
+    for half in range(2):
+        sums[half, tokens[real], (row * SEG + 11 - col + 8 * half)[real]] = 1
+        spread[half, (row * SEG + 11 + col - 8 * half)[real], tokens[real]] = 1
     quarter = np.zeros((256, 256), np.float32)
     back = np.zeros((TOK, 256), np.float32)
     for level in range(2):
@@ -144,13 +145,14 @@
         pieces = []
         for s in range(3):
             table = table_ref[group, :, s * 128 : (s + 1) * 128]
-            table = jnp.broadcast_to(table[:, None, :], (4 * ROWS, PAD, 128))
+            table = jnp.broadcast_to(table[:, None, :], (4 * ROWS, 8, 128))
             pieces.append(pltpu.roll(table, 0, 2, stride=1, stride_axis=1))
-        wide = jnp.concatenate(pieces, axis=2).reshape(4 * TOK, WIDE)
+        wide = jnp.concatenate(pieces, axis=2).reshape(2 * TOK, WIDE)
         q_win = window(north_ref, south_ref, 0, group)
         k_win = window(north_ref, south_ref, 1, group)
         scores = dot(by_head(q_win), k_win, ((1,), (1,))) * score_factor
-        scores = scores + split_dot(wide, spread_ref[...])
+        bias = [split_dot(wide, spread_ref[half]).reshape(-1, 1, 8, TOK) for half in range(2)]
+        scores = scores + jnp.concatenate(bias, axis=1).reshape(4 * TOK, TOK)
         scores = (scores.reshape(4, TOK, TOK) + mask_ref[...][None]).reshape(4 * TOK, TOK)
         expon = jnp.exp(scores - jnp.max(scores, axis=-1, keepdims=True))
         probs = expon * (1.0 / jnp.sum(expon, axis=-1, keepdims=True))
@@ -204,7 +206,7 @@
     d_probs = dot(by_head(o_win), v_win, ((1,), (1,)))
     probs = probs.astype(jnp.float32)
     delta = jnp.sum(probs * d_probs, axis=-1, keepdims=True)
-    return (probs * (d_probs - delta)).astype(jnp.bfloat16)
+    return probs * (d_probs - delta)
 
 
 def scores_kernel(
@@ -222,7 +224,11 @@
     p_ref,
     o_out_ref,
     table_ref,
+    p_buf,
+    p_sem,
 ):
+    copy = pltpu.make_async_copy(p_ref, p_buf, p_sem)
+    copy.start()
     pieces = [
         jnp.concatenate(
             [recv_ref[x * LAT + l, :, y * 128 : (y + 1) * 128] for l in range(LAT)], axis=1
@@ -244,12 +250,17 @@
     d_out = dot(back_ref[...], jnp.concatenate(stack, axis=0).astype(jnp.bfloat16))
     d_out = d_out.astype(jnp.bfloat16)
 
+    copy.wait()
     sums = [[], [], []]
     for group in range(GROUPS):
         o_win = d_out[:, group * 128 : (group + 1) * 128]
         o_out_ref[group] = o_win
-        d_low = score_grad(p_ref[group], o_win, window(north_ref, south_ref, 0, group))
-        spread = dot(d_low, sums_ref[...]).reshape(4 * ROWS, PAD, WIDE)
+        d_scores = score_grad(p_buf[group], o_win, window(north_ref, south_ref, 0, group))
+        halves = d_scores.reshape(4 * ROWS, 2, 8, TOK)
+        spread = sum(
+            dot(halves[:, half].reshape(2 * TOK, TOK).astype(jnp.bfloat16), sums_ref[half])
+            for half in range(2)
+        ).reshape(4 * ROWS, 8, WIDE)
         for s in range(3):
             part = spread[:, :, s * 128 : (s + 1) * 128]
             turned = pltpu.roll(part, 0, 2, stride=1, stride_axis=1)
@@ -292,6 +303,7 @@
         k_win = window(north_ref, south_ref, 1, group)
         o_win, p_low = o_ref[group], p_ref[group]
         d_low = score_grad(p_low, o_win, window(north_ref, south_ref, 2, group))
+        d_low = d_low.astype(jnp.bfloat16)
         q_all = dot(d_low, k_win)
         q_grad = jnp.zeros((TOK, 128), jnp.float32)
         for h in range(4):
@@ -364,7 +376,7 @@
             north_spec(0, 2),
             south_spec(0, 2),
             group_spec(4 * ROWS, WIDE),
-            whole_spec((WIDE, TOK)),
+            whole_spec((2, WIDE, TOK)),
             whole_spec((TOK, TOK)),
         ],
         out_specs=group_spec(4 * TOK, TOK),
@@ -399,10 +411,10 @@
             whole_spec((256, 256)),
             whole_spec((4, 1, 768)),
             whole_spec((TOK, 256)),
-            whole_spec((TOK, WIDE)),
+            whole_spec((2, TOK, WIDE)),
             pl.BlockSpec((1, 2, 3, PAD, 768), lambda g: (2, 0, 1, 0, 0)),
             pl.BlockSpec((1, 2, 4, PAD, 768), lambda g: (2, 0, 0, 0, 0)),
-            whole_spec((GROUPS, 4 * TOK, TOK)),
+            pl.BlockSpec(memory_space=pl.ANY),
         ],
         out_specs=(
             whole_spec((GROUPS, TOK, 128)),
@@ -412,6 +424,10 @@
             jax.ShapeDtypeStruct((GROUPS, TOK, 128), jnp.bfloat16),
             jax.ShapeDtypeStruct((16, 8 * SHARE, 128), jnp.bfloat16),
         ),
+        scratch_shapes=[
+            pltpu.VMEM((GROUPS, 4 * TOK, TOK), jnp.bfloat16),
+            pltpu.SemaphoreType.DMA,
+        ],
         compiler_params=large,
         name="score_grads",
     )(recv, order, across, across, south, quarter, gain, back, sums, across, south, probs)

time: 147 us -> 145 us (0.986)
  Pallas kernels: 27.7 us -> 25.7 us
  transfers between devices with their start and end apart: 14 -> 14, of which waited for: 5 -> 6; matrix products, arithmetic and copies ran while one was open for 9% -> 9% of each run, Pallas kernels for 12% -> 12%
where the time goes in v10:
time: 145 us; the launch traced here: 144 us
  starting transfers between devices  72.3 us (50%)
  waiting for transfers between devices  26.4 us (18%)
  Pallas kernels  25.7 us (18%)
  local copies, waits for them, and re-layouts  11.2 us (8%)
  other arithmetic  7.12 us (5%)
    all_to_all x6, starting transfers between devices, swap(): lax.all_to_all(shard, axis, 0, 0, tiled=True, axis_index_groups=groups)  33.4 us
    ppermute x5, starting transfers between devices, from_behind(): lax.ppermute(shard, axis, [(i, (i + by) % size) for i in range(size)])  29.7 us
    ppermute x5, waiting for transfers between devices, from_behind(): lax.ppermute(shard, axis, [(i, (i + by) % size) for i in range(size)])  13.4 us
    all_to_all x6, waiting for transfers between devices, swap(): lax.all_to_all(shard, axis, 0, 0, tiled=True, axis_index_groups=groups)  13.1 us
    ppermute x3, starting transfers between devices, partner(): lax.ppermute(shard, axis, [(i, i ^ bit) for i in range(lax.axis_size(axis...  9.22 us
    pallas_call x1, Pallas kernels, score_grads(): pl.pallas_call(scores_kernel, grid=(1,), in_specs=[whole_spec((8, 64, 512...  6.72 us
    pallas_call x1, Pallas kernels, window_grads(): pl.pallas_call(grads_kernel, grid=(STEPS,), in_specs=[north_spec(0, 3), s...  6.34 us
    pallas_call x1, Pallas kernels, window_probs(): pl.pallas_call(probs_kernel, grid=(STEPS,), in_specs=[north_spec(0, 2), s...  6.33 us
  transfers between devices with their start and end apart: 14, of which 6 were waited for; matrix products, arithmetic and copies ran while one was open for 9% of the time, Pallas kernels for 12%

profile of v10, /device:TPU:6, one launch (start us, length us, event | category | flops | bytes accessed | tf_op | source)
XLA Modules:
  0.0 143.8 jit_solution(13751623864484038991)
XLA Ops:
  0.6 0.9 copy-done.5
  1.5 0.9 pack_weight.1
  2.4 0.9 fusion.21
  3.4 14.1 %collective-permute-start = (bf16[2,3,3,1536]{3,0,2,1:T(2,128)(2,1)S(1)}, bf16[2,3,3,1536]{3,0,2,1:T(2,128)(2,1)S(1)}, u32[]{:S(2)}, u32[]{:S(2)}) collective-permute-start(bf16[2,3,3,1536]{3,0,2,1:T(2,128)(2,1)S(1)} %get-tuple-element.40), channel_id=1, source_target_pairs={{0,508},{4,0},{8,4},{12,8},{16,12},{20,16},{24,20},{28,24},{32,28}... | collective-permute-start | bytes 165896 | tf_op jit(solution)/shard_map/ppermute | solution.py:467
  17.5 3.6 %all-to-all-start = ((bf16[16,24,384]{2,1,0:T(8,128)(2,1)}), bf16[16,24,384]{2,1,0:T(8,128)(2,1)S(1)}, u32[]{:S(2)}, u32[]{:S(2)}) async-start(bf16[16,24,384]{2,1,0:T(8,128)(2,1)} %pack_weight.1), calls=%async_computation | async-start | bytes 589824 | tf_op jit(solution)/shard_map/all_to_all | solution.py:475
  21.1 0.3 fusion.19
  21.4 0.3 fusion.17
  21.8 0.1 pad.21.clone
  21.8 0.0 collective-permute-done
  21.8 0.2 maximum_maximum_fusion.1
  22.1 3.3 %collective-permute-start.1 = (bf16[48,1536]{1,0:T(8,128)(2,1)S(1)}, bf16[48,1536]{1,0:T(8,128)(2,1)S(1)}, u32[]{:S(2)}, u32[]{:S(2)}) collective-permute-start(bf16[48,1536]{1,0:T(8,128)(2,1)S(1)} %bitcast.32), channel_id=1, source_target_pairs={{0,2},{1,3},{2,0},{3,1},{4,6},{5,7},{6,4},{7,5},{8,10},{9,11},{10,... | collective-permute-start | bytes 442376 | tf_op jit(solution)/shard_map/ppermute | solution.py:471
  25.4 0.8 pad_maximum_fusion.2
  26.2 0.2 copy.48
  26.4 6.9 %collective-permute-start.4 = (bf16[4,2,6,6,768]{4,0,3,2,1:T(4,128)(2,1)S(1)}, bf16[4,2,6,6,768]{4,0,3,2,1:T(4,128)(2,1)S(1)}, u32[]{:S(2)}, u32[]{:S(2)}) collective-permute-start(bf16[4,2,6,6,768]{4,0,3,2,1:T(4,128)(2,1)S(1)} %copy.48), channel_id=1, source_target_pairs={{0,508},{4,0},{8,4},{12,8},{16,12},{20,16},{24,20},{28,24},{32,28}... | collective-permute-start | bytes 1327112 | tf_op jit(solution)/shard_map/ppermute | solution.py:467
  33.2 0.0 collective-permute-done.1
  33.2 0.7 pad_maximum_fusion.3
  34.0 4.0 %collective-permute-start.2 = (bf16[96,1536]{1,0:T(8,128)(2,1)}, bf16[96,1536]{1,0:T(8,128)(2,1)}, u32[]{:S(2)}, u32[]{:S(2)}) collective-permute-start(bf16[96,1536]{1,0:T(8,128)(2,1)} %pad_maximum_fusion.3), channel_id=1, source_target_pairs={{0,256},{4,260},{8,264},{12,268},{16,272},{20,276},{24,280},{28,28... | collective-permute-start | bytes 884744 | tf_op jit(solution)/shard_map/ppermute | solution.py:471
  38.0 2.3 %all-to-all-done = bf16[16,24,384]{2,1,0:T(8,128)(2,1)S(1)} async-done(((bf16[16,24,384]{2,1,0:T(8,128)(2,1)}), bf16[16,24,384]{2,1,0:T(8,128)(2,1)S(1)}, u32[]{:S(2)}, u32[]{:S(2)}) %all-to-all-start) | async-done | bytes 294944 | tf_op jit(solution)/shard_map/all_to_all | solution.py:475
  40.3 1.1 broadcast_in_dim.38
  41.4 4.6 %all-to-all-start.1 = ((bf16[4,384,384]{2,1,0:T(8,128)(2,1)}), bf16[4,384,384]{2,1,0:T(8,128)(2,1)S(1)}, u32[]{:S(2)}, u32[]{:S(2)}) async-start(bf16[4,384,384]{2,1,0:T(8,128)(2,1)} %broadcast_in_dim.38), calls=%async_computation.1 | async-start | bytes 2359296 | tf_op jit(solution)/shard_map/all_to_all | solution.py:475
  46.0 0.5 fusion.7
  46.7 0.1 pad.9.clone
  46.8 0.6 open_table.1.table_ref
  47.4 0.8 copy-done
  48.2 0.0 collective-permute-done.4
  48.2 0.1 copy.49
  48.2 0.0 collective-permute-done.2
  48.2 1.0 pad_maximum_fusion.1.near_ref
  49.2 1.9 %collective-permute-start.3 = (bf16[192,1536]{1,0:T(8,128)(2,1)S(1)}, bf16[192,1536]{1,0:T(8,128)(2,1)S(1)}, u32[]{:S(2)}, u32[]{:S(2)}) collective-permute-start(bf16[192,1536]{1,0:T(8,128)(2,1)S(1)} %pad_maximum_fusion.1.near_ref), channel_id=1, source_target_pairs={{0,1},{1,0},{2,3},{3,2},{4,5},{5,4},{6,7},{7,6},{8,9},{9,8},{10,11... | collective-permute-start | bytes 1769480 | tf_op jit(solution)/shard_map/ppermute | solution.py:471
  51.2 0.5 maximum_maximum_fusion.north_ref.y_a_ref.y_b_ref
  51.7 0.0 copy-start.13
  51.7 0.0 copy-start.1
  51.7 0.9 slice.75
  52.7 3.4 %collective-permute-start.5 = (bf16[4,2,4,16,768]{4,3,2,1,0:T(8,128)(2,1)}, bf16[4,2,4,16,768]{4,3,2,1,0:T(8,128)(2,1)S(1)}, u32[]{:S(2)}, u32[]{:S(2)}) collective-permute-start(bf16[4,2,4,16,768]{4,3,2,1,0:T(8,128)(2,1)} %slice.75), channel_id=1, source_target_pairs={{0,3},{1,0},{2,1},{3,2},{4,7},{5,4},{6,5},{7,6},{8,11},{9,8},{10,9... | collective-permute-start | bytes 2359304 | tf_op jit(solution)/shard_map/ppermute | solution.py:467
  56.1 0.8 and_select_fusion.mask_ref
  56.9 0.9 all-to-all-done.1.w_ref
  57.9 0.0 collective-permute-done.3.far_ref
  57.9 3.6 %merge_product.1 = bf16[8,64,512]{2,1,0:T(8,128)(2,1)} custom-call(s32[8]{0:T(128)S(1)} %fusion.14.spot_ref, bf16[192,1536]{1,0:T(8,128)(2,1)S(1)} %pad_maximum_fusion.1.near_ref, bf16[192,1536]{1,0:T(8,128)(2,1)S(1)} %collective-permute-done.3.far_ref, bf16[4,384,384]{2,1,0:T(8,128)(2,1)S(1)} %all-to-all-done.1.w_ref, bf16[512,384]{1,0:T(8,128)(2,1)S(1)} %copy-done.1), custom_call_target="tpu_custom_call" | custom-call | tf_op jit(solution)/shard_map/merge_product/pallas_call | solution.py:390
  61.4 5.5 %all-to-all-start.2 = ((bf16[8,64,512]{2,1,0:T(8,128)(2,1)}), bf16[8,64,512]{2,1,0:T(8,128)(2,1)S(1)}, u32[]{:S(2)}, u32[]{:S(2)}) async-start(bf16[8,64,512]{2,1,0:T(8,128)(2,1)} %merge_product.1), calls=%async_computation.2 | async-start | bytes 1048576 | tf_op jit(solution)/shard_map/all_to_all | solution.py:475
  67.0 0.9 copy-done.7
  67.8 6.3 %window_probs.1.p_ref = bf16[6,768,192]{2,1,0:T(8,128)(2,1)} custom-call(bf16[4,2,6,16,768]{4,3,2,1,0:T(8,128)(2,1)} %copy-done.6, bf16[4,2,4,16,768]{4,3,2,1,0:T(8,128)(2,1)} %copy-done.7, f32[6,48,384]{2,1,0:T(8,128)} %copy-done, bf16[2,384,192]{2,1,0:T(8,128)(2,1)} %constant.132.clone.spread_ref, f32[192,192]{1,0:T(8,128)} %and_select_fusion.mask_ref), custom_call_target="tpu_custom_call" | custom-call | tf_op jit(solution)/shard_map/window_probs/pallas_call | solution.py:372
  74.2 0.4 all-to-all-done.2.recv_ref
  74.6 0.8 copy-done.8
  75.4 6.7 %score_grads.1 = (bf16[6,192,128]{2,1,0:T(8,128)(2,1)}, bf16[16,56,128]{2,1,0:T(8,128)(2,1)}) custom-call(bf16[8,64,512]{2,1,0:T(8,128)(2,1)} %copy-done.8, bf16[512,384]{1,0:T(8,128)(2,1)} %constant.135.clone.shuffle_ref.order_ref, bf16[4,2,6,16,768]{4,3,2,1,0:T(8,128)(2,1)} %copy-done.6, bf16[4,2,6,16,768]{4,3,2,1,0:T(8,128)(2,1)} %copy-done.6, ...), custom_call_target="tpu_custom_call" | custom-call | tf_op jit(solution)/shard_map/score_grads/pallas_call | solution.py:402
  82.1 7.4 %all-to-all-start.3 = ((bf16[16,56,128]{2,1,0:T(8,128)(2,1)}), bf16[16,56,128]{2,1,0:T(8,128)(2,1)S(1)}, u32[]{:S(2)}, u32[]{:S(2)}) async-start(bf16[16,56,128]{2,1,0:T(8,128)(2,1)} %get-tuple-element.20), calls=%async_computation.3 | async-start | bytes 458752 | tf_op jit(solution)/shard_map/all_to_all | solution.py:475
  89.6 6.3 %window_grads.1 = bf16[3,192,768]{2,1,0:T(8,128)(2,1)} custom-call(bf16[4,2,6,16,768]{4,3,2,1,0:T(8,128)(2,1)} %copy-done.6, bf16[4,2,4,16,768]{4,3,2,1,0:T(8,128)(2,1)} %copy-done.7, bf16[6,192,128]{2,1,0:T(8,128)(2,1)} %get-tuple-element.21.o_ref, bf16[6,768,192]{2,1,0:T(8,128)(2,1)} %window_probs.1.p_ref), custom_call_target="tpu_custom_call" | custom-call | tf_op jit(solution)/shard_map/window_grads/pallas_call | solution.py:449
  95.9 1.4 fusion.15
  97.3 0.3 copy.56
  97.6 3.4 %collective-permute-start.6 = (bf16[3,2,6,6,768]{4,1,3,2,0:T(2,128)(2,1)S(1)}, bf16[3,2,6,6,768]{4,1,3,2,0:T(2,128)(2,1)S(1)}, u32[]{:S(2)}, u32[]{:S(2)}) collective-permute-start(bf16[3,2,6,6,768]{4,1,3,2,0:T(2,128)(2,1)S(1)} %copy.56), channel_id=1, source_target_pairs={{0,4},{4,8},{8,12},{12,16},{16,20},{20,24},{24,28},{28,32},{32,36}... | collective-permute-start | bytes 995336 | tf_op jit(solution)/shard_map/ppermute | solution.py:467
  101.0 0.0 all-to-all-done.3
  101.0 0.7 broadcast_in_dim.42
  101.7 6.6 %all-to-all-start.4 = ((bf16[8,56,128]{2,1,0:T(8,128)(2,1)}), bf16[8,56,128]{2,1,0:T(8,128)(2,1)S(1)}, u32[]{:S(2)}, u32[]{:S(2)}) async-start(bf16[8,56,128]{2,1,0:T(8,128)(2,1)} %broadcast_in_dim.42), calls=%async_computation.4 | async-start | bytes 229376 | tf_op jit(solution)/shard_map/all_to_all | solution.py:475
  108.2 0.3 copy.57
  108.5 5.4 %collective-permute-done.6 = bf16[3,2,6,6,768]{4,1,3,2,0:T(2,128)(2,1)S(1)} collective-permute-done((bf16[3,2,6,6,768]{4,1,3,2,0:T(2,128)(2,1)S(1)}, bf16[3,2,6,6,768]{4,1,3,2,0:T(2,128)(2,1)S(1)}, u32[]{:S(2)}, u32[]{:S(2)}) %collective-permute-start.6) | collective-permute-done | bytes 331808 | tf_op jit(solution)/shard_map/ppermute | solution.py:467
  113.9 0.9 pad_maximum_fusion
  114.7 9.4 %all-to-all-done.4 = bf16[8,56,128]{2,1,0:T(8,128)(2,1)S(1)} async-done(((bf16[8,56,128]{2,1,0:T(8,128)(2,1)}), bf16[8,56,128]{2,1,0:T(8,128)(2,1)S(1)}, u32[]{:S(2)}, u32[]{:S(2)}) %all-to-all-start.4) | async-done | bytes 114720 | tf_op jit(solution)/shard_map/all_to_all | solution.py:475
  124.1 0.7 broadcast_in_dim.43
  124.9 5.7 %all-to-all-start.5 = ((bf16[16,56,128]{2,1,0:T(8,128)(2,1)}), bf16[16,56,128]{2,1,0:T(8,128)(2,1)S(1)}, u32[]{:S(2)}, u32[]{:S(2)}) async-start(bf16[16,56,128]{2,1,0:T(8,128)(2,1)} %broadcast_in_dim.43), calls=%async_computation.5 | async-start | bytes 458752 | tf_op jit(solution)/shard_map/all_to_all | solution.py:475
  130.6 0.5 fusion.16
  131.1 1.9 %collective-permute-start.7 = (bf16[3,2,3,12,768]{4,1,3,2,0:T(2,128)(2,1)S(1)}, bf16[3,2,3,12,768]{4,1,3,2,0:T(2,128)(2,1)S(1)}, u32[]{:S(2)}, u32[]{:S(2)}) collective-permute-start(bf16[3,2,3,12,768]{4,1,3,2,0:T(2,128)(2,1)S(1)} %get-tuple-element.29), channel_id=1, source_target_pairs={{0,1},{1,2},{2,3},{3,0},{4,5},{5,6},{6,7},{7,4},{8,9},{9,10},{10,1... | collective-permute-start | bytes 995336 | tf_op jit(solution)/shard_map/ppermute | solution.py:467
  133.0 8.0 %collective-permute-done.7 = bf16[3,2,3,12,768]{4,1,3,2,0:T(2,128)(2,1)S(1)} collective-permute-done((bf16[3,2,3,12,768]{4,1,3,2,0:T(2,128)(2,1)S(1)}, bf16[3,2,3,12,768]{4,1,3,2,0:T(2,128)(2,1)S(1)}, u32[]{:S(2)}, u32[]{:S(2)}) %collective-permute-start.7) | collective-permute-done | bytes 331808 | tf_op jit(solution)/shard_map/ppermute | solution.py:467
  141.0 1.6 %fusion.2 = (bf16[2,6,12,768]{3,0,2,1:T(2,128)(2,1)}, bf16[2,6,12,768]{3,0,2,1:T(2,128)(2,1)}, bf16[2,6,12,768]{3,0,2,1:T(2,128)(2,1)}) fusion(bf16[3,2,3,12,768]{4,1,3,2,0:T(2,128)(2,1)S(1)} %get-tuple-element.30, bf16[3,2,3,12,768]{4,1,3,2,0:T(2,128)(2,1)S(1)} %collective-permute-done.7), kind=kLoop, calls=%fused_computation.12 | loop fusion | flops 331776 | bytes 1327104 | tf_op jit(solution)/shard_map/squeeze | solution.py:550
  142.6 0.0 all-to-all-done.5.parts_ref
  142.6 1.2 close_table.1
  (33 shorter events, 0.2 us)
Async XLA Ops:
  0.6 0.9 copy-start.5
  1.5 19.5 %copy-start.9 = (bf16[2,6,12,768]{3,0,2,1:T(2,128)(2,1)S(1)}, bf16[2,6,12,768]{3,0,2,1:T(2,128)(2,1)}, u32[]{:S(2)}) copy-start(bf16[2,6,12,768]{3,0,2,1:T(2,128)(2,1)} %param.22) | copy-start | bytes 663556
  1.5 19.5 %copy-start.10 = (bf16[2,6,12,768]{3,0,2,1:T(2,128)(2,1)S(1)}, bf16[2,6,12,768]{3,0,2,1:T(2,128)(2,1)}, u32[]{:S(2)}) copy-start(bf16[2,6,12,768]{3,0,2,1:T(2,128)(2,1)} %param.16) | copy-start | bytes 663556
  1.5 19.9 %copy-start.11 = (bf16[2,6,12,768]{3,0,2,1:T(2,128)(2,1)S(1)}, bf16[2,6,12,768]{3,0,2,1:T(2,128)(2,1)}, u32[]{:S(2)}) copy-start(bf16[2,6,12,768]{3,0,2,1:T(2,128)(2,1)} %param.20) | copy-start | bytes 663556
  1.5 19.9 %copy-start.12 = (bf16[2,6,12,768]{3,0,2,1:T(2,128)(2,1)S(1)}, bf16[2,6,12,768]{3,0,2,1:T(2,128)(2,1)}, u32[]{:S(2)}) copy-start(bf16[2,6,12,768]{3,0,2,1:T(2,128)(2,1)} %param.21) | copy-start | bytes 663556
  3.4 18.5 %collective-permute-start = (bf16[2,3,3,1536]{3,0,2,1:T(2,128)(2,1)S(1)}, bf16[2,3,3,1536]{3,0,2,1:T(2,128)(2,1)S(1)}, u32[]{:S(2)}, u32[]{:S(2)}) collective-permute-start(bf16[2,3,3,1536]{3,0,2,1:T(2,128)(2,1)S(1)} %get-tuple-element.40), channel_id=1, source_target_pairs={{0,508},{4,0},{8,4},{12,8},{16,12},{20,16},{24,20},{28,24},{32,28}... | collective-permute-start | bytes 165896 | tf_op jit(solution)/shard_map/ppermute | solution.py:467
  17.5 22.8 %all-to-all-start = ((bf16[16,24,384]{2,1,0:T(8,128)(2,1)}), bf16[16,24,384]{2,1,0:T(8,128)(2,1)S(1)}, u32[]{:S(2)}, u32[]{:S(2)}) async-start(bf16[16,24,384]{2,1,0:T(8,128)(2,1)} %pack_weight.1), calls=%async_computation | async-start | bytes 589824 | tf_op jit(solution)/shard_map/all_to_all | solution.py:475
  22.1 11.2 %collective-permute-start.1 = (bf16[48,1536]{1,0:T(8,128)(2,1)S(1)}, bf16[48,1536]{1,0:T(8,128)(2,1)S(1)}, u32[]{:S(2)}, u32[]{:S(2)}) collective-permute-start(bf16[48,1536]{1,0:T(8,128)(2,1)S(1)} %bitcast.32), channel_id=1, source_target_pairs={{0,2},{1,3},{2,0},{3,1},{4,6},{5,7},{6,4},{7,5},{8,10},{9,11},{10,... | collective-permute-start | bytes 442376 | tf_op jit(solution)/shard_map/ppermute | solution.py:471
  26.4 21.8 %collective-permute-start.4 = (bf16[4,2,6,6,768]{4,0,3,2,1:T(4,128)(2,1)S(1)}, bf16[4,2,6,6,768]{4,0,3,2,1:T(4,128)(2,1)S(1)}, u32[]{:S(2)}, u32[]{:S(2)}) collective-permute-start(bf16[4,2,6,6,768]{4,0,3,2,1:T(4,128)(2,1)S(1)} %copy.48), channel_id=1, source_target_pairs={{0,508},{4,0},{8,4},{12,8},{16,12},{20,16},{24,20},{28,24},{32,28}... | collective-permute-start | bytes 1327112 | tf_op jit(solution)/shard_map/ppermute | solution.py:467
  34.0 14.2 %collective-permute-start.2 = (bf16[96,1536]{1,0:T(8,128)(2,1)}, bf16[96,1536]{1,0:T(8,128)(2,1)}, u32[]{:S(2)}, u32[]{:S(2)}) collective-permute-start(bf16[96,1536]{1,0:T(8,128)(2,1)} %pad_maximum_fusion.3), channel_id=1, source_target_pairs={{0,256},{4,260},{8,264},{12,268},{16,272},{20,276},{24,280},{28,28... | collective-permute-start | bytes 884744 | tf_op jit(solution)/shard_map/ppermute | solution.py:471
  41.4 5.3 %copy-start.3 = (f32[1,24,3312]{2,1,0:T(8,128)S(1)}, f32[1,24,3312]{2,1,0:T(8,128)}, u32[]{:S(2)}) copy-start(f32[1,24,3312]{2,1,0:T(8,128)} %table_ref.1) | copy-start | bytes 953860
  41.4 5.3 %copy-start.4 = (bf16[2,138,384]{2,1,0:T(8,128)(2,1)S(1)}, bf16[2,138,384]{2,1,0:T(8,128)(2,1)}, u32[]{:S(2)}) copy-start(bf16[2,138,384]{2,1,0:T(8,128)(2,1)} %constant.136.clone.open_ref) | copy-start | bytes 635908
  41.4 16.4 %all-to-all-start.1 = ((bf16[4,384,384]{2,1,0:T(8,128)(2,1)}), bf16[4,384,384]{2,1,0:T(8,128)(2,1)S(1)}, u32[]{:S(2)}, u32[]{:S(2)}) async-start(bf16[4,384,384]{2,1,0:T(8,128)(2,1)} %broadcast_in_dim.38), calls=%async_computation.1 | async-start | bytes 2359296 | tf_op jit(solution)/shard_map/all_to_all | solution.py:475
  47.4 0.8 copy-start
  49.2 8.6 %collective-permute-start.3 = (bf16[192,1536]{1,0:T(8,128)(2,1)S(1)}, bf16[192,1536]{1,0:T(8,128)(2,1)S(1)}, u32[]{:S(2)}, u32[]{:S(2)}) collective-permute-start(bf16[192,1536]{1,0:T(8,128)(2,1)S(1)} %pad_maximum_fusion.1.near_ref), channel_id=1, source_target_pairs={{0,1},{1,0},{2,3},{3,2},{4,5},{5,4},{6,7},{7,6},{8,9},{9,8},{10,11... | collective-permute-start | bytes 1769480 | tf_op jit(solution)/shard_map/ppermute | solution.py:471
  51.7 4.4 %copy-start.6 = (bf16[4,2,6,16,768]{4,3,2,1,0:T(8,128)(2,1)}, bf16[4,2,6,16,768]{4,3,2,1,0:T(8,128)(2,1)S(1)}, u32[]{:S(2)}) copy-start(bf16[4,2,6,16,768]{4,3,2,1,0:T(8,128)(2,1)S(1)} %maximum_maximum_fusion.north_ref.y_a_ref.y_b_ref) | copy-start | bytes 3538948
  51.7 4.4 %copy-start.13 = (pred[192]{0:T(512)(128)(4,1)S(1)}, pred[192]{0:T(512)(128)(4,1)}, u32[]{:S(2)}) copy-start(pred[192]{0:T(512)(128)(4,1)} %get-tuple-element.41) | copy-start | bytes 580
  51.7 6.1 %copy-start.1 = (bf16[512,384]{1,0:T(8,128)(2,1)S(1)}, bf16[512,384]{1,0:T(8,128)(2,1)}, u32[]{:S(2)}) copy-start(bf16[512,384]{1,0:T(8,128)(2,1)} %constant.135.clone.shuffle_ref.order_ref) | copy-start | bytes 1179652
  52.7 14.3 %collective-permute-start.5 = (bf16[4,2,4,16,768]{4,3,2,1,0:T(8,128)(2,1)}, bf16[4,2,4,16,768]{4,3,2,1,0:T(8,128)(2,1)S(1)}, u32[]{:S(2)}, u32[]{:S(2)}) collective-permute-start(bf16[4,2,4,16,768]{4,3,2,1,0:T(8,128)(2,1)} %slice.75), channel_id=1, source_target_pairs={{0,3},{1,0},{2,1},{3,2},{4,7},{5,4},{6,5},{7,6},{8,11},{9,8},{10,9... | collective-permute-start | bytes 2359304 | tf_op jit(solution)/shard_map/ppermute | solution.py:467
  61.4 13.2 %all-to-all-start.2 = ((bf16[8,64,512]{2,1,0:T(8,128)(2,1)}), bf16[8,64,512]{2,1,0:T(8,128)(2,1)S(1)}, u32[]{:S(2)}, u32[]{:S(2)}) async-start(bf16[8,64,512]{2,1,0:T(8,128)(2,1)} %merge_product.1), calls=%async_computation.2 | async-start | bytes 1048576 | tf_op jit(solution)/shard_map/all_to_all | solution.py:475
  66.9 0.9 copy-start.7
  74.6 0.8 copy-start.8
  82.1 18.8 %all-to-all-start.3 = ((bf16[16,56,128]{2,1,0:T(8,128)(2,1)}), bf16[16,56,128]{2,1,0:T(8,128)(2,1)S(1)}, u32[]{:S(2)}, u32[]{:S(2)}) async-start(bf16[16,56,128]{2,1,0:T(8,128)(2,1)} %get-tuple-element.20), calls=%async_computation.3 | async-start | bytes 458752 | tf_op jit(solution)/shard_map/all_to_all | solution.py:475
  97.6 16.3 %collective-permute-start.6 = (bf16[3,2,6,6,768]{4,1,3,2,0:T(2,128)(2,1)S(1)}, bf16[3,2,6,6,768]{4,1,3,2,0:T(2,128)(2,1)S(1)}, u32[]{:S(2)}, u32[]{:S(2)}) collective-permute-start(bf16[3,2,6,6,768]{4,1,3,2,0:T(2,128)(2,1)S(1)} %copy.56), channel_id=1, source_target_pairs={{0,4},{4,8},{8,12},{12,16},{16,20},{20,24},{24,28},{28,32},{32,36}... | collective-permute-start | bytes 995336 | tf_op jit(solution)/shard_map/ppermute | solution.py:467
  101.7 22.4 %all-to-all-start.4 = ((bf16[8,56,128]{2,1,0:T(8,128)(2,1)}), bf16[8,56,128]{2,1,0:T(8,128)(2,1)S(1)}, u32[]{:S(2)}, u32[]{:S(2)}) async-start(bf16[8,56,128]{2,1,0:T(8,128)(2,1)} %broadcast_in_dim.42), calls=%async_computation.4 | async-start | bytes 229376 | tf_op jit(solution)/shard_map/all_to_all | solution.py:475
  124.9 17.8 %all-to-all-start.5 = ((bf16[16,56,128]{2,1,0:T(8,128)(2,1)}), bf16[16,56,128]{2,1,0:T(8,128)(2,1)S(1)}, u32[]{:S(2)}, u32[]{:S(2)}) async-start(bf16[16,56,128]{2,1,0:T(8,128)(2,1)} %broadcast_in_dim.43), calls=%async_computation.5 | async-start | bytes 458752 | tf_op jit(solution)/shard_map/all_to_all | solution.py:475
  130.6 12.0 %copy-start.2 = (bf16[384,512]{1,0:T(8,128)(2,1)S(1)}, bf16[384,512]{1,0:T(8,128)(2,1)}, u32[]{:S(2)}) copy-start(bf16[384,512]{1,0:T(8,128)(2,1)} %constant.137.clone.close_ref) | copy-start | bytes 1179652
  131.1 9.9 %collective-permute-start.7 = (bf16[3,2,3,12,768]{4,1,3,2,0:T(2,128)(2,1)S(1)}, bf16[3,2,3,12,768]{4,1,3,2,0:T(2,128)(2,1)S(1)}, u32[]{:S(2)}, u32[]{:S(2)}) collective-permute-start(bf16[3,2,3,12,768]{4,1,3,2,0:T(2,128)(2,1)S(1)} %get-tuple-element.29), channel_id=1, source_target_pairs={{0,1},{1,2},{2,3},{3,0},{4,5},{5,6},{6,7},{7,4},{8,9},{9,10},{10,1... | collective-permute-start | bytes 995336 | tf_op jit(solution)/shard_map/ppermute | solution.py:467

commit v11 on v10

--- a/solution.py
+++ b/solution.py
@@ -538,14 +538,16 @@
     table_part = jnp.sum(table_part, axis=0).astype(jnp.bfloat16)
     grads = window_grads(across, south, o_win, probs)
     grid = grads.reshape(3, 2, 6, PAD, 768)[:, :, :, :12]
-    western = from_behind(grid[:, :, :, 6:], "lon", 1)
-    fixed = jnp.concatenate([western, grid[:, :, :, :6]], axis=3)
+    own, other = grid[:, :, :, :6], grid[:, :, :, 6:]
+    table_part, own, other = lax.optimization_barrier((table_part, own, other))
+    western = from_behind(other, "lon", 1)
+    fixed = jnp.concatenate([western, own], axis=3)
+    southern = from_behind(fixed[:, :, 3:], "lat", 1)
 
     table_part = share(table_part, NZ // 2, "lon", far_groups)
-    table_part, fixed = lax.optimization_barrier((table_part, fixed))
-    southern = from_behind(fixed[:, :, 3:], "lat", 1)
+    table_part, southern = lax.optimization_barrier((table_part, southern))
+    finished = jnp.concatenate([southern, fixed[:, :, :3]], axis=2)
     table_part = jnp.sum(table_part.astype(jnp.float32), axis=0).astype(jnp.bfloat16)
-    finished = jnp.concatenate([southern, fixed[:, :, :3]], axis=2)
     table_grad = close_table(share(table_part, 16, "lon", near_groups), close)
     return (finished[0], finished[1], finished[2], table_grad)
 

time: 145 us -> 140 us (0.966)
  waiting for transfers between devices: 26.4 us -> 22.3 us
    ppermute x5, waiting for transfers between devices: 13.4 us -> 6.56 us  [from_behind(): lax.ppermute(shard, axis, [(i, (i + by) % size) for i in range(size)])]
    all_to_all x6, waiting for transfers between devices: 13.1 us -> 15.7 us  [swap(): lax.all_to_all(shard, axis, 0, 0, tiled=True, axis_index_groups=groups)]
    unnamed x34 -> x33, local copies, waits for them, and re-layouts: 3.95 us -> 3.66 us
  transfers between devices with their start and end apart: 14 -> 14, of which waited for: 6 -> 7; matrix products, arithmetic and copies ran while one was open for 9% -> 9% of each run, Pallas kernels for 12% -> 12%
where the time goes in v11:
time: 140 us; the launch traced here: 139 us
  starting transfers between devices  71.6 us (51%)
  Pallas kernels  25.7 us (18%)
  waiting for transfers between devices  22.3 us (16%)
  local copies, waits for them, and re-layouts  11.8 us (8%)
  other arithmetic  6.27 us (4%)
    all_to_all x6, starting transfers between devices, swap(): lax.all_to_all(shard, axis, 0, 0, tiled=True, axis_index_groups=groups)  32.6 us
    ppermute x5, starting transfers between devices, from_behind(): lax.ppermute(shard, axis, [(i, (i + by) % size) for i in range(size)])  29.8 us
    all_to_all x6, waiting for transfers between devices, swap(): lax.all_to_all(shard, axis, 0, 0, tiled=True, axis_index_groups=groups)  15.7 us
    ppermute x3, starting transfers between devices, partner(): lax.ppermute(shard, axis, [(i, i ^ bit) for i in range(lax.axis_size(axis...  9.22 us
    pallas_call x1, Pallas kernels, score_grads(): pl.pallas_call(scores_kernel, grid=(1,), in_specs=[whole_spec((8, 64, 512...  6.72 us
    ppermute x5, waiting for transfers between devices, from_behind(): lax.ppermute(shard, axis, [(i, (i + by) % size) for i in range(size)])  6.56 us
    pallas_call x1, Pallas kernels, window_grads(): pl.pallas_call(grads_kernel, grid=(STEPS,), in_specs=[north_spec(0, 3), s...  6.34 us
    pallas_call x1, Pallas kernels, window_probs(): pl.pallas_call(probs_kernel, grid=(STEPS,), in_specs=[north_spec(0, 2), s...  6.33 us
  transfers between devices with their start and end apart: 14, of which 7 were waited for; matrix products, arithmetic and copies ran while one was open for 9% of the time, Pallas kernels for 12%

profile of v11, /device:TPU:6, one launch (start us, length us, event | category | flops | bytes accessed | tf_op | source)
XLA Modules:
  0.0 138.6 jit_solution(10216319722026207084)
XLA Ops:
  0.6 0.9 copy-done.5
  1.5 0.9 pack_weight.1
  2.4 0.9 fusion.21
  3.4 14.1 %collective-permute-start = (bf16[2,3,3,1536]{3,0,2,1:T(2,128)(2,1)S(1)}, bf16[2,3,3,1536]{3,0,2,1:T(2,128)(2,1)S(1)}, u32[]{:S(2)}, u32[]{:S(2)}) collective-permute-start(bf16[2,3,3,1536]{3,0,2,1:T(2,128)(2,1)S(1)} %get-tuple-element.46), channel_id=1, source_target_pairs={{0,508},{4,0},{8,4},{12,8},{16,12},{20,16},{24,20},{28,24},{32,28}... | collective-permute-start | bytes 165896 | tf_op jit(solution)/shard_map/ppermute | solution.py:467
  17.5 3.6 %all-to-all-start = ((bf16[16,24,384]{2,1,0:T(8,128)(2,1)}), bf16[16,24,384]{2,1,0:T(8,128)(2,1)S(1)}, u32[]{:S(2)}, u32[]{:S(2)}) async-start(bf16[16,24,384]{2,1,0:T(8,128)(2,1)} %pack_weight.1), calls=%async_computation | async-start | bytes 589824 | tf_op jit(solution)/shard_map/all_to_all | solution.py:475
  21.1 0.3 fusion.19
  21.4 0.3 fusion.17
  21.8 0.1 pad.19.clone
  21.8 0.0 collective-permute-done
  21.8 0.2 maximum_maximum_fusion.1
  22.1 3.3 %collective-permute-start.1 = (bf16[48,1536]{1,0:T(8,128)(2,1)S(1)}, bf16[48,1536]{1,0:T(8,128)(2,1)S(1)}, u32[]{:S(2)}, u32[]{:S(2)}) collective-permute-start(bf16[48,1536]{1,0:T(8,128)(2,1)S(1)} %bitcast.32), channel_id=1, source_target_pairs={{0,2},{1,3},{2,0},{3,1},{4,6},{5,7},{6,4},{7,5},{8,10},{9,11},{10,... | collective-permute-start | bytes 442376 | tf_op jit(solution)/shard_map/ppermute | solution.py:471
  25.4 0.8 pad_maximum_fusion.1
  26.2 0.2 copy.48
  26.4 6.9 %collective-permute-start.4 = (bf16[4,2,6,6,768]{4,0,3,2,1:T(4,128)(2,1)S(1)}, bf16[4,2,6,6,768]{4,0,3,2,1:T(4,128)(2,1)S(1)}, u32[]{:S(2)}, u32[]{:S(2)}) collective-permute-start(bf16[4,2,6,6,768]{4,0,3,2,1:T(4,128)(2,1)S(1)} %copy.48), channel_id=1, source_target_pairs={{0,508},{4,0},{8,4},{12,8},{16,12},{20,16},{24,20},{28,24},{32,28}... | collective-permute-start | bytes 1327112 | tf_op jit(solution)/shard_map/ppermute | solution.py:467
  33.2 0.0 collective-permute-done.1
  33.2 0.7 pad_maximum_fusion.2
  34.0 4.0 %collective-permute-start.2 = (bf16[96,1536]{1,0:T(8,128)(2,1)}, bf16[96,1536]{1,0:T(8,128)(2,1)}, u32[]{:S(2)}, u32[]{:S(2)}) collective-permute-start(bf16[96,1536]{1,0:T(8,128)(2,1)} %pad_maximum_fusion.2), channel_id=1, source_target_pairs={{0,256},{4,260},{8,264},{12,268},{16,272},{20,276},{24,280},{28,28... | collective-permute-start | bytes 884744 | tf_op jit(solution)/shard_map/ppermute | solution.py:471
  38.0 2.3 %all-to-all-done = bf16[16,24,384]{2,1,0:T(8,128)(2,1)S(1)} async-done(((bf16[16,24,384]{2,1,0:T(8,128)(2,1)}), bf16[16,24,384]{2,1,0:T(8,128)(2,1)S(1)}, u32[]{:S(2)}, u32[]{:S(2)}) %all-to-all-start) | async-done | bytes 294944 | tf_op jit(solution)/shard_map/all_to_all | solution.py:475
  40.3 1.1 broadcast_in_dim.38
  41.4 4.6 %all-to-all-start.1 = ((bf16[4,384,384]{2,1,0:T(8,128)(2,1)}), bf16[4,384,384]{2,1,0:T(8,128)(2,1)S(1)}, u32[]{:S(2)}, u32[]{:S(2)}) async-start(bf16[4,384,384]{2,1,0:T(8,128)(2,1)} %broadcast_in_dim.38), calls=%async_computation.1 | async-start | bytes 2359296 | tf_op jit(solution)/shard_map/all_to_all | solution.py:475
  46.0 0.5 fusion.7
  46.7 0.1 pad.7.clone
  46.8 0.6 open_table.1.table_ref
  47.4 0.8 copy-done
  48.2 0.0 collective-permute-done.4
  48.2 0.1 copy.49
  48.2 1.0 pad_maximum_fusion.near_ref
  49.2 1.9 %collective-permute-start.3 = (bf16[192,1536]{1,0:T(8,128)(2,1)S(1)}, bf16[192,1536]{1,0:T(8,128)(2,1)S(1)}, u32[]{:S(2)}, u32[]{:S(2)}) collective-permute-start(bf16[192,1536]{1,0:T(8,128)(2,1)S(1)} %pad_maximum_fusion.near_ref), channel_id=1, source_target_pairs={{0,1},{1,0},{2,3},{3,2},{4,5},{5,4},{6,7},{7,6},{8,9},{9,8},{10,11... | collective-permute-start | bytes 1769480 | tf_op jit(solution)/shard_map/ppermute | solution.py:471
  51.2 0.5 maximum_maximum_fusion.north_ref.y_a_ref.y_b_ref
  51.7 0.0 copy-start.13
  51.7 0.0 copy-start.1
  51.7 0.9 slice.75
  52.7 3.4 %collective-permute-start.5 = (bf16[4,2,4,16,768]{4,3,2,1,0:T(8,128)(2,1)}, bf16[4,2,4,16,768]{4,3,2,1,0:T(8,128)(2,1)S(1)}, u32[]{:S(2)}, u32[]{:S(2)}) collective-permute-start(bf16[4,2,4,16,768]{4,3,2,1,0:T(8,128)(2,1)} %slice.75), channel_id=1, source_target_pairs={{0,3},{1,0},{2,1},{3,2},{4,7},{5,4},{6,5},{7,6},{8,11},{9,8},{10,9... | collective-permute-start | bytes 2359304 | tf_op jit(solution)/shard_map/ppermute | solution.py:467
  56.1 0.8 and_select_fusion.mask_ref
  56.9 0.9 all-to-all-done.1.w_ref
  57.9 0.0 collective-permute-done.3.far_ref
  57.9 3.6 %merge_product.1 = bf16[8,64,512]{2,1,0:T(8,128)(2,1)} custom-call(s32[8]{0:T(128)S(1)} %fusion.14.spot_ref, bf16[192,1536]{1,0:T(8,128)(2,1)S(1)} %pad_maximum_fusion.near_ref, bf16[192,1536]{1,0:T(8,128)(2,1)S(1)} %collective-permute-done.3.far_ref, bf16[4,384,384]{2,1,0:T(8,128)(2,1)S(1)} %all-to-all-done.1.w_ref, bf16[512,384]{1,0:T(8,128)(2,1)S(1)} %copy-done.1), custom_call_target="tpu_custom_call" | custom-call | tf_op jit(solution)/shard_map/merge_product/pallas_call | solution.py:390
  61.4 5.5 %all-to-all-start.2 = ((bf16[8,64,512]{2,1,0:T(8,128)(2,1)}), bf16[8,64,512]{2,1,0:T(8,128)(2,1)S(1)}, u32[]{:S(2)}, u32[]{:S(2)}) async-start(bf16[8,64,512]{2,1,0:T(8,128)(2,1)} %merge_product.1), calls=%async_computation.2 | async-start | bytes 1048576 | tf_op jit(solution)/shard_map/all_to_all | solution.py:475
  67.0 0.9 copy-done.7
  67.8 6.3 %window_probs.1.p_ref = bf16[6,768,192]{2,1,0:T(8,128)(2,1)} custom-call(bf16[4,2,6,16,768]{4,3,2,1,0:T(8,128)(2,1)} %copy-done.6, bf16[4,2,4,16,768]{4,3,2,1,0:T(8,128)(2,1)} %copy-done.7, f32[6,48,384]{2,1,0:T(8,128)} %copy-done, bf16[2,384,192]{2,1,0:T(8,128)(2,1)} %constant.132.clone.spread_ref, f32[192,192]{1,0:T(8,128)} %and_select_fusion.mask_ref), custom_call_target="tpu_custom_call" | custom-call | tf_op jit(solution)/shard_map/window_probs/pallas_call | solution.py:372
  74.2 0.4 all-to-all-done.2.recv_ref
  74.6 0.8 copy-done.8
  75.4 6.7 %score_grads.1 = (bf16[6,192,128]{2,1,0:T(8,128)(2,1)}, bf16[16,56,128]{2,1,0:T(8,128)(2,1)}) custom-call(bf16[8,64,512]{2,1,0:T(8,128)(2,1)} %copy-done.8, bf16[512,384]{1,0:T(8,128)(2,1)} %constant.135.clone.shuffle_ref.order_ref, bf16[4,2,6,16,768]{4,3,2,1,0:T(8,128)(2,1)} %copy-done.6, bf16[4,2,6,16,768]{4,3,2,1,0:T(8,128)(2,1)} %copy-done.6, ...), custom_call_target="tpu_custom_call" | custom-call | tf_op jit(solution)/shard_map/score_grads/pallas_call | solution.py:402
  82.1 7.4 %all-to-all-start.3 = ((bf16[16,56,128]{2,1,0:T(8,128)(2,1)}), bf16[16,56,128]{2,1,0:T(8,128)(2,1)S(1)}, u32[]{:S(2)}, u32[]{:S(2)}) async-start(bf16[16,56,128]{2,1,0:T(8,128)(2,1)} %get-tuple-element.23), calls=%async_computation.3 | async-start | bytes 458752 | tf_op jit(solution)/shard_map/all_to_all | solution.py:475
  89.6 6.3 %window_grads.1 = bf16[3,192,768]{2,1,0:T(8,128)(2,1)} custom-call(bf16[4,2,6,16,768]{4,3,2,1,0:T(8,128)(2,1)} %copy-done.6, bf16[4,2,4,16,768]{4,3,2,1,0:T(8,128)(2,1)} %copy-done.7, bf16[6,192,128]{2,1,0:T(8,128)(2,1)} %get-tuple-element.24.o_ref, bf16[6,768,192]{2,1,0:T(8,128)(2,1)} %window_probs.1.p_ref), custom_call_target="tpu_custom_call" | custom-call | tf_op jit(solution)/shard_map/window_grads/pallas_call | solution.py:449
  95.9 1.4 %fusion.15 = (bf16[3,2,6,6,768]{4,3,2,1,0:T(8,128)(2,1)S(1)}, bf16[3,2,6,6,768]{4,3,2,1,0:T(8,128)(2,1)S(1)}) fusion(bf16[3,2,6,16,768]{4,3,2,1,0:T(8,128)(2,1)} %bitcast.31), kind=kLoop, calls=%fused_computation.53 | loop fusion | bytes 1327104 | tf_op jit(solution)/shard_map/slice | solution.py:541
  97.3 0.3 copy.56
  97.6 0.3 copy.57
  97.9 3.4 %collective-permute-start.6 = (bf16[3,2,6,6,768]{4,1,3,2,0:T(2,128)(2,1)S(1)}, bf16[3,2,6,6,768]{4,1,3,2,0:T(2,128)(2,1)S(1)}, u32[]{:S(2)}, u32[]{:S(2)}) collective-permute-start(bf16[3,2,6,6,768]{4,1,3,2,0:T(2,128)(2,1)S(1)} %copy.57), channel_id=1, source_target_pairs={{0,4},{4,8},{8,12},{12,16},{16,20},{20,24},{24,28},{28,32},{32,36}... | collective-permute-start | bytes 995336 | tf_op jit(solution)/shard_map/ppermute | solution.py:467
  101.3 0.7 broadcast_in_dim.42
  101.9 6.6 %all-to-all-start.4 = ((bf16[8,56,128]{2,1,0:T(8,128)(2,1)}), bf16[8,56,128]{2,1,0:T(8,128)(2,1)S(1)}, u32[]{:S(2)}, u32[]{:S(2)}) async-start(bf16[8,56,128]{2,1,0:T(8,128)(2,1)} %broadcast_in_dim.42), calls=%async_computation.4 | async-start | bytes 229376 | tf_op jit(solution)/shard_map/all_to_all | solution.py:475
  108.5 5.7 %collective-permute-done.6 = bf16[3,2,6,6,768]{4,1,3,2,0:T(2,128)(2,1)S(1)} collective-permute-done((bf16[3,2,6,6,768]{4,1,3,2,0:T(2,128)(2,1)S(1)}, bf16[3,2,6,6,768]{4,1,3,2,0:T(2,128)(2,1)S(1)}, u32[]{:S(2)}, u32[]{:S(2)}) %collective-permute-start.6) | collective-permute-done | bytes 331808 | tf_op jit(solution)/shard_map/ppermute | solution.py:467
  114.2 0.2 constant_dynamic-update-slice_fusion.1
  114.4 0.3 constant_dynamic-update-slice_fusion
  114.7 0.5 fusion.16
  115.2 0.0 copy-start.2
  115.2 2.1 %collective-permute-start.7 = (bf16[3,2,3,12,768]{4,1,3,2,0:T(2,128)(2,1)S(1)}, bf16[3,2,3,12,768]{4,1,3,2,0:T(2,128)(2,1)S(1)}, u32[]{:S(2)}, u32[]{:S(2)}) collective-permute-start(bf16[3,2,3,12,768]{4,1,3,2,0:T(2,128)(2,1)S(1)} %get-tuple-element.35), channel_id=1, source_target_pairs={{0,1},{1,2},{2,3},{3,0},{4,5},{5,6},{6,7},{7,4},{8,9},{9,10},{10,1... | collective-permute-start | bytes 995336 | tf_op jit(solution)/shard_map/ppermute | solution.py:467
  117.2 7.1 %all-to-all-done.4 = bf16[8,56,128]{2,1,0:T(8,128)(2,1)S(1)} async-done(((bf16[8,56,128]{2,1,0:T(8,128)(2,1)}), bf16[8,56,128]{2,1,0:T(8,128)(2,1)S(1)}, u32[]{:S(2)}, u32[]{:S(2)}) %all-to-all-start.4) | async-done | bytes 114720 | tf_op jit(solution)/shard_map/all_to_all | solution.py:475
  124.4 0.9 collective-permute-done.7
  125.3 0.7 broadcast_in_dim.43
  126.0 4.9 %all-to-all-start.5 = ((bf16[16,56,128]{2,1,0:T(8,128)(2,1)}), bf16[16,56,128]{2,1,0:T(8,128)(2,1)S(1)}, u32[]{:S(2)}, u32[]{:S(2)}) async-start(bf16[16,56,128]{2,1,0:T(8,128)(2,1)} %broadcast_in_dim.43), calls=%async_computation.5 | async-start | bytes 458752 | tf_op jit(solution)/shard_map/all_to_all | solution.py:475
  130.9 1.6 %fusion.2 = (bf16[2,6,12,768]{3,0,2,1:T(2,128)(2,1)}, bf16[2,6,12,768]{3,0,2,1:T(2,128)(2,1)}, bf16[2,6,12,768]{3,0,2,1:T(2,128)(2,1)}) fusion(bf16[3,2,3,12,768]{4,1,3,2,0:T(2,128)(2,1)S(1)} %get-tuple-element.36, bf16[3,2,3,12,768]{4,1,3,2,0:T(2,128)(2,1)S(1)} %collective-permute-done.7), kind=kLoop, calls=%fused_computation.11 | loop fusion | flops 331776 | bytes 1327104 | tf_op jit(solution)/shard_map/squeeze | solution.py:552
  132.5 4.9 %all-to-all-done.5.parts_ref = bf16[16,56,128]{2,1,0:T(8,128)(2,1)S(1)} async-done(((bf16[16,56,128]{2,1,0:T(8,128)(2,1)}), bf16[16,56,128]{2,1,0:T(8,128)(2,1)S(1)}, u32[]{:S(2)}, u32[]{:S(2)}) %all-to-all-start.5) | async-done | bytes 229408 | tf_op jit(solution)/shard_map/all_to_all | solution.py:475
  137.4 1.2 close_table.1
  (34 shorter events, 0.2 us)
Async XLA Ops:
  0.6 0.9 copy-start.5
  1.5 19.5 %copy-start.9 = (bf16[2,6,12,768]{3,0,2,1:T(2,128)(2,1)S(1)}, bf16[2,6,12,768]{3,0,2,1:T(2,128)(2,1)}, u32[]{:S(2)}) copy-start(bf16[2,6,12,768]{3,0,2,1:T(2,128)(2,1)} %param.22) | copy-start | bytes 663556
  1.5 19.5 %copy-start.10 = (bf16[2,6,12,768]{3,0,2,1:T(2,128)(2,1)S(1)}, bf16[2,6,12,768]{3,0,2,1:T(2,128)(2,1)}, u32[]{:S(2)}) copy-start(bf16[2,6,12,768]{3,0,2,1:T(2,128)(2,1)} %param.16) | copy-start | bytes 663556
  1.5 19.9 %copy-start.11 = (bf16[2,6,12,768]{3,0,2,1:T(2,128)(2,1)S(1)}, bf16[2,6,12,768]{3,0,2,1:T(2,128)(2,1)}, u32[]{:S(2)}) copy-start(bf16[2,6,12,768]{3,0,2,1:T(2,128)(2,1)} %param.20) | copy-start | bytes 663556
  1.5 19.9 %copy-start.12 = (bf16[2,6,12,768]{3,0,2,1:T(2,128)(2,1)S(1)}, bf16[2,6,12,768]{3,0,2,1:T(2,128)(2,1)}, u32[]{:S(2)}) copy-start(bf16[2,6,12,768]{3,0,2,1:T(2,128)(2,1)} %param.21) | copy-start | bytes 663556
  3.4 18.5 %collective-permute-start = (bf16[2,3,3,1536]{3,0,2,1:T(2,128)(2,1)S(1)}, bf16[2,3,3,1536]{3,0,2,1:T(2,128)(2,1)S(1)}, u32[]{:S(2)}, u32[]{:S(2)}) collective-permute-start(bf16[2,3,3,1536]{3,0,2,1:T(2,128)(2,1)S(1)} %get-tuple-element.46), channel_id=1, source_target_pairs={{0,508},{4,0},{8,4},{12,8},{16,12},{20,16},{24,20},{28,24},{32,28}... | collective-permute-start | bytes 165896 | tf_op jit(solution)/shard_map/ppermute | solution.py:467
  17.5 22.8 %all-to-all-start = ((bf16[16,24,384]{2,1,0:T(8,128)(2,1)}), bf16[16,24,384]{2,1,0:T(8,128)(2,1)S(1)}, u32[]{:S(2)}, u32[]{:S(2)}) async-start(bf16[16,24,384]{2,1,0:T(8,128)(2,1)} %pack_weight.1), calls=%async_computation | async-start | bytes 589824 | tf_op jit(solution)/shard_map/all_to_all | solution.py:475
  22.1 11.2 %collective-permute-start.1 = (bf16[48,1536]{1,0:T(8,128)(2,1)S(1)}, bf16[48,1536]{1,0:T(8,128)(2,1)S(1)}, u32[]{:S(2)}, u32[]{:S(2)}) collective-permute-start(bf16[48,1536]{1,0:T(8,128)(2,1)S(1)} %bitcast.32), channel_id=1, source_target_pairs={{0,2},{1,3},{2,0},{3,1},{4,6},{5,7},{6,4},{7,5},{8,10},{9,11},{10,... | collective-permute-start | bytes 442376 | tf_op jit(solution)/shard_map/ppermute | solution.py:471
  26.4 21.8 %collective-permute-start.4 = (bf16[4,2,6,6,768]{4,0,3,2,1:T(4,128)(2,1)S(1)}, bf16[4,2,6,6,768]{4,0,3,2,1:T(4,128)(2,1)S(1)}, u32[]{:S(2)}, u32[]{:S(2)}) collective-permute-start(bf16[4,2,6,6,768]{4,0,3,2,1:T(4,128)(2,1)S(1)} %copy.48), channel_id=1, source_target_pairs={{0,508},{4,0},{8,4},{12,8},{16,12},{20,16},{24,20},{28,24},{32,28}... | collective-permute-start | bytes 1327112 | tf_op jit(solution)/shard_map/ppermute | solution.py:467
  34.0 14.2 %collective-permute-start.2 = (bf16[96,1536]{1,0:T(8,128)(2,1)}, bf16[96,1536]{1,0:T(8,128)(2,1)}, u32[]{:S(2)}, u32[]{:S(2)}) collective-permute-start(bf16[96,1536]{1,0:T(8,128)(2,1)} %pad_maximum_fusion.2), channel_id=1, source_target_pairs={{0,256},{4,260},{8,264},{12,268},{16,272},{20,276},{24,280},{28,28... | collective-permute-start | bytes 884744 | tf_op jit(solution)/shard_map/ppermute | solution.py:471
  41.4 5.3 %copy-start.3 = (f32[1,24,3312]{2,1,0:T(8,128)S(1)}, f32[1,24,3312]{2,1,0:T(8,128)}, u32[]{:S(2)}) copy-start(f32[1,24,3312]{2,1,0:T(8,128)} %table_ref.1) | copy-start | bytes 953860
  41.4 5.3 %copy-start.4 = (bf16[2,138,384]{2,1,0:T(8,128)(2,1)S(1)}, bf16[2,138,384]{2,1,0:T(8,128)(2,1)}, u32[]{:S(2)}) copy-start(bf16[2,138,384]{2,1,0:T(8,128)(2,1)} %constant.136.clone.open_ref) | copy-start | bytes 635908
  41.4 16.4 %all-to-all-start.1 = ((bf16[4,384,384]{2,1,0:T(8,128)(2,1)}), bf16[4,384,384]{2,1,0:T(8,128)(2,1)S(1)}, u32[]{:S(2)}, u32[]{:S(2)}) async-start(bf16[4,384,384]{2,1,0:T(8,128)(2,1)} %broadcast_in_dim.38), calls=%async_computation.1 | async-start | bytes 2359296 | tf_op jit(solution)/shard_map/all_to_all | solution.py:475
  47.4 0.8 copy-start
  49.2 8.6 %collective-permute-start.3 = (bf16[192,1536]{1,0:T(8,128)(2,1)S(1)}, bf16[192,1536]{1,0:T(8,128)(2,1)S(1)}, u32[]{:S(2)}, u32[]{:S(2)}) collective-permute-start(bf16[192,1536]{1,0:T(8,128)(2,1)S(1)} %pad_maximum_fusion.near_ref), channel_id=1, source_target_pairs={{0,1},{1,0},{2,3},{3,2},{4,5},{5,4},{6,7},{7,6},{8,9},{9,8},{10,11... | collective-permute-start | bytes 1769480 | tf_op jit(solution)/shard_map/ppermute | solution.py:471
  51.7 4.4 %copy-start.6 = (bf16[4,2,6,16,768]{4,3,2,1,0:T(8,128)(2,1)}, bf16[4,2,6,16,768]{4,3,2,1,0:T(8,128)(2,1)S(1)}, u32[]{:S(2)}) copy-start(bf16[4,2,6,16,768]{4,3,2,1,0:T(8,128)(2,1)S(1)} %maximum_maximum_fusion.north_ref.y_a_ref.y_b_ref) | copy-start | bytes 3538948
  51.7 4.4 %copy-start.13 = (pred[192]{0:T(512)(128)(4,1)S(1)}, pred[192]{0:T(512)(128)(4,1)}, u32[]{:S(2)}) copy-start(pred[192]{0:T(512)(128)(4,1)} %get-tuple-element.47) | copy-start | bytes 580
  51.7 6.1 %copy-start.1 = (bf16[512,384]{1,0:T(8,128)(2,1)S(1)}, bf16[512,384]{1,0:T(8,128)(2,1)}, u32[]{:S(2)}) copy-start(bf16[512,384]{1,0:T(8,128)(2,1)} %constant.135.clone.shuffle_ref.order_ref) | copy-start | bytes 1179652
  52.7 14.3 %collective-permute-start.5 = (bf16[4,2,4,16,768]{4,3,2,1,0:T(8,128)(2,1)}, bf16[4,2,4,16,768]{4,3,2,1,0:T(8,128)(2,1)S(1)}, u32[]{:S(2)}, u32[]{:S(2)}) collective-permute-start(bf16[4,2,4,16,768]{4,3,2,1,0:T(8,128)(2,1)} %slice.75), channel_id=1, source_target_pairs={{0,3},{1,0},{2,1},{3,2},{4,7},{5,4},{6,5},{7,6},{8,11},{9,8},{10,9... | collective-permute-start | bytes 2359304 | tf_op jit(solution)/shard_map/ppermute | solution.py:467
  61.4 13.2 %all-to-all-start.2 = ((bf16[8,64,512]{2,1,0:T(8,128)(2,1)}), bf16[8,64,512]{2,1,0:T(8,128)(2,1)S(1)}, u32[]{:S(2)}, u32[]{:S(2)}) async-start(bf16[8,64,512]{2,1,0:T(8,128)(2,1)} %merge_product.1), calls=%async_computation.2 | async-start | bytes 1048576 | tf_op jit(solution)/shard_map/all_to_all | solution.py:475
  66.9 0.9 copy-start.7
  74.6 0.8 copy-start.8
  82.1 15.7 %all-to-all-start.3 = ((bf16[16,56,128]{2,1,0:T(8,128)(2,1)}), bf16[16,56,128]{2,1,0:T(8,128)(2,1)S(1)}, u32[]{:S(2)}, u32[]{:S(2)}) async-start(bf16[16,56,128]{2,1,0:T(8,128)(2,1)} %get-tuple-element.23), calls=%async_computation.3 | async-start | bytes 458752 | tf_op jit(solution)/shard_map/all_to_all | solution.py:475
  97.9 16.3 %collective-permute-start.6 = (bf16[3,2,6,6,768]{4,1,3,2,0:T(2,128)(2,1)S(1)}, bf16[3,2,6,6,768]{4,1,3,2,0:T(2,128)(2,1)S(1)}, u32[]{:S(2)}, u32[]{:S(2)}) collective-permute-start(bf16[3,2,6,6,768]{4,1,3,2,0:T(2,128)(2,1)S(1)} %copy.57), channel_id=1, source_target_pairs={{0,4},{4,8},{8,12},{12,16},{16,20},{20,24},{24,28},{28,32},{32,36}... | collective-permute-start | bytes 995336 | tf_op jit(solution)/shard_map/ppermute | solution.py:467
  101.9 22.4 %all-to-all-start.4 = ((bf16[8,56,128]{2,1,0:T(8,128)(2,1)}), bf16[8,56,128]{2,1,0:T(8,128)(2,1)S(1)}, u32[]{:S(2)}, u32[]{:S(2)}) async-start(bf16[8,56,128]{2,1,0:T(8,128)(2,1)} %broadcast_in_dim.42), calls=%async_computation.4 | async-start | bytes 229376 | tf_op jit(solution)/shard_map/all_to_all | solution.py:475
  115.2 22.2 %copy-start.2 = (bf16[384,512]{1,0:T(8,128)(2,1)S(1)}, bf16[384,512]{1,0:T(8,128)(2,1)}, u32[]{:S(2)}) copy-start(bf16[384,512]{1,0:T(8,128)(2,1)} %constant.137.clone.close_ref) | copy-start | bytes 1179652
  115.2 10.1 %collective-permute-start.7 = (bf16[3,2,3,12,768]{4,1,3,2,0:T(2,128)(2,1)S(1)}, bf16[3,2,3,12,768]{4,1,3,2,0:T(2,128)(2,1)S(1)}, u32[]{:S(2)}, u32[]{:S(2)}) collective-permute-start(bf16[3,2,3,12,768]{4,1,3,2,0:T(2,128)(2,1)S(1)} %get-tuple-element.35), channel_id=1, source_target_pairs={{0,1},{1,2},{2,3},{3,0},{4,5},{5,6},{6,7},{7,4},{8,9},{9,10},{10,1... | collective-permute-start | bytes 995336 | tf_op jit(solution)/shard_map/ppermute | solution.py:467
  126.0 11.4 %all-to-all-start.5 = ((bf16[16,56,128]{2,1,0:T(8,128)(2,1)}), bf16[16,56,128]{2,1,0:T(8,128)(2,1)S(1)}, u32[]{:S(2)}, u32[]{:S(2)}) async-start(bf16[16,56,128]{2,1,0:T(8,128)(2,1)} %broadcast_in_dim.43), calls=%async_computation.5 | async-start | bytes 458752 | tf_op jit(solution)/shard_map/all_to_all | solution.py:475

commit v12 on v11

--- a/solution.py
+++ b/solution.py
@@ -205,7 +205,8 @@
 def score_grad(probs, o_win, v_win):
     d_probs = dot(by_head(o_win), v_win, ((1,), (1,)))
     probs = probs.astype(jnp.float32)
-    delta = jnp.sum(probs * d_probs, axis=-1, keepdims=True)
+    total = jnp.sum(probs, axis=-1, keepdims=True)
+    delta = jnp.sum(probs * d_probs, axis=-1, keepdims=True) / total
     return probs * (d_probs - delta)
 
 
@@ -539,7 +540,7 @@
     grads = window_grads(across, south, o_win, probs)
     grid = grads.reshape(3, 2, 6, PAD, 768)[:, :, :, :12]
     own, other = grid[:, :, :, :6], grid[:, :, :, 6:]
-    table_part, own, other = lax.optimization_barrier((table_part, own, other))
+    table_part, other = lax.optimization_barrier((table_part, other))
     western = from_behind(other, "lon", 1)
     fixed = jnp.concatenate([western, own], axis=3)
     southern = from_behind(fixed[:, :, 3:], "lat", 1)

time: 140 us -> 140 us (level)
  no operation moved by 1% of the time
where the time goes in v12:
time: 140 us; the launch traced here: 139 us
  starting transfers between devices  71.6 us (51%)
  Pallas kernels  26.3 us (19%)
  waiting for transfers between devices  22.3 us (16%)
  local copies, waits for them, and re-layouts  11.5 us (8%)
  other arithmetic  6.27 us (4%)
    all_to_all x6, starting transfers between devices, swap(): lax.all_to_all(shard, axis, 0, 0, tiled=True, axis_index_groups=groups)  32.5 us
    ppermute x5, starting transfers between devices, from_behind(): lax.ppermute(shard, axis, [(i, (i + by) % size) for i in range(size)])  29.8 us
    all_to_all x6, waiting for transfers between devices, swap(): lax.all_to_all(shard, axis, 0, 0, tiled=True, axis_index_groups=groups)  15.7 us
    ppermute x3, starting transfers between devices, partner(): lax.ppermute(shard, axis, [(i, i ^ bit) for i in range(lax.axis_size(axis...  9.22 us
    pallas_call x1, Pallas kernels, score_grads(): pl.pallas_call(scores_kernel, grid=(1,), in_specs=[whole_spec((8, 64, 512...  7.5 us
    ppermute x5, waiting for transfers between devices, from_behind(): lax.ppermute(shard, axis, [(i, (i + by) % size) for i in range(size)])  6.57 us
    pallas_call x1, Pallas kernels, window_probs(): pl.pallas_call(probs_kernel, grid=(STEPS,), in_specs=[north_spec(0, 2), s...  6.33 us
    pallas_call x1, Pallas kernels, window_grads(): pl.pallas_call(grads_kernel, grid=(STEPS,), in_specs=[north_spec(0, 3), s...  6.24 us
  transfers between devices with their start and end apart: 14, of which 7 were waited for; matrix products, arithmetic and copies ran while one was open for 9% of the time, Pallas kernels for 12%

profile of v12, /device:TPU:6, one launch (start us, length us, event | category | flops | bytes accessed | tf_op | source)
XLA Modules:
  0.0 139.0 jit_solution(6402823655736351648)
XLA Ops:
  0.6 0.9 copy-done.5
  1.5 0.9 pack_weight.1
  2.4 0.9 fusion.21
  3.4 14.1 %collective-permute-start = (bf16[2,3,3,1536]{3,0,2,1:T(2,128)(2,1)S(1)}, bf16[2,3,3,1536]{3,0,2,1:T(2,128)(2,1)S(1)}, u32[]{:S(2)}, u32[]{:S(2)}) collective-permute-start(bf16[2,3,3,1536]{3,0,2,1:T(2,128)(2,1)S(1)} %get-tuple-element.44), channel_id=1, source_target_pairs={{0,508},{4,0},{8,4},{12,8},{16,12},{20,16},{24,20},{28,24},{32,28}... | collective-permute-start | bytes 165896 | tf_op jit(solution)/shard_map/ppermute | solution.py:468
  17.5 3.6 %all-to-all-start = ((bf16[16,24,384]{2,1,0:T(8,128)(2,1)}), bf16[16,24,384]{2,1,0:T(8,128)(2,1)S(1)}, u32[]{:S(2)}, u32[]{:S(2)}) async-start(bf16[16,24,384]{2,1,0:T(8,128)(2,1)} %pack_weight.1), calls=%async_computation | async-start | bytes 589824 | tf_op jit(solution)/shard_map/all_to_all | solution.py:476
  21.1 0.3 fusion.19
  21.4 0.3 fusion.17
  21.8 0.1 pad.19.clone
  21.8 0.0 collective-permute-done
  21.8 0.2 maximum_maximum_fusion.1
  22.1 3.3 %collective-permute-start.1 = (bf16[48,1536]{1,0:T(8,128)(2,1)S(1)}, bf16[48,1536]{1,0:T(8,128)(2,1)S(1)}, u32[]{:S(2)}, u32[]{:S(2)}) collective-permute-start(bf16[48,1536]{1,0:T(8,128)(2,1)S(1)} %bitcast.32), channel_id=1, source_target_pairs={{0,2},{1,3},{2,0},{3,1},{4,6},{5,7},{6,4},{7,5},{8,10},{9,11},{10,... | collective-permute-start | bytes 442376 | tf_op jit(solution)/shard_map/ppermute | solution.py:472
  25.4 0.8 pad_maximum_fusion.1
  26.2 0.2 copy.48
  26.4 6.9 %collective-permute-start.4 = (bf16[4,2,6,6,768]{4,0,3,2,1:T(4,128)(2,1)S(1)}, bf16[4,2,6,6,768]{4,0,3,2,1:T(4,128)(2,1)S(1)}, u32[]{:S(2)}, u32[]{:S(2)}) collective-permute-start(bf16[4,2,6,6,768]{4,0,3,2,1:T(4,128)(2,1)S(1)} %copy.48), channel_id=1, source_target_pairs={{0,508},{4,0},{8,4},{12,8},{16,12},{20,16},{24,20},{28,24},{32,28}... | collective-permute-start | bytes 1327112 | tf_op jit(solution)/shard_map/ppermute | solution.py:468
  33.2 0.0 collective-permute-done.1
  33.2 0.7 pad_maximum_fusion.2
  34.0 4.0 %collective-permute-start.2 = (bf16[96,1536]{1,0:T(8,128)(2,1)}, bf16[96,1536]{1,0:T(8,128)(2,1)}, u32[]{:S(2)}, u32[]{:S(2)}) collective-permute-start(bf16[96,1536]{1,0:T(8,128)(2,1)} %pad_maximum_fusion.2), channel_id=1, source_target_pairs={{0,256},{4,260},{8,264},{12,268},{16,272},{20,276},{24,280},{28,28... | collective-permute-start | bytes 884744 | tf_op jit(solution)/shard_map/ppermute | solution.py:472
  38.0 2.3 %all-to-all-done = bf16[16,24,384]{2,1,0:T(8,128)(2,1)S(1)} async-done(((bf16[16,24,384]{2,1,0:T(8,128)(2,1)}), bf16[16,24,384]{2,1,0:T(8,128)(2,1)S(1)}, u32[]{:S(2)}, u32[]{:S(2)}) %all-to-all-start) | async-done | bytes 294944 | tf_op jit(solution)/shard_map/all_to_all | solution.py:476
  40.3 1.1 broadcast_in_dim.38
  41.4 4.6 %all-to-all-start.1 = ((bf16[4,384,384]{2,1,0:T(8,128)(2,1)}), bf16[4,384,384]{2,1,0:T(8,128)(2,1)S(1)}, u32[]{:S(2)}, u32[]{:S(2)}) async-start(bf16[4,384,384]{2,1,0:T(8,128)(2,1)} %broadcast_in_dim.38), calls=%async_computation.1 | async-start | bytes 2359296 | tf_op jit(solution)/shard_map/all_to_all | solution.py:476
  46.0 0.5 fusion.7
  46.7 0.1 pad.7.clone
  46.8 0.6 open_table.1.table_ref
  47.4 0.8 copy-done
  48.2 0.0 collective-permute-done.4
  48.2 0.1 copy.49
  48.2 1.0 pad_maximum_fusion.near_ref
  49.2 1.9 %collective-permute-start.3 = (bf16[192,1536]{1,0:T(8,128)(2,1)S(1)}, bf16[192,1536]{1,0:T(8,128)(2,1)S(1)}, u32[]{:S(2)}, u32[]{:S(2)}) collective-permute-start(bf16[192,1536]{1,0:T(8,128)(2,1)S(1)} %pad_maximum_fusion.near_ref), channel_id=1, source_target_pairs={{0,1},{1,0},{2,3},{3,2},{4,5},{5,4},{6,7},{7,6},{8,9},{9,8},{10,11... | collective-permute-start | bytes 1769480 | tf_op jit(solution)/shard_map/ppermute | solution.py:472
  51.2 0.5 maximum_maximum_fusion.north_ref.y_a_ref.y_b_ref
  51.7 0.0 copy-start.13
  51.7 0.0 copy-start.1
  51.7 0.9 slice.75
  52.7 3.4 %collective-permute-start.5 = (bf16[4,2,4,16,768]{4,3,2,1,0:T(8,128)(2,1)}, bf16[4,2,4,16,768]{4,3,2,1,0:T(8,128)(2,1)S(1)}, u32[]{:S(2)}, u32[]{:S(2)}) collective-permute-start(bf16[4,2,4,16,768]{4,3,2,1,0:T(8,128)(2,1)} %slice.75), channel_id=1, source_target_pairs={{0,3},{1,0},{2,1},{3,2},{4,7},{5,4},{6,5},{7,6},{8,11},{9,8},{10,9... | collective-permute-start | bytes 2359304 | tf_op jit(solution)/shard_map/ppermute | solution.py:468
  56.1 0.8 and_select_fusion.mask_ref
  56.9 0.9 all-to-all-done.1.w_ref
  57.9 0.0 collective-permute-done.3.far_ref
  57.9 3.6 %merge_product.1 = bf16[8,64,512]{2,1,0:T(8,128)(2,1)} custom-call(s32[8]{0:T(128)S(1)} %fusion.14.spot_ref, bf16[192,1536]{1,0:T(8,128)(2,1)S(1)} %pad_maximum_fusion.near_ref, bf16[192,1536]{1,0:T(8,128)(2,1)S(1)} %collective-permute-done.3.far_ref, bf16[4,384,384]{2,1,0:T(8,128)(2,1)S(1)} %all-to-all-done.1.w_ref, bf16[512,384]{1,0:T(8,128)(2,1)S(1)} %copy-done.1), custom_call_target="tpu_custom_call" | custom-call | tf_op jit(solution)/shard_map/merge_product/pallas_call | solution.py:391
  61.4 5.5 %all-to-all-start.2 = ((bf16[8,64,512]{2,1,0:T(8,128)(2,1)}), bf16[8,64,512]{2,1,0:T(8,128)(2,1)S(1)}, u32[]{:S(2)}, u32[]{:S(2)}) async-start(bf16[8,64,512]{2,1,0:T(8,128)(2,1)} %merge_product.1), calls=%async_computation.2 | async-start | bytes 1048576 | tf_op jit(solution)/shard_map/all_to_all | solution.py:476
  66.9 0.0 collective-permute-done.5.south_ref.y_south_ref
  67.0 0.9 copy-done.7
  67.8 6.3 %window_probs.1.p_ref = bf16[6,768,192]{2,1,0:T(8,128)(2,1)} custom-call(bf16[4,2,6,16,768]{4,3,2,1,0:T(8,128)(2,1)} %copy-done.6, bf16[4,2,4,16,768]{4,3,2,1,0:T(8,128)(2,1)} %copy-done.7, f32[6,48,384]{2,1,0:T(8,128)} %copy-done, bf16[2,384,192]{2,1,0:T(8,128)(2,1)} %constant.132.clone.spread_ref, f32[192,192]{1,0:T(8,128)} %and_select_fusion.mask_ref), custom_call_target="tpu_custom_call" | custom-call | tf_op jit(solution)/shard_map/window_probs/pallas_call | solution.py:373
  74.2 0.4 all-to-all-done.2.recv_ref
  74.6 0.8 copy-done.8
  75.4 7.5 %score_grads.1 = (bf16[6,192,128]{2,1,0:T(8,128)(2,1)}, bf16[16,56,128]{2,1,0:T(8,128)(2,1)}) custom-call(bf16[8,64,512]{2,1,0:T(8,128)(2,1)} %copy-done.8, bf16[512,384]{1,0:T(8,128)(2,1)} %constant.135.clone.shuffle_ref.order_ref, bf16[4,2,6,16,768]{4,3,2,1,0:T(8,128)(2,1)} %copy-done.6, bf16[4,2,6,16,768]{4,3,2,1,0:T(8,128)(2,1)} %copy-done.6, ...), custom_call_target="tpu_custom_call" | custom-call | tf_op jit(solution)/shard_map/score_grads/pallas_call | solution.py:403
  82.9 7.4 %all-to-all-start.3 = ((bf16[16,56,128]{2,1,0:T(8,128)(2,1)}), bf16[16,56,128]{2,1,0:T(8,128)(2,1)S(1)}, u32[]{:S(2)}, u32[]{:S(2)}) async-start(bf16[16,56,128]{2,1,0:T(8,128)(2,1)} %get-tuple-element.22), calls=%async_computation.3 | async-start | bytes 458752 | tf_op jit(solution)/shard_map/all_to_all | solution.py:476
  90.3 6.2 %window_grads.1 = bf16[3,192,768]{2,1,0:T(8,128)(2,1)} custom-call(bf16[4,2,6,16,768]{4,3,2,1,0:T(8,128)(2,1)} %copy-done.6, bf16[4,2,4,16,768]{4,3,2,1,0:T(8,128)(2,1)} %copy-done.7, bf16[6,192,128]{2,1,0:T(8,128)(2,1)} %get-tuple-element.23.o_ref, bf16[6,768,192]{2,1,0:T(8,128)(2,1)} %window_probs.1.p_ref), custom_call_target="tpu_custom_call" | custom-call | tf_op jit(solution)/shard_map/window_grads/pallas_call | solution.py:450
  96.6 1.4 %fusion.15 = (bf16[3,2,6,6,768]{4,3,2,1,0:T(8,128)(2,1)S(1)}, bf16[3,2,6,6,768]{4,3,2,1,0:T(8,128)(2,1)S(1)}) fusion(bf16[3,2,6,16,768]{4,3,2,1,0:T(8,128)(2,1)} %bitcast.31), kind=kLoop, calls=%fused_computation.53 | loop fusion | bytes 1327104 | tf_op jit(solution)/shard_map/slice | solution.py:542
  98.0 0.3 copy.56
  98.3 3.4 %collective-permute-start.6 = (bf16[3,2,6,6,768]{4,1,3,2,0:T(2,128)(2,1)S(1)}, bf16[3,2,6,6,768]{4,1,3,2,0:T(2,128)(2,1)S(1)}, u32[]{:S(2)}, u32[]{:S(2)}) collective-permute-start(bf16[3,2,6,6,768]{4,1,3,2,0:T(2,128)(2,1)S(1)} %copy.56), channel_id=1, source_target_pairs={{0,4},{4,8},{8,12},{12,16},{16,20},{20,24},{24,28},{28,32},{32,36}... | collective-permute-start | bytes 995336 | tf_op jit(solution)/shard_map/ppermute | solution.py:468
  101.7 0.7 broadcast_in_dim.42
  102.4 6.6 %all-to-all-start.4 = ((bf16[8,56,128]{2,1,0:T(8,128)(2,1)}), bf16[8,56,128]{2,1,0:T(8,128)(2,1)S(1)}, u32[]{:S(2)}, u32[]{:S(2)}) async-start(bf16[8,56,128]{2,1,0:T(8,128)(2,1)} %broadcast_in_dim.42), calls=%async_computation.4 | async-start | bytes 229376 | tf_op jit(solution)/shard_map/all_to_all | solution.py:476
  108.9 5.7 %collective-permute-done.6 = bf16[3,2,6,6,768]{4,1,3,2,0:T(2,128)(2,1)S(1)} collective-permute-done((bf16[3,2,6,6,768]{4,1,3,2,0:T(2,128)(2,1)S(1)}, bf16[3,2,6,6,768]{4,1,3,2,0:T(2,128)(2,1)S(1)}, u32[]{:S(2)}, u32[]{:S(2)}) %collective-permute-start.6) | collective-permute-done | bytes 331808 | tf_op jit(solution)/shard_map/ppermute | solution.py:468
  114.6 0.2 constant_dynamic-update-slice_fusion
  114.9 0.3 copy_dynamic-update-slice_fusion
  115.1 0.5 fusion.16
  115.6 0.0 copy-start.2
  115.6 2.1 %collective-permute-start.7 = (bf16[3,2,3,12,768]{4,1,3,2,0:T(2,128)(2,1)S(1)}, bf16[3,2,3,12,768]{4,1,3,2,0:T(2,128)(2,1)S(1)}, u32[]{:S(2)}, u32[]{:S(2)}) collective-permute-start(bf16[3,2,3,12,768]{4,1,3,2,0:T(2,128)(2,1)S(1)} %get-tuple-element.33), channel_id=1, source_target_pairs={{0,1},{1,2},{2,3},{3,0},{4,5},{5,6},{6,7},{7,4},{8,9},{9,10},{10,1... | collective-permute-start | bytes 995336 | tf_op jit(solution)/shard_map/ppermute | solution.py:468
  117.7 7.1 %all-to-all-done.4 = bf16[8,56,128]{2,1,0:T(8,128)(2,1)S(1)} async-done(((bf16[8,56,128]{2,1,0:T(8,128)(2,1)}), bf16[8,56,128]{2,1,0:T(8,128)(2,1)S(1)}, u32[]{:S(2)}, u32[]{:S(2)}) %all-to-all-start.4) | async-done | bytes 114720 | tf_op jit(solution)/shard_map/all_to_all | solution.py:476
  124.8 0.9 collective-permute-done.7
  125.7 0.7 broadcast_in_dim.43
  126.4 4.8 %all-to-all-start.5 = ((bf16[16,56,128]{2,1,0:T(8,128)(2,1)}), bf16[16,56,128]{2,1,0:T(8,128)(2,1)S(1)}, u32[]{:S(2)}, u32[]{:S(2)}) async-start(bf16[16,56,128]{2,1,0:T(8,128)(2,1)} %broadcast_in_dim.43), calls=%async_computation.5 | async-start | bytes 458752 | tf_op jit(solution)/shard_map/all_to_all | solution.py:476
  131.3 1.6 %fusion.2 = (bf16[2,6,12,768]{3,0,2,1:T(2,128)(2,1)}, bf16[2,6,12,768]{3,0,2,1:T(2,128)(2,1)}, bf16[2,6,12,768]{3,0,2,1:T(2,128)(2,1)}) fusion(bf16[3,2,3,12,768]{4,1,3,2,0:T(2,128)(2,1)S(1)} %get-tuple-element.34, bf16[3,2,3,12,768]{4,1,3,2,0:T(2,128)(2,1)S(1)} %collective-permute-done.7), kind=kLoop, calls=%fused_computation.12 | loop fusion | flops 331776 | bytes 1327104 | tf_op jit(solution)/shard_map/squeeze | solution.py:553
  132.9 4.9 %all-to-all-done.5.parts_ref = bf16[16,56,128]{2,1,0:T(8,128)(2,1)S(1)} async-done(((bf16[16,56,128]{2,1,0:T(8,128)(2,1)}), bf16[16,56,128]{2,1,0:T(8,128)(2,1)S(1)}, u32[]{:S(2)}, u32[]{:S(2)}) %all-to-all-start.5) | async-done | bytes 229408 | tf_op jit(solution)/shard_map/all_to_all | solution.py:476
  137.8 1.2 close_table.1
  (33 shorter events, 0.2 us)
Async XLA Ops:
  0.6 0.9 copy-start.5
  1.5 19.5 %copy-start.9 = (bf16[2,6,12,768]{3,0,2,1:T(2,128)(2,1)S(1)}, bf16[2,6,12,768]{3,0,2,1:T(2,128)(2,1)}, u32[]{:S(2)}) copy-start(bf16[2,6,12,768]{3,0,2,1:T(2,128)(2,1)} %param.22) | copy-start | bytes 663556
  1.5 19.5 %copy-start.10 = (bf16[2,6,12,768]{3,0,2,1:T(2,128)(2,1)S(1)}, bf16[2,6,12,768]{3,0,2,1:T(2,128)(2,1)}, u32[]{:S(2)}) copy-start(bf16[2,6,12,768]{3,0,2,1:T(2,128)(2,1)} %param.16) | copy-start | bytes 663556
  1.5 19.9 %copy-start.11 = (bf16[2,6,12,768]{3,0,2,1:T(2,128)(2,1)S(1)}, bf16[2,6,12,768]{3,0,2,1:T(2,128)(2,1)}, u32[]{:S(2)}) copy-start(bf16[2,6,12,768]{3,0,2,1:T(2,128)(2,1)} %param.20) | copy-start | bytes 663556
  1.5 19.9 %copy-start.12 = (bf16[2,6,12,768]{3,0,2,1:T(2,128)(2,1)S(1)}, bf16[2,6,12,768]{3,0,2,1:T(2,128)(2,1)}, u32[]{:S(2)}) copy-start(bf16[2,6,12,768]{3,0,2,1:T(2,128)(2,1)} %param.21) | copy-start | bytes 663556
  3.4 18.5 %collective-permute-start = (bf16[2,3,3,1536]{3,0,2,1:T(2,128)(2,1)S(1)}, bf16[2,3,3,1536]{3,0,2,1:T(2,128)(2,1)S(1)}, u32[]{:S(2)}, u32[]{:S(2)}) collective-permute-start(bf16[2,3,3,1536]{3,0,2,1:T(2,128)(2,1)S(1)} %get-tuple-element.44), channel_id=1, source_target_pairs={{0,508},{4,0},{8,4},{12,8},{16,12},{20,16},{24,20},{28,24},{32,28}... | collective-permute-start | bytes 165896 | tf_op jit(solution)/shard_map/ppermute | solution.py:468
  17.5 22.8 %all-to-all-start = ((bf16[16,24,384]{2,1,0:T(8,128)(2,1)}), bf16[16,24,384]{2,1,0:T(8,128)(2,1)S(1)}, u32[]{:S(2)}, u32[]{:S(2)}) async-start(bf16[16,24,384]{2,1,0:T(8,128)(2,1)} %pack_weight.1), calls=%async_computation | async-start | bytes 589824 | tf_op jit(solution)/shard_map/all_to_all | solution.py:476
  22.1 11.2 %collective-permute-start.1 = (bf16[48,1536]{1,0:T(8,128)(2,1)S(1)}, bf16[48,1536]{1,0:T(8,128)(2,1)S(1)}, u32[]{:S(2)}, u32[]{:S(2)}) collective-permute-start(bf16[48,1536]{1,0:T(8,128)(2,1)S(1)} %bitcast.32), channel_id=1, source_target_pairs={{0,2},{1,3},{2,0},{3,1},{4,6},{5,7},{6,4},{7,5},{8,10},{9,11},{10,... | collective-permute-start | bytes 442376 | tf_op jit(solution)/shard_map/ppermute | solution.py:472
  26.4 21.8 %collective-permute-start.4 = (bf16[4,2,6,6,768]{4,0,3,2,1:T(4,128)(2,1)S(1)}, bf16[4,2,6,6,768]{4,0,3,2,1:T(4,128)(2,1)S(1)}, u32[]{:S(2)}, u32[]{:S(2)}) collective-permute-start(bf16[4,2,6,6,768]{4,0,3,2,1:T(4,128)(2,1)S(1)} %copy.48), channel_id=1, source_target_pairs={{0,508},{4,0},{8,4},{12,8},{16,12},{20,16},{24,20},{28,24},{32,28}... | collective-permute-start | bytes 1327112 | tf_op jit(solution)/shard_map/ppermute | solution.py:468
  34.0 14.2 %collective-permute-start.2 = (bf16[96,1536]{1,0:T(8,128)(2,1)}, bf16[96,1536]{1,0:T(8,128)(2,1)}, u32[]{:S(2)}, u32[]{:S(2)}) collective-permute-start(bf16[96,1536]{1,0:T(8,128)(2,1)} %pad_maximum_fusion.2), channel_id=1, source_target_pairs={{0,256},{4,260},{8,264},{12,268},{16,272},{20,276},{24,280},{28,28... | collective-permute-start | bytes 884744 | tf_op jit(solution)/shard_map/ppermute | solution.py:472
  41.4 5.3 %copy-start.3 = (f32[1,24,3312]{2,1,0:T(8,128)S(1)}, f32[1,24,3312]{2,1,0:T(8,128)}, u32[]{:S(2)}) copy-start(f32[1,24,3312]{2,1,0:T(8,128)} %table_ref.1) | copy-start | bytes 953860
  41.4 5.3 %copy-start.4 = (bf16[2,138,384]{2,1,0:T(8,128)(2,1)S(1)}, bf16[2,138,384]{2,1,0:T(8,128)(2,1)}, u32[]{:S(2)}) copy-start(bf16[2,138,384]{2,1,0:T(8,128)(2,1)} %constant.136.clone.open_ref) | copy-start | bytes 635908
  41.4 16.4 %all-to-all-start.1 = ((bf16[4,384,384]{2,1,0:T(8,128)(2,1)}), bf16[4,384,384]{2,1,0:T(8,128)(2,1)S(1)}, u32[]{:S(2)}, u32[]{:S(2)}) async-start(bf16[4,384,384]{2,1,0:T(8,128)(2,1)} %broadcast_in_dim.38), calls=%async_computation.1 | async-start | bytes 2359296 | tf_op jit(solution)/shard_map/all_to_all | solution.py:476
  47.4 0.8 copy-start
  49.2 8.6 %collective-permute-start.3 = (bf16[192,1536]{1,0:T(8,128)(2,1)S(1)}, bf16[192,1536]{1,0:T(8,128)(2,1)S(1)}, u32[]{:S(2)}, u32[]{:S(2)}) collective-permute-start(bf16[192,1536]{1,0:T(8,128)(2,1)S(1)} %pad_maximum_fusion.near_ref), channel_id=1, source_target_pairs={{0,1},{1,0},{2,3},{3,2},{4,5},{5,4},{6,7},{7,6},{8,9},{9,8},{10,11... | collective-permute-start | bytes 1769480 | tf_op jit(solution)/shard_map/ppermute | solution.py:472
  51.7 4.4 %copy-start.6 = (bf16[4,2,6,16,768]{4,3,2,1,0:T(8,128)(2,1)}, bf16[4,2,6,16,768]{4,3,2,1,0:T(8,128)(2,1)S(1)}, u32[]{:S(2)}) copy-start(bf16[4,2,6,16,768]{4,3,2,1,0:T(8,128)(2,1)S(1)} %maximum_maximum_fusion.north_ref.y_a_ref.y_b_ref) | copy-start | bytes 3538948
  51.7 4.4 %copy-start.13 = (pred[192]{0:T(512)(128)(4,1)S(1)}, pred[192]{0:T(512)(128)(4,1)}, u32[]{:S(2)}) copy-start(pred[192]{0:T(512)(128)(4,1)} %get-tuple-element.45) | copy-start | bytes 580
  51.7 6.1 %copy-start.1 = (bf16[512,384]{1,0:T(8,128)(2,1)S(1)}, bf16[512,384]{1,0:T(8,128)(2,1)}, u32[]{:S(2)}) copy-start(bf16[512,384]{1,0:T(8,128)(2,1)} %constant.135.clone.shuffle_ref.order_ref) | copy-start | bytes 1179652
  52.7 14.3 %collective-permute-start.5 = (bf16[4,2,4,16,768]{4,3,2,1,0:T(8,128)(2,1)}, bf16[4,2,4,16,768]{4,3,2,1,0:T(8,128)(2,1)S(1)}, u32[]{:S(2)}, u32[]{:S(2)}) collective-permute-start(bf16[4,2,4,16,768]{4,3,2,1,0:T(8,128)(2,1)} %slice.75), channel_id=1, source_target_pairs={{0,3},{1,0},{2,1},{3,2},{4,7},{5,4},{6,5},{7,6},{8,11},{9,8},{10,9... | collective-permute-start | bytes 2359304 | tf_op jit(solution)/shard_map/ppermute | solution.py:468
  61.4 13.2 %all-to-all-start.2 = ((bf16[8,64,512]{2,1,0:T(8,128)(2,1)}), bf16[8,64,512]{2,1,0:T(8,128)(2,1)S(1)}, u32[]{:S(2)}, u32[]{:S(2)}) async-start(bf16[8,64,512]{2,1,0:T(8,128)(2,1)} %merge_product.1), calls=%async_computation.2 | async-start | bytes 1048576 | tf_op jit(solution)/shard_map/all_to_all | solution.py:476
  66.9 0.9 copy-start.7
  74.6 0.8 copy-start.8
  82.9 15.4 %all-to-all-start.3 = ((bf16[16,56,128]{2,1,0:T(8,128)(2,1)}), bf16[16,56,128]{2,1,0:T(8,128)(2,1)S(1)}, u32[]{:S(2)}, u32[]{:S(2)}) async-start(bf16[16,56,128]{2,1,0:T(8,128)(2,1)} %get-tuple-element.22), calls=%async_computation.3 | async-start | bytes 458752 | tf_op jit(solution)/shard_map/all_to_all | solution.py:476
  98.3 16.3 %collective-permute-start.6 = (bf16[3,2,6,6,768]{4,1,3,2,0:T(2,128)(2,1)S(1)}, bf16[3,2,6,6,768]{4,1,3,2,0:T(2,128)(2,1)S(1)}, u32[]{:S(2)}, u32[]{:S(2)}) collective-permute-start(bf16[3,2,6,6,768]{4,1,3,2,0:T(2,128)(2,1)S(1)} %copy.56), channel_id=1, source_target_pairs={{0,4},{4,8},{8,12},{12,16},{16,20},{20,24},{24,28},{28,32},{32,36}... | collective-permute-start | bytes 995336 | tf_op jit(solution)/shard_map/ppermute | solution.py:468
  102.4 22.4 %all-to-all-start.4 = ((bf16[8,56,128]{2,1,0:T(8,128)(2,1)}), bf16[8,56,128]{2,1,0:T(8,128)(2,1)S(1)}, u32[]{:S(2)}, u32[]{:S(2)}) async-start(bf16[8,56,128]{2,1,0:T(8,128)(2,1)} %broadcast_in_dim.42), calls=%async_computation.4 | async-start | bytes 229376 | tf_op jit(solution)/shard_map/all_to_all | solution.py:476
  115.6 22.2 %copy-start.2 = (bf16[384,512]{1,0:T(8,128)(2,1)S(1)}, bf16[384,512]{1,0:T(8,128)(2,1)}, u32[]{:S(2)}) copy-start(bf16[384,512]{1,0:T(8,128)(2,1)} %constant.137.clone.close_ref) | copy-start | bytes 1179652
  115.6 10.1 %collective-permute-start.7 = (bf16[3,2,3,12,768]{4,1,3,2,0:T(2,128)(2,1)S(1)}, bf16[3,2,3,12,768]{4,1,3,2,0:T(2,128)(2,1)S(1)}, u32[]{:S(2)}, u32[]{:S(2)}) collective-permute-start(bf16[3,2,3,12,768]{4,1,3,2,0:T(2,128)(2,1)S(1)} %get-tuple-element.33), channel_id=1, source_target_pairs={{0,1},{1,2},{2,3},{3,0},{4,5},{5,6},{6,7},{7,4},{8,9},{9,10},{10,1... | collective-permute-start | bytes 995336 | tf_op jit(solution)/shard_map/ppermute | solution.py:468
  126.4 11.4 %all-to-all-start.5 = ((bf16[16,56,128]{2,1,0:T(8,128)(2,1)}), bf16[16,56,128]{2,1,0:T(8,128)(2,1)S(1)}, u32[]{:S(2)}, u32[]{:S(2)}) async-start(bf16[16,56,128]{2,1,0:T(8,128)(2,1)} %broadcast_in_dim.43), calls=%async_computation.5 | async-start | bytes 458752 | tf_op jit(solution)/shard_map/all_to_all | solution.py:476
